TPU v7x, 32 devices: a whole 2x2x4 slice. The times are simulated.
32 devices in a mesh: groups: 2 (over x), expert: 8 (over z, y), wave: 2 (over core).
Axes of the slice: x: 2, y: 2, z: 4, core: 2. Of those that a mesh axis runs over, the one named last changes fastest.
Arguments:
- hidden_rows: bfloat16 [512, 2, 2048], P(('groups', 'expert', 'wave')), parts along dimension 0, may hold values from -6 to 6
- expert_ids: int32 [512, 2, 8], P(('groups', 'expert', 'wave')), parts along dimension 0, may hold values from 0 to 15, all different within a row; in each aligned block of 32 rows (0 to 31, 32 to 63, ..., all dimensions but the last counted through in order) at most 24 rows name the same one
- route_weights: float32 [512, 2, 8], P(('groups', 'expert', 'wave')), parts along dimension 0, may hold values from 0.1 to 1
- w_gate: bfloat16 [16, 2048, 768], P('expert', None, 'wave'), may hold values from -0.125 to 0.125
- w_up: bfloat16 [16, 2048, 768], P('expert', None, 'wave'), may hold values from -0.125 to 0.125
- w_down: bfloat16 [16, 768, 2048], P('expert', 'wave'), may hold values from -0.21875 to 0.21875
- codes: int32 [512, 2, 16], P(('groups', 'expert', 'wave')), parts along dimension 0, may hold values from 0 to 1023
- owner_slot: int32 [512], P(('groups', 'expert', 'wave')), parts along dimension 0, may hold values from 0 to 255, as said below
- code_table: bfloat16 [16, 1024, 1024], P(None, 'expert'), may hold values from -1.5 to 1.5
- conv_state: bfloat16 [512, 6, 1024], P(('groups', 'expert', 'wave')), parts along dimension 0, may hold values from -6 to 6
- conv_taps: float32 [7, 1024], replicated, may hold values from -2.4 to 2.4
- conv_bias: float32 [1024], replicated, may hold values from -3 to 3
- upsample: bfloat16 [1024, 512], replicated, may hold values from -0.1875 to 0.1875
Outputs:
- moe_out: bfloat16 [512, 2, 2048], P(('groups', 'expert', 'wave')), parts along dimension 0
- waveform: bfloat16 [512, 2, 512], P(('groups', 'expert', 'wave')), parts along dimension 0
- new_state: bfloat16 [512, 6, 1024], P(('groups', 'expert', 'wave')), parts along dimension 0
There are 2 independent parts, one for each index of `groups`. A program takes and returns all parts, laid end to end along the dimension named above; an argument that names none is the same for every part. Nothing has to cross between parts.
Inputs may be any that keep to these rules, and one draw needn't show every extreme that they name: `expert_ids`: each row names 8 different experts; among the 32 rows of one device no expert is named more than 24 times, a bound that some block reaches. `owner_slot`: A permutation of the slots. Slot o lies on the device holding rows o of the decoder's arrays; a session's slot lies on a device with the same index along wave as the session's own device, so every device holds 16 slots.
All inputs are finite; a program needn't handle non-finite values.
Results may differ from a plain program's by a relative error of at most 0.012.
Values may be sent and summed in bfloat16 or wider, within the bound.
No kernel may reach another device: no remote copies, remote signals or barrier semaphores. Data moves between devices by JAX's collectives and lax.ppermute only.
A program may use at most 64 MiB of HBM per device.

v0:
```python
import jax
import jax.numpy as jnp
from jax import lax
from jax.sharding import PartitionSpec as P


def expert_work(received, w_gate, w_up, w_down):
    gate_val = jnp.einsum("secd,edf->secf", received, w_gate, preferred_element_type=jnp.float32)
    up_val = jnp.einsum("secd,edf->secf", received, w_up, preferred_element_type=jnp.float32)
    activated = (jax.nn.silu(gate_val) * up_val).astype(jnp.bfloat16)
    result = jnp.einsum("secf,efd->secd", activated, w_down, preferred_element_type=jnp.float32)
    return result.astype(jnp.bfloat16)


def mixture(hidden_rows, expert_ids, route_weights, w_gate, w_up, w_down):
    n_expert = lax.axis_size("expert")
    n_wave = lax.axis_size("wave")
    sessions_here, steps_count, width = hidden_rows.shape
    top_count = expert_ids.shape[2]
    local_experts = w_gate.shape[0]
    experts_all = n_expert * local_experts
    row_count = sessions_here * steps_count
    capacity = max(2, 3 * row_count * top_count // (2 * experts_all))
    tok_rows = hidden_rows.reshape(row_count, width)
    chosen = expert_ids.reshape(row_count * top_count)
    matches = (chosen[:, None] == jnp.arange(experts_all, dtype=jnp.int32)[None, :]).astype(
        jnp.int32
    )
    earlier = jnp.cumsum(matches, axis=0) - matches
    rank_in = jnp.sum(earlier * matches, axis=1)
    slot_index = chosen * capacity + rank_in
    slot_total = experts_all * capacity
    picker = (slot_index[:, None] == jnp.arange(slot_total, dtype=jnp.int32)[None, :]).astype(
        jnp.bfloat16
    )
    picker = jnp.sum(picker.reshape(row_count, top_count, slot_total), axis=1)
    outgoing = jnp.einsum("rs,rd->sd", picker, tok_rows, preferred_element_type=jnp.float32).astype(
        jnp.bfloat16
    )
    block_slots = local_experts * capacity
    outgoing = outgoing.reshape(n_expert, block_slots, width)
    arrived = lax.all_to_all(outgoing, "expert", split_axis=0, concat_axis=0, tiled=True)
    pooled = lax.all_gather(arrived, "wave", axis=0, tiled=True)
    partial_value = expert_work(
        pooled.reshape(n_wave * n_expert, local_experts, capacity, width), w_gate, w_up, w_down
    )
    own_half = lax.psum_scatter(
        partial_value.astype(jnp.float32)
        .reshape(n_wave * n_expert, block_slots, width)
        .astype(jnp.bfloat16),
        "wave",
        scatter_dimension=0,
        tiled=True,
    )
    slot_out = lax.all_to_all(own_half, "expert", split_axis=0, concat_axis=0, tiled=True)
    slot_flat = slot_out.reshape(slot_total, width)
    gathered_out = slot_flat[slot_index].astype(jnp.float32).reshape(row_count, top_count, width)
    mixed = jnp.sum(gathered_out * route_weights.reshape(row_count, top_count, 1), axis=1)
    return mixed.astype(jnp.bfloat16).reshape(sessions_here, steps_count, width)


def frames_path(codes, owner_slot, code_table, conv_state, conv_taps, conv_bias, upsample):
    n_expert = lax.axis_size("expert")
    n_wave = lax.axis_size("wave")
    sessions_here, frame_count, book_count = codes.shape
    shard_codes = code_table.shape[1]
    channels = code_table.shape[2]
    all_codes, all_owners = (
        lax.all_gather(codes, "expert", axis=0, tiled=True),
        lax.all_gather(owner_slot, "expert", axis=0, tiled=True),
    )
    position = all_owners // sessions_here // n_wave * sessions_here + all_owners % sessions_here
    ordered = jnp.zeros_like(all_codes).at[position].set(all_codes)
    shifted = ordered - lax.axis_index("expert") * shard_codes
    member = (shifted[..., None] == jnp.arange(shard_codes, dtype=jnp.int32)).astype(jnp.bfloat16)
    member = member.reshape(n_expert * sessions_here * frame_count, book_count * shard_codes)
    partial_value = jnp.dot(
        member,
        code_table.reshape(book_count * shard_codes, channels),
        preferred_element_type=jnp.float32,
    )
    frames = lax.psum_scatter(
        partial_value.reshape(n_expert * sessions_here, frame_count, channels).astype(jnp.bfloat16),
        "expert",
        scatter_dimension=0,
        tiled=True,
    ).astype(jnp.float32)
    history = jnp.concatenate([conv_state.astype(jnp.float32), frames], axis=1)
    state_len = conv_state.shape[1]
    kernel_len = conv_taps.shape[0]
    filtered = jnp.broadcast_to(conv_bias, frames.shape)
    for offset in range(kernel_len):
        filtered = (
            filtered
            + conv_taps[offset] * history[:, state_len - offset : state_len - offset + frame_count]
        )
    decoded = jax.nn.gelu(filtered).astype(jnp.bfloat16)
    samples = jnp.dot(
        decoded.reshape(sessions_here * frame_count, channels),
        upsample,
        preferred_element_type=jnp.float32,
    )
    samples = samples.astype(jnp.bfloat16).reshape(sessions_here, frame_count, upsample.shape[1])
    carried = history[:, frame_count:].astype(jnp.bfloat16)
    return (samples, carried)


def per_device(
    hidden_rows,
    expert_ids,
    route_weights,
    w_gate,
    w_up,
    w_down,
    codes,
    owner_slot,
    code_table,
    conv_state,
    conv_taps,
    conv_bias,
    upsample,
):
    mixed = mixture(hidden_rows, expert_ids, route_weights, w_gate, w_up, w_down)
    samples, carried = frames_path(
        codes, owner_slot, code_table, conv_state, conv_taps, conv_bias, upsample
    )
    return (mixed, samples, carried)


def solution(mesh):
    placed = (
        P(("groups", "expert", "wave"), None, None),
        P(("groups", "expert", "wave"), None, None),
        P(("groups", "expert", "wave"), None, None),
        P("expert", None, "wave"),
        P("expert", None, "wave"),
        P("expert", "wave", None),
        P(("groups", "expert", "wave"), None, None),
        P(("groups", "expert", "wave")),
        P(None, "expert", None),
        P(("groups", "expert", "wave"), None, None),
        P(),
        P(),
        P(),
    )
    return jax.shard_map(
        per_device,
        mesh=mesh,
        in_specs=placed,
        out_specs=(
            P(("groups", "expert", "wave"), None, None),
            P(("groups", "expert", "wave"), None, None),
            P(("groups", "expert", "wave"), None, None),
        ),
        check_vma=False,
    )
```

profile of v0, /device:TPU:0, one launch (start us, length us, event | category | flops | bytes accessed | tf_op | source)
XLA Modules:
  0.0 267.9 jit_solution(18359833729936917262)
XLA Ops:
  8.0 0.0 all-gather.2.cloned.1.call-start
  8.1 0.9 broadcast_multiply_fusion
  8.9 0.8 copy.49
  9.7 0.1 eq.57
  9.8 0.1 eq.61
  9.9 0.1 copy.48
  10.0 0.6 reduce-window.6
  10.6 0.2 slice_reduce_fusion
  10.8 0.1 fusion.66
  10.9 0.1 reduce_sum.35
  11.0 0.2 fusion.47
  11.2 1.0 reshape.124
  12.2 0.6 convolution_convert_fusion.1
  12.8 44.2 %all_to_all.10 = bf16[8,48,2048]{2,1,0:T(8,128)(2,1)} all-to-all(bf16[8,48,2048]{2,1,0:T(8,128)(2,1)S(1)} %bitcast.94), channel_id=1, replica_groups=mesh['groups'=2,'expert'=8,'wave'=2] {'expert'}, dimensions={0} | all-to-all | bytes 3145728 | tf_op jit(solution)/shard_map/all_to_all | solution.py:42
  57.0 0.0 reduce-scatter.3.cloned.1.call-start
  57.1 11.2 %all-gather.2.cloned.1.call-done = bf16[16,48,2048]{2,1,0:T(8,128)(2,1)} async-done(((bf16[8,48,2048]{2,1,0:T(8,128)(2,1)}), bf16[16,48,2048]{2,1,0:T(8,128)(2,1)}) %all-gather.2.cloned.1.call-update) | async-done | bytes 3145744 | tf_op jit(solution)/shard_map/all_gather | solution.py:43
  68.3 5.7 %fusion.13 = f32[16,2,24,384]{3,2,0,1:T(8,128)} fusion(bf16[2,2048,384]{2,1,0:T(8,128)(2,1)} %param.16, bf16[16,2,24,2048]{3,2,1,0:T(8,128)(2,1)} %bitcast.106), kind=kOutput, calls=%fused_computation.17 | convolution fusion | flops 1207959552 | bytes 7471104 | tf_op jit(solution)/shard_map/secd,edf->secf/dot_general | solution.py:8
  74.0 8.3 %fusion.7 = bf16[16,2,24,2048]{3,2,0,1:T(8,128)(2,1)} fusion(bf16[2,384,2048]{2,1,0:T(8,128)(2,1)S(1)} %copy-done, bf16[2,2048,384]{2,1,0:T(8,128)(2,1)} %param.17, bf16[16,2,24,2048]{3,2,1,0:T(8,128)(2,1)} %bitcast.107, f32[16,2,24,384]{3,2,0,1:T(8,128)} %fusion.13), kind=kOutput, calls=%fused_computation.10 | convolution fusion | flops 2419261440 | bytes 13762560 | tf_op jit(solution)/shard_map/secf,efd->secd/dot_general | solution.py:11
  82.3 4.0 %copy.54 = bf16[16,2,24,2048]{3,2,1,0:T(8,128)(2,1)} copy(bf16[16,2,24,2048]{3,2,0,1:T(8,128)(2,1)} %fusion.7) | data formatting | bytes 6291456 | tf_op jit(solution)/shard_map/convert_element_type | solution.py:12
  86.3 12.2 %reduce-scatter.3.cloned.1.call-done = bf16[8,48,2048]{2,1,0:T(8,128)(2,1)} async-done(((bf16[16,48,2048]{2,1,0:T(8,128)(2,1)}), bf16[8,48,2048]{2,1,0:T(8,128)(2,1)}) %reduce-scatter.3.cloned.1.call-update) | async-done | bytes 1572880 | tf_op jit(solution)/shard_map/reduce_scatter | solution.py:47
  98.5 5.7 %all-to-all-start.1 = ((bf16[8,48,2048]{2,1,0:T(8,128)(2,1)}), bf16[8,48,2048]{2,1,0:T(8,128)(2,1)}, u32[]{:S(2)}, u32[]{:S(2)}) async-start(bf16[8,48,2048]{2,1,0:T(8,128)(2,1)} %reduce-scatter.3.cloned.1.call-done), calls=%async_computation.2 | async-start | bytes 3145728 | tf_op jit(solution)/shard_map/all_to_all | solution.py:55
  104.3 0.0 reduce-scatter.5.cloned.1.call-start
  104.3 0.6 dynamic-slice
  105.6 0.2 dynamic-update-slice
  105.8 36.2 %all-reduce = s32[128]{0:T(128)S(1)} all-reduce(s32[128]{0:T(128)S(1)} %dynamic-update-slice), channel_id=1, replica_groups=mesh['groups'=2,'expert'=8,'wave'=2] {'expert'}, use_global_device_ids=true, to_apply=%add | all-reduce | flops 128 | bytes 1024
  142.0 30.7 %all_gather.11 = s32[128,2,16]{2,1,0:T(2,128)S(1)} all-gather(s32[16,2,16]{2,1,0:T(2,128)S(1)} %copy-done.2), channel_id=1, replica_groups=mesh['groups'=2,'expert'=8,'wave'=2] {'expert'}, dimensions={0}, use_global_device_ids=true | all-gather | bytes 18432 | tf_op jit(solution)/shard_map/all_gather | solution.py:69
  172.8 4.3 %scatter_fusion = s32[128,2,16]{2,1,0:T(2,128)S(1)} fusion(s32[128,2,16]{2,1,0:T(2,128)S(1)} %broadcast_in_dim.7, s32[128]{0:T(128)S(1)} %compare_select_fusion.1, s32[128,2,16]{2,1,0:T(2,128)S(1)} %all_gather.11), kind=kCustom, calls=%fused_computation.1 | custom fusion | bytes 49664 | tf_op jit(solution)/shard_map/scatter | solution.py:73
  177.1 0.1 copy.57
  177.2 4.3 %fusion.36 = bf16[128,2,1024]{2,0,1:T(8,128)(2,1)} fusion(bf16[16,128,1024]{2,1,0:T(8,128)(2,1)} %param.21, s32[128,2,16]{0,2,1:T(8,128)S(1)} %broadcast_subtract_fusion), kind=kOutput, calls=%fused_computation.22 | convolution fusion | flops 1074528256 | bytes 4734976 | tf_op jit(solution)/shard_map/dot_general | solution.py:77
  181.5 0.0 reduce-scatter.5.cloned.1.call-update
  181.5 0.7 mul.146
  182.2 0.1 copy.56
  182.3 1.0 convert_element_type.75
  183.3 0.7 compare_select_fusion
  184.0 0.6 pad_clamp_fusion
  184.5 1.6 fusion.70
  186.2 56.5 %reduce-scatter.5.cloned.1.call-done = bf16[16,2,1024]{2,0,1:T(8,128)(2,1)} async-done(((bf16[128,2,1024]{2,0,1:T(8,128)(2,1)}), bf16[16,2,1024]{2,0,1:T(8,128)(2,1)}) %reduce-scatter.5.cloned.1.call-update) | async-done | bytes 65552 | tf_op jit(solution)/shard_map/reduce_scatter | solution.py:82
  242.7 0.8 convert_element_type.74
  243.6 0.6 copy-done.1
  244.2 0.9 fusion.55
  245.1 0.7 copy.58
  245.8 1.5 reshape.128
  247.3 2.2 convolution_convert_fusion.2
  249.4 1.4 reshape.129
  250.8 1.6 fusion.45
  252.4 5.1 %gather_fusion = bf16[256,2048]{1,0:T(8,128)(2,1)} fusion(bf16[384,2048]{1,0:T(8,128)(2,1)} %bitcast.14, s32[1024]{0:T(1024)} %pad_clamp_fusion), kind=kCustom, calls=%fused_computation | custom fusion | bytes 2098176 | tf_op jit(solution)/shard_map/gather | solution.py:57
  257.5 2.2 fusion.12
  259.7 0.8 convert_element_type.72
  (24 shorter events, 0.2 us)
Async XLA Ops:
  8.0 66.0 %copy-start = (bf16[2,384,2048]{2,1,0:T(8,128)(2,1)S(1)}, bf16[2,384,2048]{2,1,0:T(8,128)(2,1)}, u32[]{:S(2)}) copy-start(bf16[2,384,2048]{2,1,0:T(8,128)(2,1)} %param.18) | copy-start | bytes 9437188
  8.0 60.3 %all-gather.2.cloned.1.call-start = ((), (), s32[]{:S(2)}) async-start(), calls=%async_computation.4 | async-start | bytes 4718592 | tf_op jit(solution)/shard_map/all_gather | solution.py:43
  10.9 46.1 %copy-start.3 = (s32[256]{0:T(256)}, s32[256]{0:T(256)S(1)}, u32[]{:S(2)}) copy-start(s32[256]{0:T(256)S(1)} %fusion.66) | copy-start | bytes 3076
  57.0 41.5 %reduce-scatter.3.cloned.1.call-start = ((), (), s32[]{:S(2)}) async-start(), calls=%async_computation.5 | async-start | bytes 4718592 | tf_op jit(solution)/shard_map/reduce_scatter | solution.py:47
  86.3 18.1 %copy-start.6 = (u32[32]{0:T(128)S(1)}, u32[32]{0:T(128)}, u32[]{:S(2)}) copy-start(u32[32]{0:T(128)} %constant.84) | copy-start | bytes 388
  86.3 19.3 %copy-start.5 = (s32[16]{0:T(128)S(1)}, s32[16]{0:T(128)}, u32[]{:S(2)}) copy-start(s32[16]{0:T(128)} %param.20) | copy-start | bytes 196
  86.3 55.7 %copy-start.2 = (s32[16,2,16]{2,1,0:T(2,128)S(1)}, s32[16,2,16]{2,1,0:T(2,128)}, u32[]{:S(2)}) copy-start(s32[16,2,16]{2,1,0:T(2,128)} %param.19) | copy-start | bytes 6148
  98.5 153.9 %all-to-all-start.1 = ((bf16[8,48,2048]{2,1,0:T(8,128)(2,1)}), bf16[8,48,2048]{2,1,0:T(8,128)(2,1)}, u32[]{:S(2)}, u32[]{:S(2)}) async-start(bf16[8,48,2048]{2,1,0:T(8,128)(2,1)} %reduce-scatter.3.cloned.1.call-done), calls=%async_computation.2 | async-start | bytes 3145728 | tf_op jit(solution)/shard_map/all_to_all | solution.py:55
  104.3 138.5 %reduce-scatter.5.cloned.1.call-start = ((), (), s32[]{:S(2)}) async-start(), calls=%async_computation.6 | async-start | bytes 589824 | tf_op jit(solution)/shard_map/reduce_scatter | solution.py:82
  177.2 5.0 %copy-start.4 = (f32[16,2,8]{0,2,1:T(8,128)S(1)}, f32[16,2,8]{0,2,1:T(8,128)}, u32[]{:S(2)}) copy-start(f32[16,2,8]{0,2,1:T(8,128)} %param.15) | copy-start | bytes 3076
  243.6 0.7 copy-start.1
Sparse Core Ops, SparseCore 0:
  57.1 11.1 all-gather.1
  86.4 12.0 reduce-scatter.2
Sparse Core Ops, SparseCore 1:
  181.6 61.0 reduce-scatter.4
where the time goes:
time: 269 us; the launch traced here: 268 us
  blocking collectives  111 us (41%)
  waiting for transfers between devices  80 us (30%)
  local copies, waits for them, and re-layouts  24 us (9%)
  matrix products  21.1 us (8%)
  between operations  16.3 us (6%)
  other arithmetic  9.58 us (4%)
  starting transfers between devices  5.87 us (2%)
    reduce_scatter x1, waiting for transfers between devices, frames_path(): lax.psum_scatter(partial_value.reshape(n_expert * sessions_here, frame_co...  56.5 us
    all_to_all x1, blocking collectives, mixture(): lax.all_to_all(outgoing, 'expert', split_axis=0, concat_axis=0, tiled=True)  44.2 us
    unnamed x1, blocking collectives  36.2 us
    all_gather x1, blocking collectives, frames_path(): lax.all_gather(codes, 'expert', axis=0, tiled=True)  30.7 us
    reduce_scatter x1, waiting for transfers between devices, mixture(): lax.psum_scatter(partial_value.astype(jnp.float32).reshape(n_wave * n_exp...  12.2 us
    all_gather x1, waiting for transfers between devices, mixture(): pooled = lax.all_gather(arrived, 'wave', axis=0, tiled=True)  11.2 us
    dot_general x1, matrix products, expert_work(): jnp.einsum('secf,efd->secd', activated, w_down, preferred_element_type=jn...  8.29 us
    all_to_all x1, starting transfers between devices, mixture(): lax.all_to_all(own_half, 'expert', split_axis=0, concat_axis=0, tiled=True)  5.75 us
  transfers between devices with their start and end apart: 4, of which 3 were waited for; matrix products, arithmetic and copies ran while one was open for 9% of the time, Pallas kernels for 0%

commit v1 on v0

v1 whole, which is shorter than its diff:
```python
import functools

import jax
import jax.numpy as jnp
from jax import lax
from jax.experimental import pallas as pl
from jax.experimental.pallas import tpu as pltpu
from jax.sharding import PartitionSpec as P

F32 = jnp.float32
BF16 = jnp.bfloat16
VMEM_LIMIT = 56 * 1024 * 1024


def ring_order(count):
    return list(range(0, count, 2)) + list(range(1, count, 2))[::-1]


def shift(value, distance):
    count = lax.axis_size("expert")
    ring = ring_order(count)
    pairs = [(ring[i], ring[(i + distance) % count]) for i in range(count)]
    return lax.ppermute(value, "expert", pairs)


def swap_wave(value):
    return lax.ppermute(value, "wave", [(0, 1), (1, 0)])


def spread(own):
    count = lax.axis_size("expert")
    half = count // 2
    blocks, step_of = {0: own}, {0: 0}

    def put(offset, value, step):
        blocks[offset % count], step_of[offset % count] = value, step

    put(-1, shift(own, 1), 1)
    put(1, shift(own, -1), 1)
    put(half, shift(own, half), 1)
    for step in range(2, count // 4 + 1):
        put(-step, shift(blocks[(1 - step) % count], 1), step)
        put(step, shift(blocks[step - 1], -1), step)
        put(half - step + 1, shift(blocks[half - step + 2], 1), step)
        put(half + step - 1, shift(blocks[half + step - 2], -1), step)
    return blocks, step_of


def add(*parts):
    total = parts[0].astype(F32)
    for part in parts[1:]:
        total = total + part.astype(F32)
    return total


def collect(parts):
    count = lax.axis_size("expert")
    half = count // 2
    parts = dict(parts)
    for step in range(count // 4, 1, -1):
        moves = (
            (step, 1, step - 1),
            (-step, -1, 1 - step),
            (half + step - 1, 1, half + step - 2),
            (half - step + 1, -1, half - step + 2),
        )
        arrived = [(into % count, shift(parts[come % count], way)) for come, way, into in moves]
        for into in dict(arrived):
            terms = [value for place, value in arrived if place == into]
            parts[into] = add(parts[into], *terms).astype(BF16)
    return parts[0], shift(parts[1], 1), shift(parts[count - 1], -1), shift(parts[half], half)


def experts_kernel(width, expert_count, block_count, first_ref, *refs):
    blocks = refs[:block_count]
    gate_hbm, up_hbm, down_hbm, out_ref, rows_ref, gate_up, down, act_ref, sems = refs[block_count:]
    local = gate_hbm.shape[0]
    units = gate_hbm.shape[2]
    copies = []
    for j in range(local):
        copies.append(
            (
                pltpu.make_async_copy(gate_hbm.at[j], gate_up.at[j, :, 0:units], sems.at[j, 0]),
                pltpu.make_async_copy(
                    up_hbm.at[j], gate_up.at[j, :, units : 2 * units], sems.at[j, 1]
                ),
            )
        )
        for copy in copies[-1]:
            copy.start()
    down_copies = [
        pltpu.make_async_copy(down_hbm.at[j], down.at[j * units : (j + 1) * units], sems.at[j, 2])
        for j in range(local)
    ]
    for copy in down_copies:
        copy.start()
    rows = blocks[0].shape[0]
    weights = []
    for i, block in enumerate(blocks):
        rows_ref[i * rows : (i + 1) * rows, :] = block[:, 0:width]
    meta = jnp.concatenate([block[:, width:].astype(F32) for block in blocks], axis=0)
    lane = lax.broadcasted_iota(jnp.int32, meta.shape, 1)
    first = first_ref[0]
    for j in range(local):
        mine = (lane == first + j) | (lane == expert_count + first + j)
        weights.append(jnp.sum(jnp.where(mine, meta, 0.0), axis=1, keepdims=True))
    for j in range(local):
        for copy in copies[j]:
            copy.wait()
        both = jnp.dot(rows_ref[...], gate_up[j], preferred_element_type=F32)
        gate = both[:, 0:units]
        value = gate * jax.nn.sigmoid(gate) * both[:, units:]
        act_ref[:, j * units : (j + 1) * units] = (value * weights[j]).astype(BF16)
    for copy in down_copies:
        copy.wait()
    out_ref[...] = jnp.dot(act_ref[...], down[...], preferred_element_type=F32).astype(BF16)


def experts(blocks, first, w_gate, w_up, w_down, expert_count):
    local, width, units = w_gate.shape
    rows = blocks[0].shape[0]
    total = rows * len(blocks)
    vmem = pl.BlockSpec(memory_space=pltpu.VMEM)
    hbm = pl.BlockSpec(memory_space=pl.ANY)
    return pl.pallas_call(
        functools.partial(experts_kernel, width, expert_count, len(blocks)),
        out_shape=jax.ShapeDtypeStruct((total, width), BF16),
        in_specs=[pl.BlockSpec(memory_space=pltpu.SMEM)] + [vmem] * len(blocks) + [hbm] * 3,
        out_specs=vmem,
        scratch_shapes=[
            pltpu.VMEM((total, width), BF16),
            pltpu.VMEM((local, width, 2 * units), BF16),
            pltpu.VMEM((local * units, width), BF16),
            pltpu.VMEM((total, local * units), BF16),
            pltpu.SemaphoreType.DMA((local, 3)),
        ],
        compiler_params=pltpu.CompilerParams(vmem_limit_bytes=VMEM_LIMIT),
        cost_estimate=pl.CostEstimate(
            flops=6 * total * width * units * local,
            bytes_accessed=6 * local * width * units,
            transcendentals=total * units * local,
        ),
        name="experts",
    )(first, *blocks, w_gate, w_up, w_down)


def frames_kernel(columns, books, shard, sessions, steps, where_ref, *refs):
    metas = refs[:-3]
    table_ref, out_ref, hot_ref = refs[-3:]
    code_at, slot_at = columns
    rows = metas[0].shape[0]
    meta = jnp.concatenate([m[...] for m in metas], axis=0)
    total = meta.shape[0]
    slot = meta[:, slot_at : slot_at + 2].astype(F32)
    source = (slot[:, 0:1] + 256.0 * slot[:, 1:2]).astype(jnp.int32)
    lane = lax.broadcasted_iota(jnp.int32, (1, total), 1)
    inside = lane % rows
    target = (inside % sessions) * steps + inside // sessions
    for k in range(len(metas)):
        target = target + jnp.where(lane // rows == k, where_ref[k + 1] * rows, 0)
    chooser = jnp.where(source == target, 1.0, 0.0).astype(BF16)
    ordered = lax.dot_general(
        chooser, meta, (((0,), (0,)), ((), ())), preferred_element_type=F32
    )
    low = ordered[:, code_at : code_at + books]
    high = ordered[:, code_at + books : code_at + 2 * books]
    codes = (low + 256.0 * high).astype(jnp.int32) - where_ref[0] * shard
    chunk = 128
    lanes = lax.broadcasted_iota(jnp.int32, (total, chunk), 1)
    for start in range(0, books * shard, chunk):
        first, last = start // shard, (start + chunk - 1) // shard
        code = codes[:, first : first + 1] + (first * shard - start)
        for q in range(first + 1, last + 1):
            shifted = codes[:, q : q + 1] + (q * shard - start)
            code = jnp.where(lanes >= q * shard - start, shifted, code)
        low_end = jnp.maximum(lanes // shard if shard < chunk else 0, 0) * shard
        if shard < chunk:
            hit = (lanes == code) & (code >= low_end) & (code < low_end + shard)
        else:
            hit = (lanes == code)
        hot_ref[:, start : start + chunk] = jnp.where(hit, 1.0, 0.0).astype(BF16)
    out_ref[...] = jnp.dot(hot_ref[...], table_ref[...], preferred_element_type=F32).astype(BF16)


def frame_sums(blocks, where, code_table, columns, width, sessions, steps):
    books, shard, channels = code_table.shape
    rows = blocks[0].shape[0]
    total = rows * len(blocks)
    meta_width = blocks[0].shape[1] - width
    vmem = pl.BlockSpec(memory_space=pltpu.VMEM)
    return pl.pallas_call(
        functools.partial(frames_kernel, columns, books, shard, sessions, steps),
        grid=(1,),
        out_shape=jax.ShapeDtypeStruct((total, channels), BF16),
        in_specs=[pl.BlockSpec(memory_space=pltpu.SMEM)]
        + [pl.BlockSpec((rows, meta_width), lambda i: (0, width // meta_width))] * len(blocks)
        + [vmem],
        out_specs=vmem,
        scratch_shapes=[pltpu.VMEM((total, books * shard), BF16)],
        compiler_params=pltpu.CompilerParams(vmem_limit_bytes=VMEM_LIMIT),
        cost_estimate=pl.CostEstimate(
            flops=2 * total * books * shard * channels,
            bytes_accessed=2 * books * shard * channels,
            transcendentals=0,
        ),
        name="frame_sums",
    )(where, *blocks, code_table.reshape(books * shard, channels))


def decoder_kernel(
    own_ref, one_ref, two_ref, three_ref, state_ref, taps_ref, bias_ref, up_ref, wave_ref, new_ref
):
    past, sessions, _ = state_ref.shape
    taps = taps_ref.shape[0]
    frames = (
        own_ref[...].astype(F32)
        + one_ref[...].astype(F32)
        + two_ref[...].astype(F32)
        + three_ref[...].astype(F32)
    )
    steps = frames.shape[0] // sessions
    history = [state_ref[i].astype(F32) for i in range(past)]
    history += [frames[t * sessions : (t + 1) * sessions] for t in range(steps)]
    outs = []
    for t in range(steps):
        filtered = bias_ref[...] + taps_ref[0:1, :] * history[past + t]
        for j in range(1, taps):
            filtered = filtered + taps_ref[j : j + 1, :] * history[past + t - j]
        outs.append(jax.nn.gelu(filtered).astype(BF16))
    decoded = jnp.concatenate(outs, axis=0)
    wave_ref[...] = jnp.dot(decoded, up_ref[...], preferred_element_type=F32).astype(BF16)
    for i in range(past):
        new_ref[i] = history[i + steps].astype(BF16)


def decoder(terms, conv_state, conv_taps, conv_bias, upsample):
    sessions, past, channels = conv_state.shape
    rows = terms[0].shape[0]
    wave, state = pl.pallas_call(
        decoder_kernel,
        out_shape=(
            jax.ShapeDtypeStruct((rows, upsample.shape[1]), BF16),
            jax.ShapeDtypeStruct((past, sessions, channels), BF16),
        ),
        compiler_params=pltpu.CompilerParams(vmem_limit_bytes=VMEM_LIMIT),
        name="decoder",
    )(
        *terms,
        jnp.transpose(conv_state, (1, 0, 2)),
        conv_taps,
        conv_bias.reshape(1, channels),
        upsample,
    )
    wave = jnp.transpose(wave.reshape(rows // sessions, sessions, -1), (1, 0, 2))
    return wave, jnp.transpose(state, (1, 0, 2))


def per_device(
    hidden_rows,
    expert_ids,
    route_weights,
    w_gate,
    w_up,
    w_down,
    codes,
    owner_slot,
    code_table,
    conv_state,
    conv_taps,
    conv_bias,
    upsample,
):
    count = lax.axis_size("expert")
    n_wave = lax.axis_size("wave")
    sessions, steps, width = hidden_rows.shape
    books = codes.shape[2]
    rows = sessions * steps
    local = w_gate.shape[0]
    expert_count = count * local
    place = lax.axis_index("expert")

    named = (expert_ids[..., None] == jnp.arange(expert_count, dtype=jnp.int32)).astype(F32)
    weight = jnp.sum(named * route_weights[..., None], axis=2)
    high = lax.reduce_precision(weight, 8, 7)
    low = weight - high
    slot = owner_slot // sessions // n_wave * sessions + owner_slot % sessions
    slot = slot[:, None, None] * steps + jnp.arange(steps, dtype=jnp.int32)[None, :, None]
    meta = jnp.concatenate(
        [high.astype(BF16), low.astype(BF16)]
        + [v.astype(BF16) for v in (codes % 256, codes // 256, slot % 256, slot // 256)],
        axis=2,
    ).reshape(rows, -1)
    meta_width = -(-meta.shape[1] // 128) * 128
    meta = jnp.pad(meta, ((0, 0), (0, meta_width - meta.shape[1])))
    columns = (2 * expert_count, 2 * expert_count + 2 * books)

    own = jnp.concatenate([hidden_rows.reshape(rows, width), meta], axis=1)
    blocks, step_of = spread(own)
    other = {k: swap_wave(v) for k, v in blocks.items()}

    ring = jnp.asarray(ring_order(count), jnp.int32)
    mine = jnp.argmax(ring == place).astype(jnp.int32)
    order = list(range(count))
    where = jnp.concatenate([place[None], jnp.take(ring, (mine + jnp.arange(count)) % count)])
    where = where.astype(jnp.int32)
    sums = frame_sums(
        [blocks[k] for k in order], where, code_table, columns, width, sessions, steps
    )
    frame_terms = collect({k: sums[k * rows : (k + 1) * rows] for k in order})

    first = (place * local).astype(jnp.int32)[None]
    by_step = sorted(order, key=lambda k: step_of[k])
    parts = {}
    for start in range(0, count, 4):
        group = by_step[start : start + 4]
        taken = [blocks[k] for k in group] + [other[k] for k in group]
        result = experts(taken, first, w_gate, w_up, w_down, expert_count)
        split = rows * len(group)
        from_other = swap_wave(result[split:])
        for i, k in enumerate(group):
            at = slice(i * rows, (i + 1) * rows)
            parts[k] = add(result[:split][at], from_other[at]).astype(BF16)
    mixed = add(*collect(parts)).astype(BF16)
    samples, carried = decoder(frame_terms, conv_state, conv_taps, conv_bias, upsample)
    return mixed.reshape(sessions, steps, width), samples, carried


def solution(mesh):
    rows = P(("groups", "expert", "wave"), None, None)
    placed = (
        rows,
        rows,
        rows,
        P("expert", None, "wave"),
        P("expert", None, "wave"),
        P("expert", "wave", None),
        rows,
        P(("groups", "expert", "wave")),
        P(None, "expert", None),
        rows,
        P(),
        P(),
        P(),
    )
    return jax.shard_map(
        per_device,
        mesh=mesh,
        in_specs=placed,
        out_specs=(rows, rows, rows),
        check_vma=False,
    )
```

time: 269 us -> 88.1 us (0.33)
  blocking collectives: 111 us -> 0 us
  waiting for transfers between devices: 80 us -> 12.3 us
  starting transfers between devices: 5.87 us -> 32.4 us
  Pallas kernels: 0 us -> 23.3 us
  matrix products: 21.1 us -> 0 us
  between operations: 16.3 us -> 0.93 us
  local copies, waits for them, and re-layouts: 24 us -> 12 us
  other arithmetic: 9.58 us -> 6.02 us
    reduce_scatter x2 -> x0, waiting for transfers between devices: 68.8 us -> none  [the longest x1 56.5 us: frames_path(): lax.psum_scatter(partial_value.reshape(n_expert * sessions_here, frame_co...]
    all_to_all x1 -> x0, blocking collectives: 44.2 us -> none  [mixture(): lax.all_to_all(outgoing, 'expert', split_axis=0, concat_axis=0, tiled=True)]
    unnamed x1 -> x0, blocking collectives: 36.2 us -> none
    ppermute x0 -> x31, starting transfers between devices: none -> 32.4 us  [the longest x21 30.2 us: shift(): return lax.ppermute(value, 'expert', pairs)]
    all_gather x1 -> x0, blocking collectives: 30.7 us -> none  [frames_path(): lax.all_gather(codes, 'expert', axis=0, tiled=True)]
    pallas_call x0 -> x4, Pallas kernels: none -> 23.3 us  [the longest x2 15.6 us: experts(): pl.pallas_call(functools.partial(experts_kernel, width, expert_count, len...]
    dot_general x5 -> x0, matrix products: 21.1 us -> none  [the longest x1 8.29 us: expert_work(): jnp.einsum('secf,efd->secd', activated, w_down, preferred_element_type=jn...]
    ppermute x0 -> x31, waiting for transfers between devices: none -> 12.3 us  [the longest x21 12.3 us: shift(): return lax.ppermute(value, 'expert', pairs)]
  transfers between devices with their start and end apart: 4 -> 31, of which waited for: 3 -> 8; matrix products, arithmetic and copies ran while one was open for 9% -> 12% of each run, Pallas kernels for 0% -> 27%
where the time goes in v1:
time: 88.1 us; the launch traced here: 87 us
  starting transfers between devices  32.4 us (37%)
  Pallas kernels  23.3 us (26%)
  waiting for transfers between devices  12.3 us (14%)
  local copies, waits for them, and re-layouts  12 us (14%)
  other arithmetic  6.02 us (7%)
  between operations  0.93 us (1%)
    ppermute x21, starting transfers between devices, shift(): return lax.ppermute(value, 'expert', pairs)  30.2 us
    pallas_call x2, Pallas kernels, experts(): pl.pallas_call(functools.partial(experts_kernel, width, expert_count, len...  15.6 us
    ppermute x21, waiting for transfers between devices, shift(): return lax.ppermute(value, 'expert', pairs)  12.3 us
    pallas_call x1, Pallas kernels, frame_sums(): pl.pallas_call(functools.partial(frames_kernel, columns, books, shard, se...  5.28 us
    unnamed x44, local copies, waits for them, and re-layouts  3.43 us
    pallas_call x1, Pallas kernels, decoder(): pl.pallas_call(decoder_kernel, out_shape=(jax.ShapeDtypeStruct((rows, ups...  2.43 us
    slice x2, local copies, waits for them, and re-layouts, per_device(): from_other = swap_wave(result[split:])  2.25 us
    ppermute x10, starting transfers between devices, swap_wave(): return lax.ppermute(value, 'wave', [(0, 1), (1, 0)])  2.16 us
  transfers between devices with their start and end apart: 31, of which 8 were waited for; matrix products, arithmetic and copies ran while one was open for 12% of the time, Pallas kernels for 27%

profile of v1, /device:TPU:0, one launch (start us, length us, event | category | flops | bytes accessed | tf_op | source)
XLA Modules:
  0.0 87.0 jit_solution(18053307289793424229)
XLA Ops:
  0.6 0.7 fusion.13
  1.5 0.8 copy.27
  2.3 0.8 copy.28
  3.3 0.8 fusion.7
  4.1 1.0 %reshape.226 = bf16[32,2048]{1,0:T(8,128)(2,1)S(1)} reshape(bf16[16,2,2048]{2,1,0:T(2,128)(2,1)} %param.14) | data formatting | bytes 262144 | tf_op jit(solution)/shard_map/reshape | solution.py:297
  5.2 6.1 %collective-permute-start.1 = (bf16[32,2176]{1,0:T(8,128)(2,1)S(1)}, bf16[32,2176]{1,0:T(8,128)(2,1)S(1)}, u32[]{:S(2)}, u32[]{:S(2)}) collective-permute-start(bf16[32,2176]{1,0:T(8,128)(2,1)S(1)} %fusion.1.refs_0_), channel_id=1, source_target_pairs={{0,14},{4,10},{8,6},{12,2},{14,0},{10,4},{6,8},{2,12},{1,15},{5,11... | collective-permute-start | bytes 417800 | tf_op jit(solution)/shard_map/ppermute | solution.py:23
  11.2 2.0 %collective-permute-start = (bf16[32,2176]{1,0:T(8,128)(2,1)S(1)}, bf16[32,2176]{1,0:T(8,128)(2,1)S(1)}, u32[]{:S(2)}, u32[]{:S(2)}) collective-permute-start(bf16[32,2176]{1,0:T(8,128)(2,1)S(1)} %fusion.1.refs_0_), channel_id=1, source_target_pairs={{0,2},{4,0},{8,4},{12,8},{14,12},{10,14},{6,10},{2,6},{1,3},{5,1},... | collective-permute-start | bytes 417800 | tf_op jit(solution)/shard_map/ppermute | solution.py:23
  13.3 1.3 %compare_reduce_fusion = (pred[]{:T(512)}, s32[]{:T(128)}) fusion(s32[8]{0:T(128)} %constant.129.clone, s32[]{:T(128)} %axis_index.15), kind=kLoop, calls=%fused_computation.54 | loop fusion | flops 57 | bytes 41 | tf_op jit(solution)/shard_map/per_device/reduce | solution.py:302
  14.6 1.2 %collective-permute-done.1.refs_2_.refs_4_ = bf16[32,2176]{1,0:T(8,128)(2,1)S(1)} collective-permute-done((bf16[32,2176]{1,0:T(8,128)(2,1)S(1)}, bf16[32,2176]{1,0:T(8,128)(2,1)S(1)}, u32[]{:S(2)}, u32[]{:S(2)}) %collective-permute-start.1) | collective-permute-done | bytes 139296 | tf_op jit(solution)/shard_map/ppermute | solution.py:23
  15.8 1.7 %collective-permute-start.10 = (bf16[32,2176]{1,0:T(8,128)(2,1)S(1)}, bf16[32,2176]{1,0:T(8,128)(2,1)S(1)}, u32[]{:S(2)}, u32[]{:S(2)}) collective-permute-start(bf16[32,2176]{1,0:T(8,128)(2,1)S(1)} %collective-permute-done.1.refs_2_.refs_4_), channel_id=1, source_target_pairs={{0,2},{4,0},{8,4},{12,8},{14,12},{10,14},{6,10},{2,6},{1,3},{5,1},... | collective-permute-start | bytes 417800 | tf_op jit(solution)/shard_map/ppermute | solution.py:23
  17.5 1.1 %collective-permute-start.9 = (bf16[32,2176]{1,0:T(8,128)(2,1)S(1)}, bf16[32,2176]{1,0:T(8,128)(2,1)S(1)}, u32[]{:S(2)}, u32[]{:S(2)}) collective-permute-start(bf16[32,2176]{1,0:T(8,128)(2,1)S(1)} %collective-permute-done.1.refs_2_.refs_4_), channel_id=1, source_target_pairs={{0,4},{4,8},{8,12},{12,14},{14,10},{10,6},{6,2},{2,0},{1,5},{5,9},... | collective-permute-start | bytes 417800 | tf_op jit(solution)/shard_map/ppermute | solution.py:23
  18.6 2.3 %collective-permute-start.11 = (bf16[32,2176]{1,0:T(8,128)(2,1)S(1)}, bf16[32,2176]{1,0:T(8,128)(2,1)S(1)}, u32[]{:S(2)}, u32[]{:S(2)}) collective-permute-start(bf16[32,2176]{1,0:T(8,128)(2,1)S(1)} %collective-permute-done.2.refs_3_.refs_7_), channel_id=1, source_target_pairs={{0,4},{4,8},{8,12},{12,14},{14,10},{10,6},{6,2},{2,0},{1,5},{5,9},... | collective-permute-start | bytes 417800 | tf_op jit(solution)/shard_map/ppermute | solution.py:23
  20.9 0.6 fusion.12
  21.4 1.3 %gather_fusion = s32[8]{0:T(128)S(1)} fusion(s32[8]{0:T(128)} %constant.129.clone, s32[1024]{0:T(1024)S(1)} %pad_clamp_fusion), kind=kCustom, calls=%fused_computation | custom fusion | bytes 96 | tf_op jit(solution)/shard_map/jit(_take)/gather | solution.py:304
  22.7 0.7 collective-permute-done.9.refs_1_.refs_3_
  23.4 0.5 collective-permute-start.14
  23.9 2.4 %collective-permute-done.8.refs_0_.refs_2_ = bf16[32,2176]{1,0:T(8,128)(2,1)S(1)} collective-permute-done((bf16[32,2176]{1,0:T(8,128)(2,1)S(1)}, bf16[32,2176]{1,0:T(8,128)(2,1)S(1)}, u32[]{:S(2)}, u32[]{:S(2)}) %collective-permute-start.8) | collective-permute-done | bytes 139296 | tf_op jit(solution)/shard_map/ppermute | solution.py:23
  26.9 0.6 and_select_fusion.3
  27.4 0.6 pad_add_fusion.where_ref
  29.3 7.8 %experts.3 = bf16[256,2048]{1,0:T(8,128)(2,1)} custom-call(s32[1]{0:T(128)} %bitcast.first_ref, bf16[32,2176]{1,0:T(8,128)(2,1)} %copy-done.9, bf16[32,2176]{1,0:T(8,128)(2,1)} %copy-done.7, bf16[32,2176]{1,0:T(8,128)(2,1)} %copy-done.6, bf16[32,2176]{1,0:T(8,128)(2,1)} %copy-done.8, bf16[32,2176]{1,0:T(8,128)(2,1)} %copy-done.16, ...), custom_call_target="tpu_custom_call" | custom-call | flops 2415919104 | bytes 9437184 | tf_op jit(solution)/shard_map/experts/pallas_call | solution.py:125
  37.2 1.1 %slice.128 = bf16[128,2048]{1,0:T(8,128)(2,1)S(1)} slice(bf16[256,2048]{1,0:T(8,128)(2,1)} %experts.3), slice={[128:256], [0:2048]} | slice | bytes 1048576 | tf_op jit(solution)/shard_map/slice | solution.py:319
  38.7 5.3 %frame_sums.1 = bf16[256,1024]{1,0:T(8,128)(2,1)} custom-call(s32[9]{0:T(128)} %pad_add_fusion.where_ref, bf16[32,2176]{1,0:T(8,128)(2,1)} %copy-done.2, bf16[32,2176]{1,0:T(8,128)(2,1)} %copy-done.5, bf16[32,2176]{1,0:T(8,128)(2,1)} %copy-done.9, bf16[32,2176]{1,0:T(8,128)(2,1)} %copy-done.7, bf16[32,2176]{1,0:T(8,128)(2,1)} %copy-done.3, ...), custom_call_target="tpu_custom_call" | custom-call | flops 1073741824 | bytes 4194304 | tf_op jit(solution)/shard_map/frame_sums/pallas_call | solution.py:191
  44.0 1.6 %fusion.14 = (bf16[32,1024]{1,0:T(8,128)(2,1)S(1)}, bf16[32,1024]{1,0:T(8,128)(2,1)S(1)}, bf16[32,1024]{1,0:T(8,128)(2,1)S(1)}, bf16[32,1024]{1,0:T(8,128)(2,1)S(1)}, bf16[32,1024]{1,0:T(8,128)(2,1)}) fusion(bf16[256,1024]{1,0:T(8,128)(2,1)} %frame_sums.1), kind=kLoop, calls=%fused_computation.70 | loop fusion | bytes 655360 | tf_op jit(solution)/shard_map/slice | solution.py:309
  45.6 2.0 %collective-permute-start.24 = (bf16[32,1024]{1,0:T(8,128)(2,1)S(1)}, bf16[32,1024]{1,0:T(8,128)(2,1)S(1)}, u32[]{:S(2)}, u32[]{:S(2)}) collective-permute-start(bf16[32,1024]{1,0:T(8,128)(2,1)S(1)} %get-tuple-element.22), channel_id=1, source_target_pairs={{0,4},{4,8},{8,12},{12,14},{14,10},{10,6},{6,2},{2,0},{1,5},{5,9},... | collective-permute-start | bytes 196616 | tf_op jit(solution)/shard_map/ppermute | solution.py:23
  47.7 2.0 %collective-permute-start.28 = (bf16[32,1024]{1,0:T(8,128)(2,1)S(1)}, bf16[32,1024]{1,0:T(8,128)(2,1)S(1)}, u32[]{:S(2)}, u32[]{:S(2)}) collective-permute-start(bf16[32,1024]{1,0:T(8,128)(2,1)S(1)} %get-tuple-element.19), channel_id=1, source_target_pairs={{0,4},{4,8},{8,12},{12,14},{14,10},{10,6},{6,2},{2,0},{1,5},{5,9},... | collective-permute-start | bytes 196616 | tf_op jit(solution)/shard_map/ppermute | solution.py:23
  49.8 0.6 copy-done.13
  50.4 7.8 %experts.2 = bf16[256,2048]{1,0:T(8,128)(2,1)} custom-call(s32[1]{0:T(128)} %bitcast.first_ref, bf16[32,2176]{1,0:T(8,128)(2,1)} %copy-done.2, bf16[32,2176]{1,0:T(8,128)(2,1)} %copy-done.5, bf16[32,2176]{1,0:T(8,128)(2,1)} %copy-done.3, bf16[32,2176]{1,0:T(8,128)(2,1)} %copy-done.4, bf16[32,2176]{1,0:T(8,128)(2,1)} %copy-done.10, ...), custom_call_target="tpu_custom_call" | custom-call | flops 2415919104 | bytes 9437184 | tf_op jit(solution)/shard_map/experts/pallas_call | solution.py:125
  58.1 1.2 %slice.123 = bf16[128,2048]{1,0:T(8,128)(2,1)S(1)} slice(bf16[256,2048]{1,0:T(8,128)(2,1)} %experts.2), slice={[128:256], [0:2048]} | slice | bytes 1048576 | tf_op jit(solution)/shard_map/slice | solution.py:319
  59.6 1.5 %collective-permute-start.17 = (bf16[32,2048]{1,0:T(8,128)(2,1)S(1)}, bf16[32,2048]{1,0:T(8,128)(2,1)S(1)}, u32[]{:S(2)}, u32[]{:S(2)}) collective-permute-start(bf16[32,2048]{1,0:T(8,128)(2,1)S(1)} %get-tuple-element.12), channel_id=1, source_target_pairs={{0,4},{4,8},{8,12},{12,14},{14,10},{10,6},{6,2},{2,0},{1,5},{5,9},... | collective-permute-start | bytes 393224 | tf_op jit(solution)/shard_map/ppermute | solution.py:23
  61.0 0.6 collective-permute-start.19
  61.6 1.4 %collective-permute-start.21 = (bf16[32,2048]{1,0:T(8,128)(2,1)S(1)}, bf16[32,2048]{1,0:T(8,128)(2,1)S(1)}, u32[]{:S(2)}, u32[]{:S(2)}) collective-permute-start(bf16[32,2048]{1,0:T(8,128)(2,1)S(1)} %get-tuple-element.14), channel_id=1, source_target_pairs={{0,4},{4,8},{8,12},{12,14},{14,10},{10,6},{6,2},{2,0},{1,5},{5,9},... | collective-permute-start | bytes 393224 | tf_op jit(solution)/shard_map/ppermute | solution.py:23
  63.1 0.6 collective-permute-start.22
  63.7 1.0 %add_convert_fusion.12 = (bf16[32,1024]{1,0:T(8,128)(2,1)S(1)}, bf16[32,1024]{1,0:T(8,128)(2,1)S(1)}, bf16[32,1024]{1,0:T(8,128)(2,1)S(1)}) fusion(bf16[32,1024]{1,0:T(8,128)(2,1)S(1)} %collective-permute-done.29, bf16[32,1024]{1,0:T(8,128)(2,1)S(1)} %collective-permute-done.28, bf16[256,1024]{1,0:T(8,128)(2,1)} %frame_sums.1, ...), kind=kLoop, calls=%fused_computation.16 | loop fusion | flops 458752 | bytes 655360 | tf_op jit(solution)/shard_map/convert_element_type | solution.py:70
  64.6 1.5 %collective-permute-start.25 = (bf16[32,1024]{1,0:T(8,128)(2,1)S(1)}, bf16[32,1024]{1,0:T(8,128)(2,1)S(1)}, u32[]{:S(2)}, u32[]{:S(2)}) collective-permute-start(bf16[32,1024]{1,0:T(8,128)(2,1)S(1)} %get-tuple-element.18), channel_id=1, source_target_pairs={{0,4},{4,8},{8,12},{12,14},{14,10},{10,6},{6,2},{2,0},{1,5},{5,9},... | collective-permute-start | bytes 196616 | tf_op jit(solution)/shard_map/ppermute | solution.py:23
  66.1 1.3 %collective-permute-done.19 = bf16[32,2048]{1,0:T(8,128)(2,1)S(1)} collective-permute-done((bf16[32,2048]{1,0:T(8,128)(2,1)S(1)}, bf16[32,2048]{1,0:T(8,128)(2,1)S(1)}, u32[]{:S(2)}, u32[]{:S(2)}) %collective-permute-start.19) | collective-permute-done | bytes 131104 | tf_op jit(solution)/shard_map/ppermute | solution.py:23
  67.4 1.3 %collective-permute-done.21 = bf16[32,2048]{1,0:T(8,128)(2,1)S(1)} collective-permute-done((bf16[32,2048]{1,0:T(8,128)(2,1)S(1)}, bf16[32,2048]{1,0:T(8,128)(2,1)S(1)}, u32[]{:S(2)}, u32[]{:S(2)}) %collective-permute-start.21) | collective-permute-done | bytes 131104 | tf_op jit(solution)/shard_map/ppermute | solution.py:23
  68.7 0.7 collective-permute-done.22
  69.6 0.7 collective-permute-start.18
  70.4 1.3 %collective-permute-start.20 = (bf16[32,2048]{1,0:T(8,128)(2,1)S(1)}, bf16[32,2048]{1,0:T(8,128)(2,1)S(1)}, u32[]{:S(2)}, u32[]{:S(2)}) collective-permute-start(bf16[32,2048]{1,0:T(8,128)(2,1)S(1)} %get-tuple-element.11), channel_id=1, source_target_pairs={{0,2},{4,0},{8,4},{12,8},{14,12},{10,14},{6,10},{2,6},{1,3},{5,1},... | collective-permute-start | bytes 393224 | tf_op jit(solution)/shard_map/ppermute | solution.py:23
  71.7 1.5 %collective-permute-start.23 = (bf16[32,2048]{1,0:T(8,128)(2,1)S(1)}, bf16[32,2048]{1,0:T(8,128)(2,1)S(1)}, u32[]{:S(2)}, u32[]{:S(2)}) collective-permute-start(bf16[32,2048]{1,0:T(8,128)(2,1)S(1)} %get-tuple-element.10), channel_id=1, source_target_pairs={{0,14},{4,10},{8,6},{12,2},{14,0},{10,4},{6,8},{2,12},{1,15},{5,11... | collective-permute-start | bytes 393224 | tf_op jit(solution)/shard_map/ppermute | solution.py:23
  73.2 1.3 %collective-permute-start.27 = (bf16[32,1024]{1,0:T(8,128)(2,1)S(1)}, bf16[32,1024]{1,0:T(8,128)(2,1)S(1)}, u32[]{:S(2)}, u32[]{:S(2)}) collective-permute-start(bf16[32,1024]{1,0:T(8,128)(2,1)S(1)} %get-tuple-element.17), channel_id=1, source_target_pairs={{0,2},{4,0},{8,4},{12,8},{14,12},{10,14},{6,10},{2,6},{1,3},{5,1},... | collective-permute-start | bytes 196616 | tf_op jit(solution)/shard_map/ppermute | solution.py:23
  74.6 2.5 %collective-permute-start.30 = (bf16[32,1024]{1,0:T(8,128)(2,1)S(1)}, bf16[32,1024]{1,0:T(8,128)(2,1)S(1)}, u32[]{:S(2)}, u32[]{:S(2)}) collective-permute-start(bf16[32,1024]{1,0:T(8,128)(2,1)S(1)} %get-tuple-element.16), channel_id=1, source_target_pairs={{0,14},{4,10},{8,6},{12,2},{14,0},{10,4},{6,8},{2,12},{1,15},{5,11... | collective-permute-start | bytes 196616 | tf_op jit(solution)/shard_map/ppermute | solution.py:23
  77.0 2.1 %collective-permute-done.27.two_ref = bf16[32,1024]{1,0:T(8,128)(2,1)S(1)} collective-permute-done((bf16[32,1024]{1,0:T(8,128)(2,1)S(1)}, bf16[32,1024]{1,0:T(8,128)(2,1)S(1)}, u32[]{:S(2)}, u32[]{:S(2)}) %collective-permute-start.27) | collective-permute-done | bytes 65568 | tf_op jit(solution)/shard_map/ppermute | solution.py:23
  79.1 2.5 %collective-permute-done.30.three_ref = bf16[32,1024]{1,0:T(8,128)(2,1)S(1)} collective-permute-done((bf16[32,1024]{1,0:T(8,128)(2,1)S(1)}, bf16[32,1024]{1,0:T(8,128)(2,1)S(1)}, u32[]{:S(2)}, u32[]{:S(2)}) %collective-permute-start.30) | collective-permute-done | bytes 65568 | tf_op jit(solution)/shard_map/ppermute | solution.py:23
  81.6 0.6 copy-done.20
  82.3 2.4 %decoder.1 = (bf16[32,512]{1,0:T(8,128)(2,1)}, bf16[6,16,1024]{2,1,0:T(8,128)(2,1)}) custom-call(bf16[32,1024]{1,0:T(8,128)(2,1)} %get-tuple-element.23.own_ref, bf16[32,1024]{1,0:T(8,128)(2,1)} %copy-done.18, bf16[32,1024]{1,0:T(8,128)(2,1)} %copy-done.19, bf16[32,1024]{1,0:T(8,128)(2,1)} %copy-done.20, bf16[6,16,1024]{2,1,0:T(8,128)(2,1)} %bitcast.20, ...), custom_call_target="tpu_custom_call" | custom-call | tf_op jit(solution)/shard_map/decoder/pallas_call | solution.py:239
  84.7 1.4 %copy.33 = bf16[2,16,512]{2,0,1:T(2,128)(2,1)} copy(bf16[2,16,512]{2,1,0:T(8,128)(2,1)} %bitcast.23) | data formatting | bytes 65536 | tf_op jit(solution)/shard_map/reshape | solution.py:254
  86.2 0.8 reshape.227
  (89 shorter events, 3.4 us)
Async XLA Ops:
  5.2 32.0 %copy-start.2 = (bf16[32,2176]{1,0:T(8,128)(2,1)}, bf16[32,2176]{1,0:T(8,128)(2,1)S(1)}, u32[]{:S(2)}) copy-start(bf16[32,2176]{1,0:T(8,128)(2,1)S(1)} %fusion.1.refs_0_) | copy-start | bytes 417796
  5.2 10.6 %collective-permute-start.1 = (bf16[32,2176]{1,0:T(8,128)(2,1)S(1)}, bf16[32,2176]{1,0:T(8,128)(2,1)S(1)}, u32[]{:S(2)}, u32[]{:S(2)}) collective-permute-start(bf16[32,2176]{1,0:T(8,128)(2,1)S(1)} %fusion.1.refs_0_), channel_id=1, source_target_pairs={{0,14},{4,10},{8,6},{12,2},{14,0},{10,4},{6,8},{2,12},{1,15},{5,11... | collective-permute-start | bytes 417800 | tf_op jit(solution)/shard_map/ppermute | solution.py:23
  11.2 7.3 %collective-permute-start.2 = (bf16[32,2176]{1,0:T(8,128)(2,1)S(1)}, bf16[32,2176]{1,0:T(8,128)(2,1)S(1)}, u32[]{:S(2)}, u32[]{:S(2)}) collective-permute-start(bf16[32,2176]{1,0:T(8,128)(2,1)S(1)} %fusion.1.refs_0_), channel_id=1, source_target_pairs={{0,4},{4,8},{8,12},{12,14},{14,10},{10,6},{6,2},{2,0},{1,5},{5,9},... | collective-permute-start | bytes 417800 | tf_op jit(solution)/shard_map/ppermute | solution.py:23
  11.2 9.6 %collective-permute-start = (bf16[32,2176]{1,0:T(8,128)(2,1)S(1)}, bf16[32,2176]{1,0:T(8,128)(2,1)S(1)}, u32[]{:S(2)}, u32[]{:S(2)}) collective-permute-start(bf16[32,2176]{1,0:T(8,128)(2,1)S(1)} %fusion.1.refs_0_), channel_id=1, source_target_pairs={{0,2},{4,0},{8,4},{12,8},{14,12},{10,14},{6,10},{2,6},{1,3},{5,1},... | collective-permute-start | bytes 417800 | tf_op jit(solution)/shard_map/ppermute | solution.py:23
  13.3 32.4 %collective-permute-start.3 = (bf16[32,2176]{1,0:T(8,128)(2,1)S(1)}, bf16[32,2176]{1,0:T(8,128)(2,1)S(1)}, u32[]{:S(2)}, u32[]{:S(2)}) collective-permute-start(bf16[32,2176]{1,0:T(8,128)(2,1)S(1)} %fusion.1.refs_0_), channel_id=1, source_target_pairs={{0,1},{1,0},{2,3},{3,2},{4,5},{5,4},{6,7},{7,6},{8,9},{9,8},{10,11... | collective-permute-start | bytes 417800 | tf_op jit(solution)/shard_map/ppermute | solution.py:27
  15.8 21.3 %copy-start.3 = (bf16[32,2176]{1,0:T(8,128)(2,1)}, bf16[32,2176]{1,0:T(8,128)(2,1)S(1)}, u32[]{:S(2)}) copy-start(bf16[32,2176]{1,0:T(8,128)(2,1)S(1)} %collective-permute-done.1.refs_2_.refs_4_) | copy-start | bytes 417796
  15.8 7.6 %collective-permute-start.10 = (bf16[32,2176]{1,0:T(8,128)(2,1)S(1)}, bf16[32,2176]{1,0:T(8,128)(2,1)S(1)}, u32[]{:S(2)}, u32[]{:S(2)}) collective-permute-start(bf16[32,2176]{1,0:T(8,128)(2,1)S(1)} %collective-permute-done.1.refs_2_.refs_4_), channel_id=1, source_target_pairs={{0,2},{4,0},{8,4},{12,8},{14,12},{10,14},{6,10},{2,6},{1,3},{5,1},... | collective-permute-start | bytes 417800 | tf_op jit(solution)/shard_map/ppermute | solution.py:23
  17.5 5.9 %collective-permute-start.9 = (bf16[32,2176]{1,0:T(8,128)(2,1)S(1)}, bf16[32,2176]{1,0:T(8,128)(2,1)S(1)}, u32[]{:S(2)}, u32[]{:S(2)}) collective-permute-start(bf16[32,2176]{1,0:T(8,128)(2,1)S(1)} %collective-permute-done.1.refs_2_.refs_4_), channel_id=1, source_target_pairs={{0,4},{4,8},{8,12},{12,14},{14,10},{10,6},{6,2},{2,0},{1,5},{5,9},... | collective-permute-start | bytes 417800 | tf_op jit(solution)/shard_map/ppermute | solution.py:23
  18.6 18.5 %copy-start.4 = (bf16[32,2176]{1,0:T(8,128)(2,1)}, bf16[32,2176]{1,0:T(8,128)(2,1)S(1)}, u32[]{:S(2)}) copy-start(bf16[32,2176]{1,0:T(8,128)(2,1)S(1)} %collective-permute-done.2.refs_3_.refs_7_) | copy-start | bytes 417796
  18.6 7.8 %collective-permute-start.11 = (bf16[32,2176]{1,0:T(8,128)(2,1)S(1)}, bf16[32,2176]{1,0:T(8,128)(2,1)S(1)}, u32[]{:S(2)}, u32[]{:S(2)}) collective-permute-start(bf16[32,2176]{1,0:T(8,128)(2,1)S(1)} %collective-permute-done.2.refs_3_.refs_7_), channel_id=1, source_target_pairs={{0,4},{4,8},{8,12},{12,14},{14,10},{10,6},{6,2},{2,0},{1,5},{5,9},... | collective-permute-start | bytes 417800 | tf_op jit(solution)/shard_map/ppermute | solution.py:23
  20.8 16.3 %copy-start.5 = (bf16[32,2176]{1,0:T(8,128)(2,1)}, bf16[32,2176]{1,0:T(8,128)(2,1)S(1)}, u32[]{:S(2)}) copy-start(bf16[32,2176]{1,0:T(8,128)(2,1)S(1)} %collective-permute-done.refs_1_) | copy-start | bytes 417796
  20.9 5.5 %collective-permute-start.8 = (bf16[32,2176]{1,0:T(8,128)(2,1)S(1)}, bf16[32,2176]{1,0:T(8,128)(2,1)S(1)}, u32[]{:S(2)}, u32[]{:S(2)}) collective-permute-start(bf16[32,2176]{1,0:T(8,128)(2,1)S(1)} %collective-permute-done.refs_1_), channel_id=1, source_target_pairs={{0,2},{4,0},{8,4},{12,8},{14,12},{10,14},{6,10},{2,6},{1,3},{5,1},... | collective-permute-start | bytes 417800 | tf_op jit(solution)/shard_map/ppermute | solution.py:23
  23.4 5.2 %copy-start.7 = (bf16[32,2176]{1,0:T(8,128)(2,1)}, bf16[32,2176]{1,0:T(8,128)(2,1)S(1)}, u32[]{:S(2)}) copy-start(bf16[32,2176]{1,0:T(8,128)(2,1)S(1)} %collective-permute-done.9.refs_1_.refs_3_) | copy-start | bytes 417796
  23.4 4.6 %collective-permute-start.13 = (bf16[32,2176]{1,0:T(8,128)(2,1)S(1)}, bf16[32,2176]{1,0:T(8,128)(2,1)S(1)}, u32[]{:S(2)}, u32[]{:S(2)}) collective-permute-start(bf16[32,2176]{1,0:T(8,128)(2,1)S(1)} %collective-permute-done.9.refs_1_.refs_3_), channel_id=1, source_target_pairs={{0,1},{1,0},{2,3},{3,2},{4,5},{5,4},{6,7},{7,6},{8,9},{9,8},{10,11... | collective-permute-start | bytes 417800 | tf_op jit(solution)/shard_map/ppermute | solution.py:27
  23.4 5.2 %copy-start.6 = (bf16[32,2176]{1,0:T(8,128)(2,1)}, bf16[32,2176]{1,0:T(8,128)(2,1)S(1)}, u32[]{:S(2)}) copy-start(bf16[32,2176]{1,0:T(8,128)(2,1)S(1)} %collective-permute-done.10.refs_2_.refs_5_) | copy-start | bytes 417796
  23.4 4.7 %collective-permute-start.14 = (bf16[32,2176]{1,0:T(8,128)(2,1)S(1)}, bf16[32,2176]{1,0:T(8,128)(2,1)S(1)}, u32[]{:S(2)}, u32[]{:S(2)}) collective-permute-start(bf16[32,2176]{1,0:T(8,128)(2,1)S(1)} %collective-permute-done.10.refs_2_.refs_5_), channel_id=1, source_target_pairs={{0,1},{1,0},{2,3},{3,2},{4,5},{5,4},{6,7},{7,6},{8,9},{9,8},{10,11... | collective-permute-start | bytes 417800 | tf_op jit(solution)/shard_map/ppermute | solution.py:27
  26.4 2.3 %copy-start.9 = (bf16[32,2176]{1,0:T(8,128)(2,1)}, bf16[32,2176]{1,0:T(8,128)(2,1)S(1)}, u32[]{:S(2)}) copy-start(bf16[32,2176]{1,0:T(8,128)(2,1)S(1)} %collective-permute-done.8.refs_0_.refs_2_) | copy-start | bytes 417796
  26.4 2.2 %collective-permute-start.12 = (bf16[32,2176]{1,0:T(8,128)(2,1)S(1)}, bf16[32,2176]{1,0:T(8,128)(2,1)S(1)}, u32[]{:S(2)}, u32[]{:S(2)}) collective-permute-start(bf16[32,2176]{1,0:T(8,128)(2,1)S(1)} %collective-permute-done.8.refs_0_.refs_2_), channel_id=1, source_target_pairs={{0,1},{1,0},{2,3},{3,2},{4,5},{5,4},{6,7},{7,6},{8,9},{9,8},{10,11... | collective-permute-start | bytes 417800 | tf_op jit(solution)/shard_map/ppermute | solution.py:27
  26.4 2.3 %copy-start.8 = (bf16[32,2176]{1,0:T(8,128)(2,1)}, bf16[32,2176]{1,0:T(8,128)(2,1)S(1)}, u32[]{:S(2)}) copy-start(bf16[32,2176]{1,0:T(8,128)(2,1)S(1)} %collective-permute-done.11.refs_3_.refs_6_) | copy-start | bytes 417796
  26.4 2.3 %collective-permute-start.15 = (bf16[32,2176]{1,0:T(8,128)(2,1)S(1)}, bf16[32,2176]{1,0:T(8,128)(2,1)S(1)}, u32[]{:S(2)}, u32[]{:S(2)}) collective-permute-start(bf16[32,2176]{1,0:T(8,128)(2,1)S(1)} %collective-permute-done.11.refs_3_.refs_6_), channel_id=1, source_target_pairs={{0,1},{1,0},{2,3},{3,2},{4,5},{5,4},{6,7},{7,6},{8,9},{9,8},{10,11... | collective-permute-start | bytes 417800 | tf_op jit(solution)/shard_map/ppermute | solution.py:27
  28.0 0.7 copy-start.14
  28.0 19.6 %collective-permute-start.5 = (bf16[32,2176]{1,0:T(8,128)(2,1)S(1)}, bf16[32,2176]{1,0:T(8,128)(2,1)S(1)}, u32[]{:S(2)}, u32[]{:S(2)}) collective-permute-start(bf16[32,2176]{1,0:T(8,128)(2,1)S(1)} %collective-permute-done.1.refs_2_.refs_4_), channel_id=1, source_target_pairs={{0,1},{1,0},{2,3},{3,2},{4,5},{5,4},{6,7},{7,6},{8,9},{9,8},{10,11... | collective-permute-start | bytes 417800 | tf_op jit(solution)/shard_map/ppermute | solution.py:27
  28.1 19.6 %collective-permute-start.4 = (bf16[32,2176]{1,0:T(8,128)(2,1)S(1)}, bf16[32,2176]{1,0:T(8,128)(2,1)S(1)}, u32[]{:S(2)}, u32[]{:S(2)}) collective-permute-start(bf16[32,2176]{1,0:T(8,128)(2,1)S(1)} %collective-permute-done.refs_1_), channel_id=1, source_target_pairs={{0,1},{1,0},{2,3},{3,2},{4,5},{5,4},{6,7},{7,6},{8,9},{9,8},{10,11... | collective-permute-start | bytes 417800 | tf_op jit(solution)/shard_map/ppermute | solution.py:27
  28.6 21.1 %collective-permute-start.6 = (bf16[32,2176]{1,0:T(8,128)(2,1)S(1)}, bf16[32,2176]{1,0:T(8,128)(2,1)S(1)}, u32[]{:S(2)}, u32[]{:S(2)}) collective-permute-start(bf16[32,2176]{1,0:T(8,128)(2,1)S(1)} %collective-permute-done.2.refs_3_.refs_7_), channel_id=1, source_target_pairs={{0,1},{1,0},{2,3},{3,2},{4,5},{5,4},{6,7},{7,6},{8,9},{9,8},{10,11... | collective-permute-start | bytes 417800 | tf_op jit(solution)/shard_map/ppermute | solution.py:27
  28.7 0.7 copy-start.17
  38.2 21.1 %collective-permute-start.16 = (bf16[128,2048]{1,0:T(8,128)(2,1)S(1)}, bf16[128,2048]{1,0:T(8,128)(2,1)S(1)}, u32[]{:S(2)}, u32[]{:S(2)}) collective-permute-start(bf16[128,2048]{1,0:T(8,128)(2,1)S(1)} %slice.128), channel_id=1, source_target_pairs={{0,1},{1,0},{2,3},{3,2},{4,5},{5,4},{6,7},{7,6},{8,9},{9,8},{10,11... | collective-permute-start | bytes 1572872 | tf_op jit(solution)/shard_map/ppermute | solution.py:27
  45.6 4.2 %copy-start.10 = (bf16[32,2176]{1,0:T(8,128)(2,1)}, bf16[32,2176]{1,0:T(8,128)(2,1)S(1)}, u32[]{:S(2)}) copy-start(bf16[32,2176]{1,0:T(8,128)(2,1)S(1)} %collective-permute-done.3.refs_4_) | copy-start | bytes 417796
  45.6 13.9 %collective-permute-start.24 = (bf16[32,1024]{1,0:T(8,128)(2,1)S(1)}, bf16[32,1024]{1,0:T(8,128)(2,1)S(1)}, u32[]{:S(2)}, u32[]{:S(2)}) collective-permute-start(bf16[32,1024]{1,0:T(8,128)(2,1)S(1)} %get-tuple-element.22), channel_id=1, source_target_pairs={{0,4},{4,8},{8,12},{12,14},{14,10},{10,6},{6,2},{2,0},{1,5},{5,9},... | collective-permute-start | bytes 196616 | tf_op jit(solution)/shard_map/ppermute | solution.py:23
  47.7 2.1 %copy-start.11 = (bf16[32,2176]{1,0:T(8,128)(2,1)}, bf16[32,2176]{1,0:T(8,128)(2,1)S(1)}, u32[]{:S(2)}) copy-start(bf16[32,2176]{1,0:T(8,128)(2,1)S(1)} %collective-permute-done.5.refs_6_) | copy-start | bytes 417796
  47.7 13.3 %collective-permute-start.26 = (bf16[32,1024]{1,0:T(8,128)(2,1)S(1)}, bf16[32,1024]{1,0:T(8,128)(2,1)S(1)}, u32[]{:S(2)}, u32[]{:S(2)}) collective-permute-start(bf16[32,1024]{1,0:T(8,128)(2,1)S(1)} %get-tuple-element.21), channel_id=1, source_target_pairs={{0,2},{4,0},{8,4},{12,8},{14,12},{10,14},{6,10},{2,6},{1,3},{5,1},... | collective-permute-start | bytes 196616 | tf_op jit(solution)/shard_map/ppermute | solution.py:23
  47.7 2.1 %copy-start.12 = (bf16[32,2176]{1,0:T(8,128)(2,1)}, bf16[32,2176]{1,0:T(8,128)(2,1)S(1)}, u32[]{:S(2)}) copy-start(bf16[32,2176]{1,0:T(8,128)(2,1)S(1)} %collective-permute-done.4.refs_5_) | copy-start | bytes 417796
  47.7 13.9 %collective-permute-start.28 = (bf16[32,1024]{1,0:T(8,128)(2,1)S(1)}, bf16[32,1024]{1,0:T(8,128)(2,1)S(1)}, u32[]{:S(2)}, u32[]{:S(2)}) collective-permute-start(bf16[32,1024]{1,0:T(8,128)(2,1)S(1)} %get-tuple-element.19), channel_id=1, source_target_pairs={{0,4},{4,8},{8,12},{12,14},{14,10},{10,6},{6,2},{2,0},{1,5},{5,9},... | collective-permute-start | bytes 196616 | tf_op jit(solution)/shard_map/ppermute | solution.py:23
  49.7 9.7 %copy-start = (bf16[256,2048]{1,0:T(8,128)(2,1)S(1)}, bf16[256,2048]{1,0:T(8,128)(2,1)}, u32[]{:S(2)}) copy-start(bf16[256,2048]{1,0:T(8,128)(2,1)} %experts.3) | copy-start | bytes 3145732
  49.7 13.3 %collective-permute-start.29 = (bf16[32,1024]{1,0:T(8,128)(2,1)S(1)}, bf16[32,1024]{1,0:T(8,128)(2,1)S(1)}, u32[]{:S(2)}, u32[]{:S(2)}) collective-permute-start(bf16[32,1024]{1,0:T(8,128)(2,1)S(1)} %get-tuple-element.20), channel_id=1, source_target_pairs={{0,2},{4,0},{8,4},{12,8},{14,12},{10,14},{6,10},{2,6},{1,3},{5,1},... | collective-permute-start | bytes 196616 | tf_op jit(solution)/shard_map/ppermute | solution.py:23
  58.1 11.3 %copy-start.1 = (bf16[256,2048]{1,0:T(8,128)(2,1)S(1)}, bf16[256,2048]{1,0:T(8,128)(2,1)}, u32[]{:S(2)}) copy-start(bf16[256,2048]{1,0:T(8,128)(2,1)} %experts.2) | copy-start | bytes 3145732
  59.3 5.3 %collective-permute-start.7 = (bf16[128,2048]{1,0:T(8,128)(2,1)S(1)}, bf16[128,2048]{1,0:T(8,128)(2,1)S(1)}, u32[]{:S(2)}, u32[]{:S(2)}) collective-permute-start(bf16[128,2048]{1,0:T(8,128)(2,1)S(1)} %slice.123), channel_id=1, source_target_pairs={{0,1},{1,0},{2,3},{3,2},{4,5},{5,4},{6,7},{7,6},{8,9},{9,8},{10,11... | collective-permute-start | bytes 1572872 | tf_op jit(solution)/shard_map/ppermute | solution.py:27
  59.6 6.6 %collective-permute-start.17 = (bf16[32,2048]{1,0:T(8,128)(2,1)S(1)}, bf16[32,2048]{1,0:T(8,128)(2,1)S(1)}, u32[]{:S(2)}, u32[]{:S(2)}) collective-permute-start(bf16[32,2048]{1,0:T(8,128)(2,1)S(1)} %get-tuple-element.12), channel_id=1, source_target_pairs={{0,4},{4,8},{8,12},{12,14},{14,10},{10,6},{6,2},{2,0},{1,5},{5,9},... | collective-permute-start | bytes 393224 | tf_op jit(solution)/shard_map/ppermute | solution.py:23
  61.0 6.3 %collective-permute-start.19 = (bf16[32,2048]{1,0:T(8,128)(2,1)S(1)}, bf16[32,2048]{1,0:T(8,128)(2,1)S(1)}, u32[]{:S(2)}, u32[]{:S(2)}) collective-permute-start(bf16[32,2048]{1,0:T(8,128)(2,1)S(1)} %get-tuple-element.15), channel_id=1, source_target_pairs={{0,2},{4,0},{8,4},{12,8},{14,12},{10,14},{6,10},{2,6},{1,3},{5,1},... | collective-permute-start | bytes 393224 | tf_op jit(solution)/shard_map/ppermute | solution.py:23
  61.6 7.1 %collective-permute-start.21 = (bf16[32,2048]{1,0:T(8,128)(2,1)S(1)}, bf16[32,2048]{1,0:T(8,128)(2,1)S(1)}, u32[]{:S(2)}, u32[]{:S(2)}) collective-permute-start(bf16[32,2048]{1,0:T(8,128)(2,1)S(1)} %get-tuple-element.14), channel_id=1, source_target_pairs={{0,4},{4,8},{8,12},{12,14},{14,10},{10,6},{6,2},{2,0},{1,5},{5,9},... | collective-permute-start | bytes 393224 | tf_op jit(solution)/shard_map/ppermute | solution.py:23
  63.1 6.4 %collective-permute-start.22 = (bf16[32,2048]{1,0:T(8,128)(2,1)S(1)}, bf16[32,2048]{1,0:T(8,128)(2,1)S(1)}, u32[]{:S(2)}, u32[]{:S(2)}) collective-permute-start(bf16[32,2048]{1,0:T(8,128)(2,1)S(1)} %get-tuple-element.13), channel_id=1, source_target_pairs={{0,2},{4,0},{8,4},{12,8},{14,12},{10,14},{6,10},{2,6},{1,3},{5,1},... | collective-permute-start | bytes 393224 | tf_op jit(solution)/shard_map/ppermute | solution.py:23
  64.6 9.9 %collective-permute-start.25 = (bf16[32,1024]{1,0:T(8,128)(2,1)S(1)}, bf16[32,1024]{1,0:T(8,128)(2,1)S(1)}, u32[]{:S(2)}, u32[]{:S(2)}) collective-permute-start(bf16[32,1024]{1,0:T(8,128)(2,1)S(1)} %get-tuple-element.18), channel_id=1, source_target_pairs={{0,4},{4,8},{8,12},{12,14},{14,10},{10,6},{6,2},{2,0},{1,5},{5,9},... | collective-permute-start | bytes 196616 | tf_op jit(solution)/shard_map/ppermute | solution.py:23
  69.6 16.5 %collective-permute-start.18 = (bf16[32,2048]{1,0:T(8,128)(2,1)S(1)}, bf16[32,2048]{1,0:T(8,128)(2,1)S(1)}, u32[]{:S(2)}, u32[]{:S(2)}) collective-permute-start(bf16[32,2048]{1,0:T(8,128)(2,1)S(1)} %get-tuple-element.9), channel_id=1, source_target_pairs={{0,4},{4,8},{8,12},{12,14},{14,10},{10,6},{6,2},{2,0},{1,5},{5,9},... | collective-permute-start | bytes 393224 | tf_op jit(solution)/shard_map/ppermute | solution.py:23
  70.4 15.7 %collective-permute-start.20 = (bf16[32,2048]{1,0:T(8,128)(2,1)S(1)}, bf16[32,2048]{1,0:T(8,128)(2,1)S(1)}, u32[]{:S(2)}, u32[]{:S(2)}) collective-permute-start(bf16[32,2048]{1,0:T(8,128)(2,1)S(1)} %get-tuple-element.11), channel_id=1, source_target_pairs={{0,2},{4,0},{8,4},{12,8},{14,12},{10,14},{6,10},{2,6},{1,3},{5,1},... | collective-permute-start | bytes 393224 | tf_op jit(solution)/shard_map/ppermute | solution.py:23
  71.7 14.4 %collective-permute-start.23 = (bf16[32,2048]{1,0:T(8,128)(2,1)S(1)}, bf16[32,2048]{1,0:T(8,128)(2,1)S(1)}, u32[]{:S(2)}, u32[]{:S(2)}) collective-permute-start(bf16[32,2048]{1,0:T(8,128)(2,1)S(1)} %get-tuple-element.10), channel_id=1, source_target_pairs={{0,14},{4,10},{8,6},{12,2},{14,0},{10,4},{6,8},{2,12},{1,15},{5,11... | collective-permute-start | bytes 393224 | tf_op jit(solution)/shard_map/ppermute | solution.py:23
  73.2 5.9 %collective-permute-start.27 = (bf16[32,1024]{1,0:T(8,128)(2,1)S(1)}, bf16[32,1024]{1,0:T(8,128)(2,1)S(1)}, u32[]{:S(2)}, u32[]{:S(2)}) collective-permute-start(bf16[32,1024]{1,0:T(8,128)(2,1)S(1)} %get-tuple-element.17), channel_id=1, source_target_pairs={{0,2},{4,0},{8,4},{12,8},{14,12},{10,14},{6,10},{2,6},{1,3},{5,1},... | collective-permute-start | bytes 196616 | tf_op jit(solution)/shard_map/ppermute | solution.py:23
  74.6 7.1 %copy-start.18 = (bf16[32,1024]{1,0:T(8,128)(2,1)}, bf16[32,1024]{1,0:T(8,128)(2,1)S(1)}, u32[]{:S(2)}) copy-start(bf16[32,1024]{1,0:T(8,128)(2,1)S(1)} %collective-permute-done.25.one_ref) | copy-start | bytes 196612
  74.6 7.1 %collective-permute-start.30 = (bf16[32,1024]{1,0:T(8,128)(2,1)S(1)}, bf16[32,1024]{1,0:T(8,128)(2,1)S(1)}, u32[]{:S(2)}, u32[]{:S(2)}) collective-permute-start(bf16[32,1024]{1,0:T(8,128)(2,1)S(1)} %get-tuple-element.16), channel_id=1, source_target_pairs={{0,14},{4,10},{8,6},{12,2},{14,0},{10,4},{6,8},{2,12},{1,15},{5,11... | collective-permute-start | bytes 196616 | tf_op jit(solution)/shard_map/ppermute | solution.py:23
  79.1 2.5 %copy-start.19 = (bf16[32,1024]{1,0:T(8,128)(2,1)}, bf16[32,1024]{1,0:T(8,128)(2,1)S(1)}, u32[]{:S(2)}) copy-start(bf16[32,1024]{1,0:T(8,128)(2,1)S(1)} %collective-permute-done.27.two_ref) | copy-start | bytes 196612
  (4 other events, 2.6 us)

commit v2 on v1

v2 whole, which is shorter than its diff:
```python
import functools

import jax
import jax.numpy as jnp
from jax import lax
from jax.experimental import pallas as pl
from jax.experimental.pallas import tpu as pltpu
from jax.sharding import PartitionSpec as P

F32 = jnp.float32
BF16 = jnp.bfloat16
VMEM_LIMIT = 28 * 1024 * 1024


def ring_order(count):
    return list(range(0, count, 2)) + list(range(1, count, 2))[::-1]


def shift(value, distance):
    count = lax.axis_size("expert")
    ring = ring_order(count)
    pairs = [(ring[i], ring[(i + distance) % count]) for i in range(count)]
    return lax.ppermute(value, "expert", pairs)


def swap_wave(value):
    return lax.ppermute(value, "wave", [(0, 1), (1, 0)])


def spread(own):
    count = lax.axis_size("expert")
    half = count // 2
    blocks = {0: own}
    blocks[half] = shift(own, half)
    blocks[count - 1] = shift(own, 1)
    blocks[1] = shift(own, -1)
    for step in range(2, count // 4 + 1):
        blocks[count - step] = shift(blocks[count - step + 1], 1)
        blocks[step] = shift(blocks[step - 1], -1)
        blocks[half - step + 1] = shift(blocks[half - step + 2], 1)
        blocks[half + step - 1] = shift(blocks[half + step - 2], -1)
    return blocks


def groups_of_four(count):
    half = count // 2
    later = [
        [step, half + step - 1, count - step, half - step + 1] for step in range(2, count // 4 + 1)
    ]
    return [[0, 1, count - 1, half]] + later


def add(*parts):
    total = parts[0].astype(F32)
    for part in parts[1:]:
        total = total + part.astype(F32)
    return total


def collect(first, later, rows):
    forward = backward = None
    for pair in later[::-1]:
        if forward is not None:
            pair = (add(pair[0], forward).astype(BF16), add(pair[1], backward).astype(BF16))
        forward, backward = shift(pair[0], 1), shift(pair[1], -1)
    own, one, minus, across = first
    if forward is not None:
        one = add(one, forward[:rows]).astype(BF16)
        minus = add(minus, backward[:rows]).astype(BF16)
        across = add(across, forward[rows:], backward[rows:]).astype(BF16)
    half = lax.axis_size("expert") // 2
    return own, shift(across, half), shift(one, 1), shift(minus, -1)


def after(values, *earlier):
    return lax.optimization_barrier((tuple(values), earlier))[0]


def spot(rows, columns, offset):
    down = lax.broadcasted_iota(jnp.int32, (rows, columns), 0)
    across = lax.broadcasted_iota(jnp.int32, (rows, columns), 1)
    return jnp.where(across == down + offset, 1.0, 0.0).astype(BF16)


def digits(value):
    return [(value % 256).astype(F32).astype(BF16), (value // 256).astype(F32).astype(BF16)]


def pack_kernel(columns, n_wave, hidden_ref, ids_ref, weights_ref, codes_ref, owner_ref, out_ref):
    sessions, steps, width = hidden_ref.shape
    expert_count = columns[0] // 2
    books = codes_ref.shape[2]
    meta_width = out_ref.shape[1] - width
    owner = owner_ref[...]
    slots = (owner // sessions // n_wave) * sessions + owner % sessions
    down = lax.broadcasted_iota(jnp.int32, (sessions, sessions), 0)
    across = lax.broadcasted_iota(jnp.int32, (sessions, sessions), 1)
    slot = jnp.sum(jnp.where(down == across, slots, 0).astype(F32), axis=1, keepdims=True)
    slot = slot.astype(jnp.int32)
    lane = lax.broadcasted_iota(jnp.int32, (sessions, meta_width), 1)
    named = lax.broadcasted_iota(jnp.int32, (expert_count, sessions), 0)
    for t in range(steps):
        at = slice(t * sessions, (t + 1) * sessions)
        out_ref[at, 0:width] = hidden_ref[:, t, :]
        weight = jnp.zeros((expert_count, sessions), F32)
        for k in range(ids_ref.shape[1]):
            weight += jnp.where(named == ids_ref[t, k : k + 1, :], weights_ref[t, k : k + 1, :], 0.0)
        high = weight.astype(BF16)
        low = (weight - high.astype(F32)).astype(BF16)
        meta = jnp.zeros((sessions, meta_width), F32)
        for piece, offset in ((high, 0), (low, expert_count)):
            meta += lax.dot_general(
                piece,
                spot(expert_count, meta_width, offset),
                (((0,), (0,)), ((), ())),
                preferred_element_type=F32,
            )
        for i, piece in enumerate(digits(codes_ref[:, t, :])):
            move = spot(books, meta_width, columns[0] + i * books)
            meta += jnp.dot(piece, move, preferred_element_type=F32)
        for i, piece in enumerate(digits(slot * steps + t)):
            meta += jnp.where(lane == columns[1] + i, piece.astype(F32), 0.0)
        out_ref[at, width:] = meta.astype(BF16)


def pack(hidden_rows, expert_ids, route_weights, codes, owner_slot, columns, n_wave):
    sessions, steps, width = hidden_rows.shape
    meta_width = -(-(columns[1] + 2) // 128) * 128
    return pl.pallas_call(
        functools.partial(pack_kernel, columns, n_wave),
        out_shape=jax.ShapeDtypeStruct((steps * sessions, width + meta_width), BF16),
        compiler_params=pltpu.CompilerParams(vmem_limit_bytes=VMEM_LIMIT),
        name="pack",
    )(
        hidden_rows,
        jnp.transpose(expert_ids, (1, 2, 0)),
        jnp.transpose(route_weights, (1, 2, 0)),
        codes,
        owner_slot[None],
    )


def experts_kernel(width, expert_count, counts, place_ref, *refs):
    blocks = refs[: sum(counts)]
    gate_ref, up_ref, down_ref = refs[sum(counts) : sum(counts) + 3]
    outs = refs[sum(counts) + 3 : -2]
    rows_ref, act_ref = refs[-2:]
    local, _, units = gate_ref.shape
    rows = blocks[0].shape[0]
    for i, block in enumerate(blocks):
        rows_ref[i * rows : (i + 1) * rows, :] = block[:, 0:width]
    meta = jnp.concatenate([block[:, width:].astype(F32) for block in blocks], axis=0)
    lane = lax.broadcasted_iota(jnp.int32, meta.shape, 1)
    for j in range(local):
        mine = place_ref[0] * local + j
        hit = (lane == mine) | (lane == expert_count + mine)
        weight = jnp.sum(jnp.where(hit, meta, 0.0), axis=1, keepdims=True)
        gate = jnp.dot(rows_ref[...], gate_ref[j], preferred_element_type=F32)
        up = jnp.dot(rows_ref[...], up_ref[j], preferred_element_type=F32)
        value = gate * jax.nn.sigmoid(gate) * up
        act_ref[:, j * units : (j + 1) * units] = (value * weight).astype(BF16)
    start = 0
    for out_ref in outs:
        size = out_ref.shape[0]
        act = act_ref[start : start + size, :]
        out_ref[...] = jnp.dot(act, down_ref[...], preferred_element_type=F32).astype(BF16)
        start += size


def experts(parts, place, w_gate, w_up, w_down):
    local, width, units = w_gate.shape
    counts = [len(blocks) for blocks in parts]
    blocks = [block for part in parts for block in part]
    rows = blocks[0].shape[0]
    total = rows * len(blocks)
    vmem = pl.BlockSpec(memory_space=pltpu.VMEM)
    return pl.pallas_call(
        functools.partial(
            experts_kernel, width, lax.axis_size("expert") * local, tuple(counts)
        ),
        out_shape=[jax.ShapeDtypeStruct((rows * c, width), BF16) for c in counts],
        in_specs=[pl.BlockSpec(memory_space=pltpu.SMEM)] + [vmem] * (len(blocks) + 3),
        out_specs=[vmem] * len(counts),
        scratch_shapes=[
            pltpu.VMEM((total, width), BF16),
            pltpu.VMEM((total, local * units), BF16),
        ],
        compiler_params=pltpu.CompilerParams(vmem_limit_bytes=VMEM_LIMIT),
        cost_estimate=pl.CostEstimate(
            flops=6 * total * width * units * local,
            bytes_accessed=6 * local * width * units,
            transcendentals=total * units * local,
        ),
        name="experts",
    )(place, *blocks, w_gate, w_up, w_down.reshape(local * units, width))


def frames_kernel(columns, books, shard, sessions, steps, order, place_ref, *refs):
    metas = refs[: len(order)]
    table_ref, out_ref, hot_ref = refs[len(order) :]
    count = len(order)
    code_at, slot_at = columns
    rows = metas[0].shape[0]
    meta = jnp.concatenate([m[...] for m in metas], axis=0)
    total = meta.shape[0]
    slot = meta[:, slot_at : slot_at + 2].astype(F32)
    source = (slot[:, 0:1] + 256.0 * slot[:, 1:2]).astype(jnp.int32)
    lane = lax.broadcasted_iota(jnp.int32, (1, total), 1)
    inside = lane % rows
    target = (inside % sessions) * steps + inside // sessions
    place = place_ref[0]
    turn = jnp.where(place % 2 == 0, place // 2, count - 1 - place // 2)
    for i, k in enumerate(order):
        at = (turn + k) % count
        device = jnp.where(at < count // 2, 2 * at, 2 * (count - 1 - at) + 1)
        target = target + jnp.where(lane // rows == i, device * rows, 0)
    chooser = jnp.where(source == target, 1.0, 0.0).astype(BF16)
    ordered = lax.dot_general(
        chooser, meta, (((0,), (0,)), ((), ())), preferred_element_type=F32
    )
    low = ordered[:, code_at : code_at + books]
    high = ordered[:, code_at + books : code_at + 2 * books]
    codes = (low + 256.0 * high).astype(jnp.int32) - place * shard
    chunk = 128
    lanes = lax.broadcasted_iota(jnp.int32, (total, chunk), 1)
    for start in range(0, books * shard, chunk):
        first, last = start // shard, (start + chunk - 1) // shard
        code = codes[:, first : first + 1] + (first * shard - start)
        for q in range(first + 1, last + 1):
            shifted = codes[:, q : q + 1] + (q * shard - start)
            code = jnp.where(lanes >= q * shard - start, shifted, code)
        hit = lanes == code
        if shard < chunk:
            low_end = lanes // shard * shard
            hit = hit & (code >= low_end) & (code < low_end + shard)
        hot_ref[:, start : start + chunk] = jnp.where(hit, 1.0, 0.0).astype(BF16)
    out_ref[...] = jnp.dot(hot_ref[...], table_ref[...], preferred_element_type=F32).astype(BF16)


def frame_sums(blocks, order, place, code_table, columns, width, sessions, steps):
    books, shard, channels = code_table.shape
    rows = blocks[0].shape[0]
    total = rows * len(order)
    meta_width = blocks[0].shape[1] - width
    vmem = pl.BlockSpec(memory_space=pltpu.VMEM)
    return pl.pallas_call(
        functools.partial(frames_kernel, columns, books, shard, sessions, steps, order),
        grid=(1,),
        out_shape=jax.ShapeDtypeStruct((total, channels), BF16),
        in_specs=[pl.BlockSpec(memory_space=pltpu.SMEM)]
        + [pl.BlockSpec((rows, meta_width), lambda i: (0, width // meta_width))] * len(order)
        + [vmem],
        out_specs=vmem,
        scratch_shapes=[pltpu.VMEM((total, books * shard), BF16)],
        compiler_params=pltpu.CompilerParams(vmem_limit_bytes=VMEM_LIMIT),
        cost_estimate=pl.CostEstimate(
            flops=2 * total * books * shard * channels,
            bytes_accessed=2 * books * shard * channels,
            transcendentals=0,
        ),
        name="frame_sums",
    )(place, *[blocks[k] for k in order], code_table.reshape(books * shard, channels))


def decoder_kernel(*refs):
    terms, (state_ref, taps_ref, bias_ref, up_ref, wave_ref, new_ref) = refs[:-6], refs[-6:]
    past, sessions, _ = state_ref.shape
    taps = taps_ref.shape[0]
    frames = terms[0][...].astype(F32)
    for term in terms[1:]:
        frames = frames + term[...].astype(F32)
    steps = frames.shape[0] // sessions
    history = [state_ref[i].astype(F32) for i in range(past)]
    history += [frames[t * sessions : (t + 1) * sessions] for t in range(steps)]
    for t in range(steps):
        filtered = bias_ref[...] + taps_ref[0:1, :] * history[past + t]
        for j in range(1, taps):
            filtered = filtered + taps_ref[j : j + 1, :] * history[past + t - j]
        decoded = jax.nn.gelu(filtered).astype(BF16)
        sample = jnp.dot(decoded, up_ref[...], preferred_element_type=F32)
        wave_ref[:, t, :] = sample.astype(BF16)
    for i in range(past):
        new_ref[i] = history[i + steps].astype(BF16)


def decoder(terms, conv_state, conv_taps, conv_bias, upsample):
    sessions, past, channels = conv_state.shape
    steps = terms[0].shape[0] // sessions
    wave, state = pl.pallas_call(
        decoder_kernel,
        out_shape=(
            jax.ShapeDtypeStruct((sessions, steps, upsample.shape[1]), BF16),
            jax.ShapeDtypeStruct((past, sessions, channels), BF16),
        ),
        compiler_params=pltpu.CompilerParams(vmem_limit_bytes=VMEM_LIMIT),
        name="decoder",
    )(
        *terms,
        jnp.transpose(conv_state, (1, 0, 2)),
        conv_taps,
        conv_bias.reshape(1, channels),
        upsample,
    )
    return wave, jnp.transpose(state, (1, 0, 2))


def last_sum_kernel(*refs):
    terms, out_ref = refs[:-1], refs[-1]
    sessions, steps, _ = out_ref.shape
    total = terms[0][...].astype(F32)
    for term in terms[1:]:
        total = total + term[...].astype(F32)
    for t in range(steps):
        out_ref[:, t, :] = total[t * sessions : (t + 1) * sessions].astype(BF16)


def last_sum(terms, shape):
    return pl.pallas_call(
        last_sum_kernel,
        out_shape=jax.ShapeDtypeStruct(shape, BF16),
        compiler_params=pltpu.CompilerParams(vmem_limit_bytes=VMEM_LIMIT),
        name="last_sum",
    )(*terms)


def per_device(
    hidden_rows,
    expert_ids,
    route_weights,
    w_gate,
    w_up,
    w_down,
    codes,
    owner_slot,
    code_table,
    conv_state,
    conv_taps,
    conv_bias,
    upsample,
):
    count = lax.axis_size("expert")
    sessions, steps, width = hidden_rows.shape
    rows = sessions * steps
    books = codes.shape[2]
    expert_count = count * w_gate.shape[0]
    place = lax.axis_index("expert").astype(jnp.int32)[None]
    columns = (2 * expert_count, 2 * expert_count + 2 * books)

    own = pack(
        hidden_rows,
        expert_ids,
        route_weights,
        codes,
        owner_slot,
        columns,
        lax.axis_size("wave"),
    )
    blocks = spread(own)
    other = {k: swap_wave(v) for k, v in blocks.items()}
    groups = groups_of_four(count)

    def work(parts):
        return experts(parts, place, w_gate, w_up, w_down)

    near = groups[0]
    near_other, near_own = work([[other[k] for k in near], [blocks[k] for k in near]])
    near_other = swap_wave(near_other)
    for k in groups[-1]:
        blocks[k], other[k] = after((blocks[k], other[k]), near_own)

    order = [k for group in groups for k in group]
    sums = frame_sums(blocks, order, place, code_table, columns, width, sessions, steps)
    quarter = [sums[i * rows : (i + 1) * rows] for i in range(4)]
    pairs = [
        (sums[i * rows : (i + 2) * rows], sums[(i + 2) * rows : (i + 4) * rows])
        for i in range(4, count, 4)
    ]
    frames = collect(quarter, pairs, rows)

    later = []
    for group in groups[1:]:
        (from_other,) = work([[other[k] for k in group]])
        from_other = swap_wave(from_other)
        (result,) = work([[blocks[k] for k in group]])
        both = [
            add(result[at], from_other[at]).astype(BF16)
            for at in (slice(0, 2 * rows), slice(2 * rows, 4 * rows))
        ]
        later.append(both)
    first = [
        add(near_own[i * rows : (i + 1) * rows], near_other[i * rows : (i + 1) * rows])
        for i in range(4)
    ]
    first = [first[0]] + [v.astype(BF16) for v in first[1:]]
    terms = collect(first, later, rows)
    samples, carried = decoder(frames, conv_state, conv_taps, conv_bias, upsample)
    terms = after(terms, samples)
    mixed = last_sum(terms, hidden_rows.shape)
    return mixed, samples, carried


def solution(mesh):
    rows = P(("groups", "expert", "wave"), None, None)
    placed = (
        rows,
        rows,
        rows,
        P("expert", None, "wave"),
        P("expert", None, "wave"),
        P("expert", "wave", None),
        rows,
        P(("groups", "expert", "wave")),
        P(None, "expert", None),
        rows,
        P(),
        P(),
        P(),
    )
    return jax.shard_map(
        per_device,
        mesh=mesh,
        in_specs=placed,
        out_specs=(rows, rows, rows),
        check_vma=False,
    )
```

time: 88.1 us -> 68.5 us (0.78)
  Pallas kernels: 23.3 us -> 11.5 us
  waiting for transfers between devices: 12.3 us -> 18.7 us
  other arithmetic: 6.02 us -> 0.42 us
  starting transfers between devices: 32.4 us -> 27.1 us
  local copies, waits for them, and re-layouts: 12 us -> 9.4 us
    pallas_call x3 -> x6, Pallas kernels: 18 us -> 9.37 us  [the longest x3 6.98 us: experts(): pl.pallas_call(functools.partial(experts_kernel, width, lax.axis_size('ex...]
    ppermute x21 -> x17, waiting for transfers between devices: 12.3 us -> 18.7 us  [shift(): return lax.ppermute(value, 'expert', pairs)]
    unnamed x44 -> x32, local copies, waits for them, and re-layouts: 3.43 us -> 9.37 us
    ppermute x21 -> x17, starting transfers between devices: 30.2 us -> 26 us  [shift(): return lax.ppermute(value, 'expert', pairs)]
    slice x3 -> x2, local copies, waits for them, and re-layouts: 3.87 us -> 0.02 us  [the longest x1 0.02 us: per_device(): sums[i * rows:(i + 2) * rows]]
    reshape x3 -> x0, local copies, waits for them, and re-layouts: 3.12 us -> none  [the longest x1 1.41 us: decoder(): wave.reshape(rows // sessions, sessions, -1)]
    pallas_call x1, Pallas kernels: 5.28 us -> 2.18 us  [frame_sums(): pl.pallas_call(functools.partial(frames_kernel, columns, books, shard, se...]
    convert_element_type x7 -> x3, other arithmetic: 2.16 us -> 0.42 us  [the longest x2 0.29 us: collect(): minus = add(minus, backward[:rows]).astype(BF16)]
  transfers between devices with their start and end apart: 31 -> 27, of which waited for: 8 -> 8; matrix products, arithmetic and copies ran while one was open for 12% -> 1% of each run, Pallas kernels for 27% -> 12%
where the time goes in v2:
time: 68.5 us; the launch traced here: 68.1 us
  starting transfers between devices  27.1 us (40%)
  waiting for transfers between devices  18.7 us (27%)
  Pallas kernels  11.5 us (17%)
  local copies, waits for them, and re-layouts  9.4 us (14%)
  between operations  0.85 us (1%)
    ppermute x17, starting transfers between devices, shift(): return lax.ppermute(value, 'expert', pairs)  26 us
    ppermute x17, waiting for transfers between devices, shift(): return lax.ppermute(value, 'expert', pairs)  18.7 us
    unnamed x32, local copies, waits for them, and re-layouts  9.37 us
    pallas_call x3, Pallas kernels, experts(): pl.pallas_call(functools.partial(experts_kernel, width, lax.axis_size('ex...  6.98 us
    pallas_call x1, Pallas kernels, frame_sums(): pl.pallas_call(functools.partial(frames_kernel, columns, books, shard, se...  2.18 us
  transfers between devices with their start and end apart: 27, of which 8 were waited for; matrix products, arithmetic and copies ran while one was open for 1% of the time, Pallas kernels for 12%

profile of v2, /device:TPU:0, one launch (start us, length us, event | category | flops | bytes accessed | tf_op | source)
XLA Modules:
  0.0 68.1 jit_solution(17580282782727365176)
XLA Ops:
  0.6 0.9 %copy-done.9 = bf16[16,2,2048]{2,1,0:T(2,128)(2,1)S(1)} copy-done((bf16[16,2,2048]{2,1,0:T(2,128)(2,1)S(1)}, bf16[16,2,2048]{2,1,0:T(2,128)(2,1)}, u32[]{:S(2)}) %copy-start.9) | copy-done | bytes 131096
  1.5 0.7 %copy-done.11 = s32[16,2,16]{2,1,0:T(2,128)S(1)} copy-done((s32[16,2,16]{2,1,0:T(2,128)S(1)}, s32[16,2,16]{2,1,0:T(2,128)}, u32[]{:S(2)}) %copy-start.11) | copy-done | bytes 2072
  2.3 0.7 %copy-done.12 = s32[16,2,8]{0,2,1:T(8,128)S(1)} copy-done((s32[16,2,8]{0,2,1:T(8,128)S(1)}, s32[16,2,8]{0,2,1:T(8,128)}, u32[]{:S(2)}) %copy-start.12) | copy-done | bytes 1048
  3.0 0.7 %copy-done.13 = f32[16,2,8]{0,2,1:T(8,128)S(1)} copy-done((f32[16,2,8]{0,2,1:T(8,128)S(1)}, f32[16,2,8]{0,2,1:T(8,128)}, u32[]{:S(2)}) %copy-start.13) | copy-done | bytes 1048
  3.7 0.7 copy-done.15
  4.3 0.6 pack.1.refs_4_.refs_0_
  4.9 6.1 %collective-permute-start.5 = (bf16[32,2176]{1,0:T(8,128)(2,1)S(1)}, bf16[32,2176]{1,0:T(8,128)(2,1)S(1)}, u32[]{:S(2)}, u32[]{:S(2)}) collective-permute-start(bf16[32,2176]{1,0:T(8,128)(2,1)S(1)} %pack.1.refs_4_.refs_0_), channel_id=1, source_target_pairs={{0,14},{4,10},{8,6},{12,2},{14,0},{10,4},{6,8},{2,12},{1,15},{5,11... | collective-permute-start | bytes 417800 | tf_op jit(solution)/shard_map/ppermute | solution.py:23
  10.9 0.5 collective-permute-start.1
  11.4 1.5 %collective-permute-start.3 = (bf16[32,2176]{1,0:T(8,128)(2,1)S(1)}, bf16[32,2176]{1,0:T(8,128)(2,1)S(1)}, u32[]{:S(2)}, u32[]{:S(2)}) collective-permute-start(bf16[32,2176]{1,0:T(8,128)(2,1)S(1)} %pack.1.refs_4_.refs_0_), channel_id=1, source_target_pairs={{0,4},{4,8},{8,12},{12,14},{14,10},{10,6},{6,2},{2,0},{1,5},{5,9},... | collective-permute-start | bytes 417800 | tf_op jit(solution)/shard_map/ppermute | solution.py:23
  13.0 2.5 %collective-permute-done.5.refs_7_.refs_3_ = bf16[32,2176]{1,0:T(8,128)(2,1)S(1)} collective-permute-done((bf16[32,2176]{1,0:T(8,128)(2,1)S(1)}, bf16[32,2176]{1,0:T(8,128)(2,1)S(1)}, u32[]{:S(2)}, u32[]{:S(2)}) %collective-permute-start.5) | collective-permute-done | bytes 139296 | tf_op jit(solution)/shard_map/ppermute | solution.py:23
  15.5 2.1 %collective-permute-done.1.refs_5_.refs_1_ = bf16[32,2176]{1,0:T(8,128)(2,1)S(1)} collective-permute-done((bf16[32,2176]{1,0:T(8,128)(2,1)S(1)}, bf16[32,2176]{1,0:T(8,128)(2,1)S(1)}, u32[]{:S(2)}, u32[]{:S(2)}) %collective-permute-start.1) | collective-permute-done | bytes 139296 | tf_op jit(solution)/shard_map/ppermute | solution.py:23
  17.6 2.7 %collective-permute-start.14 = (bf16[32,2176]{1,0:T(8,128)(2,1)S(1)}, bf16[32,2176]{1,0:T(8,128)(2,1)S(1)}, u32[]{:S(2)}, u32[]{:S(2)}) collective-permute-start(bf16[32,2176]{1,0:T(8,128)(2,1)S(1)} %collective-permute-done.5.refs_7_.refs_3_), channel_id=1, source_target_pairs={{0,4},{4,8},{8,12},{12,14},{14,10},{10,6},{6,2},{2,0},{1,5},{5,9},... | collective-permute-start | bytes 417800 | tf_op jit(solution)/shard_map/ppermute | solution.py:23
  20.3 2.0 %collective-permute-start.12 = (bf16[32,2176]{1,0:T(8,128)(2,1)S(1)}, bf16[32,2176]{1,0:T(8,128)(2,1)S(1)}, u32[]{:S(2)}, u32[]{:S(2)}) collective-permute-start(bf16[32,2176]{1,0:T(8,128)(2,1)S(1)} %collective-permute-done.3.refs_6_.refs_2_), channel_id=1, source_target_pairs={{0,4},{4,8},{8,12},{12,14},{14,10},{10,6},{6,2},{2,0},{1,5},{5,9},... | collective-permute-start | bytes 417800 | tf_op jit(solution)/shard_map/ppermute | solution.py:23
  22.3 0.1 collective-permute-start.8
  22.4 0.0 collective-permute-start.4
  22.4 1.9 %collective-permute-done.14.refs_3_.refs_7_ = bf16[32,2176]{1,0:T(8,128)(2,1)S(1)} collective-permute-done((bf16[32,2176]{1,0:T(8,128)(2,1)S(1)}, bf16[32,2176]{1,0:T(8,128)(2,1)S(1)}, u32[]{:S(2)}, u32[]{:S(2)}) %collective-permute-start.14) | collective-permute-done | bytes 139296 | tf_op jit(solution)/shard_map/ppermute | solution.py:23
  24.3 2.5 %collective-permute-done.10.refs_1_.refs_5_ = bf16[32,2176]{1,0:T(8,128)(2,1)S(1)} collective-permute-done((bf16[32,2176]{1,0:T(8,128)(2,1)S(1)}, bf16[32,2176]{1,0:T(8,128)(2,1)S(1)}, u32[]{:S(2)}, u32[]{:S(2)}) %collective-permute-start.10) | collective-permute-done | bytes 139296 | tf_op jit(solution)/shard_map/ppermute | solution.py:23
  26.8 0.1 collective-permute-done.12.refs_2_.refs_6_
  26.9 0.4 collective-permute-start.13
  27.3 1.8 %collective-permute-done.8.refs_0_.refs_4_ = bf16[32,2176]{1,0:T(8,128)(2,1)S(1)} collective-permute-done((bf16[32,2176]{1,0:T(8,128)(2,1)S(1)}, bf16[32,2176]{1,0:T(8,128)(2,1)S(1)}, u32[]{:S(2)}, u32[]{:S(2)}) %collective-permute-start.8) | collective-permute-done | bytes 139296 | tf_op jit(solution)/shard_map/ppermute | solution.py:23
  29.1 1.9 %copy-done = bf16[2,2048,384]{2,1,0:T(8,128)(2,1)S(1)} copy-done((bf16[2,2048,384]{2,1,0:T(8,128)(2,1)S(1)}, bf16[2,2048,384]{2,1,0:T(8,128)(2,1)}, u32[]{:S(2)}) %copy-start) | copy-done | bytes 3145752
  31.0 1.9 %copy-done.2 = bf16[2,2048,384]{2,1,0:T(8,128)(2,1)S(1)} copy-done((bf16[2,2048,384]{2,1,0:T(8,128)(2,1)S(1)}, bf16[2,2048,384]{2,1,0:T(8,128)(2,1)}, u32[]{:S(2)}) %copy-start.2) | copy-done | bytes 3145752
  32.9 1.9 %copy-done.4 = bf16[2,384,2048]{2,1,0:T(8,128)(2,1)S(1)} copy-done((bf16[2,384,2048]{2,1,0:T(8,128)(2,1)S(1)}, bf16[2,384,2048]{2,1,0:T(8,128)(2,1)}, u32[]{:S(2)}) %copy-start.4) | copy-done | bytes 3145752
  34.8 3.3 %experts.3 = (bf16[128,2048]{1,0:T(8,128)(2,1)S(1)}, bf16[128,2048]{1,0:T(8,128)(2,1)S(1)}) custom-call(s32[1]{0:T(128)} %bitcast.place_ref, bf16[32,2176]{1,0:T(8,128)(2,1)S(1)} %collective-permute-done.refs_0_, bf16[32,2176]{1,0:T(8,128)(2,1)S(1)} %collective-permute-done.2.refs_1_, bf16[32,2176]{1,0:T(8,128)(2,1)S(1)} %collective-permute-done.4.refs_2_, ...), custom_call_target="tpu_custom_call" | custom-call | flops 2415919104 | bytes 9437184 | tf_op jit(solution)/shard_map/experts/pallas_call | solution.py:177
  38.1 0.0 copy-start.6
  38.2 1.8 %experts.5 = bf16[128,2048]{1,0:T(8,128)(2,1)S(1)} custom-call(s32[1]{0:T(128)} %bitcast.place_ref, bf16[32,2176]{1,0:T(8,128)(2,1)S(1)} %collective-permute-done.9.refs_0_, bf16[32,2176]{1,0:T(8,128)(2,1)S(1)} %collective-permute-done.11.refs_1_, bf16[32,2176]{1,0:T(8,128)(2,1)S(1)} %collective-permute-done.13.refs_2_, ...), custom_call_target="tpu_custom_call" | custom-call | flops 1207959552 | bytes 9437184 | tf_op jit(solution)/shard_map/experts/pallas_call | solution.py:177
  40.0 0.6 collective-permute-start.16
  40.5 0.1 collective-permute-start.7
  40.6 2.2 %frame_sums.1 = bf16[256,1024]{1,0:T(8,128)(2,1)S(1)} custom-call(s32[1]{0:T(128)} %bitcast.place_ref, bf16[32,2176]{1,0:T(8,128)(2,1)S(1)} %pack.1.refs_4_.refs_0_, bf16[32,2176]{1,0:T(8,128)(2,1)S(1)} %collective-permute-done.1.refs_5_.refs_1_, bf16[32,2176]{1,0:T(8,128)(2,1)S(1)} %collective-permute-done.3.refs_6_.refs_2_, ...), custom_call_target="tpu_custom_call" | custom-call | flops 1073741824 | bytes 4194304 | tf_op jit(solution)/shard_map/frame_sums/pallas_call | solution.py:246
  42.8 0.8 %collective-permute-start.22 = (bf16[64,1024]{1,0:T(8,128)(2,1)S(1)}, bf16[64,1024]{1,0:T(8,128)(2,1)S(1)}, u32[]{:S(2)}, u32[]{:S(2)}) collective-permute-start(bf16[64,1024]{1,0:T(8,128)(2,1)S(1)} %get-tuple-element.44), channel_id=1, source_target_pairs={{0,4},{4,8},{8,12},{12,14},{14,10},{10,6},{6,2},{2,0},{1,5},{5,9},... | collective-permute-start | bytes 393224 | tf_op jit(solution)/shard_map/ppermute | solution.py:23
  43.6 1.3 %collective-permute-start.23 = (bf16[64,1024]{1,0:T(8,128)(2,1)S(1)}, bf16[64,1024]{1,0:T(8,128)(2,1)S(1)}, u32[]{:S(2)}, u32[]{:S(2)}) collective-permute-start(bf16[64,1024]{1,0:T(8,128)(2,1)S(1)} %get-tuple-element.45), channel_id=1, source_target_pairs={{0,2},{4,0},{8,4},{12,8},{14,12},{10,14},{6,10},{2,6},{1,3},{5,1},... | collective-permute-start | bytes 393224 | tf_op jit(solution)/shard_map/ppermute | solution.py:23
  44.9 1.8 %experts.4 = bf16[128,2048]{1,0:T(8,128)(2,1)S(1)} custom-call(s32[1]{0:T(128)} %bitcast.place_ref, bf16[32,2176]{1,0:T(8,128)(2,1)S(1)} %collective-permute-done.8.refs_0_.refs_4_, bf16[32,2176]{1,0:T(8,128)(2,1)S(1)} %collective-permute-done.10.refs_1_.refs_5_, bf16[32,2176]{1,0:T(8,128)(2,1)S(1)} %collective-permute-done.12.refs_2_.refs_6_, ...), custom_call_target="tpu_custom_call" | custom-call | flops 1207959552 | bytes 9437184 | tf_op jit(solution)/shard_map/experts/pallas_call | solution.py:177
  46.8 0.0 copy-start.10
  46.8 0.1 add_convert_fusion.1
  47.0 0.8 %collective-permute-start.17 = (bf16[64,2048]{1,0:T(8,128)(2,1)S(1)}, bf16[64,2048]{1,0:T(8,128)(2,1)S(1)}, u32[]{:S(2)}, u32[]{:S(2)}) collective-permute-start(bf16[64,2048]{1,0:T(8,128)(2,1)S(1)} %get-tuple-element.39), channel_id=1, source_target_pairs={{0,4},{4,8},{8,12},{12,14},{14,10},{10,6},{6,2},{2,0},{1,5},{5,9},... | collective-permute-start | bytes 786440 | tf_op jit(solution)/shard_map/ppermute | solution.py:23
  47.7 1.3 %collective-permute-start.18 = (bf16[64,2048]{1,0:T(8,128)(2,1)S(1)}, bf16[64,2048]{1,0:T(8,128)(2,1)S(1)}, u32[]{:S(2)}, u32[]{:S(2)}) collective-permute-start(bf16[64,2048]{1,0:T(8,128)(2,1)S(1)} %get-tuple-element.40), channel_id=1, source_target_pairs={{0,2},{4,0},{8,4},{12,8},{14,12},{10,14},{6,10},{2,6},{1,3},{5,1},... | collective-permute-start | bytes 786440 | tf_op jit(solution)/shard_map/ppermute | solution.py:23
  49.1 0.1 add_convert_fusion.8
  49.1 2.5 %collective-permute-start.24 = (bf16[32,1024]{1,0:T(8,128)(2,1)S(1)}, bf16[32,1024]{1,0:T(8,128)(2,1)S(1)}, u32[]{:S(2)}, u32[]{:S(2)}) collective-permute-start(bf16[32,1024]{1,0:T(8,128)(2,1)S(1)} %get-tuple-element.42), channel_id=1, source_target_pairs={{0,14},{4,10},{8,6},{12,2},{14,0},{10,4},{6,8},{2,12},{1,15},{5,11... | collective-permute-start | bytes 196616 | tf_op jit(solution)/shard_map/ppermute | solution.py:23
  51.6 4.2 %collective-permute-done.17 = bf16[64,2048]{1,0:T(8,128)(2,1)S(1)} collective-permute-done((bf16[64,2048]{1,0:T(8,128)(2,1)S(1)}, bf16[64,2048]{1,0:T(8,128)(2,1)S(1)}, u32[]{:S(2)}, u32[]{:S(2)}) %collective-permute-start.17) | collective-permute-done | bytes 262176 | tf_op jit(solution)/shard_map/ppermute | solution.py:23
  55.8 0.2 add_convert_fusion.2
  56.1 2.5 %collective-permute-start.19 = (bf16[32,2048]{1,0:T(8,128)(2,1)S(1)}, bf16[32,2048]{1,0:T(8,128)(2,1)S(1)}, u32[]{:S(2)}, u32[]{:S(2)}) collective-permute-start(bf16[32,2048]{1,0:T(8,128)(2,1)S(1)} %get-tuple-element.36), channel_id=1, source_target_pairs={{0,14},{4,10},{8,6},{12,2},{14,0},{10,4},{6,8},{2,12},{1,15},{5,11... | collective-permute-start | bytes 393224 | tf_op jit(solution)/shard_map/ppermute | solution.py:23
  58.5 0.3 collective-permute-start.20
  58.8 1.7 %collective-permute-start.21 = (bf16[32,2048]{1,0:T(8,128)(2,1)S(1)}, bf16[32,2048]{1,0:T(8,128)(2,1)S(1)}, u32[]{:S(2)}, u32[]{:S(2)}) collective-permute-start(bf16[32,2048]{1,0:T(8,128)(2,1)S(1)} %get-tuple-element.35), channel_id=1, source_target_pairs={{0,2},{4,0},{8,4},{12,8},{14,12},{10,14},{6,10},{2,6},{1,3},{5,1},... | collective-permute-start | bytes 393224 | tf_op jit(solution)/shard_map/ppermute | solution.py:23
  60.6 0.3 collective-permute-start.25
  60.8 1.7 %collective-permute-start.26 = (bf16[32,1024]{1,0:T(8,128)(2,1)S(1)}, bf16[32,1024]{1,0:T(8,128)(2,1)S(1)}, u32[]{:S(2)}, u32[]{:S(2)}) collective-permute-start(bf16[32,1024]{1,0:T(8,128)(2,1)S(1)} %get-tuple-element.41), channel_id=1, source_target_pairs={{0,2},{4,0},{8,4},{12,8},{14,12},{10,14},{6,10},{2,6},{1,3},{5,1},... | collective-permute-start | bytes 196616 | tf_op jit(solution)/shard_map/ppermute | solution.py:23
  62.6 3.6 %collective-permute-done.25.refs_2_ = bf16[32,1024]{1,0:T(8,128)(2,1)S(1)} collective-permute-done((bf16[32,1024]{1,0:T(8,128)(2,1)S(1)}, bf16[32,1024]{1,0:T(8,128)(2,1)S(1)}, u32[]{:S(2)}, u32[]{:S(2)}) %collective-permute-start.25) | collective-permute-done | bytes 65568 | tf_op jit(solution)/shard_map/ppermute | solution.py:23
  66.2 1.1 %decoder.1 = (bf16[16,2,512]{2,1,0:T(2,128)(2,1)}, bf16[6,16,1024]{2,1,0:T(8,128)(2,1)}) custom-call(bf16[32,1024]{1,0:T(8,128)(2,1)S(1)} %slice.116.refs_0_, bf16[32,1024]{1,0:T(8,128)(2,1)S(1)} %collective-permute-done.24.refs_1_, bf16[32,1024]{1,0:T(8,128)(2,1)S(1)} %collective-permute-done.25.refs_2_, ...), custom_call_target="tpu_custom_call" | custom-call | tf_op jit(solution)/shard_map/decoder/pallas_call | solution.py:289
  67.3 0.8 %last_sum.1 = bf16[16,2,2048]{2,1,0:T(2,128)(2,1)} custom-call(f32[32,2048]{1,0:T(8,128)S(1)} %get-tuple-element.30.refs_0_, bf16[32,2048]{1,0:T(8,128)(2,1)S(1)} %collective-permute-done.19.refs_1_, bf16[32,2048]{1,0:T(8,128)(2,1)S(1)} %collective-permute-done.20.refs_2_, bf16[32,2048]{1,0:T(8,128)(2,1)S(1)} %collective-permute-done.21.refs_3_), custom_call_target="tpu_custom_call" | custom-call | tf_op jit(solution)/shard_map/last_sum/pallas_call | solution.py:318
  (50 shorter events, 0.1 us)
Async XLA Ops:
  0.6 0.9 %copy-start.9 = (bf16[16,2,2048]{2,1,0:T(2,128)(2,1)S(1)}, bf16[16,2,2048]{2,1,0:T(2,128)(2,1)}, u32[]{:S(2)}) copy-start(bf16[16,2,2048]{2,1,0:T(2,128)(2,1)} %hidden_ref.1) | copy-start | bytes 393220
  1.5 0.7 %copy-start.11 = (s32[16,2,16]{2,1,0:T(2,128)S(1)}, s32[16,2,16]{2,1,0:T(2,128)}, u32[]{:S(2)}) copy-start(s32[16,2,16]{2,1,0:T(2,128)} %codes_ref.1) | copy-start | bytes 6148
  2.3 0.7 %copy-start.12 = (s32[16,2,8]{0,2,1:T(8,128)S(1)}, s32[16,2,8]{0,2,1:T(8,128)}, u32[]{:S(2)}) copy-start(s32[16,2,8]{0,2,1:T(8,128)} %param.14) | copy-start | bytes 3076
  3.0 0.7 %copy-start.13 = (f32[16,2,8]{0,2,1:T(8,128)S(1)}, f32[16,2,8]{0,2,1:T(8,128)}, u32[]{:S(2)}) copy-start(f32[16,2,8]{0,2,1:T(8,128)} %param.15) | copy-start | bytes 3076
  3.6 0.7 copy-start.15
  4.9 10.6 %collective-permute-start.5 = (bf16[32,2176]{1,0:T(8,128)(2,1)S(1)}, bf16[32,2176]{1,0:T(8,128)(2,1)S(1)}, u32[]{:S(2)}, u32[]{:S(2)}) collective-permute-start(bf16[32,2176]{1,0:T(8,128)(2,1)S(1)} %pack.1.refs_4_.refs_0_), channel_id=1, source_target_pairs={{0,14},{4,10},{8,6},{12,2},{14,0},{10,4},{6,8},{2,12},{1,15},{5,11... | collective-permute-start | bytes 417800 | tf_op jit(solution)/shard_map/ppermute | solution.py:23
  10.9 6.7 %collective-permute-start.1 = (bf16[32,2176]{1,0:T(8,128)(2,1)S(1)}, bf16[32,2176]{1,0:T(8,128)(2,1)S(1)}, u32[]{:S(2)}, u32[]{:S(2)}) collective-permute-start(bf16[32,2176]{1,0:T(8,128)(2,1)S(1)} %pack.1.refs_4_.refs_0_), channel_id=1, source_target_pairs={{0,2},{4,0},{8,4},{12,8},{14,12},{10,14},{6,10},{2,6},{1,3},{5,1},... | collective-permute-start | bytes 417800 | tf_op jit(solution)/shard_map/ppermute | solution.py:23
  11.4 8.9 %collective-permute-start.3 = (bf16[32,2176]{1,0:T(8,128)(2,1)S(1)}, bf16[32,2176]{1,0:T(8,128)(2,1)S(1)}, u32[]{:S(2)}, u32[]{:S(2)}) collective-permute-start(bf16[32,2176]{1,0:T(8,128)(2,1)S(1)} %pack.1.refs_4_.refs_0_), channel_id=1, source_target_pairs={{0,4},{4,8},{8,12},{12,14},{14,10},{10,6},{6,2},{2,0},{1,5},{5,9},... | collective-permute-start | bytes 417800 | tf_op jit(solution)/shard_map/ppermute | solution.py:23
  13.0 7.3 %collective-permute-start = (bf16[32,2176]{1,0:T(8,128)(2,1)S(1)}, bf16[32,2176]{1,0:T(8,128)(2,1)S(1)}, u32[]{:S(2)}, u32[]{:S(2)}) collective-permute-start(bf16[32,2176]{1,0:T(8,128)(2,1)S(1)} %pack.1.refs_4_.refs_0_), channel_id=1, source_target_pairs={{0,1},{1,0},{2,3},{3,2},{4,5},{5,4},{6,7},{7,6},{8,9},{9,8},{10,11... | collective-permute-start | bytes 417800 | tf_op jit(solution)/shard_map/ppermute | solution.py:27
  15.5 6.8 %collective-permute-start.6 = (bf16[32,2176]{1,0:T(8,128)(2,1)S(1)}, bf16[32,2176]{1,0:T(8,128)(2,1)S(1)}, u32[]{:S(2)}, u32[]{:S(2)}) collective-permute-start(bf16[32,2176]{1,0:T(8,128)(2,1)S(1)} %collective-permute-done.5.refs_7_.refs_3_), channel_id=1, source_target_pairs={{0,1},{1,0},{2,3},{3,2},{4,5},{5,4},{6,7},{7,6},{8,9},{9,8},{10,11... | collective-permute-start | bytes 417800 | tf_op jit(solution)/shard_map/ppermute | solution.py:27
  17.6 4.8 %collective-permute-start.2 = (bf16[32,2176]{1,0:T(8,128)(2,1)S(1)}, bf16[32,2176]{1,0:T(8,128)(2,1)S(1)}, u32[]{:S(2)}, u32[]{:S(2)}) collective-permute-start(bf16[32,2176]{1,0:T(8,128)(2,1)S(1)} %collective-permute-done.1.refs_5_.refs_1_), channel_id=1, source_target_pairs={{0,1},{1,0},{2,3},{3,2},{4,5},{5,4},{6,7},{7,6},{8,9},{9,8},{10,11... | collective-permute-start | bytes 417800 | tf_op jit(solution)/shard_map/ppermute | solution.py:27
  17.6 6.6 %collective-permute-start.14 = (bf16[32,2176]{1,0:T(8,128)(2,1)S(1)}, bf16[32,2176]{1,0:T(8,128)(2,1)S(1)}, u32[]{:S(2)}, u32[]{:S(2)}) collective-permute-start(bf16[32,2176]{1,0:T(8,128)(2,1)S(1)} %collective-permute-done.5.refs_7_.refs_3_), channel_id=1, source_target_pairs={{0,4},{4,8},{8,12},{12,14},{14,10},{10,6},{6,2},{2,0},{1,5},{5,9},... | collective-permute-start | bytes 417800 | tf_op jit(solution)/shard_map/ppermute | solution.py:23
  20.3 6.5 %collective-permute-start.10 = (bf16[32,2176]{1,0:T(8,128)(2,1)S(1)}, bf16[32,2176]{1,0:T(8,128)(2,1)S(1)}, u32[]{:S(2)}, u32[]{:S(2)}) collective-permute-start(bf16[32,2176]{1,0:T(8,128)(2,1)S(1)} %collective-permute-done.5.refs_7_.refs_3_), channel_id=1, source_target_pairs={{0,2},{4,0},{8,4},{12,8},{14,12},{10,14},{6,10},{2,6},{1,3},{5,1},... | collective-permute-start | bytes 417800 | tf_op jit(solution)/shard_map/ppermute | solution.py:23
  20.3 6.6 %collective-permute-start.12 = (bf16[32,2176]{1,0:T(8,128)(2,1)S(1)}, bf16[32,2176]{1,0:T(8,128)(2,1)S(1)}, u32[]{:S(2)}, u32[]{:S(2)}) collective-permute-start(bf16[32,2176]{1,0:T(8,128)(2,1)S(1)} %collective-permute-done.3.refs_6_.refs_2_), channel_id=1, source_target_pairs={{0,4},{4,8},{8,12},{12,14},{14,10},{10,6},{6,2},{2,0},{1,5},{5,9},... | collective-permute-start | bytes 417800 | tf_op jit(solution)/shard_map/ppermute | solution.py:23
  22.3 6.8 %collective-permute-start.8 = (bf16[32,2176]{1,0:T(8,128)(2,1)S(1)}, bf16[32,2176]{1,0:T(8,128)(2,1)S(1)}, u32[]{:S(2)}, u32[]{:S(2)}) collective-permute-start(bf16[32,2176]{1,0:T(8,128)(2,1)S(1)} %collective-permute-done.1.refs_5_.refs_1_), channel_id=1, source_target_pairs={{0,2},{4,0},{8,4},{12,8},{14,12},{10,14},{6,10},{2,6},{1,3},{5,1},... | collective-permute-start | bytes 417800 | tf_op jit(solution)/shard_map/ppermute | solution.py:23
  22.4 6.7 %collective-permute-start.4 = (bf16[32,2176]{1,0:T(8,128)(2,1)S(1)}, bf16[32,2176]{1,0:T(8,128)(2,1)S(1)}, u32[]{:S(2)}, u32[]{:S(2)}) collective-permute-start(bf16[32,2176]{1,0:T(8,128)(2,1)S(1)} %collective-permute-done.3.refs_6_.refs_2_), channel_id=1, source_target_pairs={{0,1},{1,0},{2,3},{3,2},{4,5},{5,4},{6,7},{7,6},{8,9},{9,8},{10,11... | collective-permute-start | bytes 417800 | tf_op jit(solution)/shard_map/ppermute | solution.py:27
  24.3 13.8 %collective-permute-start.15 = (bf16[32,2176]{1,0:T(8,128)(2,1)S(1)}, bf16[32,2176]{1,0:T(8,128)(2,1)S(1)}, u32[]{:S(2)}, u32[]{:S(2)}) collective-permute-start(bf16[32,2176]{1,0:T(8,128)(2,1)S(1)} %collective-permute-done.14.refs_3_.refs_7_), channel_id=1, source_target_pairs={{0,1},{1,0},{2,3},{3,2},{4,5},{5,4},{6,7},{7,6},{8,9},{9,8},{10,11... | collective-permute-start | bytes 417800 | tf_op jit(solution)/shard_map/ppermute | solution.py:27
  26.8 11.3 %collective-permute-start.11 = (bf16[32,2176]{1,0:T(8,128)(2,1)S(1)}, bf16[32,2176]{1,0:T(8,128)(2,1)S(1)}, u32[]{:S(2)}, u32[]{:S(2)}) collective-permute-start(bf16[32,2176]{1,0:T(8,128)(2,1)S(1)} %collective-permute-done.10.refs_1_.refs_5_), channel_id=1, source_target_pairs={{0,1},{1,0},{2,3},{3,2},{4,5},{5,4},{6,7},{7,6},{8,9},{9,8},{10,11... | collective-permute-start | bytes 417800 | tf_op jit(solution)/shard_map/ppermute | solution.py:27
  26.9 11.3 %collective-permute-start.13 = (bf16[32,2176]{1,0:T(8,128)(2,1)S(1)}, bf16[32,2176]{1,0:T(8,128)(2,1)S(1)}, u32[]{:S(2)}, u32[]{:S(2)}) collective-permute-start(bf16[32,2176]{1,0:T(8,128)(2,1)S(1)} %collective-permute-done.12.refs_2_.refs_6_), channel_id=1, source_target_pairs={{0,1},{1,0},{2,3},{3,2},{4,5},{5,4},{6,7},{7,6},{8,9},{9,8},{10,11... | collective-permute-start | bytes 417800 | tf_op jit(solution)/shard_map/ppermute | solution.py:27
  29.1 9.1 %collective-permute-start.9 = (bf16[32,2176]{1,0:T(8,128)(2,1)S(1)}, bf16[32,2176]{1,0:T(8,128)(2,1)S(1)}, u32[]{:S(2)}, u32[]{:S(2)}) collective-permute-start(bf16[32,2176]{1,0:T(8,128)(2,1)S(1)} %collective-permute-done.8.refs_0_.refs_4_), channel_id=1, source_target_pairs={{0,1},{1,0},{2,3},{3,2},{4,5},{5,4},{6,7},{7,6},{8,9},{9,8},{10,11... | collective-permute-start | bytes 417800 | tf_op jit(solution)/shard_map/ppermute | solution.py:27
  29.1 1.9 %copy-start = (bf16[2,2048,384]{2,1,0:T(8,128)(2,1)S(1)}, bf16[2,2048,384]{2,1,0:T(8,128)(2,1)}, u32[]{:S(2)}) copy-start(bf16[2,2048,384]{2,1,0:T(8,128)(2,1)} %refs_4_.3) | copy-start | bytes 9437188
  31.0 1.9 %copy-start.2 = (bf16[2,2048,384]{2,1,0:T(8,128)(2,1)S(1)}, bf16[2,2048,384]{2,1,0:T(8,128)(2,1)}, u32[]{:S(2)}) copy-start(bf16[2,2048,384]{2,1,0:T(8,128)(2,1)} %refs_5_.4) | copy-start | bytes 9437188
  32.9 1.9 %copy-start.4 = (bf16[2,384,2048]{2,1,0:T(8,128)(2,1)S(1)}, bf16[2,384,2048]{2,1,0:T(8,128)(2,1)}, u32[]{:S(2)}) copy-start(bf16[2,384,2048]{2,1,0:T(8,128)(2,1)} %param.18) | copy-start | bytes 9437188
  34.8 3.4 %copy-start.1 = (bf16[2,2048,384]{2,1,0:T(8,128)(2,1)S(1)}, bf16[2,2048,384]{2,1,0:T(8,128)(2,1)}, u32[]{:S(2)}) copy-start(bf16[2,2048,384]{2,1,0:T(8,128)(2,1)} %refs_4_.3) | copy-start | bytes 9437188
  38.1 2.5 %copy-start.6 = (bf16[16,128,1024]{2,1,0:T(8,128)(2,1)S(1)}, bf16[16,128,1024]{2,1,0:T(8,128)(2,1)}, u32[]{:S(2)}) copy-start(bf16[16,128,1024]{2,1,0:T(8,128)(2,1)} %param.21) | copy-start | bytes 12582916
  40.0 6.9 %collective-permute-start.16 = (bf16[128,2048]{1,0:T(8,128)(2,1)S(1)}, bf16[128,2048]{1,0:T(8,128)(2,1)S(1)}, u32[]{:S(2)}, u32[]{:S(2)}) collective-permute-start(bf16[128,2048]{1,0:T(8,128)(2,1)S(1)} %experts.5), channel_id=1, source_target_pairs={{0,1},{1,0},{2,3},{3,2},{4,5},{5,4},{6,7},{7,6},{8,9},{9,8},{10,11... | collective-permute-start | bytes 1572872 | tf_op jit(solution)/shard_map/ppermute | solution.py:27
  40.5 11.1 %collective-permute-start.7 = (bf16[128,2048]{1,0:T(8,128)(2,1)S(1)}, bf16[128,2048]{1,0:T(8,128)(2,1)S(1)}, u32[]{:S(2)}, u32[]{:S(2)}) collective-permute-start(bf16[128,2048]{1,0:T(8,128)(2,1)S(1)} %get-tuple-element.20), channel_id=1, source_target_pairs={{0,1},{1,0},{2,3},{3,2},{4,5},{5,4},{6,7},{7,6},{8,9},{9,8},{10,11... | collective-permute-start | bytes 1572872 | tf_op jit(solution)/shard_map/ppermute | solution.py:27
  40.6 4.3 %copy-start.3 = (bf16[2,2048,384]{2,1,0:T(8,128)(2,1)S(1)}, bf16[2,2048,384]{2,1,0:T(8,128)(2,1)}, u32[]{:S(2)}) copy-start(bf16[2,2048,384]{2,1,0:T(8,128)(2,1)} %refs_5_.4) | copy-start | bytes 9437188
  40.6 4.3 %copy-start.5 = (bf16[2,384,2048]{2,1,0:T(8,128)(2,1)S(1)}, bf16[2,384,2048]{2,1,0:T(8,128)(2,1)}, u32[]{:S(2)}) copy-start(bf16[2,384,2048]{2,1,0:T(8,128)(2,1)} %param.18) | copy-start | bytes 9437188
  42.8 6.2 %collective-permute-start.22 = (bf16[64,1024]{1,0:T(8,128)(2,1)S(1)}, bf16[64,1024]{1,0:T(8,128)(2,1)S(1)}, u32[]{:S(2)}, u32[]{:S(2)}) collective-permute-start(bf16[64,1024]{1,0:T(8,128)(2,1)S(1)} %get-tuple-element.44), channel_id=1, source_target_pairs={{0,4},{4,8},{8,12},{12,14},{14,10},{10,6},{6,2},{2,0},{1,5},{5,9},... | collective-permute-start | bytes 393224 | tf_op jit(solution)/shard_map/ppermute | solution.py:23
  43.6 5.4 %collective-permute-start.23 = (bf16[64,1024]{1,0:T(8,128)(2,1)S(1)}, bf16[64,1024]{1,0:T(8,128)(2,1)S(1)}, u32[]{:S(2)}, u32[]{:S(2)}) collective-permute-start(bf16[64,1024]{1,0:T(8,128)(2,1)S(1)} %get-tuple-element.45), channel_id=1, source_target_pairs={{0,2},{4,0},{8,4},{12,8},{14,12},{10,14},{6,10},{2,6},{1,3},{5,1},... | collective-permute-start | bytes 393224 | tf_op jit(solution)/shard_map/ppermute | solution.py:23
  46.8 19.4 %copy-start.7 = (bf16[1024,512]{1,0:T(8,128)(2,1)S(1)}, bf16[1024,512]{1,0:T(8,128)(2,1)}, u32[]{:S(2)}) copy-start(bf16[1024,512]{1,0:T(8,128)(2,1)} %refs_7_.1) | copy-start | bytes 3145732
  46.8 19.4 %copy-start.8 = (bf16[16,6,1024]{2,0,1:T(8,128)(2,1)S(1)}, bf16[16,6,1024]{2,0,1:T(8,128)(2,1)}, u32[]{:S(2)}) copy-start(bf16[16,6,1024]{2,0,1:T(8,128)(2,1)} %param.22) | copy-start | bytes 589828
  46.8 19.4 %copy-start.10 = (f32[7,1024]{1,0:T(8,128)S(1)}, f32[7,1024]{1,0:T(8,128)}, u32[]{:S(2)}) copy-start(f32[7,1024]{1,0:T(8,128)} %refs_5_.5) | copy-start | bytes 86020
  46.8 19.4 %copy-start.14 = (f32[1024]{0:T(1024)S(1)}, f32[1024]{0:T(1024)}, u32[]{:S(2)}) copy-start(f32[1024]{0:T(1024)} %param.24) | copy-start | bytes 12292
  47.0 8.8 %collective-permute-start.17 = (bf16[64,2048]{1,0:T(8,128)(2,1)S(1)}, bf16[64,2048]{1,0:T(8,128)(2,1)S(1)}, u32[]{:S(2)}, u32[]{:S(2)}) collective-permute-start(bf16[64,2048]{1,0:T(8,128)(2,1)S(1)} %get-tuple-element.39), channel_id=1, source_target_pairs={{0,4},{4,8},{8,12},{12,14},{14,10},{10,6},{6,2},{2,0},{1,5},{5,9},... | collective-permute-start | bytes 786440 | tf_op jit(solution)/shard_map/ppermute | solution.py:23
  47.7 8.1 %collective-permute-start.18 = (bf16[64,2048]{1,0:T(8,128)(2,1)S(1)}, bf16[64,2048]{1,0:T(8,128)(2,1)S(1)}, u32[]{:S(2)}, u32[]{:S(2)}) collective-permute-start(bf16[64,2048]{1,0:T(8,128)(2,1)S(1)} %get-tuple-element.40), channel_id=1, source_target_pairs={{0,2},{4,0},{8,4},{12,8},{14,12},{10,14},{6,10},{2,6},{1,3},{5,1},... | collective-permute-start | bytes 786440 | tf_op jit(solution)/shard_map/ppermute | solution.py:23
  49.1 11.7 %collective-permute-start.24 = (bf16[32,1024]{1,0:T(8,128)(2,1)S(1)}, bf16[32,1024]{1,0:T(8,128)(2,1)S(1)}, u32[]{:S(2)}, u32[]{:S(2)}) collective-permute-start(bf16[32,1024]{1,0:T(8,128)(2,1)S(1)} %get-tuple-element.42), channel_id=1, source_target_pairs={{0,14},{4,10},{8,6},{12,2},{14,0},{10,4},{6,8},{2,12},{1,15},{5,11... | collective-permute-start | bytes 196616 | tf_op jit(solution)/shard_map/ppermute | solution.py:23
  56.1 11.2 %collective-permute-start.19 = (bf16[32,2048]{1,0:T(8,128)(2,1)S(1)}, bf16[32,2048]{1,0:T(8,128)(2,1)S(1)}, u32[]{:S(2)}, u32[]{:S(2)}) collective-permute-start(bf16[32,2048]{1,0:T(8,128)(2,1)S(1)} %get-tuple-element.36), channel_id=1, source_target_pairs={{0,14},{4,10},{8,6},{12,2},{14,0},{10,4},{6,8},{2,12},{1,15},{5,11... | collective-permute-start | bytes 393224 | tf_op jit(solution)/shard_map/ppermute | solution.py:23
  58.5 8.7 %collective-permute-start.20 = (bf16[32,2048]{1,0:T(8,128)(2,1)S(1)}, bf16[32,2048]{1,0:T(8,128)(2,1)S(1)}, u32[]{:S(2)}, u32[]{:S(2)}) collective-permute-start(bf16[32,2048]{1,0:T(8,128)(2,1)S(1)} %get-tuple-element.37), channel_id=1, source_target_pairs={{0,4},{4,8},{8,12},{12,14},{14,10},{10,6},{6,2},{2,0},{1,5},{5,9},... | collective-permute-start | bytes 393224 | tf_op jit(solution)/shard_map/ppermute | solution.py:23
  58.8 8.5 %collective-permute-start.21 = (bf16[32,2048]{1,0:T(8,128)(2,1)S(1)}, bf16[32,2048]{1,0:T(8,128)(2,1)S(1)}, u32[]{:S(2)}, u32[]{:S(2)}) collective-permute-start(bf16[32,2048]{1,0:T(8,128)(2,1)S(1)} %get-tuple-element.35), channel_id=1, source_target_pairs={{0,2},{4,0},{8,4},{12,8},{14,12},{10,14},{6,10},{2,6},{1,3},{5,1},... | collective-permute-start | bytes 393224 | tf_op jit(solution)/shard_map/ppermute | solution.py:23
  60.6 5.6 %collective-permute-start.25 = (bf16[32,1024]{1,0:T(8,128)(2,1)S(1)}, bf16[32,1024]{1,0:T(8,128)(2,1)S(1)}, u32[]{:S(2)}, u32[]{:S(2)}) collective-permute-start(bf16[32,1024]{1,0:T(8,128)(2,1)S(1)} %get-tuple-element.43), channel_id=1, source_target_pairs={{0,4},{4,8},{8,12},{12,14},{14,10},{10,6},{6,2},{2,0},{1,5},{5,9},... | collective-permute-start | bytes 196616 | tf_op jit(solution)/shard_map/ppermute | solution.py:23
  60.8 5.3 %collective-permute-start.26 = (bf16[32,1024]{1,0:T(8,128)(2,1)S(1)}, bf16[32,1024]{1,0:T(8,128)(2,1)S(1)}, u32[]{:S(2)}, u32[]{:S(2)}) collective-permute-start(bf16[32,1024]{1,0:T(8,128)(2,1)S(1)} %get-tuple-element.41), channel_id=1, source_target_pairs={{0,2},{4,0},{8,4},{12,8},{14,12},{10,14},{6,10},{2,6},{1,3},{5,1},... | collective-permute-start | bytes 196616 | tf_op jit(solution)/shard_map/ppermute | solution.py:23

commit v3 on v2

--- a/solution.py
+++ b/solution.py
@@ -27,27 +27,24 @@
     return lax.ppermute(value, "wave", [(0, 1), (1, 0)])
 
 
-def spread(own):
+def collect(parts, hold):
     count = lax.axis_size("expert")
     half = count // 2
-    blocks = {0: own}
-    blocks[half] = shift(own, half)
-    blocks[count - 1] = shift(own, 1)
-    blocks[1] = shift(own, -1)
-    for step in range(2, count // 4 + 1):
-        blocks[count - step] = shift(blocks[count - step + 1], 1)
-        blocks[step] = shift(blocks[step - 1], -1)
-        blocks[half - step + 1] = shift(blocks[half - step + 2], 1)
-        blocks[half + step - 1] = shift(blocks[half + step - 2], -1)
-    return blocks
-
-
-def groups_of_four(count):
-    half = count // 2
-    later = [
-        [step, half + step - 1, count - step, half - step + 1] for step in range(2, count // 4 + 1)
-    ]
-    return [[0, 1, count - 1, half]] + later
+    parts = dict(parts)
+    for step in range(count // 4, 1, -1):
+        moves = (
+            (step, 1, step - 1),
+            (count - step, -1, count + 1 - step),
+            (half + step - 1, 1, half + step - 2),
+            (half - step + 1, -1, half - step + 2),
+        )
+        arrived = [(into, shift(parts[come], way)) for come, way, into in moves]
+        for into in dict(arrived):
+            terms = [value for place, value in arrived if place == into]
+            parts[into] = add(parts[into], *terms).astype(BF16)
+    nearest = (parts[1], parts[count - 1], parts[half])
+    one, minus, across = hold(nearest) or nearest
+    return parts[0], shift(across, half), shift(one, 1), shift(minus, -1)
 
 
 def add(*parts):
@@ -57,21 +54,6 @@
     return total
 
 
-def collect(first, later, rows):
-    forward = backward = None
-    for pair in later[::-1]:
-        if forward is not None:
-            pair = (add(pair[0], forward).astype(BF16), add(pair[1], backward).astype(BF16))
-        forward, backward = shift(pair[0], 1), shift(pair[1], -1)
-    own, one, minus, across = first
-    if forward is not None:
-        one = add(one, forward[:rows]).astype(BF16)
-        minus = add(minus, backward[:rows]).astype(BF16)
-        across = add(across, forward[rows:], backward[rows:]).astype(BF16)
-    half = lax.axis_size("expert") // 2
-    return own, shift(across, half), shift(one, 1), shift(minus, -1)
-
-
 def after(values, *earlier):
     return lax.optimization_barrier((tuple(values), earlier))[0]
 
@@ -86,7 +68,20 @@
     return [(value % 256).astype(F32).astype(BF16), (value // 256).astype(F32).astype(BF16)]
 
 
-def pack_kernel(columns, n_wave, hidden_ref, ids_ref, weights_ref, codes_ref, owner_ref, out_ref):
+def pack_kernel(columns, n_wave, *refs):
+    sources, out_ref, (hidden_ref, ids_ref, weights_ref, codes_ref, owner_ref, sems) = (
+        refs[:5],
+        refs[5],
+        refs[6:],
+    )
+    copies = [
+        pltpu.make_async_copy(source, held, sems.at[i])
+        for i, (source, held) in enumerate(zip(sources, refs[6:11]))
+    ]
+    for copy in copies:
+        copy.start()
+    for copy in copies:
+        copy.wait()
     sessions, steps, width = hidden_ref.shape
     expert_count = columns[0] // 2
     books = codes_ref.shape[2]
@@ -126,18 +121,52 @@
 def pack(hidden_rows, expert_ids, route_weights, codes, owner_slot, columns, n_wave):
     sessions, steps, width = hidden_rows.shape
     meta_width = -(-(columns[1] + 2) // 128) * 128
-    return pl.pallas_call(
-        functools.partial(pack_kernel, columns, n_wave),
-        out_shape=jax.ShapeDtypeStruct((steps * sessions, width + meta_width), BF16),
-        compiler_params=pltpu.CompilerParams(vmem_limit_bytes=VMEM_LIMIT),
-        name="pack",
-    )(
+    args = (
         hidden_rows,
         jnp.transpose(expert_ids, (1, 2, 0)),
         jnp.transpose(route_weights, (1, 2, 0)),
         codes,
         owner_slot[None],
     )
+    return pl.pallas_call(
+        functools.partial(pack_kernel, columns, n_wave),
+        out_shape=jax.ShapeDtypeStruct((steps * sessions, width + meta_width), BF16),
+        in_specs=[pl.BlockSpec(memory_space=pltpu.HBM)] * len(args),
+        out_specs=pl.BlockSpec(memory_space=pltpu.VMEM),
+        scratch_shapes=[pltpu.VMEM(arg.shape, arg.dtype) for arg in args]
+        + [pltpu.SemaphoreType.DMA((len(args),))],
+        compiler_params=pltpu.CompilerParams(vmem_limit_bytes=VMEM_LIMIT),
+        name="pack",
+    )(*[pltpu.with_memory_space_constraint(arg, pltpu.HBM) for arg in args])
+
+
+def load_kernel(*refs):
+    count = len(refs) // 2 - 1
+    sources, held, sems = refs[1 : count + 1], refs[count + 1 : -1], refs[-1]
+    copies = [
+        pltpu.make_async_copy(source, ref, sems.at[i])
+        for i, (source, ref) in enumerate(zip(sources, held))
+    ]
+    for copy in copies:
+        copy.start()
+    for copy in copies:
+        copy.wait()
+
+
+def load(earlier, *arrays):
+    hbm = pl.BlockSpec(memory_space=pltpu.HBM)
+    return pl.pallas_call(
+        load_kernel,
+        out_shape=[pltpu.VMEM(v.shape, v.dtype) for v in arrays],
+        in_specs=[pl.BlockSpec(memory_space=pl.ANY)] + [hbm] * len(arrays),
+        out_specs=[pl.BlockSpec(memory_space=pltpu.VMEM)] * len(arrays),
+        scratch_shapes=[pltpu.SemaphoreType.DMA((len(arrays),))],
+        compiler_params=pltpu.CompilerParams(vmem_limit_bytes=VMEM_LIMIT),
+        cost_estimate=pl.CostEstimate(
+            flops=0, bytes_accessed=sum(2 * v.size for v in arrays), transcendentals=0
+        ),
+        name="load",
+    )(earlier, *[pltpu.with_memory_space_constraint(v, pltpu.HBM) for v in arrays])
 
 
 def experts_kernel(width, expert_count, counts, place_ref, *refs):
@@ -192,7 +221,7 @@
             transcendentals=total * units * local,
         ),
         name="experts",
-    )(place, *blocks, w_gate, w_up, w_down.reshape(local * units, width))
+    )(place, *blocks, w_gate, w_up, w_down)
 
 
 def frames_kernel(columns, books, shard, sessions, steps, order, place_ref, *refs):
@@ -355,46 +384,55 @@
         columns,
         lax.axis_size("wave"),
     )
-    blocks = spread(own)
-    other = {k: swap_wave(v) for k, v in blocks.items()}
-    groups = groups_of_four(count)
-
-    def work(parts):
-        return experts(parts, place, w_gate, w_up, w_down)
-
-    near = groups[0]
-    near_other, near_own = work([[other[k] for k in near], [blocks[k] for k in near]])
-    near_other = swap_wave(near_other)
-    for k in groups[-1]:
-        blocks[k], other[k] = after((blocks[k], other[k]), near_own)
-
-    order = [k for group in groups for k in group]
-    sums = frame_sums(blocks, order, place, code_table, columns, width, sessions, steps)
-    quarter = [sums[i * rows : (i + 1) * rows] for i in range(4)]
-    pairs = [
-        (sums[i * rows : (i + 2) * rows], sums[(i + 2) * rows : (i + 4) * rows])
-        for i in range(4, count, 4)
-    ]
-    frames = collect(quarter, pairs, rows)
-
-    later = []
-    for group in groups[1:]:
-        (from_other,) = work([[other[k] for k in group]])
-        from_other = swap_wave(from_other)
-        (result,) = work([[blocks[k] for k in group]])
-        both = [
-            add(result[at], from_other[at]).astype(BF16)
-            for at in (slice(0, 2 * rows), slice(2 * rows, 4 * rows))
-        ]
-        later.append(both)
-    first = [
-        add(near_own[i * rows : (i + 1) * rows], near_other[i * rows : (i + 1) * rows])
-        for i in range(4)
-    ]
-    first = [first[0]] + [v.astype(BF16) for v in first[1:]]
-    terms = collect(first, later, rows)
+    half = count // 2
+    local, _, units = w_gate.shape
+    held = load(own, w_gate, w_up, w_down.reshape(local * units, width))
+
+    token = [held]
+
+    def work(*parts):
+        (turn,) = after((place,), token[0])
+        token[0] = experts(parts, turn, *held)
+        return token[0]
+
+    blocks, other, mine, swapped = {0: own}, {0: swap_wave(own)}, {}, {}
+    behind = ahead = own
+    fresh = [0]
+    for step in range(1, half + 1):
+        behind = shift(behind, 1)
+        got = [(count - step, behind)]
+        if step < half:
+            ahead = shift(ahead, -1)
+            got.append((step, ahead))
+        got = list(zip([k for k, _ in got], after([v for _, v in got], token[0])))
+        behind, ahead = got[0][1], got[-1][1]
+        for k, value in got:
+            blocks[k], other[k] = value, swap_wave(value)
+        if step == 1:
+            fresh += [k for k, _ in got]
+            continue
+        if step < half:
+            theirs, ours = work([other[k] for k in fresh], [blocks[k] for k in fresh])
+        else:
+            (theirs,) = work([other[k] for k in fresh])
+            (ours,) = work([blocks[k] for k in fresh])
+        theirs = swap_wave(theirs)
+        for i, k in enumerate(fresh):
+            mine[k], swapped[k] = [v[i * rows : (i + 1) * rows] for v in (ours, theirs)]
+        fresh = [k for k, _ in got]
+    order = list(range(count))
+    parts = {k: add(mine[k], swapped[k]) for k in mine}
+    parts = {k: v.astype(BF16) if k else v for k, v in parts.items()}
+    (turn,) = after((place,), [parts[k] for k in parts if k not in (0, 1, count - 1)])
+    sums = frame_sums(blocks, order, turn, code_table, columns, width, sessions, steps)
+    token[0] = sums
+    theirs, ours = work([other[k] for k in fresh], [blocks[k] for k in fresh])
+    parts[half] = add(ours, swap_wave(theirs)).astype(BF16)
+
+    sends = []
+    frames = collect({k: sums[k * rows : (k + 1) * rows] for k in order}, sends.extend)
     samples, carried = decoder(frames, conv_state, conv_taps, conv_bias, upsample)
-    terms = after(terms, samples)
+    terms = collect(parts, lambda values: after(values, sends))
     mixed = last_sum(terms, hidden_rows.shape)
     return mixed, samples, carried
 

time: 68.5 us -> 73.7 us (1.076)
  Pallas kernels: 11.5 us -> 23.6 us
  waiting for transfers between devices: 18.7 us -> 11.8 us
  local copies, waits for them, and re-layouts: 9.4 us -> 7.13 us
  starting transfers between devices: 27.1 us -> 29.1 us
    ppermute x17 -> x21, waiting for transfers between devices: 18.7 us -> 11.7 us  [shift(): return lax.ppermute(value, 'expert', pairs)]
    pallas_call x3 -> x5, Pallas kernels: 6.98 us -> 13.4 us  [experts(): pl.pallas_call(functools.partial(experts_kernel, width, lax.axis_size('ex...]
    pallas_call x0 -> x1, Pallas kernels: none -> 3.78 us  [load(): pl.pallas_call(load_kernel, out_shape=[pltpu.VMEM(v.shape, v.dtype) for v...]
    unnamed x32 -> x22, local copies, waits for them, and re-layouts: 9.37 us -> 7.1 us
    ppermute x10 -> x12, starting transfers between devices: 1.12 us -> 2.17 us  [swap_wave(): return lax.ppermute(value, 'wave', [(0, 1), (1, 0)])]
    pallas_call x1, Pallas kernels: 0.56 us -> 1.59 us  [pack(): pl.pallas_call(functools.partial(pack_kernel, columns, n_wave), out_shape...]
    ppermute x17 -> x21, starting transfers between devices: 26 us -> 26.9 us  [shift(): return lax.ppermute(value, 'expert', pairs)]
    pallas_call x1, Pallas kernels: 2.18 us -> 3.05 us  [frame_sums(): pl.pallas_call(functools.partial(frames_kernel, columns, books, shard, se...]
  transfers between devices with their start and end apart: 27 -> 33, of which waited for: 8 -> 6; matrix products, arithmetic and copies ran while one was open for 1% -> 1% of each run, Pallas kernels for 12% -> 29%
where the time goes in v3:
time: 73.7 us; the launch traced here: 72.9 us
  starting transfers between devices  29.1 us (39%)
  Pallas kernels  23.6 us (32%)
  waiting for transfers between devices  11.8 us (16%)
  local copies, waits for them, and re-layouts  7.13 us (10%)
  between operations  0.86 us (1%)
    ppermute x21, starting transfers between devices, shift(): return lax.ppermute(value, 'expert', pairs)  26.9 us
    pallas_call x5, Pallas kernels, experts(): pl.pallas_call(functools.partial(experts_kernel, width, lax.axis_size('ex...  13.4 us
    ppermute x21, waiting for transfers between devices, shift(): return lax.ppermute(value, 'expert', pairs)  11.7 us
    unnamed x22, local copies, waits for them, and re-layouts  7.1 us
    pallas_call x1, Pallas kernels, load(): pl.pallas_call(load_kernel, out_shape=[pltpu.VMEM(v.shape, v.dtype) for v...  3.78 us
    pallas_call x1, Pallas kernels, frame_sums(): pl.pallas_call(functools.partial(frames_kernel, columns, books, shard, se...  3.05 us
    ppermute x12, starting transfers between devices, swap_wave(): return lax.ppermute(value, 'wave', [(0, 1), (1, 0)])  2.17 us
    pallas_call x1, Pallas kernels, pack(): pl.pallas_call(functools.partial(pack_kernel, columns, n_wave), out_shape...  1.59 us
  transfers between devices with their start and end apart: 33, of which 6 were waited for; matrix products, arithmetic and copies ran while one was open for 1% of the time, Pallas kernels for 29%

profile of v3, /device:TPU:0, one launch (start us, length us, event | category | flops | bytes accessed | tf_op | source)
XLA Modules:
  0.0 72.9 jit_solution(89629233800976465)
XLA Ops:
  0.6 1.6 %pack.1.refs_0_.refs_3_ = bf16[32,2176]{1,0:T(8,128)(2,1)S(1)} custom-call(bf16[16,2,2048]{2,1,0:T(2,128)(2,1)} %refs_0_.1, s32[2,8,16]{2,1,0:T(8,128)} %bitcast.13, f32[2,8,16]{2,1,0:T(8,128)} %bitcast.14, s32[16,2,16]{2,1,0:T(2,128)} %refs_3_.1, s32[1,16]{1,0:T(1,128)} %bitcast.15), custom_call_target="tpu_custom_call" | custom-call | tf_op jit(solution)/shard_map/pack/pallas_call | solution.py:131
  2.2 3.1 %collective-permute-start.1 = (bf16[32,2176]{1,0:T(8,128)(2,1)S(1)}, bf16[32,2176]{1,0:T(8,128)(2,1)S(1)}, u32[]{:S(2)}, u32[]{:S(2)}) collective-permute-start(bf16[32,2176]{1,0:T(8,128)(2,1)S(1)} %pack.1.refs_0_.refs_3_), channel_id=1, source_target_pairs={{0,4},{4,8},{8,12},{12,14},{14,10},{10,6},{6,2},{2,0},{1,5},{5,9},... | collective-permute-start | bytes 417800 | tf_op jit(solution)/shard_map/ppermute | solution.py:23
  5.3 3.8 %load.1 = (bf16[2,2048,384]{2,1,0:T(8,128)(2,1)S(1)}, bf16[2,2048,384]{2,1,0:T(8,128)(2,1)S(1)}, bf16[768,2048]{1,0:T(8,128)(2,1)S(1)}) custom-call(bf16[32,2176]{1,0:T(8,128)(2,1)S(1)} %pack.1.refs_0_.refs_3_, bf16[2,2048,384]{2,1,0:T(8,128)(2,1)} %refs_1_.1, bf16[2,2048,384]{2,1,0:T(8,128)(2,1)} %refs_2_.1, bf16[768,2048]{1,0:T(8,128)(2,1)} %bitcast.12), custom_call_target="tpu_custom_call" | custom-call | bytes 9437184 | tf_op jit(solution)/shard_map/load/pallas_call | solution.py:158
  9.1 1.6 %copy-done = bf16[2,2048,384]{2,1,0:T(8,128)(2,1)} copy-done((bf16[2,2048,384]{2,1,0:T(8,128)(2,1)}, bf16[2,2048,384]{2,1,0:T(8,128)(2,1)S(1)}, u32[]{:S(2)}) %copy-start) | copy-done | bytes 3145752
  10.7 1.7 %copy-done.3 = bf16[768,2048]{1,0:T(8,128)(2,1)} copy-done((bf16[768,2048]{1,0:T(8,128)(2,1)}, bf16[768,2048]{1,0:T(8,128)(2,1)S(1)}, u32[]{:S(2)}) %copy-start.3) | copy-done | bytes 3145752
  12.4 2.0 %collective-permute-start.6 = (bf16[32,2176]{1,0:T(8,128)(2,1)S(1)}, bf16[32,2176]{1,0:T(8,128)(2,1)}, u32[]{:S(2)}, u32[]{:S(2)}) collective-permute-start(bf16[32,2176]{1,0:T(8,128)(2,1)S(1)} %collective-permute-done.1.refs_4_.refs_7_), channel_id=1, source_target_pairs={{0,4},{4,8},{8,12},{12,14},{14,10},{10,6},{6,2},{2,0},{1,5},{5,9},... | collective-permute-start | bytes 417800 | tf_op jit(solution)/shard_map/ppermute | solution.py:23
  14.4 0.5 collective-permute-start.3
  14.9 2.7 %collective-permute-done.6.refs_2_.refs_6_ = bf16[32,2176]{1,0:T(8,128)(2,1)} collective-permute-done((bf16[32,2176]{1,0:T(8,128)(2,1)S(1)}, bf16[32,2176]{1,0:T(8,128)(2,1)}, u32[]{:S(2)}, u32[]{:S(2)}) %collective-permute-start.6) | collective-permute-done | bytes 139296 | tf_op jit(solution)/shard_map/ppermute | solution.py:23
  17.6 2.2 %collective-permute-done.7.refs_3_.refs_2_ = bf16[32,2176]{1,0:T(8,128)(2,1)} collective-permute-done((bf16[32,2176]{1,0:T(8,128)(2,1)}, bf16[32,2176]{1,0:T(8,128)(2,1)}, u32[]{:S(2)}, u32[]{:S(2)}) %collective-permute-start.7) | collective-permute-done | bytes 139296 | tf_op jit(solution)/shard_map/ppermute | solution.py:23
  19.8 1.6 %collective-permute-start.13 = (bf16[32,2176]{1,0:T(8,128)(2,1)}, bf16[32,2176]{1,0:T(8,128)(2,1)S(1)}, u32[]{:S(2)}, u32[]{:S(2)}) collective-permute-start(bf16[32,2176]{1,0:T(8,128)(2,1)} %collective-permute-done.6.refs_2_.refs_6_), channel_id=1, source_target_pairs={{0,4},{4,8},{8,12},{12,14},{14,10},{10,6},{6,2},{2,0},{1,5},{5,9},... | collective-permute-start | bytes 417800 | tf_op jit(solution)/shard_map/ppermute | solution.py:23
  21.4 0.5 collective-permute-start.14
  21.8 0.2 collective-permute-start.9
  22.1 1.9 %copy-done.1 = bf16[2,2048,384]{2,1,0:T(8,128)(2,1)S(1)} copy-done((bf16[2,2048,384]{2,1,0:T(8,128)(2,1)S(1)}, bf16[2,2048,384]{2,1,0:T(8,128)(2,1)}, u32[]{:S(2)}) %copy-start.1) | copy-done | bytes 3145752
  24.0 1.9 %copy-done.4 = bf16[768,2048]{1,0:T(8,128)(2,1)S(1)} copy-done((bf16[768,2048]{1,0:T(8,128)(2,1)S(1)}, bf16[768,2048]{1,0:T(8,128)(2,1)}, u32[]{:S(2)}) %copy-start.4) | copy-done | bytes 3145752
  25.8 4.1 %experts.5 = (bf16[96,2048]{1,0:T(8,128)(2,1)S(1)}, bf16[96,2048]{1,0:T(8,128)(2,1)S(1)}) custom-call(s32[1]{0:T(128)} %bitcast.place_ref, bf16[32,2176]{1,0:T(8,128)(2,1)} %collective-permute-done.refs_0_, bf16[32,2176]{1,0:T(8,128)(2,1)} %collective-permute-done.3.refs_1_, bf16[32,2176]{1,0:T(8,128)(2,1)} %collective-permute-done.4.refs_2_, ...), custom_call_target="tpu_custom_call" | custom-call | flops 1811939328 | bytes 9437184 | tf_op jit(solution)/shard_map/experts/pallas_call | solution.py:206
  29.9 3.4 %experts.6 = (bf16[64,2048]{1,0:T(8,128)(2,1)S(1)}, bf16[64,2048]{1,0:T(8,128)(2,1)S(1)}) custom-call(s32[1]{0:T(128)} %bitcast.place_ref, bf16[32,2176]{1,0:T(8,128)(2,1)S(1)} %collective-permute-done.8.refs_0_, bf16[32,2176]{1,0:T(8,128)(2,1)S(1)} %collective-permute-done.9.refs_1_, bf16[32,2176]{1,0:T(8,128)(2,1)} %collective-permute-done.6.refs_2_.refs_6_, ...), custom_call_target="tpu_custom_call" | custom-call | flops 1207959552 | bytes 9437184 | tf_op jit(solution)/shard_map/experts/pallas_call | solution.py:206
  33.3 0.3 collective-permute-start.10
  33.7 0.2 collective-permute-start.15
  33.9 0.3 collective-permute-start.16
  34.2 1.6 %collective-permute-start.18 = (bf16[32,2176]{1,0:T(8,128)(2,1)S(1)}, bf16[32,2176]{1,0:T(8,128)(2,1)S(1)}, u32[]{:S(2)}, u32[]{:S(2)}) collective-permute-start(bf16[32,2176]{1,0:T(8,128)(2,1)S(1)} %collective-permute-done.13.refs_0_.refs_5_), channel_id=1, source_target_pairs={{0,4},{4,8},{8,12},{12,14},{14,10},{10,6},{6,2},{2,0},{1,5},{5,9},... | collective-permute-start | bytes 417800 | tf_op jit(solution)/shard_map/ppermute | solution.py:23
  35.8 1.8 %experts.7 = bf16[64,2048]{1,0:T(8,128)(2,1)S(1)} custom-call(s32[1]{0:T(128)} %bitcast.place_ref, bf16[32,2176]{1,0:T(8,128)(2,1)S(1)} %collective-permute-done.15.refs_0_, bf16[32,2176]{1,0:T(8,128)(2,1)S(1)} %collective-permute-done.16.refs_1_, bf16[2,2048,384]{2,1,0:T(8,128)(2,1)S(1)} %get-tuple-element.30.refs_6_.refs_4_.refs_2_, ...), custom_call_target="tpu_custom_call" | custom-call | flops 603979776 | bytes 9437184 | tf_op jit(solution)/shard_map/experts/pallas_call | solution.py:206
  37.6 0.6 collective-permute-start.17
  38.2 1.9 %collective-permute-done.18.refs_4_.refs_1_ = bf16[32,2176]{1,0:T(8,128)(2,1)S(1)} collective-permute-done((bf16[32,2176]{1,0:T(8,128)(2,1)S(1)}, bf16[32,2176]{1,0:T(8,128)(2,1)S(1)}, u32[]{:S(2)}, u32[]{:S(2)}) %collective-permute-start.18) | collective-permute-done | bytes 139296 | tf_op jit(solution)/shard_map/ppermute | solution.py:23
  40.0 1.8 %experts.8 = bf16[64,2048]{1,0:T(8,128)(2,1)S(1)} custom-call(s32[1]{0:T(128)} %bitcast.place_ref, bf16[32,2176]{1,0:T(8,128)(2,1)S(1)} %collective-permute-done.13.refs_0_.refs_5_, bf16[32,2176]{1,0:T(8,128)(2,1)S(1)} %collective-permute-done.14.refs_1_.refs_3_, bf16[2,2048,384]{2,1,0:T(8,128)(2,1)S(1)} %get-tuple-element.30.refs_6_.refs_4_.refs_2_, ...), custom_call_target="tpu_custom_call" | custom-call | flops 603979776 | bytes 9437184 | tf_op jit(solution)/shard_map/experts/pallas_call | solution.py:206
  41.8 0.1 add_convert_fusion.5
  41.9 1.6 %collective-permute-start.11 = (bf16[32,2048]{1,0:T(8,128)(2,1)S(1)}, bf16[32,2048]{1,0:T(8,128)(2,1)S(1)}, u32[]{:S(2)}, u32[]{:S(2)}) collective-permute-start(bf16[32,2048]{1,0:T(8,128)(2,1)S(1)} %get-tuple-element.71), channel_id=1, source_target_pairs={{0,4},{4,8},{8,12},{12,14},{14,10},{10,6},{6,2},{2,0},{1,5},{5,9},... | collective-permute-start | bytes 393224 | tf_op jit(solution)/shard_map/ppermute | solution.py:23
  43.5 0.4 collective-permute-start.12
  44.1 3.1 %frame_sums.1 = bf16[256,1024]{1,0:T(8,128)(2,1)S(1)} custom-call(s32[1]{0:T(128)} %bitcast.place_ref, bf16[32,2176]{1,0:T(8,128)(2,1)S(1)} %pack.1.refs_0_.refs_3_, bf16[32,2176]{1,0:T(8,128)(2,1)} %collective-permute-done.2.refs_5_.refs_1_, bf16[32,2176]{1,0:T(8,128)(2,1)} %collective-permute-done.7.refs_3_.refs_2_, ...), custom_call_target="tpu_custom_call" | custom-call | flops 1073741824 | bytes 4194304 | tf_op jit(solution)/shard_map/frame_sums/pallas_call | solution.py:275
  47.2 1.6 %collective-permute-start.23 = (bf16[32,1024]{1,0:T(8,128)(2,1)S(1)}, bf16[32,1024]{1,0:T(8,128)(2,1)S(1)}, u32[]{:S(2)}, u32[]{:S(2)}) collective-permute-start(bf16[32,1024]{1,0:T(8,128)(2,1)S(1)} %get-tuple-element.64), channel_id=1, source_target_pairs={{0,4},{4,8},{8,12},{12,14},{14,10},{10,6},{6,2},{2,0},{1,5},{5,9},... | collective-permute-start | bytes 196616 | tf_op jit(solution)/shard_map/ppermute | solution.py:23
  48.8 0.4 collective-permute-start.24
  49.3 1.6 %collective-permute-start.25 = (bf16[32,1024]{1,0:T(8,128)(2,1)S(1)}, bf16[32,1024]{1,0:T(8,128)(2,1)S(1)}, u32[]{:S(2)}, u32[]{:S(2)}) collective-permute-start(bf16[32,1024]{1,0:T(8,128)(2,1)S(1)} %get-tuple-element.62), channel_id=1, source_target_pairs={{0,4},{4,8},{8,12},{12,14},{14,10},{10,6},{6,2},{2,0},{1,5},{5,9},... | collective-permute-start | bytes 196616 | tf_op jit(solution)/shard_map/ppermute | solution.py:23
  50.8 0.4 collective-permute-start.26
  51.3 0.1 add_convert_fusion.4
  51.5 1.6 %collective-permute-start.21 = (bf16[32,2048]{1,0:T(8,128)(2,1)S(1)}, bf16[32,2048]{1,0:T(8,128)(2,1)S(1)}, u32[]{:S(2)}, u32[]{:S(2)}) collective-permute-start(bf16[32,2048]{1,0:T(8,128)(2,1)S(1)} %get-tuple-element.68), channel_id=1, source_target_pairs={{0,4},{4,8},{8,12},{12,14},{14,10},{10,6},{6,2},{2,0},{1,5},{5,9},... | collective-permute-start | bytes 393224 | tf_op jit(solution)/shard_map/ppermute | solution.py:23
  53.1 2.3 %experts.9 = (bf16[32,2048]{1,0:T(8,128)(2,1)S(1)}, bf16[32,2048]{1,0:T(8,128)(2,1)S(1)}) custom-call(s32[1]{0:T(128)} %bitcast.place_ref, bf16[32,2176]{1,0:T(8,128)(2,1)S(1)} %collective-permute-done.19.refs_0_, bf16[32,2176]{1,0:T(8,128)(2,1)S(1)} %collective-permute-done.18.refs_4_.refs_1_, ...), custom_call_target="tpu_custom_call" | custom-call | flops 603979776 | bytes 9437184 | tf_op jit(solution)/shard_map/experts/pallas_call | solution.py:206
  55.4 0.5 collective-permute-start.22
  56.0 3.5 %collective-permute-start.30 = (bf16[32,1024]{1,0:T(8,128)(2,1)S(1)}, bf16[32,1024]{1,0:T(8,128)(2,1)S(1)}, u32[]{:S(2)}, u32[]{:S(2)}) collective-permute-start(bf16[32,1024]{1,0:T(8,128)(2,1)S(1)} %get-tuple-element.65), channel_id=1, source_target_pairs={{0,14},{4,10},{8,6},{12,2},{14,0},{10,4},{6,8},{2,12},{1,15},{5,11... | collective-permute-start | bytes 196616 | tf_op jit(solution)/shard_map/ppermute | solution.py:23
  59.5 0.9 %collective-permute-done.22 = bf16[32,2048]{1,0:T(8,128)(2,1)S(1)} collective-permute-done((bf16[32,2048]{1,0:T(8,128)(2,1)S(1)}, bf16[32,2048]{1,0:T(8,128)(2,1)S(1)}, u32[]{:S(2)}, u32[]{:S(2)}) %collective-permute-start.22) | collective-permute-done | bytes 131104 | tf_op jit(solution)/shard_map/ppermute | solution.py:23
  60.5 0.1 add_convert_fusion
  60.5 2.4 %collective-permute-start.27 = (bf16[32,2048]{1,0:T(8,128)(2,1)S(1)}, bf16[32,2048]{1,0:T(8,128)(2,1)S(1)}, u32[]{:S(2)}, u32[]{:S(2)}) collective-permute-start(bf16[32,2048]{1,0:T(8,128)(2,1)S(1)} %add_convert_fusion), channel_id=1, source_target_pairs={{0,14},{4,10},{8,6},{12,2},{14,0},{10,4},{6,8},{2,12},{1,15},{5,11... | collective-permute-start | bytes 393224 | tf_op jit(solution)/shard_map/ppermute | solution.py:23
  62.9 0.9 %collective-permute-start.28 = (bf16[32,2048]{1,0:T(8,128)(2,1)S(1)}, bf16[32,2048]{1,0:T(8,128)(2,1)S(1)}, u32[]{:S(2)}, u32[]{:S(2)}) collective-permute-start(bf16[32,2048]{1,0:T(8,128)(2,1)S(1)} %get-tuple-element.53), channel_id=1, source_target_pairs={{0,4},{4,8},{8,12},{12,14},{14,10},{10,6},{6,2},{2,0},{1,5},{5,9},... | collective-permute-start | bytes 393224 | tf_op jit(solution)/shard_map/ppermute | solution.py:23
  63.8 1.1 %collective-permute-start.29 = (bf16[32,2048]{1,0:T(8,128)(2,1)S(1)}, bf16[32,2048]{1,0:T(8,128)(2,1)S(1)}, u32[]{:S(2)}, u32[]{:S(2)}) collective-permute-start(bf16[32,2048]{1,0:T(8,128)(2,1)S(1)} %get-tuple-element.54), channel_id=1, source_target_pairs={{0,2},{4,0},{8,4},{12,8},{14,12},{10,14},{6,10},{2,6},{1,3},{5,1},... | collective-permute-start | bytes 393224 | tf_op jit(solution)/shard_map/ppermute | solution.py:23
  64.9 0.9 %collective-permute-start.31 = (bf16[32,1024]{1,0:T(8,128)(2,1)S(1)}, bf16[32,1024]{1,0:T(8,128)(2,1)S(1)}, u32[]{:S(2)}, u32[]{:S(2)}) collective-permute-start(bf16[32,1024]{1,0:T(8,128)(2,1)S(1)} %get-tuple-element.67), channel_id=1, source_target_pairs={{0,4},{4,8},{8,12},{12,14},{14,10},{10,6},{6,2},{2,0},{1,5},{5,9},... | collective-permute-start | bytes 196616 | tf_op jit(solution)/shard_map/ppermute | solution.py:23
  65.9 1.1 %collective-permute-start.32 = (bf16[32,1024]{1,0:T(8,128)(2,1)S(1)}, bf16[32,1024]{1,0:T(8,128)(2,1)S(1)}, u32[]{:S(2)}, u32[]{:S(2)}) collective-permute-start(bf16[32,1024]{1,0:T(8,128)(2,1)S(1)} %get-tuple-element.66), channel_id=1, source_target_pairs={{0,2},{4,0},{8,4},{12,8},{14,12},{10,14},{6,10},{2,6},{1,3},{5,1},... | collective-permute-start | bytes 196616 | tf_op jit(solution)/shard_map/ppermute | solution.py:23
  66.9 3.6 %collective-permute-done.31.refs_2_ = bf16[32,1024]{1,0:T(8,128)(2,1)S(1)} collective-permute-done((bf16[32,1024]{1,0:T(8,128)(2,1)S(1)}, bf16[32,1024]{1,0:T(8,128)(2,1)S(1)}, u32[]{:S(2)}, u32[]{:S(2)}) %collective-permute-start.31) | collective-permute-done | bytes 65568 | tf_op jit(solution)/shard_map/ppermute | solution.py:23
  70.6 0.4 collective-permute-done.32.refs_3_
  71.0 1.1 %decoder.1 = (bf16[16,2,512]{2,1,0:T(2,128)(2,1)}, bf16[6,16,1024]{2,1,0:T(8,128)(2,1)}) custom-call(bf16[32,1024]{1,0:T(8,128)(2,1)S(1)} %get-tuple-element.60.refs_0_, bf16[32,1024]{1,0:T(8,128)(2,1)S(1)} %collective-permute-done.30.refs_1_, bf16[32,1024]{1,0:T(8,128)(2,1)S(1)} %collective-permute-done.31.refs_2_, ...), custom_call_target="tpu_custom_call" | custom-call | tf_op jit(solution)/shard_map/decoder/pallas_call | solution.py:318
  72.1 0.8 %last_sum.1 = bf16[16,2,2048]{2,1,0:T(2,128)(2,1)} custom-call(f32[32,2048]{1,0:T(8,128)S(1)} %get-tuple-element.59.refs_0_, bf16[32,2048]{1,0:T(8,128)(2,1)S(1)} %collective-permute-done.27.refs_1_, bf16[32,2048]{1,0:T(8,128)(2,1)S(1)} %collective-permute-done.28.refs_2_, bf16[32,2048]{1,0:T(8,128)(2,1)S(1)} %collective-permute-done.29.refs_3_), custom_call_target="tpu_custom_call" | custom-call | tf_op jit(solution)/shard_map/last_sum/pallas_call | solution.py:347
  (56 shorter events, 0.3 us)
Async XLA Ops:
  2.2 10.2 %collective-permute-start.1 = (bf16[32,2176]{1,0:T(8,128)(2,1)S(1)}, bf16[32,2176]{1,0:T(8,128)(2,1)S(1)}, u32[]{:S(2)}, u32[]{:S(2)}) collective-permute-start(bf16[32,2176]{1,0:T(8,128)(2,1)S(1)} %pack.1.refs_0_.refs_3_), channel_id=1, source_target_pairs={{0,4},{4,8},{8,12},{12,14},{14,10},{10,6},{6,2},{2,0},{1,5},{5,9},... | collective-permute-start | bytes 417800 | tf_op jit(solution)/shard_map/ppermute | solution.py:23
  5.3 7.1 %collective-permute-start.2 = (bf16[32,2176]{1,0:T(8,128)(2,1)S(1)}, bf16[32,2176]{1,0:T(8,128)(2,1)}, u32[]{:S(2)}, u32[]{:S(2)}) collective-permute-start(bf16[32,2176]{1,0:T(8,128)(2,1)S(1)} %pack.1.refs_0_.refs_3_), channel_id=1, source_target_pairs={{0,2},{4,0},{8,4},{12,8},{14,12},{10,14},{6,10},{2,6},{1,3},{5,1},... | collective-permute-start | bytes 417800 | tf_op jit(solution)/shard_map/ppermute | solution.py:23
  9.1 1.6 %copy-start = (bf16[2,2048,384]{2,1,0:T(8,128)(2,1)}, bf16[2,2048,384]{2,1,0:T(8,128)(2,1)S(1)}, u32[]{:S(2)}) copy-start(bf16[2,2048,384]{2,1,0:T(8,128)(2,1)S(1)} %get-tuple-element.31.refs_7_.refs_5_.refs_3_) | copy-start | bytes 9437188
  10.7 1.7 %copy-start.3 = (bf16[768,2048]{1,0:T(8,128)(2,1)}, bf16[768,2048]{1,0:T(8,128)(2,1)S(1)}, u32[]{:S(2)}) copy-start(bf16[768,2048]{1,0:T(8,128)(2,1)S(1)} %get-tuple-element.32.refs_8_.refs_6_.refs_4_) | copy-start | bytes 9437188
  12.4 5.2 %collective-permute-start.6 = (bf16[32,2176]{1,0:T(8,128)(2,1)S(1)}, bf16[32,2176]{1,0:T(8,128)(2,1)}, u32[]{:S(2)}, u32[]{:S(2)}) collective-permute-start(bf16[32,2176]{1,0:T(8,128)(2,1)S(1)} %collective-permute-done.1.refs_4_.refs_7_), channel_id=1, source_target_pairs={{0,4},{4,8},{8,12},{12,14},{14,10},{10,6},{6,2},{2,0},{1,5},{5,9},... | collective-permute-start | bytes 417800 | tf_op jit(solution)/shard_map/ppermute | solution.py:23
  14.4 5.4 %collective-permute-start.7 = (bf16[32,2176]{1,0:T(8,128)(2,1)}, bf16[32,2176]{1,0:T(8,128)(2,1)}, u32[]{:S(2)}, u32[]{:S(2)}) collective-permute-start(bf16[32,2176]{1,0:T(8,128)(2,1)} %collective-permute-done.2.refs_5_.refs_1_), channel_id=1, source_target_pairs={{0,2},{4,0},{8,4},{12,8},{14,12},{10,14},{6,10},{2,6},{1,3},{5,1},... | collective-permute-start | bytes 417800 | tf_op jit(solution)/shard_map/ppermute | solution.py:23
  14.4 6.9 %collective-permute-start = (bf16[32,2176]{1,0:T(8,128)(2,1)S(1)}, bf16[32,2176]{1,0:T(8,128)(2,1)}, u32[]{:S(2)}, u32[]{:S(2)}) collective-permute-start(bf16[32,2176]{1,0:T(8,128)(2,1)S(1)} %pack.1.refs_0_.refs_3_), channel_id=1, source_target_pairs={{0,1},{1,0},{2,3},{3,2},{4,5},{5,4},{6,7},{7,6},{8,9},{9,8},{10,11... | collective-permute-start | bytes 417800 | tf_op jit(solution)/shard_map/ppermute | solution.py:27
  14.4 7.4 %collective-permute-start.3 = (bf16[32,2176]{1,0:T(8,128)(2,1)S(1)}, bf16[32,2176]{1,0:T(8,128)(2,1)}, u32[]{:S(2)}, u32[]{:S(2)}) collective-permute-start(bf16[32,2176]{1,0:T(8,128)(2,1)S(1)} %collective-permute-done.1.refs_4_.refs_7_), channel_id=1, source_target_pairs={{0,1},{1,0},{2,3},{3,2},{4,5},{5,4},{6,7},{7,6},{8,9},{9,8},{10,11... | collective-permute-start | bytes 417800 | tf_op jit(solution)/shard_map/ppermute | solution.py:27
  14.9 7.1 %collective-permute-start.4 = (bf16[32,2176]{1,0:T(8,128)(2,1)}, bf16[32,2176]{1,0:T(8,128)(2,1)}, u32[]{:S(2)}, u32[]{:S(2)}) collective-permute-start(bf16[32,2176]{1,0:T(8,128)(2,1)} %collective-permute-done.2.refs_5_.refs_1_), channel_id=1, source_target_pairs={{0,1},{1,0},{2,3},{3,2},{4,5},{5,4},{6,7},{7,6},{8,9},{9,8},{10,11... | collective-permute-start | bytes 417800 | tf_op jit(solution)/shard_map/ppermute | solution.py:27
  19.8 13.9 %collective-permute-start.13 = (bf16[32,2176]{1,0:T(8,128)(2,1)}, bf16[32,2176]{1,0:T(8,128)(2,1)S(1)}, u32[]{:S(2)}, u32[]{:S(2)}) collective-permute-start(bf16[32,2176]{1,0:T(8,128)(2,1)} %collective-permute-done.6.refs_2_.refs_6_), channel_id=1, source_target_pairs={{0,4},{4,8},{8,12},{12,14},{14,10},{10,6},{6,2},{2,0},{1,5},{5,9},... | collective-permute-start | bytes 417800 | tf_op jit(solution)/shard_map/ppermute | solution.py:23
  21.4 8.5 %collective-permute-start.8 = (bf16[32,2176]{1,0:T(8,128)(2,1)}, bf16[32,2176]{1,0:T(8,128)(2,1)S(1)}, u32[]{:S(2)}, u32[]{:S(2)}) collective-permute-start(bf16[32,2176]{1,0:T(8,128)(2,1)} %collective-permute-done.6.refs_2_.refs_6_), channel_id=1, source_target_pairs={{0,1},{1,0},{2,3},{3,2},{4,5},{5,4},{6,7},{7,6},{8,9},{9,8},{10,11... | collective-permute-start | bytes 417800 | tf_op jit(solution)/shard_map/ppermute | solution.py:27
  21.4 12.3 %collective-permute-start.14 = (bf16[32,2176]{1,0:T(8,128)(2,1)}, bf16[32,2176]{1,0:T(8,128)(2,1)S(1)}, u32[]{:S(2)}, u32[]{:S(2)}) collective-permute-start(bf16[32,2176]{1,0:T(8,128)(2,1)} %collective-permute-done.7.refs_3_.refs_2_), channel_id=1, source_target_pairs={{0,2},{4,0},{8,4},{12,8},{14,12},{10,14},{6,10},{2,6},{1,3},{5,1},... | collective-permute-start | bytes 417800 | tf_op jit(solution)/shard_map/ppermute | solution.py:23
  21.8 8.1 %collective-permute-start.9 = (bf16[32,2176]{1,0:T(8,128)(2,1)}, bf16[32,2176]{1,0:T(8,128)(2,1)S(1)}, u32[]{:S(2)}, u32[]{:S(2)}) collective-permute-start(bf16[32,2176]{1,0:T(8,128)(2,1)} %collective-permute-done.7.refs_3_.refs_2_), channel_id=1, source_target_pairs={{0,1},{1,0},{2,3},{3,2},{4,5},{5,4},{6,7},{7,6},{8,9},{9,8},{10,11... | collective-permute-start | bytes 417800 | tf_op jit(solution)/shard_map/ppermute | solution.py:27
  22.1 1.9 %copy-start.1 = (bf16[2,2048,384]{2,1,0:T(8,128)(2,1)S(1)}, bf16[2,2048,384]{2,1,0:T(8,128)(2,1)}, u32[]{:S(2)}) copy-start(bf16[2,2048,384]{2,1,0:T(8,128)(2,1)} %copy-done) | copy-start | bytes 9437188
  24.0 1.9 %copy-start.4 = (bf16[768,2048]{1,0:T(8,128)(2,1)S(1)}, bf16[768,2048]{1,0:T(8,128)(2,1)}, u32[]{:S(2)}) copy-start(bf16[768,2048]{1,0:T(8,128)(2,1)} %copy-done.3) | copy-start | bytes 9437188
  33.3 8.5 %collective-permute-start.10 = (bf16[64,2048]{1,0:T(8,128)(2,1)S(1)}, bf16[64,2048]{1,0:T(8,128)(2,1)S(1)}, u32[]{:S(2)}, u32[]{:S(2)}) collective-permute-start(bf16[64,2048]{1,0:T(8,128)(2,1)S(1)} %get-tuple-element.42), channel_id=1, source_target_pairs={{0,1},{1,0},{2,3},{3,2},{4,5},{5,4},{6,7},{7,6},{8,9},{9,8},{10,11... | collective-permute-start | bytes 786440 | tf_op jit(solution)/shard_map/ppermute | solution.py:27
  33.7 2.1 %collective-permute-start.15 = (bf16[32,2176]{1,0:T(8,128)(2,1)S(1)}, bf16[32,2176]{1,0:T(8,128)(2,1)S(1)}, u32[]{:S(2)}, u32[]{:S(2)}) collective-permute-start(bf16[32,2176]{1,0:T(8,128)(2,1)S(1)} %collective-permute-done.13.refs_0_.refs_5_), channel_id=1, source_target_pairs={{0,1},{1,0},{2,3},{3,2},{4,5},{5,4},{6,7},{7,6},{8,9},{9,8},{10,11... | collective-permute-start | bytes 417800 | tf_op jit(solution)/shard_map/ppermute | solution.py:27
  33.9 1.9 %collective-permute-start.16 = (bf16[32,2176]{1,0:T(8,128)(2,1)S(1)}, bf16[32,2176]{1,0:T(8,128)(2,1)S(1)}, u32[]{:S(2)}, u32[]{:S(2)}) collective-permute-start(bf16[32,2176]{1,0:T(8,128)(2,1)S(1)} %collective-permute-done.14.refs_1_.refs_3_), channel_id=1, source_target_pairs={{0,1},{1,0},{2,3},{3,2},{4,5},{5,4},{6,7},{7,6},{8,9},{9,8},{10,11... | collective-permute-start | bytes 417800 | tf_op jit(solution)/shard_map/ppermute | solution.py:27
  34.2 5.8 %collective-permute-start.18 = (bf16[32,2176]{1,0:T(8,128)(2,1)S(1)}, bf16[32,2176]{1,0:T(8,128)(2,1)S(1)}, u32[]{:S(2)}, u32[]{:S(2)}) collective-permute-start(bf16[32,2176]{1,0:T(8,128)(2,1)S(1)} %collective-permute-done.13.refs_0_.refs_5_), channel_id=1, source_target_pairs={{0,4},{4,8},{8,12},{12,14},{14,10},{10,6},{6,2},{2,0},{1,5},{5,9},... | collective-permute-start | bytes 417800 | tf_op jit(solution)/shard_map/ppermute | solution.py:23
  35.8 13.0 %collective-permute-start.5 = (bf16[96,2048]{1,0:T(8,128)(2,1)S(1)}, bf16[96,2048]{1,0:T(8,128)(2,1)S(1)}, u32[]{:S(2)}, u32[]{:S(2)}) collective-permute-start(bf16[96,2048]{1,0:T(8,128)(2,1)S(1)} %get-tuple-element.37), channel_id=1, source_target_pairs={{0,1},{1,0},{2,3},{3,2},{4,5},{5,4},{6,7},{7,6},{8,9},{9,8},{10,11... | collective-permute-start | bytes 1179656 | tf_op jit(solution)/shard_map/ppermute | solution.py:27
  37.6 6.4 %collective-permute-start.17 = (bf16[64,2048]{1,0:T(8,128)(2,1)S(1)}, bf16[64,2048]{1,0:T(8,128)(2,1)S(1)}, u32[]{:S(2)}, u32[]{:S(2)}) collective-permute-start(bf16[64,2048]{1,0:T(8,128)(2,1)S(1)} %experts.7), channel_id=1, source_target_pairs={{0,1},{1,0},{2,3},{3,2},{4,5},{5,4},{6,7},{7,6},{8,9},{9,8},{10,11... | collective-permute-start | bytes 786440 | tf_op jit(solution)/shard_map/ppermute | solution.py:27
  40.0 11.4 %collective-permute-start.19 = (bf16[32,2176]{1,0:T(8,128)(2,1)S(1)}, bf16[32,2176]{1,0:T(8,128)(2,1)S(1)}, u32[]{:S(2)}, u32[]{:S(2)}) collective-permute-start(bf16[32,2176]{1,0:T(8,128)(2,1)S(1)} %collective-permute-done.18.refs_4_.refs_1_), channel_id=1, source_target_pairs={{0,1},{1,0},{2,3},{3,2},{4,5},{5,4},{6,7},{7,6},{8,9},{9,8},{10,11... | collective-permute-start | bytes 417800 | tf_op jit(solution)/shard_map/ppermute | solution.py:27
  40.0 4.0 %copy-start.6 = (bf16[16,128,1024]{2,1,0:T(8,128)(2,1)S(1)}, bf16[16,128,1024]{2,1,0:T(8,128)(2,1)}, u32[]{:S(2)}) copy-start(bf16[16,128,1024]{2,1,0:T(8,128)(2,1)} %param.21) | copy-start | bytes 12582916
  41.9 7.4 %collective-permute-start.11 = (bf16[32,2048]{1,0:T(8,128)(2,1)S(1)}, bf16[32,2048]{1,0:T(8,128)(2,1)S(1)}, u32[]{:S(2)}, u32[]{:S(2)}) collective-permute-start(bf16[32,2048]{1,0:T(8,128)(2,1)S(1)} %get-tuple-element.71), channel_id=1, source_target_pairs={{0,4},{4,8},{8,12},{12,14},{14,10},{10,6},{6,2},{2,0},{1,5},{5,9},... | collective-permute-start | bytes 393224 | tf_op jit(solution)/shard_map/ppermute | solution.py:23
  43.5 7.3 %collective-permute-start.12 = (bf16[32,2048]{1,0:T(8,128)(2,1)S(1)}, bf16[32,2048]{1,0:T(8,128)(2,1)S(1)}, u32[]{:S(2)}, u32[]{:S(2)}) collective-permute-start(bf16[32,2048]{1,0:T(8,128)(2,1)S(1)} %get-tuple-element.70), channel_id=1, source_target_pairs={{0,2},{4,0},{8,4},{12,8},{14,12},{10,14},{6,10},{2,6},{1,3},{5,1},... | collective-permute-start | bytes 393224 | tf_op jit(solution)/shard_map/ppermute | solution.py:23
  44.1 9.0 %copy-start.2 = (bf16[2,2048,384]{2,1,0:T(8,128)(2,1)S(1)}, bf16[2,2048,384]{2,1,0:T(8,128)(2,1)}, u32[]{:S(2)}) copy-start(bf16[2,2048,384]{2,1,0:T(8,128)(2,1)} %copy-done) | copy-start | bytes 9437188
  44.1 9.0 %copy-start.5 = (bf16[768,2048]{1,0:T(8,128)(2,1)S(1)}, bf16[768,2048]{1,0:T(8,128)(2,1)}, u32[]{:S(2)}) copy-start(bf16[768,2048]{1,0:T(8,128)(2,1)} %copy-done.3) | copy-start | bytes 9437188
  47.2 8.3 %collective-permute-start.23 = (bf16[32,1024]{1,0:T(8,128)(2,1)S(1)}, bf16[32,1024]{1,0:T(8,128)(2,1)S(1)}, u32[]{:S(2)}, u32[]{:S(2)}) collective-permute-start(bf16[32,1024]{1,0:T(8,128)(2,1)S(1)} %get-tuple-element.64), channel_id=1, source_target_pairs={{0,4},{4,8},{8,12},{12,14},{14,10},{10,6},{6,2},{2,0},{1,5},{5,9},... | collective-permute-start | bytes 196616 | tf_op jit(solution)/shard_map/ppermute | solution.py:23
  48.8 7.1 %collective-permute-start.24 = (bf16[32,1024]{1,0:T(8,128)(2,1)S(1)}, bf16[32,1024]{1,0:T(8,128)(2,1)S(1)}, u32[]{:S(2)}, u32[]{:S(2)}) collective-permute-start(bf16[32,1024]{1,0:T(8,128)(2,1)S(1)} %get-tuple-element.63), channel_id=1, source_target_pairs={{0,2},{4,0},{8,4},{12,8},{14,12},{10,14},{6,10},{2,6},{1,3},{5,1},... | collective-permute-start | bytes 196616 | tf_op jit(solution)/shard_map/ppermute | solution.py:23
  49.3 6.7 %collective-permute-start.25 = (bf16[32,1024]{1,0:T(8,128)(2,1)S(1)}, bf16[32,1024]{1,0:T(8,128)(2,1)S(1)}, u32[]{:S(2)}, u32[]{:S(2)}) collective-permute-start(bf16[32,1024]{1,0:T(8,128)(2,1)S(1)} %get-tuple-element.62), channel_id=1, source_target_pairs={{0,4},{4,8},{8,12},{12,14},{14,10},{10,6},{6,2},{2,0},{1,5},{5,9},... | collective-permute-start | bytes 196616 | tf_op jit(solution)/shard_map/ppermute | solution.py:23
  50.8 5.1 %collective-permute-start.26 = (bf16[32,1024]{1,0:T(8,128)(2,1)S(1)}, bf16[32,1024]{1,0:T(8,128)(2,1)S(1)}, u32[]{:S(2)}, u32[]{:S(2)}) collective-permute-start(bf16[32,1024]{1,0:T(8,128)(2,1)S(1)} %get-tuple-element.61), channel_id=1, source_target_pairs={{0,2},{4,0},{8,4},{12,8},{14,12},{10,14},{6,10},{2,6},{1,3},{5,1},... | collective-permute-start | bytes 196616 | tf_op jit(solution)/shard_map/ppermute | solution.py:23
  51.4 19.6 %copy-start.7 = (bf16[1024,512]{1,0:T(8,128)(2,1)S(1)}, bf16[1024,512]{1,0:T(8,128)(2,1)}, u32[]{:S(2)}) copy-start(bf16[1024,512]{1,0:T(8,128)(2,1)} %refs_7_.1) | copy-start | bytes 3145732
  51.4 19.6 %copy-start.8 = (bf16[16,6,1024]{2,0,1:T(8,128)(2,1)S(1)}, bf16[16,6,1024]{2,0,1:T(8,128)(2,1)}, u32[]{:S(2)}) copy-start(bf16[16,6,1024]{2,0,1:T(8,128)(2,1)} %param.22) | copy-start | bytes 589828
  51.4 19.6 %copy-start.9 = (f32[7,1024]{1,0:T(8,128)S(1)}, f32[7,1024]{1,0:T(8,128)}, u32[]{:S(2)}) copy-start(f32[7,1024]{1,0:T(8,128)} %refs_5_.1) | copy-start | bytes 86020
  51.4 19.6 %copy-start.10 = (f32[1024]{0:T(1024)S(1)}, f32[1024]{0:T(1024)}, u32[]{:S(2)}) copy-start(f32[1024]{0:T(1024)} %param.24) | copy-start | bytes 12292
  51.5 8.1 %collective-permute-start.21 = (bf16[32,2048]{1,0:T(8,128)(2,1)S(1)}, bf16[32,2048]{1,0:T(8,128)(2,1)S(1)}, u32[]{:S(2)}, u32[]{:S(2)}) collective-permute-start(bf16[32,2048]{1,0:T(8,128)(2,1)S(1)} %get-tuple-element.68), channel_id=1, source_target_pairs={{0,4},{4,8},{8,12},{12,14},{14,10},{10,6},{6,2},{2,0},{1,5},{5,9},... | collective-permute-start | bytes 393224 | tf_op jit(solution)/shard_map/ppermute | solution.py:23
  55.4 5.0 %collective-permute-start.22 = (bf16[32,2048]{1,0:T(8,128)(2,1)S(1)}, bf16[32,2048]{1,0:T(8,128)(2,1)S(1)}, u32[]{:S(2)}, u32[]{:S(2)}) collective-permute-start(bf16[32,2048]{1,0:T(8,128)(2,1)S(1)} %get-tuple-element.69), channel_id=1, source_target_pairs={{0,2},{4,0},{8,4},{12,8},{14,12},{10,14},{6,10},{2,6},{1,3},{5,1},... | collective-permute-start | bytes 393224 | tf_op jit(solution)/shard_map/ppermute | solution.py:23
  55.9 3.6 %collective-permute-start.20 = (bf16[32,2048]{1,0:T(8,128)(2,1)S(1)}, bf16[32,2048]{1,0:T(8,128)(2,1)S(1)}, u32[]{:S(2)}, u32[]{:S(2)}) collective-permute-start(bf16[32,2048]{1,0:T(8,128)(2,1)S(1)} %get-tuple-element.51), channel_id=1, source_target_pairs={{0,1},{1,0},{2,3},{3,2},{4,5},{5,4},{6,7},{7,6},{8,9},{9,8},{10,11... | collective-permute-start | bytes 393224 | tf_op jit(solution)/shard_map/ppermute | solution.py:27
  56.0 9.8 %collective-permute-start.30 = (bf16[32,1024]{1,0:T(8,128)(2,1)S(1)}, bf16[32,1024]{1,0:T(8,128)(2,1)S(1)}, u32[]{:S(2)}, u32[]{:S(2)}) collective-permute-start(bf16[32,1024]{1,0:T(8,128)(2,1)S(1)} %get-tuple-element.65), channel_id=1, source_target_pairs={{0,14},{4,10},{8,6},{12,2},{14,0},{10,4},{6,8},{2,12},{1,15},{5,11... | collective-permute-start | bytes 196616 | tf_op jit(solution)/shard_map/ppermute | solution.py:23
  60.5 11.6 %collective-permute-start.27 = (bf16[32,2048]{1,0:T(8,128)(2,1)S(1)}, bf16[32,2048]{1,0:T(8,128)(2,1)S(1)}, u32[]{:S(2)}, u32[]{:S(2)}) collective-permute-start(bf16[32,2048]{1,0:T(8,128)(2,1)S(1)} %add_convert_fusion), channel_id=1, source_target_pairs={{0,14},{4,10},{8,6},{12,2},{14,0},{10,4},{6,8},{2,12},{1,15},{5,11... | collective-permute-start | bytes 393224 | tf_op jit(solution)/shard_map/ppermute | solution.py:23
  62.9 9.2 %collective-permute-start.28 = (bf16[32,2048]{1,0:T(8,128)(2,1)S(1)}, bf16[32,2048]{1,0:T(8,128)(2,1)S(1)}, u32[]{:S(2)}, u32[]{:S(2)}) collective-permute-start(bf16[32,2048]{1,0:T(8,128)(2,1)S(1)} %get-tuple-element.53), channel_id=1, source_target_pairs={{0,4},{4,8},{8,12},{12,14},{14,10},{10,6},{6,2},{2,0},{1,5},{5,9},... | collective-permute-start | bytes 393224 | tf_op jit(solution)/shard_map/ppermute | solution.py:23
  63.8 8.3 %collective-permute-start.29 = (bf16[32,2048]{1,0:T(8,128)(2,1)S(1)}, bf16[32,2048]{1,0:T(8,128)(2,1)S(1)}, u32[]{:S(2)}, u32[]{:S(2)}) collective-permute-start(bf16[32,2048]{1,0:T(8,128)(2,1)S(1)} %get-tuple-element.54), channel_id=1, source_target_pairs={{0,2},{4,0},{8,4},{12,8},{14,12},{10,14},{6,10},{2,6},{1,3},{5,1},... | collective-permute-start | bytes 393224 | tf_op jit(solution)/shard_map/ppermute | solution.py:23
  64.9 5.7 %collective-permute-start.31 = (bf16[32,1024]{1,0:T(8,128)(2,1)S(1)}, bf16[32,1024]{1,0:T(8,128)(2,1)S(1)}, u32[]{:S(2)}, u32[]{:S(2)}) collective-permute-start(bf16[32,1024]{1,0:T(8,128)(2,1)S(1)} %get-tuple-element.67), channel_id=1, source_target_pairs={{0,4},{4,8},{8,12},{12,14},{14,10},{10,6},{6,2},{2,0},{1,5},{5,9},... | collective-permute-start | bytes 196616 | tf_op jit(solution)/shard_map/ppermute | solution.py:23
  65.9 5.2 %collective-permute-start.32 = (bf16[32,1024]{1,0:T(8,128)(2,1)S(1)}, bf16[32,1024]{1,0:T(8,128)(2,1)S(1)}, u32[]{:S(2)}, u32[]{:S(2)}) collective-permute-start(bf16[32,1024]{1,0:T(8,128)(2,1)S(1)} %get-tuple-element.66), channel_id=1, source_target_pairs={{0,2},{4,0},{8,4},{12,8},{14,12},{10,14},{6,10},{2,6},{1,3},{5,1},... | collective-permute-start | bytes 196616 | tf_op jit(solution)/shard_map/ppermute | solution.py:23

commit v4 on v3

--- a/solution.py
+++ b/solution.py
@@ -9,7 +9,7 @@
 
 F32 = jnp.float32
 BF16 = jnp.bfloat16
-VMEM_LIMIT = 28 * 1024 * 1024
+VMEM_LIMIT = 8 * 1024 * 1024
 
 
 def ring_order(count):
@@ -27,31 +27,70 @@
     return lax.ppermute(value, "wave", [(0, 1), (1, 0)])
 
 
-def collect(parts, hold):
+def tidy(plan):
+    arrays, numbers = [], {}
+
+    def number(source):
+        array, row = source
+        if id(array) not in numbers:
+            numbers[id(array)] = len(arrays)
+            arrays.append(array)
+        return numbers[id(array)], row
+
+    return arrays, [[[[number(v) for v in part] for part in block] for block in out] for out in plan]
+
+
+def summed(refs, sources, rows, columns):
+    total = None
+    for index, row in sources:
+        value = refs[index][row : row + rows, columns].astype(F32)
+        total = value if total is None else total + value
+    return total
+
+
+def join_kernel(plan, rows, width, *refs):
+    outs = refs[-len(plan) :]
+    for out_ref, blocks in zip(outs, plan):
+        for i, (left, right, whole) in enumerate(blocks):
+            at = slice(i * rows, (i + 1) * rows)
+            total = summed(refs, left, rows, slice(None))
+            for index, row in whole:
+                total = total + refs[index][row : row + rows, 0:width].astype(F32)
+            out_ref[at, 0:width] = total.astype(BF16)
+            total = summed(refs, right, rows, slice(None))
+            for index, row in whole:
+                total = total + refs[index][row : row + rows, width:].astype(F32)
+            out_ref[at, width:] = total.astype(BF16)
+
+
+def join(plan, rows, width, channels):
+    arrays, numbered = tidy(plan)
+    return pl.pallas_call(
+        functools.partial(join_kernel, numbered, rows, width),
+        out_shape=[jax.ShapeDtypeStruct((rows * len(out), width + channels), BF16) for out in plan],
+        compiler_params=pltpu.CompilerParams(vmem_limit_bytes=VMEM_LIMIT),
+        cost_estimate=pl.CostEstimate(flops=0, bytes_accessed=1 << 20, transcendentals=0),
+        name="join",
+    )(*arrays)
+
+
+def collect(left, right, rows, width, channels):
     count = lax.axis_size("expert")
     half = count // 2
-    parts = dict(parts)
+    ahead, back = [], []
     for step in range(count // 4, 1, -1):
-        moves = (
-            (step, 1, step - 1),
-            (count - step, -1, count + 1 - step),
-            (half + step - 1, 1, half + step - 2),
-            (half - step + 1, -1, half - step + 2),
-        )
-        arrived = [(into, shift(parts[come], way)) for come, way, into in moves]
-        for into in dict(arrived):
-            terms = [value for place, value in arrived if place == into]
-            parts[into] = add(parts[into], *terms).astype(BF16)
-    nearest = (parts[1], parts[count - 1], parts[half])
-    one, minus, across = hold(nearest) or nearest
-    return parts[0], shift(across, half), shift(one, 1), shift(minus, -1)
-
-
-def add(*parts):
-    total = parts[0].astype(F32)
-    for part in parts[1:]:
-        total = total + part.astype(F32)
-    return total
+        pairs = ((step, half + step - 1), (count - step, half - step + 1))
+        plan = [
+            [(left[k], right[k], [(v, i * rows) for v in got]) for i, k in enumerate(pair)]
+            for pair, got in zip(pairs, (ahead, back))
+        ]
+        forward, backward = join(plan, rows, width, channels)
+        ahead, back = [shift(forward, 1)], [shift(backward, -1)]
+    one = (left[1], right[1], [(v, 0) for v in ahead])
+    minus = (left[count - 1], right[count - 1], [(v, 0) for v in back])
+    across = (left[half], right[half], [(v, rows) for v in ahead + back])
+    one, minus, across = join([[one], [minus], [across]], rows, width, channels)
+    return shift(one, 1), shift(minus, -1), shift(across, half)
 
 
 def after(values, *earlier):
@@ -68,16 +107,14 @@
     return [(value % 256).astype(F32).astype(BF16), (value // 256).astype(F32).astype(BF16)]
 
 
-def pack_kernel(columns, n_wave, *refs):
-    sources, out_ref, (hidden_ref, ids_ref, weights_ref, codes_ref, owner_ref, sems) = (
-        refs[:5],
-        refs[5],
-        refs[6:],
-    )
+def pack_kernel(columns, n_wave, _, *refs):
+    sources, out_ref, held = refs[:5], refs[5], refs[6:11]
+    sems = refs[11]
     copies = [
-        pltpu.make_async_copy(source, held, sems.at[i])
-        for i, (source, held) in enumerate(zip(sources, refs[6:11]))
+        pltpu.make_async_copy(source, ref, sems.at[i])
+        for i, (source, ref) in enumerate(zip(sources, held))
     ]
+    hidden_ref, ids_ref, weights_ref, codes_ref, owner_ref = held
     for copy in copies:
         copy.start()
     for copy in copies:
@@ -118,7 +155,7 @@
         out_ref[at, width:] = meta.astype(BF16)
 
 
-def pack(hidden_rows, expert_ids, route_weights, codes, owner_slot, columns, n_wave):
+def pack(place, hidden_rows, expert_ids, route_weights, codes, owner_slot, columns, n_wave):
     sessions, steps, width = hidden_rows.shape
     meta_width = -(-(columns[1] + 2) // 128) * 128
     args = (
@@ -131,13 +168,14 @@
     return pl.pallas_call(
         functools.partial(pack_kernel, columns, n_wave),
         out_shape=jax.ShapeDtypeStruct((steps * sessions, width + meta_width), BF16),
-        in_specs=[pl.BlockSpec(memory_space=pltpu.HBM)] * len(args),
+        in_specs=[pl.BlockSpec(memory_space=pltpu.SMEM)]
+        + [pl.BlockSpec(memory_space=pltpu.HBM)] * len(args),
         out_specs=pl.BlockSpec(memory_space=pltpu.VMEM),
         scratch_shapes=[pltpu.VMEM(arg.shape, arg.dtype) for arg in args]
         + [pltpu.SemaphoreType.DMA((len(args),))],
         compiler_params=pltpu.CompilerParams(vmem_limit_bytes=VMEM_LIMIT),
         name="pack",
-    )(*[pltpu.with_memory_space_constraint(arg, pltpu.HBM) for arg in args])
+    )(place, *[pltpu.with_memory_space_constraint(arg, pltpu.HBM) for arg in args])
 
 
 def load_kernel(*refs):
@@ -169,59 +207,56 @@
     )(earlier, *[pltpu.with_memory_space_constraint(v, pltpu.HBM) for v in arrays])
 
 
-def experts_kernel(width, expert_count, counts, place_ref, *refs):
-    blocks = refs[: sum(counts)]
-    gate_ref, up_ref, down_ref = refs[sum(counts) : sum(counts) + 3]
-    outs = refs[sum(counts) + 3 : -2]
-    rows_ref, act_ref = refs[-2:]
-    local, _, units = gate_ref.shape
+def experts_kernel(width, expert_count, block_count, place_ref, *refs):
+    blocks = refs[:block_count]
+    parts = [refs[i : i + 3] for i in range(block_count, len(refs) - 3, 3)]
+    out_ref, rows_ref, act_ref = refs[-3:]
     rows = blocks[0].shape[0]
     for i, block in enumerate(blocks):
         rows_ref[i * rows : (i + 1) * rows, :] = block[:, 0:width]
     meta = jnp.concatenate([block[:, width:].astype(F32) for block in blocks], axis=0)
     lane = lax.broadcasted_iota(jnp.int32, meta.shape, 1)
-    for j in range(local):
-        mine = place_ref[0] * local + j
-        hit = (lane == mine) | (lane == expert_count + mine)
-        weight = jnp.sum(jnp.where(hit, meta, 0.0), axis=1, keepdims=True)
-        gate = jnp.dot(rows_ref[...], gate_ref[j], preferred_element_type=F32)
-        up = jnp.dot(rows_ref[...], up_ref[j], preferred_element_type=F32)
-        value = gate * jax.nn.sigmoid(gate) * up
-        act_ref[:, j * units : (j + 1) * units] = (value * weight).astype(BF16)
-    start = 0
-    for out_ref in outs:
-        size = out_ref.shape[0]
-        act = act_ref[start : start + size, :]
-        out_ref[...] = jnp.dot(act, down_ref[...], preferred_element_type=F32).astype(BF16)
-        start += size
-
-
-def experts(parts, place, w_gate, w_up, w_down):
-    local, width, units = w_gate.shape
-    counts = [len(blocks) for blocks in parts]
-    blocks = [block for part in parts for block in part]
+    total = None
+    for gate_ref, up_ref, down_ref in parts:
+        local, _, units = gate_ref.shape
+        for j in range(local):
+            mine = place_ref[0] * local + j
+            hit = (lane == mine) | (lane == expert_count + mine)
+            weight = jnp.sum(jnp.where(hit, meta, 0.0), axis=1, keepdims=True)
+            gate = jnp.dot(rows_ref[...], gate_ref[j], preferred_element_type=F32)
+            up = jnp.dot(rows_ref[...], up_ref[j], preferred_element_type=F32)
+            value = gate * jax.nn.sigmoid(gate) * up
+            act_ref[:, j * units : (j + 1) * units] = (value * weight).astype(BF16)
+        result = jnp.dot(act_ref[...], down_ref[...], preferred_element_type=F32)
+        total = result if total is None else total + result
+    out_ref[...] = total.astype(BF16)
+
+
+def experts(blocks, place, held):
+    local, width, units = held[0][0].shape
     rows = blocks[0].shape[0]
     total = rows * len(blocks)
     vmem = pl.BlockSpec(memory_space=pltpu.VMEM)
+    weights = [v for part in held for v in part]
     return pl.pallas_call(
         functools.partial(
-            experts_kernel, width, lax.axis_size("expert") * local, tuple(counts)
+            experts_kernel, width, lax.axis_size("expert") * local, len(blocks)
         ),
-        out_shape=[jax.ShapeDtypeStruct((rows * c, width), BF16) for c in counts],
-        in_specs=[pl.BlockSpec(memory_space=pltpu.SMEM)] + [vmem] * (len(blocks) + 3),
-        out_specs=[vmem] * len(counts),
+        out_shape=jax.ShapeDtypeStruct((total, width), BF16),
+        in_specs=[pl.BlockSpec(memory_space=pltpu.SMEM)] + [vmem] * (len(blocks) + len(weights)),
+        out_specs=vmem,
         scratch_shapes=[
             pltpu.VMEM((total, width), BF16),
             pltpu.VMEM((total, local * units), BF16),
         ],
         compiler_params=pltpu.CompilerParams(vmem_limit_bytes=VMEM_LIMIT),
         cost_estimate=pl.CostEstimate(
-            flops=6 * total * width * units * local,
-            bytes_accessed=6 * local * width * units,
-            transcendentals=total * units * local,
+            flops=6 * total * width * units * local * len(held),
+            bytes_accessed=2 * sum(v.size for v in weights),
+            transcendentals=total * units * local * len(held),
         ),
         name="experts",
-    )(place, *blocks, w_gate, w_up, w_down)
+    )(place, *blocks, *weights)
 
 
 def frames_kernel(columns, books, shard, sessions, steps, order, place_ref, *refs):
@@ -281,7 +316,7 @@
         + [vmem],
         out_specs=vmem,
         scratch_shapes=[pltpu.VMEM((total, books * shard), BF16)],
-        compiler_params=pltpu.CompilerParams(vmem_limit_bytes=VMEM_LIMIT),
+        compiler_params=pltpu.CompilerParams(vmem_limit_bytes=VMEM_LIMIT + 12 * total * total),
         cost_estimate=pl.CostEstimate(
             flops=2 * total * books * shard * channels,
             bytes_accessed=2 * books * shard * channels,
@@ -291,65 +326,56 @@
     )(place, *[blocks[k] for k in order], code_table.reshape(books * shard, channels))
 
 
-def decoder_kernel(*refs):
-    terms, (state_ref, taps_ref, bias_ref, up_ref, wave_ref, new_ref) = refs[:-6], refs[-6:]
+def finish_kernel(left, right, whole, width, *refs):
+    state_ref, taps_ref, bias_ref, up_ref, mixed_ref, wave_ref, new_ref = refs[-7:]
     past, sessions, _ = state_ref.shape
+    steps = mixed_ref.shape[1]
+    rows = steps * sessions
     taps = taps_ref.shape[0]
-    frames = terms[0][...].astype(F32)
-    for term in terms[1:]:
-        frames = frames + term[...].astype(F32)
-    steps = frames.shape[0] // sessions
+    frames = summed(refs, right, rows, slice(None))
+    for index, row in whole:
+        frames = frames + refs[index][row : row + rows, width:].astype(F32)
     history = [state_ref[i].astype(F32) for i in range(past)]
     history += [frames[t * sessions : (t + 1) * sessions] for t in range(steps)]
+    decoded = []
     for t in range(steps):
         filtered = bias_ref[...] + taps_ref[0:1, :] * history[past + t]
         for j in range(1, taps):
             filtered = filtered + taps_ref[j : j + 1, :] * history[past + t - j]
-        decoded = jax.nn.gelu(filtered).astype(BF16)
-        sample = jnp.dot(decoded, up_ref[...], preferred_element_type=F32)
-        wave_ref[:, t, :] = sample.astype(BF16)
+        decoded.append(jax.nn.gelu(filtered).astype(BF16))
+    samples = jnp.dot(jnp.concatenate(decoded), up_ref[...], preferred_element_type=F32)
+    total = summed(refs, left, rows, slice(None))
+    for index, row in whole:
+        total = total + refs[index][row : row + rows, 0:width].astype(F32)
+    for t in range(steps):
+        at = slice(t * sessions, (t + 1) * sessions)
+        wave_ref[:, t, :] = samples[at].astype(BF16)
+        mixed_ref[:, t, :] = total[at].astype(BF16)
     for i in range(past):
         new_ref[i] = history[i + steps].astype(BF16)
 
 
-def decoder(terms, conv_state, conv_taps, conv_bias, upsample):
+def finish(left, right, arrived, width, conv_state, conv_taps, conv_bias, upsample, steps):
     sessions, past, channels = conv_state.shape
-    steps = terms[0].shape[0] // sessions
-    wave, state = pl.pallas_call(
-        decoder_kernel,
+    arrays, numbered = tidy([[(left, right, [(v, 0) for v in arrived])]])
+    mixed, wave, state = pl.pallas_call(
+        functools.partial(finish_kernel, *numbered[0][0], width),
         out_shape=(
+            jax.ShapeDtypeStruct((sessions, steps, width), BF16),
             jax.ShapeDtypeStruct((sessions, steps, upsample.shape[1]), BF16),
             jax.ShapeDtypeStruct((past, sessions, channels), BF16),
         ),
         compiler_params=pltpu.CompilerParams(vmem_limit_bytes=VMEM_LIMIT),
-        name="decoder",
+        cost_estimate=pl.CostEstimate(flops=0, bytes_accessed=1 << 21, transcendentals=0),
+        name="finish",
     )(
-        *terms,
+        *arrays,
         jnp.transpose(conv_state, (1, 0, 2)),
         conv_taps,
         conv_bias.reshape(1, channels),
         upsample,
     )
-    return wave, jnp.transpose(state, (1, 0, 2))
-
-
-def last_sum_kernel(*refs):
-    terms, out_ref = refs[:-1], refs[-1]
-    sessions, steps, _ = out_ref.shape
-    total = terms[0][...].astype(F32)
-    for term in terms[1:]:
-        total = total + term[...].astype(F32)
-    for t in range(steps):
-        out_ref[:, t, :] = total[t * sessions : (t + 1) * sessions].astype(BF16)
-
-
-def last_sum(terms, shape):
-    return pl.pallas_call(
-        last_sum_kernel,
-        out_shape=jax.ShapeDtypeStruct(shape, BF16),
-        compiler_params=pltpu.CompilerParams(vmem_limit_bytes=VMEM_LIMIT),
-        name="last_sum",
-    )(*terms)
+    return mixed, wave, jnp.transpose(state, (1, 0, 2))
 
 
 def per_device(
@@ -376,6 +402,7 @@
     columns = (2 * expert_count, 2 * expert_count + 2 * books)
 
     own = pack(
+        place,
         hidden_rows,
         expert_ids,
         route_weights,
@@ -385,56 +412,43 @@
         lax.axis_size("wave"),
     )
     half = count // 2
-    local, _, units = w_gate.shape
-    held = load(own, w_gate, w_up, w_down.reshape(local * units, width))
-
-    token = [held]
-
-    def work(*parts):
-        (turn,) = after((place,), token[0])
-        token[0] = experts(parts, turn, *held)
-        return token[0]
-
-    blocks, other, mine, swapped = {0: own}, {0: swap_wave(own)}, {}, {}
+    weights = (w_gate, w_up, w_down.reshape(-1, width))
+    sibling = [swap_wave(v) for v in weights]
+    held = [load(own, *weights)]
+
+    blocks = {0: own}
     behind = ahead = own
-    fresh = [0]
     for step in range(1, half + 1):
         behind = shift(behind, 1)
-        got = [(count - step, behind)]
+        got = {count - step: behind}
         if step < half:
             ahead = shift(ahead, -1)
-            got.append((step, ahead))
-        got = list(zip([k for k, _ in got], after([v for _, v in got], token[0])))
-        behind, ahead = got[0][1], got[-1][1]
-        for k, value in got:
-            blocks[k], other[k] = value, swap_wave(value)
-        if step == 1:
-            fresh += [k for k, _ in got]
-            continue
-        if step < half:
-            theirs, ours = work([other[k] for k in fresh], [blocks[k] for k in fresh])
-        else:
-            (theirs,) = work([other[k] for k in fresh])
-            (ours,) = work([blocks[k] for k in fresh])
-        theirs = swap_wave(theirs)
-        for i, k in enumerate(fresh):
-            mine[k], swapped[k] = [v[i * rows : (i + 1) * rows] for v in (ours, theirs)]
-        fresh = [k for k, _ in got]
+            got[step] = ahead
+        first = held[0] if step == 1 else sibling[step - 2 : step - 1]
+        got = dict(zip(got, after(got.values(), first)))
+        behind, ahead = got[count - step], got.get(step)
+        blocks.update(got)
+
+    held.append(sibling)
     order = list(range(count))
-    parts = {k: add(mine[k], swapped[k]) for k in mine}
-    parts = {k: v.astype(BF16) if k else v for k, v in parts.items()}
-    (turn,) = after((place,), [parts[k] for k in parts if k not in (0, 1, count - 1)])
-    sums = frame_sums(blocks, order, turn, code_table, columns, width, sessions, steps)
-    token[0] = sums
-    theirs, ours = work([other[k] for k in fresh], [blocks[k] for k in fresh])
-    parts[half] = add(ours, swap_wave(theirs)).astype(BF16)
-
-    sends = []
-    frames = collect({k: sums[k * rows : (k + 1) * rows] for k in order}, sends.extend)
-    samples, carried = decoder(frames, conv_state, conv_taps, conv_bias, upsample)
-    terms = collect(parts, lambda values: after(values, sends))
-    mixed = last_sum(terms, hidden_rows.shape)
-    return mixed, samples, carried
+    near = [0, 1, count - 1, half]
+    groups = [near]
+    for step in range(2, count // 4 + 1):
+        groups.append([step, half + step - 1, count - step, half - step + 1])
+    left, turn = {}, place
+    for group in groups[::-1]:
+        if group is near:
+            sums = frame_sums(blocks, order, turn, code_table, columns, width, sessions, steps)
+            (turn,) = after((place,), sums)
+        result = experts([blocks[k] for k in group], turn, held)
+        (turn,) = after((place,), result)
+        for i, k in enumerate(group):
+            left[k] = [(result, i * rows)]
+    right = {k: [(sums, k * rows)] for k in order}
+    arrived = collect(left, right, rows, width, code_table.shape[2])
+    return finish(
+        left[0], right[0], arrived, width, conv_state, conv_taps, conv_bias, upsample, steps
+    )
 
 
 def solution(mesh):

time: 73.7 us -> 55.2 us (0.75)
  starting transfers between devices: 29.1 us -> 16.2 us
  local copies, waits for them, and re-layouts: 7.13 us -> 0.02 us
  waiting for transfers between devices: 11.8 us -> 16.7 us
  Pallas kernels: 23.6 us -> 21.4 us
    ppermute x21 -> x12, starting transfers between devices: 26.9 us -> 15.2 us  [shift(): return lax.ppermute(value, 'expert', pairs)]
    unnamed x22 -> x10, local copies, waits for them, and re-layouts: 7.1 us -> 0.02 us
    ppermute x21 -> x12, waiting for transfers between devices: 11.7 us -> 16.7 us  [shift(): return lax.ppermute(value, 'expert', pairs)]
    ppermute x12 -> x3, starting transfers between devices: 2.17 us -> 1.03 us  [swap_wave(): return lax.ppermute(value, 'wave', [(0, 1), (1, 0)])]
    pallas_call x1, Pallas kernels: 3.05 us -> 2.17 us  [frame_sums(): pl.pallas_call(functools.partial(frames_kernel, columns, books, shard, se...]
    pallas_call x5 -> x2, Pallas kernels: 13.4 us -> 12.5 us  [experts(): pl.pallas_call(functools.partial(experts_kernel, width, lax.axis_size('ex...]
    pallas_call x2 -> x3, Pallas kernels: 1.83 us -> 1.31 us  [the longest x1 1.1 us: finish(): pl.pallas_call(functools.partial(finish_kernel, *numbered[0][0], width),...]
  transfers between devices with their start and end apart: 33 -> 15, of which waited for: 6 -> 10; matrix products, arithmetic and copies ran while one was open for 1% -> 0% of each run, Pallas kernels for 29% -> 33%
where the time goes in v4:
time: 55.2 us; the launch traced here: 55 us
  Pallas kernels  21.4 us (39%)
  waiting for transfers between devices  16.7 us (30%)
  starting transfers between devices  16.2 us (29%)
  between operations  0.73 us (1%)
    ppermute x12, waiting for transfers between devices, shift(): return lax.ppermute(value, 'expert', pairs)  16.7 us
    ppermute x12, starting transfers between devices, shift(): return lax.ppermute(value, 'expert', pairs)  15.2 us
    pallas_call x2, Pallas kernels, experts(): pl.pallas_call(functools.partial(experts_kernel, width, lax.axis_size('ex...  12.5 us
    pallas_call x1, Pallas kernels, load(): pl.pallas_call(load_kernel, out_shape=[pltpu.VMEM(v.shape, v.dtype) for v...  3.78 us
    pallas_call x1, Pallas kernels, frame_sums(): pl.pallas_call(functools.partial(frames_kernel, columns, books, shard, se...  2.17 us
    pallas_call x1, Pallas kernels, pack(): pl.pallas_call(functools.partial(pack_kernel, columns, n_wave), out_shape...  1.59 us
  transfers between devices with their start and end apart: 15, of which 10 were waited for; matrix products, arithmetic and copies ran while one was open for 0% of the time, Pallas kernels for 33%

profile of v4, /device:TPU:0, one launch (start us, length us, event | category | flops | bytes accessed | tf_op | source)
XLA Modules:
  0.0 55.0 jit_solution(9905766910316729908)
XLA Ops:
  0.6 0.5 collective-permute-start.4
  1.1 0.1 collective-permute-start.7
  1.2 0.4 collective-permute-start.8
  1.7 1.6 %pack.1.refs_0_ = bf16[32,2176]{1,0:T(8,128)(2,1)S(1)} custom-call(s32[1]{0:T(128)} %bitcast._.place_ref, bf16[16,2,2048]{2,1,0:T(2,128)(2,1)} %refs_0_.1, s32[2,8,16]{2,1,0:T(8,128)} %bitcast.14, f32[2,8,16]{2,1,0:T(8,128)} %bitcast.15, s32[16,2,16]{2,1,0:T(2,128)} %refs_3_.1, s32[1,16]{1,0:T(1,128)} %bitcast.16), custom_call_target="tpu_custom_call" | custom-call | tf_op jit(solution)/shard_map/pack/pallas_call | solution.py:168
  3.3 2.6 %collective-permute-start.1 = (bf16[32,2176]{1,0:T(8,128)(2,1)S(1)}, bf16[32,2176]{1,0:T(8,128)(2,1)S(1)}, u32[]{:S(2)}, u32[]{:S(2)}) collective-permute-start(bf16[32,2176]{1,0:T(8,128)(2,1)S(1)} %pack.1.refs_0_), channel_id=1, source_target_pairs={{0,2},{4,0},{8,4},{12,8},{14,12},{10,14},{6,10},{2,6},{1,3},{5,1},... | collective-permute-start | bytes 417800 | tf_op jit(solution)/shard_map/ppermute | solution.py:23
  5.9 0.1 collective-permute-start
  6.0 3.8 %load.1 = (bf16[2,2048,384]{2,1,0:T(8,128)(2,1)S(1)}, bf16[2,2048,384]{2,1,0:T(8,128)(2,1)S(1)}, bf16[768,2048]{1,0:T(8,128)(2,1)S(1)}) custom-call(bf16[32,2176]{1,0:T(8,128)(2,1)S(1)} %pack.1.refs_0_, bf16[2,2048,384]{2,1,0:T(8,128)(2,1)} %refs_1_.1, bf16[2,2048,384]{2,1,0:T(8,128)(2,1)} %refs_2_.1, bf16[768,2048]{1,0:T(8,128)(2,1)} %bitcast.13), custom_call_target="tpu_custom_call" | custom-call | bytes 9437184 | tf_op jit(solution)/shard_map/load/pallas_call | solution.py:196
  9.8 0.4 collective-permute-done.1.refs_1_
  10.2 1.4 %collective-permute-done.refs_7_.refs_2_ = bf16[32,2176]{1,0:T(8,128)(2,1)S(1)} collective-permute-done((bf16[32,2176]{1,0:T(8,128)(2,1)S(1)}, bf16[32,2176]{1,0:T(8,128)(2,1)S(1)}, u32[]{:S(2)}, u32[]{:S(2)}) %collective-permute-start) | collective-permute-done | bytes 139296 | tf_op jit(solution)/shard_map/ppermute | solution.py:23
  11.6 0.0 copy-start
  11.7 0.4 collective-permute-start.2
  12.1 1.6 %collective-permute-start.3 = (bf16[32,2176]{1,0:T(8,128)(2,1)S(1)}, bf16[32,2176]{1,0:T(8,128)(2,1)S(1)}, u32[]{:S(2)}, u32[]{:S(2)}) collective-permute-start(bf16[32,2176]{1,0:T(8,128)(2,1)S(1)} %collective-permute-done.1.refs_1_), channel_id=1, source_target_pairs={{0,2},{4,0},{8,4},{12,8},{14,12},{10,14},{6,10},{2,6},{1,3},{5,1},... | collective-permute-start | bytes 417800 | tf_op jit(solution)/shard_map/ppermute | solution.py:23
  13.7 3.0 %collective-permute-done.2.refs_2_.refs_6_ = bf16[32,2176]{1,0:T(8,128)(2,1)S(1)} collective-permute-done((bf16[32,2176]{1,0:T(8,128)(2,1)S(1)}, bf16[32,2176]{1,0:T(8,128)(2,1)S(1)}, u32[]{:S(2)}, u32[]{:S(2)}) %collective-permute-start.2) | collective-permute-done | bytes 139296 | tf_op jit(solution)/shard_map/ppermute | solution.py:23
  16.7 0.4 collective-permute-done.3.refs_0_.refs_2_
  17.1 0.0 collective-permute-done.4.refs_7_
  17.1 1.6 %collective-permute-start.6 = (bf16[32,2176]{1,0:T(8,128)(2,1)S(1)}, bf16[32,2176]{1,0:T(8,128)(2,1)S(1)}, u32[]{:S(2)}, u32[]{:S(2)}) collective-permute-start(bf16[32,2176]{1,0:T(8,128)(2,1)S(1)} %collective-permute-done.3.refs_0_.refs_2_), channel_id=1, source_target_pairs={{0,2},{4,0},{8,4},{12,8},{14,12},{10,14},{6,10},{2,6},{1,3},{5,1},... | collective-permute-start | bytes 417800 | tf_op jit(solution)/shard_map/ppermute | solution.py:23
  18.7 0.4 collective-permute-start.5
  19.1 0.0 collective-permute-done.7.refs_8_
  19.1 3.0 %collective-permute-done.6.refs_3_ = bf16[32,2176]{1,0:T(8,128)(2,1)S(1)} collective-permute-done((bf16[32,2176]{1,0:T(8,128)(2,1)S(1)}, bf16[32,2176]{1,0:T(8,128)(2,1)S(1)}, u32[]{:S(2)}, u32[]{:S(2)}) %collective-permute-start.6) | collective-permute-done | bytes 139296 | tf_op jit(solution)/shard_map/ppermute | solution.py:23
  22.2 1.9 %collective-permute-done.5.refs_1_.refs_5_ = bf16[32,2176]{1,0:T(8,128)(2,1)S(1)} collective-permute-done((bf16[32,2176]{1,0:T(8,128)(2,1)S(1)}, bf16[32,2176]{1,0:T(8,128)(2,1)S(1)}, u32[]{:S(2)}, u32[]{:S(2)}) %collective-permute-start.5) | collective-permute-done | bytes 139296 | tf_op jit(solution)/shard_map/ppermute | solution.py:23
  24.1 0.3 collective-permute-start.9
  24.4 0.0 collective-permute-done.8.refs_9_
  24.4 6.2 %experts.2.refs_0_ = bf16[128,2048]{1,0:T(8,128)(2,1)S(1)} custom-call(s32[1]{0:T(128)} %bitcast._.place_ref, bf16[32,2176]{1,0:T(8,128)(2,1)S(1)} %collective-permute-done.3.refs_0_.refs_2_, bf16[32,2176]{1,0:T(8,128)(2,1)S(1)} %collective-permute-done.5.refs_1_.refs_5_, bf16[32,2176]{1,0:T(8,128)(2,1)S(1)} %collective-permute-done.2.refs_2_.refs_6_, ...), custom_call_target="tpu_custom_call" | custom-call | flops 2415919104 | bytes 18874368 | tf_op jit(solution)/shard_map/experts/pallas_call | solution.py:241
  30.7 0.0 collective-permute-done.9.refs_4_.refs_3_
  30.7 0.0 copy-done
  30.7 2.2 %frame_sums.1.refs_1_ = bf16[256,1024]{1,0:T(8,128)(2,1)S(1)} custom-call(s32[1]{0:T(128)} %bitcast._.place_ref, bf16[32,2176]{1,0:T(8,128)(2,1)S(1)} %pack.1.refs_0_, bf16[32,2176]{1,0:T(8,128)(2,1)S(1)} %collective-permute-done.1.refs_1_, bf16[32,2176]{1,0:T(8,128)(2,1)S(1)} %collective-permute-done.3.refs_0_.refs_2_, ...), custom_call_target="tpu_custom_call" | custom-call | flops 1073741824 | bytes 4194304 | tf_op jit(solution)/shard_map/frame_sums/pallas_call | solution.py:310
  32.9 0.1 join.2
  32.9 1.8 %collective-permute-start.10 = (bf16[64,3072]{1,0:T(8,128)(2,1)S(1)}, bf16[64,3072]{1,0:T(8,128)(2,1)S(1)}, u32[]{:S(2)}, u32[]{:S(2)}) collective-permute-start(bf16[64,3072]{1,0:T(8,128)(2,1)S(1)} %get-tuple-element.35), channel_id=1, source_target_pairs={{0,4},{4,8},{8,12},{12,14},{14,10},{10,6},{6,2},{2,0},{1,5},{5,9},... | collective-permute-start | bytes 1179656 | tf_op jit(solution)/shard_map/ppermute | solution.py:23
  34.8 0.0 copy-start.1
  34.8 0.0 copy-start.2
  34.8 0.0 copy-start.3
  34.8 0.0 copy-start.4
  34.8 0.3 collective-permute-start.11
  35.1 6.3 %experts.3.refs_0_ = bf16[128,2048]{1,0:T(8,128)(2,1)S(1)} custom-call(s32[1]{0:T(128)} %bitcast._.place_ref, bf16[32,2176]{1,0:T(8,128)(2,1)S(1)} %pack.1.refs_0_, bf16[32,2176]{1,0:T(8,128)(2,1)S(1)} %collective-permute-done.1.refs_1_, bf16[32,2176]{1,0:T(8,128)(2,1)S(1)} %collective-permute-done.refs_7_.refs_2_, ...), custom_call_target="tpu_custom_call" | custom-call | flops 2415919104 | bytes 18874368 | tf_op jit(solution)/shard_map/experts/pallas_call | solution.py:241
  41.4 0.0 collective-permute-done.10.refs_2_
  41.4 1.8 %collective-permute-done.11.refs_3_ = bf16[64,3072]{1,0:T(8,128)(2,1)S(1)} collective-permute-done((bf16[64,3072]{1,0:T(8,128)(2,1)S(1)}, bf16[64,3072]{1,0:T(8,128)(2,1)S(1)}, u32[]{:S(2)}, u32[]{:S(2)}) %collective-permute-start.11) | collective-permute-done | bytes 393248 | tf_op jit(solution)/shard_map/ppermute | solution.py:23
  43.2 0.2 join.3
  43.4 1.7 %collective-permute-start.12 = (bf16[32,3072]{1,0:T(8,128)(2,1)S(1)}, bf16[32,3072]{1,0:T(8,128)(2,1)S(1)}, u32[]{:S(2)}, u32[]{:S(2)}) collective-permute-start(bf16[32,3072]{1,0:T(8,128)(2,1)S(1)} %get-tuple-element.37), channel_id=1, source_target_pairs={{0,4},{4,8},{8,12},{12,14},{14,10},{10,6},{6,2},{2,0},{1,5},{5,9},... | collective-permute-start | bytes 589832 | tf_op jit(solution)/shard_map/ppermute | solution.py:23
  45.1 0.4 collective-permute-start.13
  45.4 3.8 %collective-permute-start.14 = (bf16[32,3072]{1,0:T(8,128)(2,1)S(1)}, bf16[32,3072]{1,0:T(8,128)(2,1)S(1)}, u32[]{:S(2)}, u32[]{:S(2)}) collective-permute-start(bf16[32,3072]{1,0:T(8,128)(2,1)S(1)} %get-tuple-element.39), channel_id=1, source_target_pairs={{0,14},{4,10},{8,6},{12,2},{14,0},{10,4},{6,8},{2,12},{1,15},{5,11... | collective-permute-start | bytes 589832 | tf_op jit(solution)/shard_map/ppermute | solution.py:23
  49.2 1.1 %collective-permute-done.12.refs_2_ = bf16[32,3072]{1,0:T(8,128)(2,1)S(1)} collective-permute-done((bf16[32,3072]{1,0:T(8,128)(2,1)S(1)}, bf16[32,3072]{1,0:T(8,128)(2,1)S(1)}, u32[]{:S(2)}, u32[]{:S(2)}) %collective-permute-start.12) | collective-permute-done | bytes 196640 | tf_op jit(solution)/shard_map/ppermute | solution.py:23
  50.4 0.8 %collective-permute-done.13.refs_3_ = bf16[32,3072]{1,0:T(8,128)(2,1)S(1)} collective-permute-done((bf16[32,3072]{1,0:T(8,128)(2,1)S(1)}, bf16[32,3072]{1,0:T(8,128)(2,1)S(1)}, u32[]{:S(2)}, u32[]{:S(2)}) %collective-permute-start.13) | collective-permute-done | bytes 196640 | tf_op jit(solution)/shard_map/ppermute | solution.py:23
  51.1 2.8 %collective-permute-done.14.refs_4_ = bf16[32,3072]{1,0:T(8,128)(2,1)S(1)} collective-permute-done((bf16[32,3072]{1,0:T(8,128)(2,1)S(1)}, bf16[32,3072]{1,0:T(8,128)(2,1)S(1)}, u32[]{:S(2)}, u32[]{:S(2)}) %collective-permute-start.14) | collective-permute-done | bytes 196640 | tf_op jit(solution)/shard_map/ppermute | solution.py:23
  53.9 0.0 copy-done.1
  53.9 0.0 copy-done.2
  53.9 0.0 copy-done.3
  53.9 0.0 copy-done.4
  53.9 1.1 %finish.1 = (bf16[16,2,2048]{2,1,0:T(2,128)(2,1)}, bf16[16,2,512]{2,1,0:T(2,128)(2,1)}, bf16[6,16,1024]{2,1,0:T(8,128)(2,1)}) custom-call(bf16[128,2048]{1,0:T(8,128)(2,1)S(1)} %experts.3.refs_0_, bf16[256,1024]{1,0:T(8,128)(2,1)S(1)} %frame_sums.1.refs_1_, bf16[32,3072]{1,0:T(8,128)(2,1)S(1)} %collective-permute-done.12.refs_2_, ...), custom_call_target="tpu_custom_call" | custom-call | bytes 2097152 | tf_op jit(solution)/shard_map/finish/pallas_call | solution.py:361
Async XLA Ops:
  0.6 16.5 %collective-permute-start.4 = (bf16[2,2048,384]{2,1,0:T(8,128)(2,1)}, bf16[2,2048,384]{2,1,0:T(8,128)(2,1)S(1)}, u32[]{:S(2)}, u32[]{:S(2)}) collective-permute-start(bf16[2,2048,384]{2,1,0:T(8,128)(2,1)} %refs_1_.1), channel_id=1, source_target_pairs={{0,1},{1,0},{2,3},{3,2},{4,5},{5,4},{6,7},{7,6},{8,9},{9,8},{10,11... | collective-permute-start | bytes 9437192 | tf_op jit(solution)/shard_map/ppermute | solution.py:27
  1.1 18.0 %collective-permute-start.7 = (bf16[2,2048,384]{2,1,0:T(8,128)(2,1)}, bf16[2,2048,384]{2,1,0:T(8,128)(2,1)}, u32[]{:S(2)}, u32[]{:S(2)}) collective-permute-start(bf16[2,2048,384]{2,1,0:T(8,128)(2,1)} %refs_2_.1), channel_id=1, source_target_pairs={{0,1},{1,0},{2,3},{3,2},{4,5},{5,4},{6,7},{7,6},{8,9},{9,8},{10,11... | collective-permute-start | bytes 9437192 | tf_op jit(solution)/shard_map/ppermute | solution.py:27
  1.2 23.2 %collective-permute-start.8 = (bf16[768,2048]{1,0:T(8,128)(2,1)}, bf16[768,2048]{1,0:T(8,128)(2,1)}, u32[]{:S(2)}, u32[]{:S(2)}) collective-permute-start(bf16[768,2048]{1,0:T(8,128)(2,1)} %bitcast.12), channel_id=1, source_target_pairs={{0,1},{1,0},{2,3},{3,2},{4,5},{5,4},{6,7},{7,6},{8,9},{9,8},{10,11... | collective-permute-start | bytes 9437192 | tf_op jit(solution)/shard_map/ppermute | solution.py:27
  3.3 7.0 %collective-permute-start.1 = (bf16[32,2176]{1,0:T(8,128)(2,1)S(1)}, bf16[32,2176]{1,0:T(8,128)(2,1)S(1)}, u32[]{:S(2)}, u32[]{:S(2)}) collective-permute-start(bf16[32,2176]{1,0:T(8,128)(2,1)S(1)} %pack.1.refs_0_), channel_id=1, source_target_pairs={{0,2},{4,0},{8,4},{12,8},{14,12},{10,14},{6,10},{2,6},{1,3},{5,1},... | collective-permute-start | bytes 417800 | tf_op jit(solution)/shard_map/ppermute | solution.py:23
  5.9 5.7 %collective-permute-start = (bf16[32,2176]{1,0:T(8,128)(2,1)S(1)}, bf16[32,2176]{1,0:T(8,128)(2,1)S(1)}, u32[]{:S(2)}, u32[]{:S(2)}) collective-permute-start(bf16[32,2176]{1,0:T(8,128)(2,1)S(1)} %pack.1.refs_0_), channel_id=1, source_target_pairs={{0,4},{4,8},{8,12},{12,14},{14,10},{10,6},{6,2},{2,0},{1,5},{5,9},... | collective-permute-start | bytes 417800 | tf_op jit(solution)/shard_map/ppermute | solution.py:23
  11.6 19.0 %copy-start = (bf16[16,128,1024]{2,1,0:T(8,128)(2,1)S(1)}, bf16[16,128,1024]{2,1,0:T(8,128)(2,1)}, u32[]{:S(2)}) copy-start(bf16[16,128,1024]{2,1,0:T(8,128)(2,1)} %param.21) | copy-start | bytes 12582916
  11.7 5.1 %collective-permute-start.2 = (bf16[32,2176]{1,0:T(8,128)(2,1)S(1)}, bf16[32,2176]{1,0:T(8,128)(2,1)S(1)}, u32[]{:S(2)}, u32[]{:S(2)}) collective-permute-start(bf16[32,2176]{1,0:T(8,128)(2,1)S(1)} %collective-permute-done.refs_7_.refs_2_), channel_id=1, source_target_pairs={{0,4},{4,8},{8,12},{12,14},{14,10},{10,6},{6,2},{2,0},{1,5},{5,9},... | collective-permute-start | bytes 417800 | tf_op jit(solution)/shard_map/ppermute | solution.py:23
  12.1 5.1 %collective-permute-start.3 = (bf16[32,2176]{1,0:T(8,128)(2,1)S(1)}, bf16[32,2176]{1,0:T(8,128)(2,1)S(1)}, u32[]{:S(2)}, u32[]{:S(2)}) collective-permute-start(bf16[32,2176]{1,0:T(8,128)(2,1)S(1)} %collective-permute-done.1.refs_1_), channel_id=1, source_target_pairs={{0,2},{4,0},{8,4},{12,8},{14,12},{10,14},{6,10},{2,6},{1,3},{5,1},... | collective-permute-start | bytes 417800 | tf_op jit(solution)/shard_map/ppermute | solution.py:23
  17.1 5.1 %collective-permute-start.6 = (bf16[32,2176]{1,0:T(8,128)(2,1)S(1)}, bf16[32,2176]{1,0:T(8,128)(2,1)S(1)}, u32[]{:S(2)}, u32[]{:S(2)}) collective-permute-start(bf16[32,2176]{1,0:T(8,128)(2,1)S(1)} %collective-permute-done.3.refs_0_.refs_2_), channel_id=1, source_target_pairs={{0,2},{4,0},{8,4},{12,8},{14,12},{10,14},{6,10},{2,6},{1,3},{5,1},... | collective-permute-start | bytes 417800 | tf_op jit(solution)/shard_map/ppermute | solution.py:23
  18.7 5.4 %collective-permute-start.5 = (bf16[32,2176]{1,0:T(8,128)(2,1)S(1)}, bf16[32,2176]{1,0:T(8,128)(2,1)S(1)}, u32[]{:S(2)}, u32[]{:S(2)}) collective-permute-start(bf16[32,2176]{1,0:T(8,128)(2,1)S(1)} %collective-permute-done.2.refs_2_.refs_6_), channel_id=1, source_target_pairs={{0,4},{4,8},{8,12},{12,14},{14,10},{10,6},{6,2},{2,0},{1,5},{5,9},... | collective-permute-start | bytes 417800 | tf_op jit(solution)/shard_map/ppermute | solution.py:23
  24.1 6.6 %collective-permute-start.9 = (bf16[32,2176]{1,0:T(8,128)(2,1)S(1)}, bf16[32,2176]{1,0:T(8,128)(2,1)S(1)}, u32[]{:S(2)}, u32[]{:S(2)}) collective-permute-start(bf16[32,2176]{1,0:T(8,128)(2,1)S(1)} %collective-permute-done.5.refs_1_.refs_5_), channel_id=1, source_target_pairs={{0,4},{4,8},{8,12},{12,14},{14,10},{10,6},{6,2},{2,0},{1,5},{5,9},... | collective-permute-start | bytes 417800 | tf_op jit(solution)/shard_map/ppermute | solution.py:23
  32.9 8.5 %collective-permute-start.10 = (bf16[64,3072]{1,0:T(8,128)(2,1)S(1)}, bf16[64,3072]{1,0:T(8,128)(2,1)S(1)}, u32[]{:S(2)}, u32[]{:S(2)}) collective-permute-start(bf16[64,3072]{1,0:T(8,128)(2,1)S(1)} %get-tuple-element.35), channel_id=1, source_target_pairs={{0,4},{4,8},{8,12},{12,14},{14,10},{10,6},{6,2},{2,0},{1,5},{5,9},... | collective-permute-start | bytes 1179656 | tf_op jit(solution)/shard_map/ppermute | solution.py:23
  34.8 19.1 %copy-start.1 = (bf16[1024,512]{1,0:T(8,128)(2,1)S(1)}, bf16[1024,512]{1,0:T(8,128)(2,1)}, u32[]{:S(2)}) copy-start(bf16[1024,512]{1,0:T(8,128)(2,1)} %refs_8_.1) | copy-start | bytes 3145732
  34.8 19.1 %copy-start.2 = (bf16[16,6,1024]{2,0,1:T(8,128)(2,1)S(1)}, bf16[16,6,1024]{2,0,1:T(8,128)(2,1)}, u32[]{:S(2)}) copy-start(bf16[16,6,1024]{2,0,1:T(8,128)(2,1)} %param.22) | copy-start | bytes 589828
  34.8 19.1 %copy-start.3 = (f32[7,1024]{1,0:T(8,128)S(1)}, f32[7,1024]{1,0:T(8,128)}, u32[]{:S(2)}) copy-start(f32[7,1024]{1,0:T(8,128)} %refs_6_.1) | copy-start | bytes 86020
  34.8 19.1 %copy-start.4 = (f32[1024]{0:T(1024)S(1)}, f32[1024]{0:T(1024)}, u32[]{:S(2)}) copy-start(f32[1024]{0:T(1024)} %param.24) | copy-start | bytes 12292
  34.8 8.4 %collective-permute-start.11 = (bf16[64,3072]{1,0:T(8,128)(2,1)S(1)}, bf16[64,3072]{1,0:T(8,128)(2,1)S(1)}, u32[]{:S(2)}, u32[]{:S(2)}) collective-permute-start(bf16[64,3072]{1,0:T(8,128)(2,1)S(1)} %get-tuple-element.36), channel_id=1, source_target_pairs={{0,2},{4,0},{8,4},{12,8},{14,12},{10,14},{6,10},{2,6},{1,3},{5,1},... | collective-permute-start | bytes 1179656 | tf_op jit(solution)/shard_map/ppermute | solution.py:23
  43.4 7.0 %collective-permute-start.12 = (bf16[32,3072]{1,0:T(8,128)(2,1)S(1)}, bf16[32,3072]{1,0:T(8,128)(2,1)S(1)}, u32[]{:S(2)}, u32[]{:S(2)}) collective-permute-start(bf16[32,3072]{1,0:T(8,128)(2,1)S(1)} %get-tuple-element.37), channel_id=1, source_target_pairs={{0,4},{4,8},{8,12},{12,14},{14,10},{10,6},{6,2},{2,0},{1,5},{5,9},... | collective-permute-start | bytes 589832 | tf_op jit(solution)/shard_map/ppermute | solution.py:23
  45.1 6.1 %collective-permute-start.13 = (bf16[32,3072]{1,0:T(8,128)(2,1)S(1)}, bf16[32,3072]{1,0:T(8,128)(2,1)S(1)}, u32[]{:S(2)}, u32[]{:S(2)}) collective-permute-start(bf16[32,3072]{1,0:T(8,128)(2,1)S(1)} %get-tuple-element.38), channel_id=1, source_target_pairs={{0,2},{4,0},{8,4},{12,8},{14,12},{10,14},{6,10},{2,6},{1,3},{5,1},... | collective-permute-start | bytes 589832 | tf_op jit(solution)/shard_map/ppermute | solution.py:23
  45.4 8.5 %collective-permute-start.14 = (bf16[32,3072]{1,0:T(8,128)(2,1)S(1)}, bf16[32,3072]{1,0:T(8,128)(2,1)S(1)}, u32[]{:S(2)}, u32[]{:S(2)}) collective-permute-start(bf16[32,3072]{1,0:T(8,128)(2,1)S(1)} %get-tuple-element.39), channel_id=1, source_target_pairs={{0,14},{4,10},{8,6},{12,2},{14,0},{10,4},{6,8},{2,12},{1,15},{5,11... | collective-permute-start | bytes 589832 | tf_op jit(solution)/shard_map/ppermute | solution.py:23

commit v5 on v4

--- a/solution.py
+++ b/solution.py
@@ -49,48 +49,39 @@
 
 
 def join_kernel(plan, rows, width, *refs):
-    outs = refs[-len(plan) :]
-    for out_ref, blocks in zip(outs, plan):
-        for i, (left, right, whole) in enumerate(blocks):
-            at = slice(i * rows, (i + 1) * rows)
-            total = summed(refs, left, rows, slice(None))
-            for index, row in whole:
-                total = total + refs[index][row : row + rows, 0:width].astype(F32)
-            out_ref[at, 0:width] = total.astype(BF16)
-            total = summed(refs, right, rows, slice(None))
-            for index, row in whole:
-                total = total + refs[index][row : row + rows, width:].astype(F32)
-            out_ref[at, width:] = total.astype(BF16)
+    for out_ref, ((left, right),) in zip(refs[-len(plan) :], plan):
+        out_ref[:, 0:width] = summed(refs, left, rows, slice(None)).astype(BF16)
+        out_ref[:, width:] = summed(refs, right, rows, slice(None)).astype(BF16)
 
 
 def join(plan, rows, width, channels):
-    arrays, numbered = tidy(plan)
+    arrays, numbered = tidy([[pair] for pair in plan])
     return pl.pallas_call(
         functools.partial(join_kernel, numbered, rows, width),
-        out_shape=[jax.ShapeDtypeStruct((rows * len(out), width + channels), BF16) for out in plan],
+        out_shape=[jax.ShapeDtypeStruct((rows, width + channels), BF16)] * len(plan),
         compiler_params=pltpu.CompilerParams(vmem_limit_bytes=VMEM_LIMIT),
         cost_estimate=pl.CostEstimate(flops=0, bytes_accessed=1 << 20, transcendentals=0),
         name="join",
     )(*arrays)
 
 
-def collect(left, right, rows, width, channels):
-    count = lax.axis_size("expert")
-    half = count // 2
-    ahead, back = [], []
-    for step in range(count // 4, 1, -1):
-        pairs = ((step, half + step - 1), (count - step, half - step + 1))
-        plan = [
-            [(left[k], right[k], [(v, i * rows) for v in got]) for i, k in enumerate(pair)]
-            for pair, got in zip(pairs, (ahead, back))
-        ]
-        forward, backward = join(plan, rows, width, channels)
-        ahead, back = [shift(forward, 1)], [shift(backward, -1)]
-    one = (left[1], right[1], [(v, 0) for v in ahead])
-    minus = (left[count - 1], right[count - 1], [(v, 0) for v in back])
-    across = (left[half], right[half], [(v, rows) for v in ahead + back])
-    one, minus, across = join([[one], [minus], [across]], rows, width, channels)
-    return shift(one, 1), shift(minus, -1), shift(across, half)
+def carry(pairs):
+    ahead = back = None
+    for forward, backward in pairs[::-1]:
+        if ahead is not None:
+            forward = (forward.astype(F32) + ahead.astype(F32)).astype(BF16)
+            backward = (backward.astype(F32) + back.astype(F32)).astype(BF16)
+        ahead, back = shift(forward, 1), shift(backward, -1)
+    return ahead, back
+
+
+def towards(near, arrived, rows):
+    ahead, back = arrived
+    return (
+        [(near, rows), (ahead, 0)],
+        [(near, 2 * rows), (back, 0)],
+        [(near, 3 * rows), (ahead, rows), (back, rows)],
+    )
 
 
 def after(values, *earlier):
@@ -207,10 +198,10 @@
     )(earlier, *[pltpu.with_memory_space_constraint(v, pltpu.HBM) for v in arrays])
 
 
-def experts_kernel(width, expert_count, block_count, place_ref, *refs):
+def experts_kernel(width, expert_count, block_count, out_count, place_ref, *refs):
     blocks = refs[:block_count]
-    parts = [refs[i : i + 3] for i in range(block_count, len(refs) - 3, 3)]
-    out_ref, rows_ref, act_ref = refs[-3:]
+    parts = [refs[i : i + 3] for i in range(block_count, len(refs) - 2 - out_count, 3)]
+    outs, (rows_ref, act_ref) = refs[-2 - out_count : -2], refs[-2:]
     rows = blocks[0].shape[0]
     for i, block in enumerate(blocks):
         rows_ref[i * rows : (i + 1) * rows, :] = block[:, 0:width]
@@ -229,10 +220,14 @@
             act_ref[:, j * units : (j + 1) * units] = (value * weight).astype(BF16)
         result = jnp.dot(act_ref[...], down_ref[...], preferred_element_type=F32)
         total = result if total is None else total + result
-    out_ref[...] = total.astype(BF16)
-
-
-def experts(blocks, place, held):
+    start = 0
+    for out_ref in outs:
+        size = out_ref.shape[0]
+        out_ref[...] = total[start : start + size].astype(BF16)
+        start += size
+
+
+def experts(blocks, split, place, held):
     local, width, units = held[0][0].shape
     rows = blocks[0].shape[0]
     total = rows * len(blocks)
@@ -240,11 +235,11 @@
     weights = [v for part in held for v in part]
     return pl.pallas_call(
         functools.partial(
-            experts_kernel, width, lax.axis_size("expert") * local, len(blocks)
+            experts_kernel, width, lax.axis_size("expert") * local, len(blocks), split
         ),
-        out_shape=jax.ShapeDtypeStruct((total, width), BF16),
+        out_shape=[jax.ShapeDtypeStruct((total // split, width), BF16)] * split,
         in_specs=[pl.BlockSpec(memory_space=pltpu.SMEM)] + [vmem] * (len(blocks) + len(weights)),
-        out_specs=vmem,
+        out_specs=[vmem] * split,
         scratch_shapes=[
             pltpu.VMEM((total, width), BF16),
             pltpu.VMEM((total, local * units), BF16),
@@ -261,7 +256,7 @@
 
 def frames_kernel(columns, books, shard, sessions, steps, order, place_ref, *refs):
     metas = refs[: len(order)]
-    table_ref, out_ref, hot_ref = refs[len(order) :]
+    table_ref, *outs, hot_ref = refs[len(order) :]
     count = len(order)
     code_at, slot_at = columns
     rows = metas[0].shape[0]
@@ -298,10 +293,15 @@
             low_end = lanes // shard * shard
             hit = hit & (code >= low_end) & (code < low_end + shard)
         hot_ref[:, start : start + chunk] = jnp.where(hit, 1.0, 0.0).astype(BF16)
-    out_ref[...] = jnp.dot(hot_ref[...], table_ref[...], preferred_element_type=F32).astype(BF16)
-
-
-def frame_sums(blocks, order, place, code_table, columns, width, sessions, steps):
+    result = jnp.dot(hot_ref[...], table_ref[...], preferred_element_type=F32)
+    start = 0
+    for out_ref in outs:
+        size = out_ref.shape[0]
+        out_ref[...] = result[start : start + size].astype(BF16)
+        start += size
+
+
+def frame_sums(blocks, order, sizes, place, code_table, columns, width, sessions, steps):
     books, shard, channels = code_table.shape
     rows = blocks[0].shape[0]
     total = rows * len(order)
@@ -310,11 +310,11 @@
     return pl.pallas_call(
         functools.partial(frames_kernel, columns, books, shard, sessions, steps, order),
         grid=(1,),
-        out_shape=jax.ShapeDtypeStruct((total, channels), BF16),
+        out_shape=[jax.ShapeDtypeStruct((rows * size, channels), BF16) for size in sizes],
         in_specs=[pl.BlockSpec(memory_space=pltpu.SMEM)]
         + [pl.BlockSpec((rows, meta_width), lambda i: (0, width // meta_width))] * len(order)
         + [vmem],
-        out_specs=vmem,
+        out_specs=[vmem] * len(sizes),
         scratch_shapes=[pltpu.VMEM((total, books * shard), BF16)],
         compiler_params=pltpu.CompilerParams(vmem_limit_bytes=VMEM_LIMIT + 12 * total * total),
         cost_estimate=pl.CostEstimate(
@@ -413,7 +413,7 @@
     )
     half = count // 2
     weights = (w_gate, w_up, w_down.reshape(-1, width))
-    sibling = [swap_wave(v) for v in weights]
+    sibling = [swap_wave(v) for v in after(weights, own)]
     held = [load(own, *weights)]
 
     blocks = {0: own}
@@ -430,24 +430,37 @@
         blocks.update(got)
 
     held.append(sibling)
-    order = list(range(count))
     near = [0, 1, count - 1, half]
-    groups = [near]
-    for step in range(2, count // 4 + 1):
-        groups.append([step, half + step - 1, count - step, half - step + 1])
-    left, turn = {}, place
-    for group in groups[::-1]:
-        if group is near:
-            sums = frame_sums(blocks, order, turn, code_table, columns, width, sessions, steps)
-            (turn,) = after((place,), sums)
-        result = experts([blocks[k] for k in group], turn, held)
-        (turn,) = after((place,), result)
-        for i, k in enumerate(group):
-            left[k] = [(result, i * rows)]
-    right = {k: [(sums, k * rows)] for k in order}
-    arrived = collect(left, right, rows, width, code_table.shape[2])
+    far = [
+        [step, half + step - 1, count - step, half - step + 1] for step in range(2, count // 4 + 1)
+    ]
+    pairs, turn = [], place
+    for group in far[::-1]:
+        pairs.insert(0, experts([blocks[k] for k in group], 2, turn, held))
+        (turn,) = after((place,), pairs[0])
+    arrived = carry(pairs)
+    order = near + [k for group in far for k in group]
+    sizes = [4] + [2] * (2 * len(far))
+    near_frames, *rest = frame_sums(
+        blocks, order, sizes, turn, code_table, columns, width, sessions, steps
+    )
+    frames_arrived = carry(list(zip(rest[::2], rest[1::2])))
+    (turn,) = after((place,), near_frames)
+    (near_rows,) = experts([blocks[k] for k in near], 1, turn, held)
+    left = towards(near_rows, arrived, rows)
+    right = towards(near_frames, frames_arrived, rows)
+    one, minus, across = join(list(zip(left, right)), rows, width, code_table.shape[2])
+    last = [shift(one, 1), shift(minus, -1), shift(across, half)]
     return finish(
-        left[0], right[0], arrived, width, conv_state, conv_taps, conv_bias, upsample, steps
+        [(near_rows, 0)],
+        [(near_frames, 0)],
+        last,
+        width,
+        conv_state,
+        conv_taps,
+        conv_bias,
+        upsample,
+        steps,
     )
 
 

time: 55.2 us -> 52 us (0.942)
  Pallas kernels: 21.4 us -> 15.5 us
  starting transfers between devices: 16.2 us -> 18.6 us
    pallas_call x2, Pallas kernels: 12.5 us -> 6.69 us  [experts(): pl.pallas_call(functools.partial(experts_kernel, width, lax.axis_size('ex...]
    ppermute x12 -> x14, starting transfers between devices: 15.2 us -> 17.5 us  [shift(): return lax.ppermute(value, 'expert', pairs)]
    ppermute x12 -> x14, waiting for transfers between devices: 16.7 us -> 17.1 us  [shift(): return lax.ppermute(value, 'expert', pairs)]
  transfers between devices with their start and end apart: 15 -> 17, of which waited for: 10 -> 12; matrix products, arithmetic and copies ran while one was open for 0% -> 0% of each run, Pallas kernels for 33% -> 24%
where the time goes in v5:
time: 52 us; the launch traced here: 51.9 us
  starting transfers between devices  18.6 us (36%)
  waiting for transfers between devices  17.1 us (33%)
  Pallas kernels  15.5 us (30%)
  between operations  0.72 us (1%)
    ppermute x14, starting transfers between devices, shift(): return lax.ppermute(value, 'expert', pairs)  17.5 us
    ppermute x14, waiting for transfers between devices, shift(): return lax.ppermute(value, 'expert', pairs)  17.1 us
    pallas_call x2, Pallas kernels, experts(): pl.pallas_call(functools.partial(experts_kernel, width, lax.axis_size('ex...  6.69 us
    pallas_call x1, Pallas kernels, load(): pl.pallas_call(load_kernel, out_shape=[pltpu.VMEM(v.shape, v.dtype) for v...  3.78 us
    pallas_call x1, Pallas kernels, frame_sums(): pl.pallas_call(functools.partial(frames_kernel, columns, books, shard, se...  2.17 us
    pallas_call x1, Pallas kernels, pack(): pl.pallas_call(functools.partial(pack_kernel, columns, n_wave), out_shape...  1.59 us
    pallas_call x1, Pallas kernels, finish(): pl.pallas_call(functools.partial(finish_kernel, *numbered[0][0], width),...  1.09 us
  transfers between devices with their start and end apart: 17, of which 12 were waited for; matrix products, arithmetic and copies ran while one was open for 0% of the time, Pallas kernels for 24%

profile of v5, /device:TPU:0, one launch (start us, length us, event | category | flops | bytes accessed | tf_op | source)
XLA Modules:
  0.0 51.9 jit_solution(10072132911242976409)
XLA Ops:
  0.6 1.6 %pack.1.refs_0_ = bf16[32,2176]{1,0:T(8,128)(2,1)S(1)} custom-call(s32[1]{0:T(128)} %bitcast._.place_ref, bf16[16,2,2048]{2,1,0:T(2,128)(2,1)} %refs_0_.1, s32[2,8,16]{2,1,0:T(8,128)} %bitcast.14, f32[2,8,16]{2,1,0:T(8,128)} %bitcast.15, s32[16,2,16]{2,1,0:T(2,128)} %refs_3_.1, s32[1,16]{1,0:T(1,128)} %bitcast.16), custom_call_target="tpu_custom_call" | custom-call | tf_op jit(solution)/shard_map/pack/pallas_call | solution.py:159
  2.2 0.5 collective-permute-start.4
  2.8 0.1 collective-permute-start.7
  2.8 0.4 collective-permute-start.8
  3.3 2.6 %collective-permute-start.1 = (bf16[32,2176]{1,0:T(8,128)(2,1)S(1)}, bf16[32,2176]{1,0:T(8,128)(2,1)S(1)}, u32[]{:S(2)}, u32[]{:S(2)}) collective-permute-start(bf16[32,2176]{1,0:T(8,128)(2,1)S(1)} %pack.1.refs_0_), channel_id=1, source_target_pairs={{0,2},{4,0},{8,4},{12,8},{14,12},{10,14},{6,10},{2,6},{1,3},{5,1},... | collective-permute-start | bytes 417800 | tf_op jit(solution)/shard_map/ppermute | solution.py:23
  5.9 0.1 collective-permute-start
  5.9 3.8 %load.1 = (bf16[2,2048,384]{2,1,0:T(8,128)(2,1)S(1)}, bf16[2,2048,384]{2,1,0:T(8,128)(2,1)S(1)}, bf16[768,2048]{1,0:T(8,128)(2,1)S(1)}) custom-call(bf16[32,2176]{1,0:T(8,128)(2,1)S(1)} %pack.1.refs_0_, bf16[2,2048,384]{2,1,0:T(8,128)(2,1)} %refs_1_.1, bf16[2,2048,384]{2,1,0:T(8,128)(2,1)} %refs_2_.1, bf16[768,2048]{1,0:T(8,128)(2,1)} %bitcast.13), custom_call_target="tpu_custom_call" | custom-call | bytes 9437184 | tf_op jit(solution)/shard_map/load/pallas_call | solution.py:187
  9.7 0.5 collective-permute-done.1.refs_1_
  10.2 1.4 %collective-permute-done.refs_2_ = bf16[32,2176]{1,0:T(8,128)(2,1)S(1)} collective-permute-done((bf16[32,2176]{1,0:T(8,128)(2,1)S(1)}, bf16[32,2176]{1,0:T(8,128)(2,1)S(1)}, u32[]{:S(2)}, u32[]{:S(2)}) %collective-permute-start) | collective-permute-done | bytes 139296 | tf_op jit(solution)/shard_map/ppermute | solution.py:23
  11.6 0.0 copy-start
  11.6 0.3 collective-permute-start.2
  11.9 1.7 %collective-permute-start.3 = (bf16[32,2176]{1,0:T(8,128)(2,1)S(1)}, bf16[32,2176]{1,0:T(8,128)(2,1)S(1)}, u32[]{:S(2)}, u32[]{:S(2)}) collective-permute-start(bf16[32,2176]{1,0:T(8,128)(2,1)S(1)} %collective-permute-done.1.refs_1_), channel_id=1, source_target_pairs={{0,2},{4,0},{8,4},{12,8},{14,12},{10,14},{6,10},{2,6},{1,3},{5,1},... | collective-permute-start | bytes 417800 | tf_op jit(solution)/shard_map/ppermute | solution.py:23
  13.6 3.0 %collective-permute-done.2.refs_2_.refs_6_ = bf16[32,2176]{1,0:T(8,128)(2,1)S(1)} collective-permute-done((bf16[32,2176]{1,0:T(8,128)(2,1)S(1)}, bf16[32,2176]{1,0:T(8,128)(2,1)S(1)}, u32[]{:S(2)}, u32[]{:S(2)}) %collective-permute-start.2) | collective-permute-done | bytes 139296 | tf_op jit(solution)/shard_map/ppermute | solution.py:23
  16.7 0.3 collective-permute-done.3.refs_0_.refs_4_
  17.0 0.0 collective-permute-done.4.refs_7_
  17.0 1.7 %collective-permute-start.6 = (bf16[32,2176]{1,0:T(8,128)(2,1)S(1)}, bf16[32,2176]{1,0:T(8,128)(2,1)S(1)}, u32[]{:S(2)}, u32[]{:S(2)}) collective-permute-start(bf16[32,2176]{1,0:T(8,128)(2,1)S(1)} %collective-permute-done.3.refs_0_.refs_4_), channel_id=1, source_target_pairs={{0,2},{4,0},{8,4},{12,8},{14,12},{10,14},{6,10},{2,6},{1,3},{5,1},... | collective-permute-start | bytes 417800 | tf_op jit(solution)/shard_map/ppermute | solution.py:23
  18.7 0.3 collective-permute-start.5
  19.0 0.0 collective-permute-done.7.refs_8_
  19.0 3.0 %collective-permute-done.6.refs_3_.refs_7_ = bf16[32,2176]{1,0:T(8,128)(2,1)S(1)} collective-permute-done((bf16[32,2176]{1,0:T(8,128)(2,1)S(1)}, bf16[32,2176]{1,0:T(8,128)(2,1)S(1)}, u32[]{:S(2)}, u32[]{:S(2)}) %collective-permute-start.6) | collective-permute-done | bytes 139296 | tf_op jit(solution)/shard_map/ppermute | solution.py:23
  22.1 2.0 %collective-permute-done.5.refs_1_.refs_5_ = bf16[32,2176]{1,0:T(8,128)(2,1)S(1)} collective-permute-done((bf16[32,2176]{1,0:T(8,128)(2,1)S(1)}, bf16[32,2176]{1,0:T(8,128)(2,1)S(1)}, u32[]{:S(2)}, u32[]{:S(2)}) %collective-permute-start.5) | collective-permute-done | bytes 139296 | tf_op jit(solution)/shard_map/ppermute | solution.py:23
  24.1 0.2 collective-permute-start.9
  24.3 0.0 collective-permute-done.8.refs_9_
  24.3 3.4 %experts.2 = (bf16[64,2048]{1,0:T(8,128)(2,1)S(1)}, bf16[64,2048]{1,0:T(8,128)(2,1)S(1)}) custom-call(s32[1]{0:T(128)} %bitcast._.place_ref, bf16[32,2176]{1,0:T(8,128)(2,1)S(1)} %collective-permute-done.3.refs_0_.refs_4_, bf16[32,2176]{1,0:T(8,128)(2,1)S(1)} %collective-permute-done.5.refs_1_.refs_5_, ...), custom_call_target="tpu_custom_call" | custom-call | flops 2415919104 | bytes 18874368 | tf_op jit(solution)/shard_map/experts/pallas_call | solution.py:236
  27.6 2.0 %collective-permute-start.10 = (bf16[64,2048]{1,0:T(8,128)(2,1)S(1)}, bf16[64,2048]{1,0:T(8,128)(2,1)S(1)}, u32[]{:S(2)}, u32[]{:S(2)}) collective-permute-start(bf16[64,2048]{1,0:T(8,128)(2,1)S(1)} %get-tuple-element.41), channel_id=1, source_target_pairs={{0,4},{4,8},{8,12},{12,14},{14,10},{10,6},{6,2},{2,0},{1,5},{5,9},... | collective-permute-start | bytes 786440 | tf_op jit(solution)/shard_map/ppermute | solution.py:23
  29.6 0.1 collective-permute-start.12
  29.7 0.9 %collective-permute-done.9.refs_3_ = bf16[32,2176]{1,0:T(8,128)(2,1)S(1)} collective-permute-done((bf16[32,2176]{1,0:T(8,128)(2,1)S(1)}, bf16[32,2176]{1,0:T(8,128)(2,1)S(1)}, u32[]{:S(2)}, u32[]{:S(2)}) %collective-permute-start.9) | collective-permute-done | bytes 139296 | tf_op jit(solution)/shard_map/ppermute | solution.py:23
  30.6 0.0 copy-done
  30.6 2.2 %frame_sums.1 = (bf16[128,1024]{1,0:T(8,128)(2,1)S(1)}, bf16[64,1024]{1,0:T(8,128)(2,1)S(1)}, bf16[64,1024]{1,0:T(8,128)(2,1)S(1)}) custom-call(s32[1]{0:T(128)} %bitcast._.place_ref, bf16[32,2176]{1,0:T(8,128)(2,1)S(1)} %pack.1.refs_0_, bf16[32,2176]{1,0:T(8,128)(2,1)S(1)} %collective-permute-done.1.refs_1_, ...), custom_call_target="tpu_custom_call" | custom-call | flops 1073741824 | bytes 4194304 | tf_op jit(solution)/shard_map/frame_sums/pallas_call | solution.py:310
  32.7 1.1 %collective-permute-start.11 = (bf16[64,1024]{1,0:T(8,128)(2,1)S(1)}, bf16[64,1024]{1,0:T(8,128)(2,1)S(1)}, u32[]{:S(2)}, u32[]{:S(2)}) collective-permute-start(bf16[64,1024]{1,0:T(8,128)(2,1)S(1)} %get-tuple-element.47), channel_id=1, source_target_pairs={{0,4},{4,8},{8,12},{12,14},{14,10},{10,6},{6,2},{2,0},{1,5},{5,9},... | collective-permute-start | bytes 393224 | tf_op jit(solution)/shard_map/ppermute | solution.py:23
  33.9 0.0 copy-start.1
  33.9 1.0 %collective-permute-start.13 = (bf16[64,1024]{1,0:T(8,128)(2,1)S(1)}, bf16[64,1024]{1,0:T(8,128)(2,1)S(1)}, u32[]{:S(2)}, u32[]{:S(2)}) collective-permute-start(bf16[64,1024]{1,0:T(8,128)(2,1)S(1)} %get-tuple-element.48), channel_id=1, source_target_pairs={{0,2},{4,0},{8,4},{12,8},{14,12},{10,14},{6,10},{2,6},{1,3},{5,1},... | collective-permute-start | bytes 393224 | tf_op jit(solution)/shard_map/ppermute | solution.py:23
  34.9 3.3 %experts.3.refs_0_ = bf16[128,2048]{1,0:T(8,128)(2,1)S(1)} custom-call(s32[1]{0:T(128)} %bitcast._.place_ref, bf16[32,2176]{1,0:T(8,128)(2,1)S(1)} %pack.1.refs_0_, bf16[32,2176]{1,0:T(8,128)(2,1)S(1)} %collective-permute-done.1.refs_1_, bf16[32,2176]{1,0:T(8,128)(2,1)S(1)} %collective-permute-done.refs_2_, ...), custom_call_target="tpu_custom_call" | custom-call | flops 2415919104 | bytes 18874368 | tf_op jit(solution)/shard_map/experts/pallas_call | solution.py:236
  38.2 0.0 collective-permute-done.10.refs_1_
  38.2 0.0 collective-permute-done.12.refs_4_
  38.2 0.3 collective-permute-done.11.refs_3_
  38.5 1.4 %collective-permute-done.13.refs_5_ = bf16[64,1024]{1,0:T(8,128)(2,1)S(1)} collective-permute-done((bf16[64,1024]{1,0:T(8,128)(2,1)S(1)}, bf16[64,1024]{1,0:T(8,128)(2,1)S(1)}, u32[]{:S(2)}, u32[]{:S(2)}) %collective-permute-start.13) | collective-permute-done | bytes 131104 | tf_op jit(solution)/shard_map/ppermute | solution.py:23
  39.9 0.2 join.1
  40.0 1.7 %collective-permute-start.14 = (bf16[32,3072]{1,0:T(8,128)(2,1)S(1)}, bf16[32,3072]{1,0:T(8,128)(2,1)S(1)}, u32[]{:S(2)}, u32[]{:S(2)}) collective-permute-start(bf16[32,3072]{1,0:T(8,128)(2,1)S(1)} %get-tuple-element.49), channel_id=1, source_target_pairs={{0,4},{4,8},{8,12},{12,14},{14,10},{10,6},{6,2},{2,0},{1,5},{5,9},... | collective-permute-start | bytes 589832 | tf_op jit(solution)/shard_map/ppermute | solution.py:23
  41.8 0.3 collective-permute-start.15
  42.1 4.3 %collective-permute-start.16 = (bf16[32,3072]{1,0:T(8,128)(2,1)S(1)}, bf16[32,3072]{1,0:T(8,128)(2,1)S(1)}, u32[]{:S(2)}, u32[]{:S(2)}) collective-permute-start(bf16[32,3072]{1,0:T(8,128)(2,1)S(1)} %get-tuple-element.51), channel_id=1, source_target_pairs={{0,14},{4,10},{8,6},{12,2},{14,0},{10,4},{6,8},{2,12},{1,15},{5,11... | collective-permute-start | bytes 589832 | tf_op jit(solution)/shard_map/ppermute | solution.py:23
  46.5 0.8 %collective-permute-done.14.refs_2_ = bf16[32,3072]{1,0:T(8,128)(2,1)S(1)} collective-permute-done((bf16[32,3072]{1,0:T(8,128)(2,1)S(1)}, bf16[32,3072]{1,0:T(8,128)(2,1)S(1)}, u32[]{:S(2)}, u32[]{:S(2)}) %collective-permute-start.14) | collective-permute-done | bytes 196640 | tf_op jit(solution)/shard_map/ppermute | solution.py:23
  47.2 0.2 collective-permute-done.15.refs_3_
  47.4 3.3 %collective-permute-done.16.refs_4_ = bf16[32,3072]{1,0:T(8,128)(2,1)S(1)} collective-permute-done((bf16[32,3072]{1,0:T(8,128)(2,1)S(1)}, bf16[32,3072]{1,0:T(8,128)(2,1)S(1)}, u32[]{:S(2)}, u32[]{:S(2)}) %collective-permute-start.16) | collective-permute-done | bytes 196640 | tf_op jit(solution)/shard_map/ppermute | solution.py:23
  50.7 0.0 copy-done.1
  50.8 0.0 copy-done.2
  50.8 0.0 copy-done.3
  50.8 0.0 copy-done.4
  50.8 1.1 %finish.1 = (bf16[16,2,2048]{2,1,0:T(2,128)(2,1)}, bf16[16,2,512]{2,1,0:T(2,128)(2,1)}, bf16[6,16,1024]{2,1,0:T(8,128)(2,1)}) custom-call(bf16[128,2048]{1,0:T(8,128)(2,1)S(1)} %experts.3.refs_0_, bf16[128,1024]{1,0:T(8,128)(2,1)S(1)} %get-tuple-element.45.refs_2_.refs_1_, bf16[32,3072]{1,0:T(8,128)(2,1)S(1)} %collective-permute-done.14.refs_2_, ...), custom_call_target="tpu_custom_call" | custom-call | bytes 2097152 | tf_op jit(solution)/shard_map/finish/pallas_call | solution.py:361
  (3 shorter events, 0.0 us)
Async XLA Ops:
  2.2 14.8 %collective-permute-start.4 = (bf16[2,2048,384]{2,1,0:T(8,128)(2,1)}, bf16[2,2048,384]{2,1,0:T(8,128)(2,1)S(1)}, u32[]{:S(2)}, u32[]{:S(2)}) collective-permute-start(bf16[2,2048,384]{2,1,0:T(8,128)(2,1)} %refs_1_.1), channel_id=1, source_target_pairs={{0,1},{1,0},{2,3},{3,2},{4,5},{5,4},{6,7},{7,6},{8,9},{9,8},{10,11... | collective-permute-start | bytes 9437192 | tf_op jit(solution)/shard_map/ppermute | solution.py:27
  2.8 16.3 %collective-permute-start.7 = (bf16[2,2048,384]{2,1,0:T(8,128)(2,1)}, bf16[2,2048,384]{2,1,0:T(8,128)(2,1)S(1)}, u32[]{:S(2)}, u32[]{:S(2)}) collective-permute-start(bf16[2,2048,384]{2,1,0:T(8,128)(2,1)} %refs_2_.1), channel_id=1, source_target_pairs={{0,1},{1,0},{2,3},{3,2},{4,5},{5,4},{6,7},{7,6},{8,9},{9,8},{10,11... | collective-permute-start | bytes 9437192 | tf_op jit(solution)/shard_map/ppermute | solution.py:27
  2.8 21.4 %collective-permute-start.8 = (bf16[768,2048]{1,0:T(8,128)(2,1)}, bf16[768,2048]{1,0:T(8,128)(2,1)S(1)}, u32[]{:S(2)}, u32[]{:S(2)}) collective-permute-start(bf16[768,2048]{1,0:T(8,128)(2,1)} %bitcast.12), channel_id=1, source_target_pairs={{0,1},{1,0},{2,3},{3,2},{4,5},{5,4},{6,7},{7,6},{8,9},{9,8},{10,11... | collective-permute-start | bytes 9437192 | tf_op jit(solution)/shard_map/ppermute | solution.py:27
  3.3 6.9 %collective-permute-start.1 = (bf16[32,2176]{1,0:T(8,128)(2,1)S(1)}, bf16[32,2176]{1,0:T(8,128)(2,1)S(1)}, u32[]{:S(2)}, u32[]{:S(2)}) collective-permute-start(bf16[32,2176]{1,0:T(8,128)(2,1)S(1)} %pack.1.refs_0_), channel_id=1, source_target_pairs={{0,2},{4,0},{8,4},{12,8},{14,12},{10,14},{6,10},{2,6},{1,3},{5,1},... | collective-permute-start | bytes 417800 | tf_op jit(solution)/shard_map/ppermute | solution.py:23
  5.9 5.7 %collective-permute-start = (bf16[32,2176]{1,0:T(8,128)(2,1)S(1)}, bf16[32,2176]{1,0:T(8,128)(2,1)S(1)}, u32[]{:S(2)}, u32[]{:S(2)}) collective-permute-start(bf16[32,2176]{1,0:T(8,128)(2,1)S(1)} %pack.1.refs_0_), channel_id=1, source_target_pairs={{0,4},{4,8},{8,12},{12,14},{14,10},{10,6},{6,2},{2,0},{1,5},{5,9},... | collective-permute-start | bytes 417800 | tf_op jit(solution)/shard_map/ppermute | solution.py:23
  11.6 19.0 %copy-start = (bf16[16,128,1024]{2,1,0:T(8,128)(2,1)S(1)}, bf16[16,128,1024]{2,1,0:T(8,128)(2,1)}, u32[]{:S(2)}) copy-start(bf16[16,128,1024]{2,1,0:T(8,128)(2,1)} %param.21) | copy-start | bytes 12582916
  11.6 5.1 %collective-permute-start.2 = (bf16[32,2176]{1,0:T(8,128)(2,1)S(1)}, bf16[32,2176]{1,0:T(8,128)(2,1)S(1)}, u32[]{:S(2)}, u32[]{:S(2)}) collective-permute-start(bf16[32,2176]{1,0:T(8,128)(2,1)S(1)} %collective-permute-done.refs_2_), channel_id=1, source_target_pairs={{0,4},{4,8},{8,12},{12,14},{14,10},{10,6},{6,2},{2,0},{1,5},{5,9},... | collective-permute-start | bytes 417800 | tf_op jit(solution)/shard_map/ppermute | solution.py:23
  11.9 5.1 %collective-permute-start.3 = (bf16[32,2176]{1,0:T(8,128)(2,1)S(1)}, bf16[32,2176]{1,0:T(8,128)(2,1)S(1)}, u32[]{:S(2)}, u32[]{:S(2)}) collective-permute-start(bf16[32,2176]{1,0:T(8,128)(2,1)S(1)} %collective-permute-done.1.refs_1_), channel_id=1, source_target_pairs={{0,2},{4,0},{8,4},{12,8},{14,12},{10,14},{6,10},{2,6},{1,3},{5,1},... | collective-permute-start | bytes 417800 | tf_op jit(solution)/shard_map/ppermute | solution.py:23
  17.0 5.1 %collective-permute-start.6 = (bf16[32,2176]{1,0:T(8,128)(2,1)S(1)}, bf16[32,2176]{1,0:T(8,128)(2,1)S(1)}, u32[]{:S(2)}, u32[]{:S(2)}) collective-permute-start(bf16[32,2176]{1,0:T(8,128)(2,1)S(1)} %collective-permute-done.3.refs_0_.refs_4_), channel_id=1, source_target_pairs={{0,2},{4,0},{8,4},{12,8},{14,12},{10,14},{6,10},{2,6},{1,3},{5,1},... | collective-permute-start | bytes 417800 | tf_op jit(solution)/shard_map/ppermute | solution.py:23
  18.7 5.4 %collective-permute-start.5 = (bf16[32,2176]{1,0:T(8,128)(2,1)S(1)}, bf16[32,2176]{1,0:T(8,128)(2,1)S(1)}, u32[]{:S(2)}, u32[]{:S(2)}) collective-permute-start(bf16[32,2176]{1,0:T(8,128)(2,1)S(1)} %collective-permute-done.2.refs_2_.refs_6_), channel_id=1, source_target_pairs={{0,4},{4,8},{8,12},{12,14},{14,10},{10,6},{6,2},{2,0},{1,5},{5,9},... | collective-permute-start | bytes 417800 | tf_op jit(solution)/shard_map/ppermute | solution.py:23
  24.1 6.5 %collective-permute-start.9 = (bf16[32,2176]{1,0:T(8,128)(2,1)S(1)}, bf16[32,2176]{1,0:T(8,128)(2,1)S(1)}, u32[]{:S(2)}, u32[]{:S(2)}) collective-permute-start(bf16[32,2176]{1,0:T(8,128)(2,1)S(1)} %collective-permute-done.5.refs_1_.refs_5_), channel_id=1, source_target_pairs={{0,4},{4,8},{8,12},{12,14},{14,10},{10,6},{6,2},{2,0},{1,5},{5,9},... | collective-permute-start | bytes 417800 | tf_op jit(solution)/shard_map/ppermute | solution.py:23
  27.6 10.6 %collective-permute-start.10 = (bf16[64,2048]{1,0:T(8,128)(2,1)S(1)}, bf16[64,2048]{1,0:T(8,128)(2,1)S(1)}, u32[]{:S(2)}, u32[]{:S(2)}) collective-permute-start(bf16[64,2048]{1,0:T(8,128)(2,1)S(1)} %get-tuple-element.41), channel_id=1, source_target_pairs={{0,4},{4,8},{8,12},{12,14},{14,10},{10,6},{6,2},{2,0},{1,5},{5,9},... | collective-permute-start | bytes 786440 | tf_op jit(solution)/shard_map/ppermute | solution.py:23
  29.6 8.6 %collective-permute-start.12 = (bf16[64,2048]{1,0:T(8,128)(2,1)S(1)}, bf16[64,2048]{1,0:T(8,128)(2,1)S(1)}, u32[]{:S(2)}, u32[]{:S(2)}) collective-permute-start(bf16[64,2048]{1,0:T(8,128)(2,1)S(1)} %get-tuple-element.42), channel_id=1, source_target_pairs={{0,2},{4,0},{8,4},{12,8},{14,12},{10,14},{6,10},{2,6},{1,3},{5,1},... | collective-permute-start | bytes 786440 | tf_op jit(solution)/shard_map/ppermute | solution.py:23
  32.7 5.8 %collective-permute-start.11 = (bf16[64,1024]{1,0:T(8,128)(2,1)S(1)}, bf16[64,1024]{1,0:T(8,128)(2,1)S(1)}, u32[]{:S(2)}, u32[]{:S(2)}) collective-permute-start(bf16[64,1024]{1,0:T(8,128)(2,1)S(1)} %get-tuple-element.47), channel_id=1, source_target_pairs={{0,4},{4,8},{8,12},{12,14},{14,10},{10,6},{6,2},{2,0},{1,5},{5,9},... | collective-permute-start | bytes 393224 | tf_op jit(solution)/shard_map/ppermute | solution.py:23
  33.9 16.9 %copy-start.1 = (bf16[1024,512]{1,0:T(8,128)(2,1)S(1)}, bf16[1024,512]{1,0:T(8,128)(2,1)}, u32[]{:S(2)}) copy-start(bf16[1024,512]{1,0:T(8,128)(2,1)} %refs_8_.1) | copy-start | bytes 3145732
  33.9 16.9 %copy-start.2 = (bf16[16,6,1024]{2,0,1:T(8,128)(2,1)S(1)}, bf16[16,6,1024]{2,0,1:T(8,128)(2,1)}, u32[]{:S(2)}) copy-start(bf16[16,6,1024]{2,0,1:T(8,128)(2,1)} %param.22) | copy-start | bytes 589828
  33.9 16.9 %copy-start.3 = (f32[7,1024]{1,0:T(8,128)S(1)}, f32[7,1024]{1,0:T(8,128)}, u32[]{:S(2)}) copy-start(f32[7,1024]{1,0:T(8,128)} %refs_6_.1) | copy-start | bytes 86020
  33.9 16.9 %copy-start.4 = (f32[1024]{0:T(1024)S(1)}, f32[1024]{0:T(1024)}, u32[]{:S(2)}) copy-start(f32[1024]{0:T(1024)} %param.24) | copy-start | bytes 12292
  33.9 6.0 %collective-permute-start.13 = (bf16[64,1024]{1,0:T(8,128)(2,1)S(1)}, bf16[64,1024]{1,0:T(8,128)(2,1)S(1)}, u32[]{:S(2)}, u32[]{:S(2)}) collective-permute-start(bf16[64,1024]{1,0:T(8,128)(2,1)S(1)} %get-tuple-element.48), channel_id=1, source_target_pairs={{0,2},{4,0},{8,4},{12,8},{14,12},{10,14},{6,10},{2,6},{1,3},{5,1},... | collective-permute-start | bytes 393224 | tf_op jit(solution)/shard_map/ppermute | solution.py:23
  40.0 7.2 %collective-permute-start.14 = (bf16[32,3072]{1,0:T(8,128)(2,1)S(1)}, bf16[32,3072]{1,0:T(8,128)(2,1)S(1)}, u32[]{:S(2)}, u32[]{:S(2)}) collective-permute-start(bf16[32,3072]{1,0:T(8,128)(2,1)S(1)} %get-tuple-element.49), channel_id=1, source_target_pairs={{0,4},{4,8},{8,12},{12,14},{14,10},{10,6},{6,2},{2,0},{1,5},{5,9},... | collective-permute-start | bytes 589832 | tf_op jit(solution)/shard_map/ppermute | solution.py:23
  41.8 5.7 %collective-permute-start.15 = (bf16[32,3072]{1,0:T(8,128)(2,1)S(1)}, bf16[32,3072]{1,0:T(8,128)(2,1)S(1)}, u32[]{:S(2)}, u32[]{:S(2)}) collective-permute-start(bf16[32,3072]{1,0:T(8,128)(2,1)S(1)} %get-tuple-element.50), channel_id=1, source_target_pairs={{0,2},{4,0},{8,4},{12,8},{14,12},{10,14},{6,10},{2,6},{1,3},{5,1},... | collective-permute-start | bytes 589832 | tf_op jit(solution)/shard_map/ppermute | solution.py:23
  42.1 8.6 %collective-permute-start.16 = (bf16[32,3072]{1,0:T(8,128)(2,1)S(1)}, bf16[32,3072]{1,0:T(8,128)(2,1)S(1)}, u32[]{:S(2)}, u32[]{:S(2)}) collective-permute-start(bf16[32,3072]{1,0:T(8,128)(2,1)S(1)} %get-tuple-element.51), channel_id=1, source_target_pairs={{0,14},{4,10},{8,6},{12,2},{14,0},{10,4},{6,8},{2,12},{1,15},{5,11... | collective-permute-start | bytes 589832 | tf_op jit(solution)/shard_map/ppermute | solution.py:23

commit v6 on v5

--- a/solution.py
+++ b/solution.py
@@ -214,8 +214,9 @@
             mine = place_ref[0] * local + j
             hit = (lane == mine) | (lane == expert_count + mine)
             weight = jnp.sum(jnp.where(hit, meta, 0.0), axis=1, keepdims=True)
-            gate = jnp.dot(rows_ref[...], gate_ref[j], preferred_element_type=F32)
-            up = jnp.dot(rows_ref[...], up_ref[j], preferred_element_type=F32)
+            both = jnp.concatenate([gate_ref[j], up_ref[j]], axis=1)
+            both = jnp.dot(rows_ref[...], both, preferred_element_type=F32)
+            gate, up = both[:, 0:units], both[:, units:]
             value = gate * jax.nn.sigmoid(gate) * up
             act_ref[:, j * units : (j + 1) * units] = (value * weight).astype(BF16)
         result = jnp.dot(act_ref[...], down_ref[...], preferred_element_type=F32)
@@ -262,37 +263,29 @@
     rows = metas[0].shape[0]
     meta = jnp.concatenate([m[...] for m in metas], axis=0)
     total = meta.shape[0]
-    slot = meta[:, slot_at : slot_at + 2].astype(F32)
-    source = (slot[:, 0:1] + 256.0 * slot[:, 1:2]).astype(jnp.int32)
-    lane = lax.broadcasted_iota(jnp.int32, (1, total), 1)
-    inside = lane % rows
+    column = lax.broadcasted_iota(jnp.int32, (8, meta.shape[1]), 1)
+    digit = lax.broadcasted_iota(jnp.int32, (8, meta.shape[1]), 0)
+    picks = jnp.where((column == slot_at + digit) & (digit < 2), 1.0, 0.0).astype(BF16)
+    slots = lax.dot_general(picks, meta, (((1,), (1,)), ((), ())), preferred_element_type=F32)
+    source = (slots[0:1] + 256.0 * slots[1:2]).astype(jnp.int32)
+    row = lax.broadcasted_iota(jnp.int32, (total, 1), 0)
+    inside = row % rows
     target = (inside % sessions) * steps + inside // sessions
     place = place_ref[0]
     turn = jnp.where(place % 2 == 0, place // 2, count - 1 - place // 2)
     for i, k in enumerate(order):
         at = (turn + k) % count
         device = jnp.where(at < count // 2, 2 * at, 2 * (count - 1 - at) + 1)
-        target = target + jnp.where(lane // rows == i, device * rows, 0)
-    chooser = jnp.where(source == target, 1.0, 0.0).astype(BF16)
-    ordered = lax.dot_general(
-        chooser, meta, (((0,), (0,)), ((), ())), preferred_element_type=F32
-    )
-    low = ordered[:, code_at : code_at + books]
-    high = ordered[:, code_at + books : code_at + 2 * books]
-    codes = (low + 256.0 * high).astype(jnp.int32) - place * shard
-    chunk = 128
-    lanes = lax.broadcasted_iota(jnp.int32, (total, chunk), 1)
-    for start in range(0, books * shard, chunk):
-        first, last = start // shard, (start + chunk - 1) // shard
-        code = codes[:, first : first + 1] + (first * shard - start)
-        for q in range(first + 1, last + 1):
-            shifted = codes[:, q : q + 1] + (q * shard - start)
-            code = jnp.where(lanes >= q * shard - start, shifted, code)
-        hit = lanes == code
-        if shard < chunk:
-            low_end = lanes // shard * shard
-            hit = hit & (code >= low_end) & (code < low_end + shard)
-        hot_ref[:, start : start + chunk] = jnp.where(hit, 1.0, 0.0).astype(BF16)
+        target = target + jnp.where(row // rows == i, device * rows, 0)
+    chooser = jnp.where(target == source, 1.0, 0.0).astype(BF16)
+    ordered = jnp.dot(chooser, meta, preferred_element_type=F32).astype(BF16)
+    lanes = books * shard
+    column = lax.broadcasted_iota(jnp.int32, (meta.shape[1], lanes), 0) - code_at
+    book = lax.broadcasted_iota(jnp.int32, (meta.shape[1], lanes), 1) // shard
+    spread = jnp.where(column == book, 1.0, jnp.where(column == book + books, 256.0, 0.0))
+    codes = jnp.dot(ordered, spread.astype(BF16), preferred_element_type=F32)
+    entry = lax.broadcasted_iota(jnp.int32, (1, lanes), 1) % shard + place * shard
+    hot_ref[...] = jnp.where(codes == entry.astype(F32), 1.0, 0.0).astype(BF16)
     result = jnp.dot(hot_ref[...], table_ref[...], preferred_element_type=F32)
     start = 0
     for out_ref in outs:
@@ -425,7 +418,7 @@
             ahead = shift(ahead, -1)
             got[step] = ahead
         first = held[0] if step == 1 else sibling[step - 2 : step - 1]
-        got = dict(zip(got, after(got.values(), first)))
+        got = {k: after((v,), first)[0] for k, v in got.items()}
         behind, ahead = got[count - step], got.get(step)
         blocks.update(got)
 

time: 52 us -> 50 us (0.962); the launches traced: 51.9 us -> 49.1 us
  waiting for transfers between devices: 17.1 us -> 15.3 us
  Pallas kernels: 15.5 us -> 14 us
    ppermute x14, waiting for transfers between devices: 17.1 us -> 15.3 us  [shift(): return lax.ppermute(value, 'expert', pairs)]
    pallas_call x2, Pallas kernels: 6.69 us -> 5.58 us  [experts(): pl.pallas_call(functools.partial(experts_kernel, width, lax.axis_size('ex...]
    ppermute x14, starting transfers between devices: 17.5 us -> 18.1 us  [shift(): return lax.ppermute(value, 'expert', pairs)]
  transfers between devices with their start and end apart: 17 -> 17, of which waited for: 12 -> 10; matrix products, arithmetic and copies ran while one was open for 0% -> 0% of each run, Pallas kernels for 24% -> 23%
where the time goes in v6:
time: 50 us; the launch traced here: 49.1 us
  starting transfers between devices  19.1 us (38%)
  waiting for transfers between devices  15.3 us (31%)
  Pallas kernels  14 us (28%)
  between operations  0.73 us (1%)
    ppermute x14, starting transfers between devices, shift(): return lax.ppermute(value, 'expert', pairs)  18.1 us
    ppermute x14, waiting for transfers between devices, shift(): return lax.ppermute(value, 'expert', pairs)  15.3 us
    pallas_call x2, Pallas kernels, experts(): pl.pallas_call(functools.partial(experts_kernel, width, lax.axis_size('ex...  5.58 us
    pallas_call x1, Pallas kernels, load(): pl.pallas_call(load_kernel, out_shape=[pltpu.VMEM(v.shape, v.dtype) for v...  3.78 us
    pallas_call x1, Pallas kernels, frame_sums(): pl.pallas_call(functools.partial(frames_kernel, columns, books, shard, se...  1.8 us
    pallas_call x1, Pallas kernels, pack(): pl.pallas_call(functools.partial(pack_kernel, columns, n_wave), out_shape...  1.59 us
    pallas_call x1, Pallas kernels, finish(): pl.pallas_call(functools.partial(finish_kernel, *numbered[0][0], width),...  1.08 us
    ppermute x3, starting transfers between devices, swap_wave(): return lax.ppermute(value, 'wave', [(0, 1), (1, 0)])  1.03 us
  transfers between devices with their start and end apart: 17, of which 10 were waited for; matrix products, arithmetic and copies ran while one was open for 0% of the time, Pallas kernels for 23%

profile of v6, /device:TPU:0, one launch (start us, length us, event | category | flops | bytes accessed | tf_op | source)
XLA Modules:
  0.0 49.1 jit_solution(15535803194160926381)
XLA Ops:
  0.6 1.6 %pack.1.refs_0_ = bf16[32,2176]{1,0:T(8,128)(2,1)S(1)} custom-call(s32[1]{0:T(128)} %bitcast._.place_ref, bf16[16,2,2048]{2,1,0:T(2,128)(2,1)} %refs_0_.1, s32[2,8,16]{2,1,0:T(8,128)} %bitcast.14, f32[2,8,16]{2,1,0:T(8,128)} %bitcast.15, s32[16,2,16]{2,1,0:T(2,128)} %refs_3_.1, s32[1,16]{1,0:T(1,128)} %bitcast.16), custom_call_target="tpu_custom_call" | custom-call | tf_op jit(solution)/shard_map/pack/pallas_call | solution.py:159
  2.2 0.5 %collective-permute-start.2 = (bf16[2,2048,384]{2,1,0:T(8,128)(2,1)}, bf16[2,2048,384]{2,1,0:T(8,128)(2,1)S(1)}, u32[]{:S(2)}, u32[]{:S(2)}) collective-permute-start(bf16[2,2048,384]{2,1,0:T(8,128)(2,1)} %refs_1_.1), channel_id=1, source_target_pairs={{0,1},{1,0},{2,3},{3,2},{4,5},{5,4},{6,7},{7,6},{8,9},{9,8},{10,11... | collective-permute-start | bytes 9437192 | tf_op jit(solution)/shard_map/ppermute | solution.py:27
  2.8 0.1 collective-permute-start.6
  2.8 0.4 collective-permute-start.8
  3.3 2.6 %collective-permute-start = (bf16[32,2176]{1,0:T(8,128)(2,1)S(1)}, bf16[32,2176]{1,0:T(8,128)(2,1)S(1)}, u32[]{:S(2)}, u32[]{:S(2)}) collective-permute-start(bf16[32,2176]{1,0:T(8,128)(2,1)S(1)} %pack.1.refs_0_), channel_id=1, source_target_pairs={{0,2},{4,0},{8,4},{12,8},{14,12},{10,14},{6,10},{2,6},{1,3},{5,1},... | collective-permute-start | bytes 417800 | tf_op jit(solution)/shard_map/ppermute | solution.py:23
  5.9 0.1 collective-permute-start.3
  5.9 3.8 %load.1 = (bf16[2,2048,384]{2,1,0:T(8,128)(2,1)S(1)}, bf16[2,2048,384]{2,1,0:T(8,128)(2,1)S(1)}, bf16[768,2048]{1,0:T(8,128)(2,1)S(1)}) custom-call(bf16[32,2176]{1,0:T(8,128)(2,1)S(1)} %pack.1.refs_0_, bf16[2,2048,384]{2,1,0:T(8,128)(2,1)} %refs_1_.1, bf16[2,2048,384]{2,1,0:T(8,128)(2,1)} %refs_2_.1, bf16[768,2048]{1,0:T(8,128)(2,1)} %bitcast.13), custom_call_target="tpu_custom_call" | custom-call | bytes 9437184 | tf_op jit(solution)/shard_map/load/pallas_call | solution.py:187
  9.7 0.5 collective-permute-done.refs_1_
  10.2 0.0 copy-start
  10.2 1.7 %collective-permute-start.1 = (bf16[32,2176]{1,0:T(8,128)(2,1)S(1)}, bf16[32,2176]{1,0:T(8,128)(2,1)S(1)}, u32[]{:S(2)}, u32[]{:S(2)}) collective-permute-start(bf16[32,2176]{1,0:T(8,128)(2,1)S(1)} %collective-permute-done.refs_1_), channel_id=1, source_target_pairs={{0,2},{4,0},{8,4},{12,8},{14,12},{10,14},{6,10},{2,6},{1,3},{5,1},... | collective-permute-start | bytes 417800 | tf_op jit(solution)/shard_map/ppermute | solution.py:23
  11.9 0.0 collective-permute-done.3.refs_2_
  11.9 0.3 collective-permute-start.4
  12.2 3.4 %collective-permute-done.1.refs_0_.refs_4_ = bf16[32,2176]{1,0:T(8,128)(2,1)S(1)} collective-permute-done((bf16[32,2176]{1,0:T(8,128)(2,1)S(1)}, bf16[32,2176]{1,0:T(8,128)(2,1)S(1)}, u32[]{:S(2)}, u32[]{:S(2)}) %collective-permute-start.1) | collective-permute-done | bytes 139296 | tf_op jit(solution)/shard_map/ppermute | solution.py:23
  15.6 0.0 collective-permute-done.2.refs_7_
  15.6 1.6 %collective-permute-start.7 = (bf16[32,2176]{1,0:T(8,128)(2,1)S(1)}, bf16[32,2176]{1,0:T(8,128)(2,1)S(1)}, u32[]{:S(2)}, u32[]{:S(2)}) collective-permute-start(bf16[32,2176]{1,0:T(8,128)(2,1)S(1)} %collective-permute-done.1.refs_0_.refs_4_), channel_id=1, source_target_pairs={{0,2},{4,0},{8,4},{12,8},{14,12},{10,14},{6,10},{2,6},{1,3},{5,1},... | collective-permute-start | bytes 417800 | tf_op jit(solution)/shard_map/ppermute | solution.py:23
  17.2 0.0 collective-permute-done.4.refs_2_.refs_6_
  17.2 0.4 collective-permute-start.5
  17.6 0.0 collective-permute-done.6.refs_8_
  17.7 3.0 %collective-permute-done.7.refs_3_.refs_7_ = bf16[32,2176]{1,0:T(8,128)(2,1)S(1)} collective-permute-done((bf16[32,2176]{1,0:T(8,128)(2,1)S(1)}, bf16[32,2176]{1,0:T(8,128)(2,1)S(1)}, u32[]{:S(2)}, u32[]{:S(2)}) %collective-permute-start.7) | collective-permute-done | bytes 139296 | tf_op jit(solution)/shard_map/ppermute | solution.py:23
  20.7 1.6 %collective-permute-done.5.refs_1_.refs_5_ = bf16[32,2176]{1,0:T(8,128)(2,1)S(1)} collective-permute-done((bf16[32,2176]{1,0:T(8,128)(2,1)S(1)}, bf16[32,2176]{1,0:T(8,128)(2,1)S(1)}, u32[]{:S(2)}, u32[]{:S(2)}) %collective-permute-start.5) | collective-permute-done | bytes 139296 | tf_op jit(solution)/shard_map/ppermute | solution.py:23
  22.3 0.4 collective-permute-start.9
  22.7 0.0 collective-permute-done.8.refs_9_
  22.7 2.8 %experts.2 = (bf16[64,2048]{1,0:T(8,128)(2,1)S(1)}, bf16[64,2048]{1,0:T(8,128)(2,1)S(1)}) custom-call(s32[1]{0:T(128)} %bitcast._.place_ref, bf16[32,2176]{1,0:T(8,128)(2,1)S(1)} %collective-permute-done.1.refs_0_.refs_4_, bf16[32,2176]{1,0:T(8,128)(2,1)S(1)} %collective-permute-done.5.refs_1_.refs_5_, ...), custom_call_target="tpu_custom_call" | custom-call | flops 2415919104 | bytes 18874368 | tf_op jit(solution)/shard_map/experts/pallas_call | solution.py:237
  25.5 1.7 %collective-permute-start.10 = (bf16[64,2048]{1,0:T(8,128)(2,1)S(1)}, bf16[64,2048]{1,0:T(8,128)(2,1)S(1)}, u32[]{:S(2)}, u32[]{:S(2)}) collective-permute-start(bf16[64,2048]{1,0:T(8,128)(2,1)S(1)} %get-tuple-element.41), channel_id=1, source_target_pairs={{0,4},{4,8},{8,12},{12,14},{14,10},{10,6},{6,2},{2,0},{1,5},{5,9},... | collective-permute-start | bytes 786440 | tf_op jit(solution)/shard_map/ppermute | solution.py:23
  27.2 0.4 collective-permute-start.12
  27.6 1.1 %collective-permute-done.9.refs_3_ = bf16[32,2176]{1,0:T(8,128)(2,1)S(1)} collective-permute-done((bf16[32,2176]{1,0:T(8,128)(2,1)S(1)}, bf16[32,2176]{1,0:T(8,128)(2,1)S(1)}, u32[]{:S(2)}, u32[]{:S(2)}) %collective-permute-start.9) | collective-permute-done | bytes 139296 | tf_op jit(solution)/shard_map/ppermute | solution.py:23
  28.7 0.0 copy-done
  28.7 1.8 %frame_sums.1 = (bf16[128,1024]{1,0:T(8,128)(2,1)S(1)}, bf16[64,1024]{1,0:T(8,128)(2,1)S(1)}, bf16[64,1024]{1,0:T(8,128)(2,1)S(1)}) custom-call(s32[1]{0:T(128)} %bitcast._.place_ref, bf16[32,2176]{1,0:T(8,128)(2,1)S(1)} %pack.1.refs_0_, bf16[32,2176]{1,0:T(8,128)(2,1)S(1)} %collective-permute-done.refs_1_, ...), custom_call_target="tpu_custom_call" | custom-call | flops 1073741824 | bytes 4194304 | tf_op jit(solution)/shard_map/frame_sums/pallas_call | solution.py:303
  30.5 0.6 %collective-permute-start.11 = (bf16[64,1024]{1,0:T(8,128)(2,1)S(1)}, bf16[64,1024]{1,0:T(8,128)(2,1)S(1)}, u32[]{:S(2)}, u32[]{:S(2)}) collective-permute-start(bf16[64,1024]{1,0:T(8,128)(2,1)S(1)} %get-tuple-element.47), channel_id=1, source_target_pairs={{0,4},{4,8},{8,12},{12,14},{14,10},{10,6},{6,2},{2,0},{1,5},{5,9},... | collective-permute-start | bytes 393224 | tf_op jit(solution)/shard_map/ppermute | solution.py:23
  31.1 0.0 copy-start.1
  31.1 1.6 %collective-permute-start.13 = (bf16[64,1024]{1,0:T(8,128)(2,1)S(1)}, bf16[64,1024]{1,0:T(8,128)(2,1)S(1)}, u32[]{:S(2)}, u32[]{:S(2)}) collective-permute-start(bf16[64,1024]{1,0:T(8,128)(2,1)S(1)} %get-tuple-element.48), channel_id=1, source_target_pairs={{0,2},{4,0},{8,4},{12,8},{14,12},{10,14},{6,10},{2,6},{1,3},{5,1},... | collective-permute-start | bytes 393224 | tf_op jit(solution)/shard_map/ppermute | solution.py:23
  32.7 2.8 %experts.3.refs_0_ = bf16[128,2048]{1,0:T(8,128)(2,1)S(1)} custom-call(s32[1]{0:T(128)} %bitcast._.place_ref, bf16[32,2176]{1,0:T(8,128)(2,1)S(1)} %pack.1.refs_0_, bf16[32,2176]{1,0:T(8,128)(2,1)S(1)} %collective-permute-done.refs_1_, bf16[32,2176]{1,0:T(8,128)(2,1)S(1)} %collective-permute-done.3.refs_2_, ...), custom_call_target="tpu_custom_call" | custom-call | flops 2415919104 | bytes 18874368 | tf_op jit(solution)/shard_map/experts/pallas_call | solution.py:237
  35.5 0.0 collective-permute-done.10.refs_1_
  35.5 0.0 collective-permute-done.12.refs_4_
  35.5 0.1 collective-permute-done.11.refs_3_
  35.6 0.6 %collective-permute-done.13.refs_5_ = bf16[64,1024]{1,0:T(8,128)(2,1)S(1)} collective-permute-done((bf16[64,1024]{1,0:T(8,128)(2,1)S(1)}, bf16[64,1024]{1,0:T(8,128)(2,1)S(1)}, u32[]{:S(2)}, u32[]{:S(2)}) %collective-permute-start.13) | collective-permute-done | bytes 131104 | tf_op jit(solution)/shard_map/ppermute | solution.py:23
  36.1 0.2 join.1
  36.3 1.6 %collective-permute-start.14 = (bf16[32,3072]{1,0:T(8,128)(2,1)S(1)}, bf16[32,3072]{1,0:T(8,128)(2,1)S(1)}, u32[]{:S(2)}, u32[]{:S(2)}) collective-permute-start(bf16[32,3072]{1,0:T(8,128)(2,1)S(1)} %get-tuple-element.49), channel_id=1, source_target_pairs={{0,4},{4,8},{8,12},{12,14},{14,10},{10,6},{6,2},{2,0},{1,5},{5,9},... | collective-permute-start | bytes 589832 | tf_op jit(solution)/shard_map/ppermute | solution.py:23
  37.9 0.4 collective-permute-start.15
  38.4 4.6 %collective-permute-start.16 = (bf16[32,3072]{1,0:T(8,128)(2,1)S(1)}, bf16[32,3072]{1,0:T(8,128)(2,1)S(1)}, u32[]{:S(2)}, u32[]{:S(2)}) collective-permute-start(bf16[32,3072]{1,0:T(8,128)(2,1)S(1)} %get-tuple-element.51), channel_id=1, source_target_pairs={{0,14},{4,10},{8,6},{12,2},{14,0},{10,4},{6,8},{2,12},{1,15},{5,11... | collective-permute-start | bytes 589832 | tf_op jit(solution)/shard_map/ppermute | solution.py:23
  43.0 0.9 %collective-permute-done.14.refs_2_ = bf16[32,3072]{1,0:T(8,128)(2,1)S(1)} collective-permute-done((bf16[32,3072]{1,0:T(8,128)(2,1)S(1)}, bf16[32,3072]{1,0:T(8,128)(2,1)S(1)}, u32[]{:S(2)}, u32[]{:S(2)}) %collective-permute-start.14) | collective-permute-done | bytes 196640 | tf_op jit(solution)/shard_map/ppermute | solution.py:23
  43.9 1.5 %collective-permute-done.15.refs_3_ = bf16[32,3072]{1,0:T(8,128)(2,1)S(1)} collective-permute-done((bf16[32,3072]{1,0:T(8,128)(2,1)S(1)}, bf16[32,3072]{1,0:T(8,128)(2,1)S(1)}, u32[]{:S(2)}, u32[]{:S(2)}) %collective-permute-start.15) | collective-permute-done | bytes 196640 | tf_op jit(solution)/shard_map/ppermute | solution.py:23
  45.5 2.5 %collective-permute-done.16.refs_4_ = bf16[32,3072]{1,0:T(8,128)(2,1)S(1)} collective-permute-done((bf16[32,3072]{1,0:T(8,128)(2,1)S(1)}, bf16[32,3072]{1,0:T(8,128)(2,1)S(1)}, u32[]{:S(2)}, u32[]{:S(2)}) %collective-permute-start.16) | collective-permute-done | bytes 196640 | tf_op jit(solution)/shard_map/ppermute | solution.py:23
  48.0 0.0 copy-done.1
  48.0 0.0 copy-done.2
  48.0 0.0 copy-done.3
  48.0 0.0 copy-done.4
  48.0 1.1 %finish.1 = (bf16[16,2,2048]{2,1,0:T(2,128)(2,1)}, bf16[16,2,512]{2,1,0:T(2,128)(2,1)}, bf16[6,16,1024]{2,1,0:T(8,128)(2,1)}) custom-call(bf16[128,2048]{1,0:T(8,128)(2,1)S(1)} %experts.3.refs_0_, bf16[128,1024]{1,0:T(8,128)(2,1)S(1)} %get-tuple-element.45.refs_2_.refs_1_, bf16[32,3072]{1,0:T(8,128)(2,1)S(1)} %collective-permute-done.14.refs_2_, ...), custom_call_target="tpu_custom_call" | custom-call | bytes 2097152 | tf_op jit(solution)/shard_map/finish/pallas_call | solution.py:354
  (3 shorter events, 0.0 us)
Async XLA Ops:
  2.2 13.4 %collective-permute-start.2 = (bf16[2,2048,384]{2,1,0:T(8,128)(2,1)}, bf16[2,2048,384]{2,1,0:T(8,128)(2,1)S(1)}, u32[]{:S(2)}, u32[]{:S(2)}) collective-permute-start(bf16[2,2048,384]{2,1,0:T(8,128)(2,1)} %refs_1_.1), channel_id=1, source_target_pairs={{0,1},{1,0},{2,3},{3,2},{4,5},{5,4},{6,7},{7,6},{8,9},{9,8},{10,11... | collective-permute-start | bytes 9437192 | tf_op jit(solution)/shard_map/ppermute | solution.py:27
  2.8 14.9 %collective-permute-start.6 = (bf16[2,2048,384]{2,1,0:T(8,128)(2,1)}, bf16[2,2048,384]{2,1,0:T(8,128)(2,1)S(1)}, u32[]{:S(2)}, u32[]{:S(2)}) collective-permute-start(bf16[2,2048,384]{2,1,0:T(8,128)(2,1)} %refs_2_.1), channel_id=1, source_target_pairs={{0,1},{1,0},{2,3},{3,2},{4,5},{5,4},{6,7},{7,6},{8,9},{9,8},{10,11... | collective-permute-start | bytes 9437192 | tf_op jit(solution)/shard_map/ppermute | solution.py:27
  2.8 19.9 %collective-permute-start.8 = (bf16[768,2048]{1,0:T(8,128)(2,1)}, bf16[768,2048]{1,0:T(8,128)(2,1)S(1)}, u32[]{:S(2)}, u32[]{:S(2)}) collective-permute-start(bf16[768,2048]{1,0:T(8,128)(2,1)} %bitcast.12), channel_id=1, source_target_pairs={{0,1},{1,0},{2,3},{3,2},{4,5},{5,4},{6,7},{7,6},{8,9},{9,8},{10,11... | collective-permute-start | bytes 9437192 | tf_op jit(solution)/shard_map/ppermute | solution.py:27
  3.3 6.9 %collective-permute-start = (bf16[32,2176]{1,0:T(8,128)(2,1)S(1)}, bf16[32,2176]{1,0:T(8,128)(2,1)S(1)}, u32[]{:S(2)}, u32[]{:S(2)}) collective-permute-start(bf16[32,2176]{1,0:T(8,128)(2,1)S(1)} %pack.1.refs_0_), channel_id=1, source_target_pairs={{0,2},{4,0},{8,4},{12,8},{14,12},{10,14},{6,10},{2,6},{1,3},{5,1},... | collective-permute-start | bytes 417800 | tf_op jit(solution)/shard_map/ppermute | solution.py:23
  5.9 6.0 %collective-permute-start.3 = (bf16[32,2176]{1,0:T(8,128)(2,1)S(1)}, bf16[32,2176]{1,0:T(8,128)(2,1)S(1)}, u32[]{:S(2)}, u32[]{:S(2)}) collective-permute-start(bf16[32,2176]{1,0:T(8,128)(2,1)S(1)} %pack.1.refs_0_), channel_id=1, source_target_pairs={{0,4},{4,8},{8,12},{12,14},{14,10},{10,6},{6,2},{2,0},{1,5},{5,9},... | collective-permute-start | bytes 417800 | tf_op jit(solution)/shard_map/ppermute | solution.py:23
  10.2 18.6 %copy-start = (bf16[16,128,1024]{2,1,0:T(8,128)(2,1)S(1)}, bf16[16,128,1024]{2,1,0:T(8,128)(2,1)}, u32[]{:S(2)}) copy-start(bf16[16,128,1024]{2,1,0:T(8,128)(2,1)} %param.21) | copy-start | bytes 12582916
  10.2 5.4 %collective-permute-start.1 = (bf16[32,2176]{1,0:T(8,128)(2,1)S(1)}, bf16[32,2176]{1,0:T(8,128)(2,1)S(1)}, u32[]{:S(2)}, u32[]{:S(2)}) collective-permute-start(bf16[32,2176]{1,0:T(8,128)(2,1)S(1)} %collective-permute-done.refs_1_), channel_id=1, source_target_pairs={{0,2},{4,0},{8,4},{12,8},{14,12},{10,14},{6,10},{2,6},{1,3},{5,1},... | collective-permute-start | bytes 417800 | tf_op jit(solution)/shard_map/ppermute | solution.py:23
  11.9 5.3 %collective-permute-start.4 = (bf16[32,2176]{1,0:T(8,128)(2,1)S(1)}, bf16[32,2176]{1,0:T(8,128)(2,1)S(1)}, u32[]{:S(2)}, u32[]{:S(2)}) collective-permute-start(bf16[32,2176]{1,0:T(8,128)(2,1)S(1)} %collective-permute-done.3.refs_2_), channel_id=1, source_target_pairs={{0,4},{4,8},{8,12},{12,14},{14,10},{10,6},{6,2},{2,0},{1,5},{5,9},... | collective-permute-start | bytes 417800 | tf_op jit(solution)/shard_map/ppermute | solution.py:23
  15.6 5.1 %collective-permute-start.7 = (bf16[32,2176]{1,0:T(8,128)(2,1)S(1)}, bf16[32,2176]{1,0:T(8,128)(2,1)S(1)}, u32[]{:S(2)}, u32[]{:S(2)}) collective-permute-start(bf16[32,2176]{1,0:T(8,128)(2,1)S(1)} %collective-permute-done.1.refs_0_.refs_4_), channel_id=1, source_target_pairs={{0,2},{4,0},{8,4},{12,8},{14,12},{10,14},{6,10},{2,6},{1,3},{5,1},... | collective-permute-start | bytes 417800 | tf_op jit(solution)/shard_map/ppermute | solution.py:23
  17.2 5.1 %collective-permute-start.5 = (bf16[32,2176]{1,0:T(8,128)(2,1)S(1)}, bf16[32,2176]{1,0:T(8,128)(2,1)S(1)}, u32[]{:S(2)}, u32[]{:S(2)}) collective-permute-start(bf16[32,2176]{1,0:T(8,128)(2,1)S(1)} %collective-permute-done.4.refs_2_.refs_6_), channel_id=1, source_target_pairs={{0,4},{4,8},{8,12},{12,14},{14,10},{10,6},{6,2},{2,0},{1,5},{5,9},... | collective-permute-start | bytes 417800 | tf_op jit(solution)/shard_map/ppermute | solution.py:23
  22.3 6.5 %collective-permute-start.9 = (bf16[32,2176]{1,0:T(8,128)(2,1)S(1)}, bf16[32,2176]{1,0:T(8,128)(2,1)S(1)}, u32[]{:S(2)}, u32[]{:S(2)}) collective-permute-start(bf16[32,2176]{1,0:T(8,128)(2,1)S(1)} %collective-permute-done.5.refs_1_.refs_5_), channel_id=1, source_target_pairs={{0,4},{4,8},{8,12},{12,14},{14,10},{10,6},{6,2},{2,0},{1,5},{5,9},... | collective-permute-start | bytes 417800 | tf_op jit(solution)/shard_map/ppermute | solution.py:23
  25.5 10.0 %collective-permute-start.10 = (bf16[64,2048]{1,0:T(8,128)(2,1)S(1)}, bf16[64,2048]{1,0:T(8,128)(2,1)S(1)}, u32[]{:S(2)}, u32[]{:S(2)}) collective-permute-start(bf16[64,2048]{1,0:T(8,128)(2,1)S(1)} %get-tuple-element.41), channel_id=1, source_target_pairs={{0,4},{4,8},{8,12},{12,14},{14,10},{10,6},{6,2},{2,0},{1,5},{5,9},... | collective-permute-start | bytes 786440 | tf_op jit(solution)/shard_map/ppermute | solution.py:23
  27.2 8.3 %collective-permute-start.12 = (bf16[64,2048]{1,0:T(8,128)(2,1)S(1)}, bf16[64,2048]{1,0:T(8,128)(2,1)S(1)}, u32[]{:S(2)}, u32[]{:S(2)}) collective-permute-start(bf16[64,2048]{1,0:T(8,128)(2,1)S(1)} %get-tuple-element.42), channel_id=1, source_target_pairs={{0,2},{4,0},{8,4},{12,8},{14,12},{10,14},{6,10},{2,6},{1,3},{5,1},... | collective-permute-start | bytes 786440 | tf_op jit(solution)/shard_map/ppermute | solution.py:23
  30.5 5.0 %collective-permute-start.11 = (bf16[64,1024]{1,0:T(8,128)(2,1)S(1)}, bf16[64,1024]{1,0:T(8,128)(2,1)S(1)}, u32[]{:S(2)}, u32[]{:S(2)}) collective-permute-start(bf16[64,1024]{1,0:T(8,128)(2,1)S(1)} %get-tuple-element.47), channel_id=1, source_target_pairs={{0,4},{4,8},{8,12},{12,14},{14,10},{10,6},{6,2},{2,0},{1,5},{5,9},... | collective-permute-start | bytes 393224 | tf_op jit(solution)/shard_map/ppermute | solution.py:23
  31.1 16.9 %copy-start.1 = (bf16[1024,512]{1,0:T(8,128)(2,1)S(1)}, bf16[1024,512]{1,0:T(8,128)(2,1)}, u32[]{:S(2)}) copy-start(bf16[1024,512]{1,0:T(8,128)(2,1)} %refs_8_.1) | copy-start | bytes 3145732
  31.1 16.9 %copy-start.2 = (bf16[16,6,1024]{2,0,1:T(8,128)(2,1)S(1)}, bf16[16,6,1024]{2,0,1:T(8,128)(2,1)}, u32[]{:S(2)}) copy-start(bf16[16,6,1024]{2,0,1:T(8,128)(2,1)} %param.22) | copy-start | bytes 589828
  31.1 16.9 %copy-start.3 = (f32[7,1024]{1,0:T(8,128)S(1)}, f32[7,1024]{1,0:T(8,128)}, u32[]{:S(2)}) copy-start(f32[7,1024]{1,0:T(8,128)} %refs_6_.1) | copy-start | bytes 86020
  31.1 16.9 %copy-start.4 = (f32[1024]{0:T(1024)S(1)}, f32[1024]{0:T(1024)}, u32[]{:S(2)}) copy-start(f32[1024]{0:T(1024)} %param.24) | copy-start | bytes 12292
  31.1 5.0 %collective-permute-start.13 = (bf16[64,1024]{1,0:T(8,128)(2,1)S(1)}, bf16[64,1024]{1,0:T(8,128)(2,1)S(1)}, u32[]{:S(2)}, u32[]{:S(2)}) collective-permute-start(bf16[64,1024]{1,0:T(8,128)(2,1)S(1)} %get-tuple-element.48), channel_id=1, source_target_pairs={{0,2},{4,0},{8,4},{12,8},{14,12},{10,14},{6,10},{2,6},{1,3},{5,1},... | collective-permute-start | bytes 393224 | tf_op jit(solution)/shard_map/ppermute | solution.py:23
  36.3 7.6 %collective-permute-start.14 = (bf16[32,3072]{1,0:T(8,128)(2,1)S(1)}, bf16[32,3072]{1,0:T(8,128)(2,1)S(1)}, u32[]{:S(2)}, u32[]{:S(2)}) collective-permute-start(bf16[32,3072]{1,0:T(8,128)(2,1)S(1)} %get-tuple-element.49), channel_id=1, source_target_pairs={{0,4},{4,8},{8,12},{12,14},{14,10},{10,6},{6,2},{2,0},{1,5},{5,9},... | collective-permute-start | bytes 589832 | tf_op jit(solution)/shard_map/ppermute | solution.py:23
  37.9 7.5 %collective-permute-start.15 = (bf16[32,3072]{1,0:T(8,128)(2,1)S(1)}, bf16[32,3072]{1,0:T(8,128)(2,1)S(1)}, u32[]{:S(2)}, u32[]{:S(2)}) collective-permute-start(bf16[32,3072]{1,0:T(8,128)(2,1)S(1)} %get-tuple-element.50), channel_id=1, source_target_pairs={{0,2},{4,0},{8,4},{12,8},{14,12},{10,14},{6,10},{2,6},{1,3},{5,1},... | collective-permute-start | bytes 589832 | tf_op jit(solution)/shard_map/ppermute | solution.py:23
  38.4 9.6 %collective-permute-start.16 = (bf16[32,3072]{1,0:T(8,128)(2,1)S(1)}, bf16[32,3072]{1,0:T(8,128)(2,1)S(1)}, u32[]{:S(2)}, u32[]{:S(2)}) collective-permute-start(bf16[32,3072]{1,0:T(8,128)(2,1)S(1)} %get-tuple-element.51), channel_id=1, source_target_pairs={{0,14},{4,10},{8,6},{12,2},{14,0},{10,4},{6,8},{2,12},{1,15},{5,11... | collective-permute-start | bytes 589832 | tf_op jit(solution)/shard_map/ppermute | solution.py:23

commit v7 on v6

--- a/solution.py
+++ b/solution.py
@@ -412,14 +412,12 @@
     blocks = {0: own}
     behind = ahead = own
     for step in range(1, half + 1):
-        behind = shift(behind, 1)
-        got = {count - step: behind}
+        got = {step: shift(ahead, -1)}
         if step < half:
-            ahead = shift(ahead, -1)
-            got[step] = ahead
+            got[count - step] = shift(behind, 1)
         first = held[0] if step == 1 else sibling[step - 2 : step - 1]
         got = {k: after((v,), first)[0] for k, v in got.items()}
-        behind, ahead = got[count - step], got.get(step)
+        ahead, behind = got[step], got.get(count - step)
         blocks.update(got)
 
     held.append(sibling)

time: 50 us -> 48.3 us (0.966)
  waiting for transfers between devices: 15.3 us -> 12.3 us
  starting transfers between devices: 19.1 us -> 20.3 us
    ppermute x14, waiting for transfers between devices: 15.3 us -> 12.3 us  [shift(): return lax.ppermute(value, 'expert', pairs)]
    ppermute x14, starting transfers between devices: 18.1 us -> 19.3 us  [shift(): return lax.ppermute(value, 'expert', pairs)]
  transfers between devices with their start and end apart: 17 -> 17, of which waited for: 10 -> 8; matrix products, arithmetic and copies ran while one was open for 0% -> 0% of each run, Pallas kernels for 23% -> 24%
where the time goes in v7:
time: 48.3 us; the launch traced here: 47.4 us
  starting transfers between devices  20.3 us (42%)
  Pallas kernels  14 us (29%)
  waiting for transfers between devices  12.3 us (25%)
  between operations  0.73 us (2%)
    ppermute x14, starting transfers between devices, shift(): return lax.ppermute(value, 'expert', pairs)  19.3 us
    ppermute x14, waiting for transfers between devices, shift(): return lax.ppermute(value, 'expert', pairs)  12.3 us
    pallas_call x2, Pallas kernels, experts(): pl.pallas_call(functools.partial(experts_kernel, width, lax.axis_size('ex...  5.57 us
    pallas_call x1, Pallas kernels, load(): pl.pallas_call(load_kernel, out_shape=[pltpu.VMEM(v.shape, v.dtype) for v...  3.78 us
    pallas_call x1, Pallas kernels, frame_sums(): pl.pallas_call(functools.partial(frames_kernel, columns, books, shard, se...  1.79 us
    pallas_call x1, Pallas kernels, pack(): pl.pallas_call(functools.partial(pack_kernel, columns, n_wave), out_shape...  1.59 us
    pallas_call x1, Pallas kernels, finish(): pl.pallas_call(functools.partial(finish_kernel, *numbered[0][0], width),...  1.08 us
    ppermute x3, starting transfers between devices, swap_wave(): return lax.ppermute(value, 'wave', [(0, 1), (1, 0)])  1.03 us
  transfers between devices with their start and end apart: 17, of which 8 were waited for; matrix products, arithmetic and copies ran while one was open for 0% of the time, Pallas kernels for 24%

profile of v7, /device:TPU:0, one launch (start us, length us, event | category | flops | bytes accessed | tf_op | source)
XLA Modules:
  0.0 47.4 jit_solution(16347179068221274560)
XLA Ops:
  0.6 1.6 %pack.1.refs_0_ = bf16[32,2176]{1,0:T(8,128)(2,1)S(1)} custom-call(s32[1]{0:T(128)} %bitcast._.place_ref, bf16[16,2,2048]{2,1,0:T(2,128)(2,1)} %refs_0_.1, s32[2,8,16]{2,1,0:T(8,128)} %bitcast.14, f32[2,8,16]{2,1,0:T(8,128)} %bitcast.15, s32[16,2,16]{2,1,0:T(2,128)} %refs_3_.1, s32[1,16]{1,0:T(1,128)} %bitcast.16), custom_call_target="tpu_custom_call" | custom-call | tf_op jit(solution)/shard_map/pack/pallas_call | solution.py:159
  2.2 0.5 %collective-permute-start.2 = (bf16[2,2048,384]{2,1,0:T(8,128)(2,1)}, bf16[2,2048,384]{2,1,0:T(8,128)(2,1)S(1)}, u32[]{:S(2)}, u32[]{:S(2)}) collective-permute-start(bf16[2,2048,384]{2,1,0:T(8,128)(2,1)} %refs_1_.1), channel_id=1, source_target_pairs={{0,1},{1,0},{2,3},{3,2},{4,5},{5,4},{6,7},{7,6},{8,9},{9,8},{10,11... | collective-permute-start | bytes 9437192 | tf_op jit(solution)/shard_map/ppermute | solution.py:27
  2.8 0.1 collective-permute-start.6
  2.8 0.4 collective-permute-start.8
  3.3 2.6 %collective-permute-start = (bf16[32,2176]{1,0:T(8,128)(2,1)S(1)}, bf16[32,2176]{1,0:T(8,128)(2,1)S(1)}, u32[]{:S(2)}, u32[]{:S(2)}) collective-permute-start(bf16[32,2176]{1,0:T(8,128)(2,1)S(1)} %pack.1.refs_0_), channel_id=1, source_target_pairs={{0,2},{4,0},{8,4},{12,8},{14,12},{10,14},{6,10},{2,6},{1,3},{5,1},... | collective-permute-start | bytes 417800 | tf_op jit(solution)/shard_map/ppermute | solution.py:23
  5.9 0.1 collective-permute-start.3
  5.9 3.8 %load.1 = (bf16[2,2048,384]{2,1,0:T(8,128)(2,1)S(1)}, bf16[2,2048,384]{2,1,0:T(8,128)(2,1)S(1)}, bf16[768,2048]{1,0:T(8,128)(2,1)S(1)}) custom-call(bf16[32,2176]{1,0:T(8,128)(2,1)S(1)} %pack.1.refs_0_, bf16[2,2048,384]{2,1,0:T(8,128)(2,1)} %refs_1_.1, bf16[2,2048,384]{2,1,0:T(8,128)(2,1)} %refs_2_.1, bf16[768,2048]{1,0:T(8,128)(2,1)} %bitcast.13), custom_call_target="tpu_custom_call" | custom-call | bytes 9437184 | tf_op jit(solution)/shard_map/load/pallas_call | solution.py:187
  9.7 0.5 collective-permute-done.refs_1_
  10.2 0.0 copy-start
  10.2 1.7 %collective-permute-start.1 = (bf16[32,2176]{1,0:T(8,128)(2,1)S(1)}, bf16[32,2176]{1,0:T(8,128)(2,1)S(1)}, u32[]{:S(2)}, u32[]{:S(2)}) collective-permute-start(bf16[32,2176]{1,0:T(8,128)(2,1)S(1)} %collective-permute-done.refs_1_), channel_id=1, source_target_pairs={{0,2},{4,0},{8,4},{12,8},{14,12},{10,14},{6,10},{2,6},{1,3},{5,1},... | collective-permute-start | bytes 417800 | tf_op jit(solution)/shard_map/ppermute | solution.py:23
  11.9 0.0 collective-permute-done.3.refs_2_
  11.9 0.3 collective-permute-start.4
  12.2 3.4 %collective-permute-done.1.refs_0_.refs_4_ = bf16[32,2176]{1,0:T(8,128)(2,1)S(1)} collective-permute-done((bf16[32,2176]{1,0:T(8,128)(2,1)S(1)}, bf16[32,2176]{1,0:T(8,128)(2,1)S(1)}, u32[]{:S(2)}, u32[]{:S(2)}) %collective-permute-start.1) | collective-permute-done | bytes 139296 | tf_op jit(solution)/shard_map/ppermute | solution.py:23
  15.6 0.0 collective-permute-done.2.refs_7_
  15.6 1.6 %collective-permute-start.7 = (bf16[32,2176]{1,0:T(8,128)(2,1)S(1)}, bf16[32,2176]{1,0:T(8,128)(2,1)S(1)}, u32[]{:S(2)}, u32[]{:S(2)}) collective-permute-start(bf16[32,2176]{1,0:T(8,128)(2,1)S(1)} %collective-permute-done.1.refs_0_.refs_4_), channel_id=1, source_target_pairs={{0,2},{4,0},{8,4},{12,8},{14,12},{10,14},{6,10},{2,6},{1,3},{5,1},... | collective-permute-start | bytes 417800 | tf_op jit(solution)/shard_map/ppermute | solution.py:23
  17.2 0.0 collective-permute-done.4.refs_2_.refs_6_
  17.2 0.4 collective-permute-start.5
  17.6 0.0 collective-permute-done.6.refs_8_
  17.7 3.0 %collective-permute-done.7.refs_3_.refs_7_ = bf16[32,2176]{1,0:T(8,128)(2,1)S(1)} collective-permute-done((bf16[32,2176]{1,0:T(8,128)(2,1)S(1)}, bf16[32,2176]{1,0:T(8,128)(2,1)S(1)}, u32[]{:S(2)}, u32[]{:S(2)}) %collective-permute-start.7) | collective-permute-done | bytes 139296 | tf_op jit(solution)/shard_map/ppermute | solution.py:23
  20.7 1.6 %collective-permute-start.9 = (bf16[32,2176]{1,0:T(8,128)(2,1)S(1)}, bf16[32,2176]{1,0:T(8,128)(2,1)S(1)}, u32[]{:S(2)}, u32[]{:S(2)}) collective-permute-start(bf16[32,2176]{1,0:T(8,128)(2,1)S(1)} %collective-permute-done.7.refs_3_.refs_7_), channel_id=1, source_target_pairs={{0,2},{4,0},{8,4},{12,8},{14,12},{10,14},{6,10},{2,6},{1,3},{5,1},... | collective-permute-start | bytes 417800 | tf_op jit(solution)/shard_map/ppermute | solution.py:23
  22.3 0.0 collective-permute-done.5.refs_1_.refs_5_
  22.3 0.0 collective-permute-done.8.refs_9_
  22.3 2.8 %experts.2 = (bf16[64,2048]{1,0:T(8,128)(2,1)S(1)}, bf16[64,2048]{1,0:T(8,128)(2,1)S(1)}) custom-call(s32[1]{0:T(128)} %bitcast._.place_ref, bf16[32,2176]{1,0:T(8,128)(2,1)S(1)} %collective-permute-done.1.refs_0_.refs_4_, bf16[32,2176]{1,0:T(8,128)(2,1)S(1)} %collective-permute-done.5.refs_1_.refs_5_, ...), custom_call_target="tpu_custom_call" | custom-call | flops 2415919104 | bytes 18874368 | tf_op jit(solution)/shard_map/experts/pallas_call | solution.py:237
  25.1 0.5 %collective-permute-start.10 = (bf16[64,2048]{1,0:T(8,128)(2,1)S(1)}, bf16[64,2048]{1,0:T(8,128)(2,1)S(1)}, u32[]{:S(2)}, u32[]{:S(2)}) collective-permute-start(bf16[64,2048]{1,0:T(8,128)(2,1)S(1)} %get-tuple-element.41), channel_id=1, source_target_pairs={{0,4},{4,8},{8,12},{12,14},{14,10},{10,6},{6,2},{2,0},{1,5},{5,9},... | collective-permute-start | bytes 786440 | tf_op jit(solution)/shard_map/ppermute | solution.py:23
  25.6 1.6 %collective-permute-start.12 = (bf16[64,2048]{1,0:T(8,128)(2,1)S(1)}, bf16[64,2048]{1,0:T(8,128)(2,1)S(1)}, u32[]{:S(2)}, u32[]{:S(2)}) collective-permute-start(bf16[64,2048]{1,0:T(8,128)(2,1)S(1)} %get-tuple-element.42), channel_id=1, source_target_pairs={{0,2},{4,0},{8,4},{12,8},{14,12},{10,14},{6,10},{2,6},{1,3},{5,1},... | collective-permute-start | bytes 786440 | tf_op jit(solution)/shard_map/ppermute | solution.py:23
  27.2 0.0 collective-permute-done.9.refs_3_
  27.2 0.0 copy-done
  27.2 1.8 %frame_sums.1 = (bf16[128,1024]{1,0:T(8,128)(2,1)S(1)}, bf16[64,1024]{1,0:T(8,128)(2,1)S(1)}, bf16[64,1024]{1,0:T(8,128)(2,1)S(1)}) custom-call(s32[1]{0:T(128)} %bitcast._.place_ref, bf16[32,2176]{1,0:T(8,128)(2,1)S(1)} %pack.1.refs_0_, bf16[32,2176]{1,0:T(8,128)(2,1)S(1)} %collective-permute-done.refs_1_, ...), custom_call_target="tpu_custom_call" | custom-call | flops 1073741824 | bytes 4194304 | tf_op jit(solution)/shard_map/frame_sums/pallas_call | solution.py:303
  29.0 0.6 %collective-permute-start.11 = (bf16[64,1024]{1,0:T(8,128)(2,1)S(1)}, bf16[64,1024]{1,0:T(8,128)(2,1)S(1)}, u32[]{:S(2)}, u32[]{:S(2)}) collective-permute-start(bf16[64,1024]{1,0:T(8,128)(2,1)S(1)} %get-tuple-element.47), channel_id=1, source_target_pairs={{0,4},{4,8},{8,12},{12,14},{14,10},{10,6},{6,2},{2,0},{1,5},{5,9},... | collective-permute-start | bytes 393224 | tf_op jit(solution)/shard_map/ppermute | solution.py:23
  29.5 0.0 copy-start.1
  29.6 1.6 %collective-permute-start.13 = (bf16[64,1024]{1,0:T(8,128)(2,1)S(1)}, bf16[64,1024]{1,0:T(8,128)(2,1)S(1)}, u32[]{:S(2)}, u32[]{:S(2)}) collective-permute-start(bf16[64,1024]{1,0:T(8,128)(2,1)S(1)} %get-tuple-element.48), channel_id=1, source_target_pairs={{0,2},{4,0},{8,4},{12,8},{14,12},{10,14},{6,10},{2,6},{1,3},{5,1},... | collective-permute-start | bytes 393224 | tf_op jit(solution)/shard_map/ppermute | solution.py:23
  31.1 2.8 %experts.3.refs_0_ = bf16[128,2048]{1,0:T(8,128)(2,1)S(1)} custom-call(s32[1]{0:T(128)} %bitcast._.place_ref, bf16[32,2176]{1,0:T(8,128)(2,1)S(1)} %pack.1.refs_0_, bf16[32,2176]{1,0:T(8,128)(2,1)S(1)} %collective-permute-done.refs_1_, bf16[32,2176]{1,0:T(8,128)(2,1)S(1)} %collective-permute-done.3.refs_2_, ...), custom_call_target="tpu_custom_call" | custom-call | flops 2415919104 | bytes 18874368 | tf_op jit(solution)/shard_map/experts/pallas_call | solution.py:237
  33.9 0.0 collective-permute-done.10.refs_1_
  33.9 0.0 collective-permute-done.12.refs_4_
  33.9 0.4 collective-permute-done.11.refs_3_
  34.3 0.3 collective-permute-done.13.refs_5_
  34.6 0.2 join.1
  34.7 1.6 %collective-permute-start.14 = (bf16[32,3072]{1,0:T(8,128)(2,1)S(1)}, bf16[32,3072]{1,0:T(8,128)(2,1)S(1)}, u32[]{:S(2)}, u32[]{:S(2)}) collective-permute-start(bf16[32,3072]{1,0:T(8,128)(2,1)S(1)} %get-tuple-element.49), channel_id=1, source_target_pairs={{0,4},{4,8},{8,12},{12,14},{14,10},{10,6},{6,2},{2,0},{1,5},{5,9},... | collective-permute-start | bytes 589832 | tf_op jit(solution)/shard_map/ppermute | solution.py:23
  36.4 0.4 collective-permute-start.15
  36.8 4.7 %collective-permute-start.16 = (bf16[32,3072]{1,0:T(8,128)(2,1)S(1)}, bf16[32,3072]{1,0:T(8,128)(2,1)S(1)}, u32[]{:S(2)}, u32[]{:S(2)}) collective-permute-start(bf16[32,3072]{1,0:T(8,128)(2,1)S(1)} %get-tuple-element.51), channel_id=1, source_target_pairs={{0,14},{4,10},{8,6},{12,2},{14,0},{10,4},{6,8},{2,12},{1,15},{5,11... | collective-permute-start | bytes 589832 | tf_op jit(solution)/shard_map/ppermute | solution.py:23
  41.5 1.1 %collective-permute-done.14.refs_2_ = bf16[32,3072]{1,0:T(8,128)(2,1)S(1)} collective-permute-done((bf16[32,3072]{1,0:T(8,128)(2,1)S(1)}, bf16[32,3072]{1,0:T(8,128)(2,1)S(1)}, u32[]{:S(2)}, u32[]{:S(2)}) %collective-permute-start.14) | collective-permute-done | bytes 196640 | tf_op jit(solution)/shard_map/ppermute | solution.py:23
  42.6 1.6 %collective-permute-done.15.refs_3_ = bf16[32,3072]{1,0:T(8,128)(2,1)S(1)} collective-permute-done((bf16[32,3072]{1,0:T(8,128)(2,1)S(1)}, bf16[32,3072]{1,0:T(8,128)(2,1)S(1)}, u32[]{:S(2)}, u32[]{:S(2)}) %collective-permute-start.15) | collective-permute-done | bytes 196640 | tf_op jit(solution)/shard_map/ppermute | solution.py:23
  44.1 2.1 %collective-permute-done.16.refs_4_ = bf16[32,3072]{1,0:T(8,128)(2,1)S(1)} collective-permute-done((bf16[32,3072]{1,0:T(8,128)(2,1)S(1)}, bf16[32,3072]{1,0:T(8,128)(2,1)S(1)}, u32[]{:S(2)}, u32[]{:S(2)}) %collective-permute-start.16) | collective-permute-done | bytes 196640 | tf_op jit(solution)/shard_map/ppermute | solution.py:23
  46.2 0.0 copy-done.1
  46.2 0.0 copy-done.2
  46.2 0.0 copy-done.3
  46.3 0.0 copy-done.4
  46.3 1.1 %finish.1 = (bf16[16,2,2048]{2,1,0:T(2,128)(2,1)}, bf16[16,2,512]{2,1,0:T(2,128)(2,1)}, bf16[6,16,1024]{2,1,0:T(8,128)(2,1)}) custom-call(bf16[128,2048]{1,0:T(8,128)(2,1)S(1)} %experts.3.refs_0_, bf16[128,1024]{1,0:T(8,128)(2,1)S(1)} %get-tuple-element.45.refs_2_.refs_1_, bf16[32,3072]{1,0:T(8,128)(2,1)S(1)} %collective-permute-done.14.refs_2_, ...), custom_call_target="tpu_custom_call" | custom-call | bytes 2097152 | tf_op jit(solution)/shard_map/finish/pallas_call | solution.py:354
  (3 shorter events, 0.0 us)
Async XLA Ops:
  2.2 13.4 %collective-permute-start.2 = (bf16[2,2048,384]{2,1,0:T(8,128)(2,1)}, bf16[2,2048,384]{2,1,0:T(8,128)(2,1)S(1)}, u32[]{:S(2)}, u32[]{:S(2)}) collective-permute-start(bf16[2,2048,384]{2,1,0:T(8,128)(2,1)} %refs_1_.1), channel_id=1, source_target_pairs={{0,1},{1,0},{2,3},{3,2},{4,5},{5,4},{6,7},{7,6},{8,9},{9,8},{10,11... | collective-permute-start | bytes 9437192 | tf_op jit(solution)/shard_map/ppermute | solution.py:27
  2.8 14.9 %collective-permute-start.6 = (bf16[2,2048,384]{2,1,0:T(8,128)(2,1)}, bf16[2,2048,384]{2,1,0:T(8,128)(2,1)S(1)}, u32[]{:S(2)}, u32[]{:S(2)}) collective-permute-start(bf16[2,2048,384]{2,1,0:T(8,128)(2,1)} %refs_2_.1), channel_id=1, source_target_pairs={{0,1},{1,0},{2,3},{3,2},{4,5},{5,4},{6,7},{7,6},{8,9},{9,8},{10,11... | collective-permute-start | bytes 9437192 | tf_op jit(solution)/shard_map/ppermute | solution.py:27
  2.8 19.4 %collective-permute-start.8 = (bf16[768,2048]{1,0:T(8,128)(2,1)}, bf16[768,2048]{1,0:T(8,128)(2,1)S(1)}, u32[]{:S(2)}, u32[]{:S(2)}) collective-permute-start(bf16[768,2048]{1,0:T(8,128)(2,1)} %bitcast.12), channel_id=1, source_target_pairs={{0,1},{1,0},{2,3},{3,2},{4,5},{5,4},{6,7},{7,6},{8,9},{9,8},{10,11... | collective-permute-start | bytes 9437192 | tf_op jit(solution)/shard_map/ppermute | solution.py:27
  3.3 6.9 %collective-permute-start = (bf16[32,2176]{1,0:T(8,128)(2,1)S(1)}, bf16[32,2176]{1,0:T(8,128)(2,1)S(1)}, u32[]{:S(2)}, u32[]{:S(2)}) collective-permute-start(bf16[32,2176]{1,0:T(8,128)(2,1)S(1)} %pack.1.refs_0_), channel_id=1, source_target_pairs={{0,2},{4,0},{8,4},{12,8},{14,12},{10,14},{6,10},{2,6},{1,3},{5,1},... | collective-permute-start | bytes 417800 | tf_op jit(solution)/shard_map/ppermute | solution.py:23
  5.9 6.0 %collective-permute-start.3 = (bf16[32,2176]{1,0:T(8,128)(2,1)S(1)}, bf16[32,2176]{1,0:T(8,128)(2,1)S(1)}, u32[]{:S(2)}, u32[]{:S(2)}) collective-permute-start(bf16[32,2176]{1,0:T(8,128)(2,1)S(1)} %pack.1.refs_0_), channel_id=1, source_target_pairs={{0,4},{4,8},{8,12},{12,14},{14,10},{10,6},{6,2},{2,0},{1,5},{5,9},... | collective-permute-start | bytes 417800 | tf_op jit(solution)/shard_map/ppermute | solution.py:23
  10.2 17.0 %copy-start = (bf16[16,128,1024]{2,1,0:T(8,128)(2,1)S(1)}, bf16[16,128,1024]{2,1,0:T(8,128)(2,1)}, u32[]{:S(2)}) copy-start(bf16[16,128,1024]{2,1,0:T(8,128)(2,1)} %param.21) | copy-start | bytes 12582916
  10.2 5.4 %collective-permute-start.1 = (bf16[32,2176]{1,0:T(8,128)(2,1)S(1)}, bf16[32,2176]{1,0:T(8,128)(2,1)S(1)}, u32[]{:S(2)}, u32[]{:S(2)}) collective-permute-start(bf16[32,2176]{1,0:T(8,128)(2,1)S(1)} %collective-permute-done.refs_1_), channel_id=1, source_target_pairs={{0,2},{4,0},{8,4},{12,8},{14,12},{10,14},{6,10},{2,6},{1,3},{5,1},... | collective-permute-start | bytes 417800 | tf_op jit(solution)/shard_map/ppermute | solution.py:23
  11.9 5.3 %collective-permute-start.4 = (bf16[32,2176]{1,0:T(8,128)(2,1)S(1)}, bf16[32,2176]{1,0:T(8,128)(2,1)S(1)}, u32[]{:S(2)}, u32[]{:S(2)}) collective-permute-start(bf16[32,2176]{1,0:T(8,128)(2,1)S(1)} %collective-permute-done.3.refs_2_), channel_id=1, source_target_pairs={{0,4},{4,8},{8,12},{12,14},{14,10},{10,6},{6,2},{2,0},{1,5},{5,9},... | collective-permute-start | bytes 417800 | tf_op jit(solution)/shard_map/ppermute | solution.py:23
  15.6 5.1 %collective-permute-start.7 = (bf16[32,2176]{1,0:T(8,128)(2,1)S(1)}, bf16[32,2176]{1,0:T(8,128)(2,1)S(1)}, u32[]{:S(2)}, u32[]{:S(2)}) collective-permute-start(bf16[32,2176]{1,0:T(8,128)(2,1)S(1)} %collective-permute-done.1.refs_0_.refs_4_), channel_id=1, source_target_pairs={{0,2},{4,0},{8,4},{12,8},{14,12},{10,14},{6,10},{2,6},{1,3},{5,1},... | collective-permute-start | bytes 417800 | tf_op jit(solution)/shard_map/ppermute | solution.py:23
  17.2 5.1 %collective-permute-start.5 = (bf16[32,2176]{1,0:T(8,128)(2,1)S(1)}, bf16[32,2176]{1,0:T(8,128)(2,1)S(1)}, u32[]{:S(2)}, u32[]{:S(2)}) collective-permute-start(bf16[32,2176]{1,0:T(8,128)(2,1)S(1)} %collective-permute-done.4.refs_2_.refs_6_), channel_id=1, source_target_pairs={{0,4},{4,8},{8,12},{12,14},{14,10},{10,6},{6,2},{2,0},{1,5},{5,9},... | collective-permute-start | bytes 417800 | tf_op jit(solution)/shard_map/ppermute | solution.py:23
  20.7 6.5 %collective-permute-start.9 = (bf16[32,2176]{1,0:T(8,128)(2,1)S(1)}, bf16[32,2176]{1,0:T(8,128)(2,1)S(1)}, u32[]{:S(2)}, u32[]{:S(2)}) collective-permute-start(bf16[32,2176]{1,0:T(8,128)(2,1)S(1)} %collective-permute-done.7.refs_3_.refs_7_), channel_id=1, source_target_pairs={{0,2},{4,0},{8,4},{12,8},{14,12},{10,14},{6,10},{2,6},{1,3},{5,1},... | collective-permute-start | bytes 417800 | tf_op jit(solution)/shard_map/ppermute | solution.py:23
  25.1 8.8 %collective-permute-start.10 = (bf16[64,2048]{1,0:T(8,128)(2,1)S(1)}, bf16[64,2048]{1,0:T(8,128)(2,1)S(1)}, u32[]{:S(2)}, u32[]{:S(2)}) collective-permute-start(bf16[64,2048]{1,0:T(8,128)(2,1)S(1)} %get-tuple-element.41), channel_id=1, source_target_pairs={{0,4},{4,8},{8,12},{12,14},{14,10},{10,6},{6,2},{2,0},{1,5},{5,9},... | collective-permute-start | bytes 786440 | tf_op jit(solution)/shard_map/ppermute | solution.py:23
  25.6 8.3 %collective-permute-start.12 = (bf16[64,2048]{1,0:T(8,128)(2,1)S(1)}, bf16[64,2048]{1,0:T(8,128)(2,1)S(1)}, u32[]{:S(2)}, u32[]{:S(2)}) collective-permute-start(bf16[64,2048]{1,0:T(8,128)(2,1)S(1)} %get-tuple-element.42), channel_id=1, source_target_pairs={{0,2},{4,0},{8,4},{12,8},{14,12},{10,14},{6,10},{2,6},{1,3},{5,1},... | collective-permute-start | bytes 786440 | tf_op jit(solution)/shard_map/ppermute | solution.py:23
  29.0 5.3 %collective-permute-start.11 = (bf16[64,1024]{1,0:T(8,128)(2,1)S(1)}, bf16[64,1024]{1,0:T(8,128)(2,1)S(1)}, u32[]{:S(2)}, u32[]{:S(2)}) collective-permute-start(bf16[64,1024]{1,0:T(8,128)(2,1)S(1)} %get-tuple-element.47), channel_id=1, source_target_pairs={{0,4},{4,8},{8,12},{12,14},{14,10},{10,6},{6,2},{2,0},{1,5},{5,9},... | collective-permute-start | bytes 393224 | tf_op jit(solution)/shard_map/ppermute | solution.py:23
  29.5 16.7 %copy-start.1 = (bf16[1024,512]{1,0:T(8,128)(2,1)S(1)}, bf16[1024,512]{1,0:T(8,128)(2,1)}, u32[]{:S(2)}) copy-start(bf16[1024,512]{1,0:T(8,128)(2,1)} %refs_8_.1) | copy-start | bytes 3145732
  29.5 16.7 %copy-start.2 = (bf16[16,6,1024]{2,0,1:T(8,128)(2,1)S(1)}, bf16[16,6,1024]{2,0,1:T(8,128)(2,1)}, u32[]{:S(2)}) copy-start(bf16[16,6,1024]{2,0,1:T(8,128)(2,1)} %param.22) | copy-start | bytes 589828
  29.5 16.7 %copy-start.3 = (f32[7,1024]{1,0:T(8,128)S(1)}, f32[7,1024]{1,0:T(8,128)}, u32[]{:S(2)}) copy-start(f32[7,1024]{1,0:T(8,128)} %refs_6_.1) | copy-start | bytes 86020
  29.5 16.7 %copy-start.4 = (f32[1024]{0:T(1024)S(1)}, f32[1024]{0:T(1024)}, u32[]{:S(2)}) copy-start(f32[1024]{0:T(1024)} %param.24) | copy-start | bytes 12292
  29.6 5.0 %collective-permute-start.13 = (bf16[64,1024]{1,0:T(8,128)(2,1)S(1)}, bf16[64,1024]{1,0:T(8,128)(2,1)S(1)}, u32[]{:S(2)}, u32[]{:S(2)}) collective-permute-start(bf16[64,1024]{1,0:T(8,128)(2,1)S(1)} %get-tuple-element.48), channel_id=1, source_target_pairs={{0,2},{4,0},{8,4},{12,8},{14,12},{10,14},{6,10},{2,6},{1,3},{5,1},... | collective-permute-start | bytes 393224 | tf_op jit(solution)/shard_map/ppermute | solution.py:23
  34.7 7.8 %collective-permute-start.14 = (bf16[32,3072]{1,0:T(8,128)(2,1)S(1)}, bf16[32,3072]{1,0:T(8,128)(2,1)S(1)}, u32[]{:S(2)}, u32[]{:S(2)}) collective-permute-start(bf16[32,3072]{1,0:T(8,128)(2,1)S(1)} %get-tuple-element.49), channel_id=1, source_target_pairs={{0,4},{4,8},{8,12},{12,14},{14,10},{10,6},{6,2},{2,0},{1,5},{5,9},... | collective-permute-start | bytes 589832 | tf_op jit(solution)/shard_map/ppermute | solution.py:23
  36.4 7.8 %collective-permute-start.15 = (bf16[32,3072]{1,0:T(8,128)(2,1)S(1)}, bf16[32,3072]{1,0:T(8,128)(2,1)S(1)}, u32[]{:S(2)}, u32[]{:S(2)}) collective-permute-start(bf16[32,3072]{1,0:T(8,128)(2,1)S(1)} %get-tuple-element.50), channel_id=1, source_target_pairs={{0,2},{4,0},{8,4},{12,8},{14,12},{10,14},{6,10},{2,6},{1,3},{5,1},... | collective-permute-start | bytes 589832 | tf_op jit(solution)/shard_map/ppermute | solution.py:23
  36.8 9.4 %collective-permute-start.16 = (bf16[32,3072]{1,0:T(8,128)(2,1)S(1)}, bf16[32,3072]{1,0:T(8,128)(2,1)S(1)}, u32[]{:S(2)}, u32[]{:S(2)}) collective-permute-start(bf16[32,3072]{1,0:T(8,128)(2,1)S(1)} %get-tuple-element.51), channel_id=1, source_target_pairs={{0,14},{4,10},{8,6},{12,2},{14,0},{10,4},{6,8},{2,12},{1,15},{5,11... | collective-permute-start | bytes 589832 | tf_op jit(solution)/shard_map/ppermute | solution.py:23

commit v8 on v7

--- a/solution.py
+++ b/solution.py
@@ -108,7 +108,7 @@
     hidden_ref, ids_ref, weights_ref, codes_ref, owner_ref = held
     for copy in copies:
         copy.start()
-    for copy in copies:
+    for copy in copies[1:]:
         copy.wait()
     sessions, steps, width = hidden_ref.shape
     expert_count = columns[0] // 2
@@ -124,7 +124,6 @@
     named = lax.broadcasted_iota(jnp.int32, (expert_count, sessions), 0)
     for t in range(steps):
         at = slice(t * sessions, (t + 1) * sessions)
-        out_ref[at, 0:width] = hidden_ref[:, t, :]
         weight = jnp.zeros((expert_count, sessions), F32)
         for k in range(ids_ref.shape[1]):
             weight += jnp.where(named == ids_ref[t, k : k + 1, :], weights_ref[t, k : k + 1, :], 0.0)
@@ -144,6 +143,9 @@
         for i, piece in enumerate(digits(slot * steps + t)):
             meta += jnp.where(lane == columns[1] + i, piece.astype(F32), 0.0)
         out_ref[at, width:] = meta.astype(BF16)
+    copies[0].wait()
+    for t in range(steps):
+        out_ref[t * sessions : (t + 1) * sessions, 0:width] = hidden_ref[:, t, :]
 
 
 def pack(place, hidden_rows, expert_ids, route_weights, codes, owner_slot, columns, n_wave):
@@ -169,26 +171,31 @@
     )(place, *[pltpu.with_memory_space_constraint(arg, pltpu.HBM) for arg in args])
 
 
-def load_kernel(*refs):
-    count = len(refs) // 2 - 1
-    sources, held, sems = refs[1 : count + 1], refs[count + 1 : -1], refs[-1]
+def load_kernel(code_at, books, shard, *refs):
+    count = (len(refs) - 3) // 2
+    sources, held, spread_ref, sems = refs[1 : count + 1], refs[count + 1 : -2], refs[-2], refs[-1]
     copies = [
         pltpu.make_async_copy(source, ref, sems.at[i])
         for i, (source, ref) in enumerate(zip(sources, held))
     ]
     for copy in copies:
         copy.start()
+    column = lax.broadcasted_iota(jnp.int32, spread_ref.shape, 0) - code_at
+    book = lax.broadcasted_iota(jnp.int32, spread_ref.shape, 1) // shard
+    spread = jnp.where(column == book, 1.0, jnp.where(column == book + books, 256.0, 0.0))
+    spread_ref[...] = spread.astype(BF16)
     for copy in copies:
         copy.wait()
 
 
-def load(earlier, *arrays):
+def load(earlier, arrays, meta_width, code_at, books, shard):
     hbm = pl.BlockSpec(memory_space=pltpu.HBM)
     return pl.pallas_call(
-        load_kernel,
-        out_shape=[pltpu.VMEM(v.shape, v.dtype) for v in arrays],
+        functools.partial(load_kernel, code_at, books, shard),
+        out_shape=[pltpu.VMEM(v.shape, v.dtype) for v in arrays]
+        + [pltpu.VMEM((meta_width, books * shard), BF16)],
         in_specs=[pl.BlockSpec(memory_space=pl.ANY)] + [hbm] * len(arrays),
-        out_specs=[pl.BlockSpec(memory_space=pltpu.VMEM)] * len(arrays),
+        out_specs=[pl.BlockSpec(memory_space=pltpu.VMEM)] * (len(arrays) + 1),
         scratch_shapes=[pltpu.SemaphoreType.DMA((len(arrays),))],
         compiler_params=pltpu.CompilerParams(vmem_limit_bytes=VMEM_LIMIT),
         cost_estimate=pl.CostEstimate(
@@ -255,20 +262,17 @@
     )(place, *blocks, *weights)
 
 
-def frames_kernel(columns, books, shard, sessions, steps, order, place_ref, *refs):
-    metas = refs[: len(order)]
-    table_ref, *outs, hot_ref = refs[len(order) :]
-    count = len(order)
-    code_at, slot_at = columns
+def frames_kernel(slot_at, shard, sessions, steps, sources, order, place_ref, *refs):
+    count = len(sources)
+    metas, (spread_ref, table_ref, *outs, hot_ref) = refs[:count], refs[count:]
     rows = metas[0].shape[0]
     meta = jnp.concatenate([m[...] for m in metas], axis=0)
-    total = meta.shape[0]
     column = lax.broadcasted_iota(jnp.int32, (8, meta.shape[1]), 1)
     digit = lax.broadcasted_iota(jnp.int32, (8, meta.shape[1]), 0)
     picks = jnp.where((column == slot_at + digit) & (digit < 2), 1.0, 0.0).astype(BF16)
     slots = lax.dot_general(picks, meta, (((1,), (1,)), ((), ())), preferred_element_type=F32)
     source = (slots[0:1] + 256.0 * slots[1:2]).astype(jnp.int32)
-    row = lax.broadcasted_iota(jnp.int32, (total, 1), 0)
+    row = lax.broadcasted_iota(jnp.int32, (rows * len(order), 1), 0)
     inside = row % rows
     target = (inside % sessions) * steps + inside // sessions
     place = place_ref[0]
@@ -279,12 +283,8 @@
         target = target + jnp.where(row // rows == i, device * rows, 0)
     chooser = jnp.where(target == source, 1.0, 0.0).astype(BF16)
     ordered = jnp.dot(chooser, meta, preferred_element_type=F32).astype(BF16)
-    lanes = books * shard
-    column = lax.broadcasted_iota(jnp.int32, (meta.shape[1], lanes), 0) - code_at
-    book = lax.broadcasted_iota(jnp.int32, (meta.shape[1], lanes), 1) // shard
-    spread = jnp.where(column == book, 1.0, jnp.where(column == book + books, 256.0, 0.0))
-    codes = jnp.dot(ordered, spread.astype(BF16), preferred_element_type=F32)
-    entry = lax.broadcasted_iota(jnp.int32, (1, lanes), 1) % shard + place * shard
+    codes = jnp.dot(ordered, spread_ref[...], preferred_element_type=F32)
+    entry = lax.broadcasted_iota(jnp.int32, (1, hot_ref.shape[1]), 1) % shard + place * shard
     hot_ref[...] = jnp.where(codes == entry.astype(F32), 1.0, 0.0).astype(BF16)
     result = jnp.dot(hot_ref[...], table_ref[...], preferred_element_type=F32)
     start = 0
@@ -294,29 +294,31 @@
         start += size
 
 
-def frame_sums(blocks, order, sizes, place, code_table, columns, width, sessions, steps):
+def frame_sums(blocks, order, split, place, code_table, spread, slot_at, sessions, steps):
     books, shard, channels = code_table.shape
-    rows = blocks[0].shape[0]
+    meta_width = spread.shape[0]
+    sources = list(range(len(blocks)))
+    rows, width = blocks[0].shape
     total = rows * len(order)
-    meta_width = blocks[0].shape[1] - width
+    block = pl.BlockSpec((rows, meta_width), lambda i: (0, width // meta_width - 1))
     vmem = pl.BlockSpec(memory_space=pltpu.VMEM)
     return pl.pallas_call(
-        functools.partial(frames_kernel, columns, books, shard, sessions, steps, order),
+        functools.partial(frames_kernel, slot_at, shard, sessions, steps, sources, order),
         grid=(1,),
-        out_shape=[jax.ShapeDtypeStruct((rows * size, channels), BF16) for size in sizes],
-        in_specs=[pl.BlockSpec(memory_space=pltpu.SMEM)]
-        + [pl.BlockSpec((rows, meta_width), lambda i: (0, width // meta_width))] * len(order)
-        + [vmem],
-        out_specs=[vmem] * len(sizes),
+        out_shape=[jax.ShapeDtypeStruct((total // split, channels), BF16)] * split,
+        in_specs=[pl.BlockSpec(memory_space=pltpu.SMEM)] + [block] * len(sources) + [vmem] * 2,
+        out_specs=[vmem] * split,
         scratch_shapes=[pltpu.VMEM((total, books * shard), BF16)],
-        compiler_params=pltpu.CompilerParams(vmem_limit_bytes=VMEM_LIMIT + 12 * total * total),
+        compiler_params=pltpu.CompilerParams(
+            vmem_limit_bytes=VMEM_LIMIT + 12 * total * rows * len(sources)
+        ),
         cost_estimate=pl.CostEstimate(
             flops=2 * total * books * shard * channels,
             bytes_accessed=2 * books * shard * channels,
             transcendentals=0,
         ),
         name="frame_sums",
-    )(place, *[blocks[k] for k in order], code_table.reshape(books * shard, channels))
+    )(place, *[blocks[k] for k in sources], spread, code_table.reshape(books * shard, channels))
 
 
 def finish_kernel(left, right, whole, width, *refs):
@@ -407,7 +409,11 @@
     half = count // 2
     weights = (w_gate, w_up, w_down.reshape(-1, width))
     sibling = [swap_wave(v) for v in after(weights, own)]
-    held = [load(own, *weights)]
+    meta_width = own.shape[1] - width
+    *loaded, spread = load(
+        own, weights, meta_width, columns[0], books, code_table.shape[1]
+    )
+    held = [loaded]
 
     blocks = {0: own}
     behind = ahead = own
@@ -430,14 +436,18 @@
         pairs.insert(0, experts([blocks[k] for k in group], 2, turn, held))
         (turn,) = after((place,), pairs[0])
     arrived = carry(pairs)
-    order = near + [k for group in far for k in group]
-    sizes = [4] + [2] * (2 * len(far))
-    near_frames, *rest = frame_sums(
-        blocks, order, sizes, turn, code_table, columns, width, sessions, steps
-    )
-    frames_arrived = carry(list(zip(rest[::2], rest[1::2])))
-    (turn,) = after((place,), near_frames)
+
+    def frames(order, split, turn):
+        return frame_sums(
+            blocks, order, split, turn, code_table, spread, columns[1], sessions, steps
+        )
+
+    far_frames = frames([k for group in far for k in group], 2 * len(far), turn)
+    frames_arrived = carry(list(zip(far_frames[::2], far_frames[1::2])))
+    (turn,) = after((place,), far_frames)
     (near_rows,) = experts([blocks[k] for k in near], 1, turn, held)
+    (turn,) = after((place,), near_rows)
+    (near_frames,) = frames(near, 1, turn)
     left = towards(near_rows, arrived, rows)
     right = towards(near_frames, frames_arrived, rows)
     one, minus, across = join(list(zip(left, right)), rows, width, code_table.shape[2])

time: 48.3 us -> 47.5 us (0.983)
  waiting for transfers between devices: 12.3 us -> 11.5 us
  Pallas kernels: 14 us -> 14.5 us
    ppermute x14, waiting for transfers between devices: 12.3 us -> 11.5 us  [shift(): return lax.ppermute(value, 'expert', pairs)]
    pallas_call x2 -> x3, Pallas kernels: 5.57 us -> 5.98 us  [the longest x1 3.78 us: load(): pl.pallas_call(functools.partial(load_kernel, code_at, books, shard), out...]
  transfers between devices with their start and end apart: 17 -> 17, of which waited for: 8 -> 6; matrix products, arithmetic and copies ran while one was open for 0% -> 0% of each run, Pallas kernels for 24% -> 25%
where the time goes in v8:
time: 47.5 us; the launch traced here: 46.7 us
  starting transfers between devices  19.9 us (42%)
  Pallas kernels  14.5 us (31%)
  waiting for transfers between devices  11.5 us (24%)
  between operations  0.78 us (2%)
    ppermute x14, starting transfers between devices, shift(): return lax.ppermute(value, 'expert', pairs)  18.8 us
    ppermute x14, waiting for transfers between devices, shift(): return lax.ppermute(value, 'expert', pairs)  11.5 us
    pallas_call x2, Pallas kernels, experts(): pl.pallas_call(functools.partial(experts_kernel, width, lax.axis_size('ex...  5.75 us
    pallas_call x1, Pallas kernels, load(): pl.pallas_call(functools.partial(load_kernel, code_at, books, shard), out...  3.78 us
    pallas_call x2, Pallas kernels, frame_sums(): pl.pallas_call(functools.partial(frames_kernel, slot_at, shard, sessions,...  2.19 us
    pallas_call x1, Pallas kernels, pack(): pl.pallas_call(functools.partial(pack_kernel, columns, n_wave), out_shape...  1.46 us
    pallas_call x1, Pallas kernels, finish(): pl.pallas_call(functools.partial(finish_kernel, *numbered[0][0], width),...  1.1 us
    ppermute x3, starting transfers between devices, swap_wave(): return lax.ppermute(value, 'wave', [(0, 1), (1, 0)])  1.03 us
  transfers between devices with their start and end apart: 17, of which 6 were waited for; matrix products, arithmetic and copies ran while one was open for 0% of the time, Pallas kernels for 25%

profile of v8, /device:TPU:0, one launch (start us, length us, event | category | flops | bytes accessed | tf_op | source)
XLA Modules:
  0.0 46.7 jit_solution(9751704178169920184)
XLA Ops:
  0.6 1.5 %pack.1.refs_0_ = bf16[32,2176]{1,0:T(8,128)(2,1)S(1)} custom-call(s32[1]{0:T(128)} %bitcast._.place_ref, bf16[16,2,2048]{2,1,0:T(2,128)(2,1)} %refs_0_.1, s32[2,8,16]{2,1,0:T(8,128)} %bitcast.15, f32[2,8,16]{2,1,0:T(8,128)} %bitcast.16, s32[16,2,16]{2,1,0:T(2,128)} %refs_3_.1, s32[1,16]{1,0:T(1,128)} %bitcast.17), custom_call_target="tpu_custom_call" | custom-call | tf_op jit(solution)/shard_map/pack/pallas_call | solution.py:161
  2.1 0.5 %collective-permute-start.2 = (bf16[2,2048,384]{2,1,0:T(8,128)(2,1)}, bf16[2,2048,384]{2,1,0:T(8,128)(2,1)S(1)}, u32[]{:S(2)}, u32[]{:S(2)}) collective-permute-start(bf16[2,2048,384]{2,1,0:T(8,128)(2,1)} %refs_1_.1), channel_id=1, source_target_pairs={{0,1},{1,0},{2,3},{3,2},{4,5},{5,4},{6,7},{7,6},{8,9},{9,8},{10,11... | collective-permute-start | bytes 9437192 | tf_op jit(solution)/shard_map/ppermute | solution.py:27
  2.6 0.1 collective-permute-start.6
  2.7 0.4 collective-permute-start.8
  3.1 2.6 %collective-permute-start = (bf16[32,2176]{1,0:T(8,128)(2,1)S(1)}, bf16[32,2176]{1,0:T(8,128)(2,1)S(1)}, u32[]{:S(2)}, u32[]{:S(2)}) collective-permute-start(bf16[32,2176]{1,0:T(8,128)(2,1)S(1)} %pack.1.refs_0_), channel_id=1, source_target_pairs={{0,2},{4,0},{8,4},{12,8},{14,12},{10,14},{6,10},{2,6},{1,3},{5,1},... | collective-permute-start | bytes 417800 | tf_op jit(solution)/shard_map/ppermute | solution.py:23
  5.7 0.1 collective-permute-start.3
  5.8 3.8 %load.1 = (bf16[2,2048,384]{2,1,0:T(8,128)(2,1)S(1)}, bf16[2,2048,384]{2,1,0:T(8,128)(2,1)S(1)}, bf16[768,2048]{1,0:T(8,128)(2,1)S(1)}, bf16[128,2048]{1,0:T(8,128)(2,1)S(1)}) custom-call(bf16[32,2176]{1,0:T(8,128)(2,1)S(1)} %pack.1.refs_0_, bf16[2,2048,384]{2,1,0:T(8,128)(2,1)} %refs_1_.1, bf16[2,2048,384]{2,1,0:T(8,128)(2,1)} %refs_2_.1, ...), custom_call_target="tpu_custom_call" | custom-call | bytes 9437184 | tf_op jit(solution)/shard_map/load/pallas_call | solution.py:193
  9.6 0.5 %collective-permute-done.refs_1_ = bf16[32,2176]{1,0:T(8,128)(2,1)S(1)} collective-permute-done((bf16[32,2176]{1,0:T(8,128)(2,1)S(1)}, bf16[32,2176]{1,0:T(8,128)(2,1)S(1)}, u32[]{:S(2)}, u32[]{:S(2)}) %collective-permute-start) | collective-permute-done | bytes 139296 | tf_op jit(solution)/shard_map/ppermute | solution.py:23
  10.1 1.7 %collective-permute-start.1 = (bf16[32,2176]{1,0:T(8,128)(2,1)S(1)}, bf16[32,2176]{1,0:T(8,128)(2,1)S(1)}, u32[]{:S(2)}, u32[]{:S(2)}) collective-permute-start(bf16[32,2176]{1,0:T(8,128)(2,1)S(1)} %collective-permute-done.refs_1_), channel_id=1, source_target_pairs={{0,2},{4,0},{8,4},{12,8},{14,12},{10,14},{6,10},{2,6},{1,3},{5,1},... | collective-permute-start | bytes 417800 | tf_op jit(solution)/shard_map/ppermute | solution.py:23
  11.8 0.0 collective-permute-done.3.refs_7_.refs_2_
  11.8 0.3 collective-permute-start.4
  12.1 3.4 %collective-permute-done.1.refs_0_.refs_2_ = bf16[32,2176]{1,0:T(8,128)(2,1)S(1)} collective-permute-done((bf16[32,2176]{1,0:T(8,128)(2,1)S(1)}, bf16[32,2176]{1,0:T(8,128)(2,1)S(1)}, u32[]{:S(2)}, u32[]{:S(2)}) %collective-permute-start.1) | collective-permute-done | bytes 139296 | tf_op jit(solution)/shard_map/ppermute | solution.py:23
  15.5 0.0 collective-permute-done.2.refs_7_
  15.5 1.6 %collective-permute-start.7 = (bf16[32,2176]{1,0:T(8,128)(2,1)S(1)}, bf16[32,2176]{1,0:T(8,128)(2,1)S(1)}, u32[]{:S(2)}, u32[]{:S(2)}) collective-permute-start(bf16[32,2176]{1,0:T(8,128)(2,1)S(1)} %collective-permute-done.1.refs_0_.refs_2_), channel_id=1, source_target_pairs={{0,2},{4,0},{8,4},{12,8},{14,12},{10,14},{6,10},{2,6},{1,3},{5,1},... | collective-permute-start | bytes 417800 | tf_op jit(solution)/shard_map/ppermute | solution.py:23
  17.1 0.0 collective-permute-done.4.refs_2_.refs_6_
  17.1 0.4 collective-permute-start.5
  17.5 0.0 collective-permute-done.6.refs_8_
  17.5 3.0 %collective-permute-done.7.refs_3_ = bf16[32,2176]{1,0:T(8,128)(2,1)S(1)} collective-permute-done((bf16[32,2176]{1,0:T(8,128)(2,1)S(1)}, bf16[32,2176]{1,0:T(8,128)(2,1)S(1)}, u32[]{:S(2)}, u32[]{:S(2)}) %collective-permute-start.7) | collective-permute-done | bytes 139296 | tf_op jit(solution)/shard_map/ppermute | solution.py:23
  20.5 1.6 %collective-permute-start.9 = (bf16[32,2176]{1,0:T(8,128)(2,1)S(1)}, bf16[32,2176]{1,0:T(8,128)(2,1)S(1)}, u32[]{:S(2)}, u32[]{:S(2)}) collective-permute-start(bf16[32,2176]{1,0:T(8,128)(2,1)S(1)} %collective-permute-done.7.refs_3_), channel_id=1, source_target_pairs={{0,2},{4,0},{8,4},{12,8},{14,12},{10,14},{6,10},{2,6},{1,3},{5,1},... | collective-permute-start | bytes 417800 | tf_op jit(solution)/shard_map/ppermute | solution.py:23
  22.1 0.0 collective-permute-done.5.refs_1_.refs_5_
  22.1 0.0 collective-permute-done.8.refs_9_
  22.1 2.9 %experts.2 = (bf16[64,2048]{1,0:T(8,128)(2,1)S(1)}, bf16[64,2048]{1,0:T(8,128)(2,1)S(1)}) custom-call(s32[1]{0:T(128)} %bitcast._.place_ref, bf16[32,2176]{1,0:T(8,128)(2,1)S(1)} %collective-permute-done.1.refs_0_.refs_2_, bf16[32,2176]{1,0:T(8,128)(2,1)S(1)} %collective-permute-done.5.refs_1_.refs_5_, ...), custom_call_target="tpu_custom_call" | custom-call | flops 2415919104 | bytes 18874368 | tf_op jit(solution)/shard_map/experts/pallas_call | solution.py:244
  25.1 0.5 collective-permute-start.10
  25.5 1.6 %collective-permute-start.12 = (bf16[64,2048]{1,0:T(8,128)(2,1)S(1)}, bf16[64,2048]{1,0:T(8,128)(2,1)S(1)}, u32[]{:S(2)}, u32[]{:S(2)}) collective-permute-start(bf16[64,2048]{1,0:T(8,128)(2,1)S(1)} %get-tuple-element.43), channel_id=1, source_target_pairs={{0,2},{4,0},{8,4},{12,8},{14,12},{10,14},{6,10},{2,6},{1,3},{5,1},... | collective-permute-start | bytes 786440 | tf_op jit(solution)/shard_map/ppermute | solution.py:23
  27.1 0.0 collective-permute-done.9.refs_4_.refs_3_
  27.1 0.0 copy-done
  27.1 1.1 %frame_sums.2 = (bf16[64,1024]{1,0:T(8,128)(2,1)S(1)}, bf16[64,1024]{1,0:T(8,128)(2,1)S(1)}) custom-call(s32[1]{0:T(128)} %bitcast._.place_ref, bf16[32,2176]{1,0:T(8,128)(2,1)S(1)} %pack.1.refs_0_, bf16[32,2176]{1,0:T(8,128)(2,1)S(1)} %collective-permute-done.refs_1_, bf16[32,2176]{1,0:T(8,128)(2,1)S(1)} %collective-permute-done.1.refs_0_.refs_2_, ...), custom_call_target="tpu_custom_call" | custom-call | flops 536870912 | bytes 4194304 | tf_op jit(solution)/shard_map/frame_sums/pallas_call | solution.py:305
  28.2 0.5 collective-permute-start.11
  28.7 1.6 %collective-permute-start.13 = (bf16[64,1024]{1,0:T(8,128)(2,1)S(1)}, bf16[64,1024]{1,0:T(8,128)(2,1)S(1)}, u32[]{:S(2)}, u32[]{:S(2)}) collective-permute-start(bf16[64,1024]{1,0:T(8,128)(2,1)S(1)} %get-tuple-element.48), channel_id=1, source_target_pairs={{0,2},{4,0},{8,4},{12,8},{14,12},{10,14},{6,10},{2,6},{1,3},{5,1},... | collective-permute-start | bytes 393224 | tf_op jit(solution)/shard_map/ppermute | solution.py:23
  30.3 2.9 %experts.3.refs_0_ = bf16[128,2048]{1,0:T(8,128)(2,1)S(1)} custom-call(s32[1]{0:T(128)} %bitcast._.place_ref, bf16[32,2176]{1,0:T(8,128)(2,1)S(1)} %pack.1.refs_0_, bf16[32,2176]{1,0:T(8,128)(2,1)S(1)} %collective-permute-done.refs_1_, bf16[32,2176]{1,0:T(8,128)(2,1)S(1)} %collective-permute-done.3.refs_7_.refs_2_, ...), custom_call_target="tpu_custom_call" | custom-call | flops 2415919104 | bytes 18874368 | tf_op jit(solution)/shard_map/experts/pallas_call | solution.py:244
  33.2 0.0 copy-start.1
  33.2 0.0 copy-start.2
  33.2 0.0 copy-start.3
  33.2 0.0 copy-start.4
  33.2 1.1 %frame_sums.3.refs_2_.refs_1_ = bf16[128,1024]{1,0:T(8,128)(2,1)S(1)} custom-call(s32[1]{0:T(128)} %bitcast._.place_ref, bf16[32,2176]{1,0:T(8,128)(2,1)S(1)} %pack.1.refs_0_, bf16[32,2176]{1,0:T(8,128)(2,1)S(1)} %collective-permute-done.refs_1_, bf16[32,2176]{1,0:T(8,128)(2,1)S(1)} %collective-permute-done.1.refs_0_.refs_2_, ...), custom_call_target="tpu_custom_call" | custom-call | flops 536870912 | bytes 4194304 | tf_op jit(solution)/shard_map/frame_sums/pallas_call | solution.py:305
  34.3 0.0 collective-permute-done.10.refs_1_
  34.4 0.0 collective-permute-done.12.refs_4_
  34.4 0.0 collective-permute-done.11.refs_3_
  34.4 0.0 collective-permute-done.13.refs_5_
  34.4 0.2 join.1
  34.6 1.3 %collective-permute-start.14 = (bf16[32,3072]{1,0:T(8,128)(2,1)S(1)}, bf16[32,3072]{1,0:T(8,128)(2,1)S(1)}, u32[]{:S(2)}, u32[]{:S(2)}) collective-permute-start(bf16[32,3072]{1,0:T(8,128)(2,1)S(1)} %get-tuple-element.51), channel_id=1, source_target_pairs={{0,4},{4,8},{8,12},{12,14},{14,10},{10,6},{6,2},{2,0},{1,5},{5,9},... | collective-permute-start | bytes 589832 | tf_op jit(solution)/shard_map/ppermute | solution.py:23
  35.9 0.7 %collective-permute-start.15 = (bf16[32,3072]{1,0:T(8,128)(2,1)S(1)}, bf16[32,3072]{1,0:T(8,128)(2,1)S(1)}, u32[]{:S(2)}, u32[]{:S(2)}) collective-permute-start(bf16[32,3072]{1,0:T(8,128)(2,1)S(1)} %get-tuple-element.52), channel_id=1, source_target_pairs={{0,2},{4,0},{8,4},{12,8},{14,12},{10,14},{6,10},{2,6},{1,3},{5,1},... | collective-permute-start | bytes 589832 | tf_op jit(solution)/shard_map/ppermute | solution.py:23
  36.6 4.3 %collective-permute-start.16 = (bf16[32,3072]{1,0:T(8,128)(2,1)S(1)}, bf16[32,3072]{1,0:T(8,128)(2,1)S(1)}, u32[]{:S(2)}, u32[]{:S(2)}) collective-permute-start(bf16[32,3072]{1,0:T(8,128)(2,1)S(1)} %get-tuple-element.53), channel_id=1, source_target_pairs={{0,14},{4,10},{8,6},{12,2},{14,0},{10,4},{6,8},{2,12},{1,15},{5,11... | collective-permute-start | bytes 589832 | tf_op jit(solution)/shard_map/ppermute | solution.py:23
  40.9 1.5 %collective-permute-done.14.refs_2_ = bf16[32,3072]{1,0:T(8,128)(2,1)S(1)} collective-permute-done((bf16[32,3072]{1,0:T(8,128)(2,1)S(1)}, bf16[32,3072]{1,0:T(8,128)(2,1)S(1)}, u32[]{:S(2)}, u32[]{:S(2)}) %collective-permute-start.14) | collective-permute-done | bytes 196640 | tf_op jit(solution)/shard_map/ppermute | solution.py:23
  42.4 0.8 %collective-permute-done.15.refs_3_ = bf16[32,3072]{1,0:T(8,128)(2,1)S(1)} collective-permute-done((bf16[32,3072]{1,0:T(8,128)(2,1)S(1)}, bf16[32,3072]{1,0:T(8,128)(2,1)S(1)}, u32[]{:S(2)}, u32[]{:S(2)}) %collective-permute-start.15) | collective-permute-done | bytes 196640 | tf_op jit(solution)/shard_map/ppermute | solution.py:23
  43.2 2.3 %collective-permute-done.16.refs_4_ = bf16[32,3072]{1,0:T(8,128)(2,1)S(1)} collective-permute-done((bf16[32,3072]{1,0:T(8,128)(2,1)S(1)}, bf16[32,3072]{1,0:T(8,128)(2,1)S(1)}, u32[]{:S(2)}, u32[]{:S(2)}) %collective-permute-start.16) | collective-permute-done | bytes 196640 | tf_op jit(solution)/shard_map/ppermute | solution.py:23
  45.5 0.0 copy-done.2
  45.6 1.1 %finish.1 = (bf16[16,2,2048]{2,1,0:T(2,128)(2,1)}, bf16[16,2,512]{2,1,0:T(2,128)(2,1)}, bf16[6,16,1024]{2,1,0:T(8,128)(2,1)}) custom-call(bf16[128,2048]{1,0:T(8,128)(2,1)S(1)} %experts.3.refs_0_, bf16[128,1024]{1,0:T(8,128)(2,1)S(1)} %frame_sums.3.refs_2_.refs_1_, bf16[32,3072]{1,0:T(8,128)(2,1)S(1)} %collective-permute-done.14.refs_2_, ...), custom_call_target="tpu_custom_call" | custom-call | bytes 2097152 | tf_op jit(solution)/shard_map/finish/pallas_call | solution.py:356
  (4 shorter events, 0.0 us)
Async XLA Ops:
  2.1 13.4 %collective-permute-start.2 = (bf16[2,2048,384]{2,1,0:T(8,128)(2,1)}, bf16[2,2048,384]{2,1,0:T(8,128)(2,1)S(1)}, u32[]{:S(2)}, u32[]{:S(2)}) collective-permute-start(bf16[2,2048,384]{2,1,0:T(8,128)(2,1)} %refs_1_.1), channel_id=1, source_target_pairs={{0,1},{1,0},{2,3},{3,2},{4,5},{5,4},{6,7},{7,6},{8,9},{9,8},{10,11... | collective-permute-start | bytes 9437192 | tf_op jit(solution)/shard_map/ppermute | solution.py:27
  2.6 14.9 %collective-permute-start.6 = (bf16[2,2048,384]{2,1,0:T(8,128)(2,1)}, bf16[2,2048,384]{2,1,0:T(8,128)(2,1)S(1)}, u32[]{:S(2)}, u32[]{:S(2)}) collective-permute-start(bf16[2,2048,384]{2,1,0:T(8,128)(2,1)} %refs_2_.1), channel_id=1, source_target_pairs={{0,1},{1,0},{2,3},{3,2},{4,5},{5,4},{6,7},{7,6},{8,9},{9,8},{10,11... | collective-permute-start | bytes 9437192 | tf_op jit(solution)/shard_map/ppermute | solution.py:27
  2.7 19.4 %collective-permute-start.8 = (bf16[768,2048]{1,0:T(8,128)(2,1)}, bf16[768,2048]{1,0:T(8,128)(2,1)S(1)}, u32[]{:S(2)}, u32[]{:S(2)}) collective-permute-start(bf16[768,2048]{1,0:T(8,128)(2,1)} %bitcast.13), channel_id=1, source_target_pairs={{0,1},{1,0},{2,3},{3,2},{4,5},{5,4},{6,7},{7,6},{8,9},{9,8},{10,11... | collective-permute-start | bytes 9437192 | tf_op jit(solution)/shard_map/ppermute | solution.py:27
  3.1 6.9 %collective-permute-start = (bf16[32,2176]{1,0:T(8,128)(2,1)S(1)}, bf16[32,2176]{1,0:T(8,128)(2,1)S(1)}, u32[]{:S(2)}, u32[]{:S(2)}) collective-permute-start(bf16[32,2176]{1,0:T(8,128)(2,1)S(1)} %pack.1.refs_0_), channel_id=1, source_target_pairs={{0,2},{4,0},{8,4},{12,8},{14,12},{10,14},{6,10},{2,6},{1,3},{5,1},... | collective-permute-start | bytes 417800 | tf_op jit(solution)/shard_map/ppermute | solution.py:23
  5.7 6.0 %collective-permute-start.3 = (bf16[32,2176]{1,0:T(8,128)(2,1)S(1)}, bf16[32,2176]{1,0:T(8,128)(2,1)S(1)}, u32[]{:S(2)}, u32[]{:S(2)}) collective-permute-start(bf16[32,2176]{1,0:T(8,128)(2,1)S(1)} %pack.1.refs_0_), channel_id=1, source_target_pairs={{0,4},{4,8},{8,12},{12,14},{14,10},{10,6},{6,2},{2,0},{1,5},{5,9},... | collective-permute-start | bytes 417800 | tf_op jit(solution)/shard_map/ppermute | solution.py:23
  10.0 17.1 %copy-start = (bf16[16,128,1024]{2,1,0:T(8,128)(2,1)S(1)}, bf16[16,128,1024]{2,1,0:T(8,128)(2,1)}, u32[]{:S(2)}) copy-start(bf16[16,128,1024]{2,1,0:T(8,128)(2,1)} %param.21) | copy-start | bytes 12582916
  10.1 5.4 %collective-permute-start.1 = (bf16[32,2176]{1,0:T(8,128)(2,1)S(1)}, bf16[32,2176]{1,0:T(8,128)(2,1)S(1)}, u32[]{:S(2)}, u32[]{:S(2)}) collective-permute-start(bf16[32,2176]{1,0:T(8,128)(2,1)S(1)} %collective-permute-done.refs_1_), channel_id=1, source_target_pairs={{0,2},{4,0},{8,4},{12,8},{14,12},{10,14},{6,10},{2,6},{1,3},{5,1},... | collective-permute-start | bytes 417800 | tf_op jit(solution)/shard_map/ppermute | solution.py:23
  11.8 5.3 %collective-permute-start.4 = (bf16[32,2176]{1,0:T(8,128)(2,1)S(1)}, bf16[32,2176]{1,0:T(8,128)(2,1)S(1)}, u32[]{:S(2)}, u32[]{:S(2)}) collective-permute-start(bf16[32,2176]{1,0:T(8,128)(2,1)S(1)} %collective-permute-done.3.refs_7_.refs_2_), channel_id=1, source_target_pairs={{0,4},{4,8},{8,12},{12,14},{14,10},{10,6},{6,2},{2,0},{1,5},{5,9},... | collective-permute-start | bytes 417800 | tf_op jit(solution)/shard_map/ppermute | solution.py:23
  15.5 5.1 %collective-permute-start.7 = (bf16[32,2176]{1,0:T(8,128)(2,1)S(1)}, bf16[32,2176]{1,0:T(8,128)(2,1)S(1)}, u32[]{:S(2)}, u32[]{:S(2)}) collective-permute-start(bf16[32,2176]{1,0:T(8,128)(2,1)S(1)} %collective-permute-done.1.refs_0_.refs_2_), channel_id=1, source_target_pairs={{0,2},{4,0},{8,4},{12,8},{14,12},{10,14},{6,10},{2,6},{1,3},{5,1},... | collective-permute-start | bytes 417800 | tf_op jit(solution)/shard_map/ppermute | solution.py:23
  17.1 5.1 %collective-permute-start.5 = (bf16[32,2176]{1,0:T(8,128)(2,1)S(1)}, bf16[32,2176]{1,0:T(8,128)(2,1)S(1)}, u32[]{:S(2)}, u32[]{:S(2)}) collective-permute-start(bf16[32,2176]{1,0:T(8,128)(2,1)S(1)} %collective-permute-done.4.refs_2_.refs_6_), channel_id=1, source_target_pairs={{0,4},{4,8},{8,12},{12,14},{14,10},{10,6},{6,2},{2,0},{1,5},{5,9},... | collective-permute-start | bytes 417800 | tf_op jit(solution)/shard_map/ppermute | solution.py:23
  20.5 6.6 %collective-permute-start.9 = (bf16[32,2176]{1,0:T(8,128)(2,1)S(1)}, bf16[32,2176]{1,0:T(8,128)(2,1)S(1)}, u32[]{:S(2)}, u32[]{:S(2)}) collective-permute-start(bf16[32,2176]{1,0:T(8,128)(2,1)S(1)} %collective-permute-done.7.refs_3_), channel_id=1, source_target_pairs={{0,2},{4,0},{8,4},{12,8},{14,12},{10,14},{6,10},{2,6},{1,3},{5,1},... | collective-permute-start | bytes 417800 | tf_op jit(solution)/shard_map/ppermute | solution.py:23
  25.1 9.3 %collective-permute-start.10 = (bf16[64,2048]{1,0:T(8,128)(2,1)S(1)}, bf16[64,2048]{1,0:T(8,128)(2,1)S(1)}, u32[]{:S(2)}, u32[]{:S(2)}) collective-permute-start(bf16[64,2048]{1,0:T(8,128)(2,1)S(1)} %get-tuple-element.42), channel_id=1, source_target_pairs={{0,4},{4,8},{8,12},{12,14},{14,10},{10,6},{6,2},{2,0},{1,5},{5,9},... | collective-permute-start | bytes 786440 | tf_op jit(solution)/shard_map/ppermute | solution.py:23
  25.5 8.8 %collective-permute-start.12 = (bf16[64,2048]{1,0:T(8,128)(2,1)S(1)}, bf16[64,2048]{1,0:T(8,128)(2,1)S(1)}, u32[]{:S(2)}, u32[]{:S(2)}) collective-permute-start(bf16[64,2048]{1,0:T(8,128)(2,1)S(1)} %get-tuple-element.43), channel_id=1, source_target_pairs={{0,2},{4,0},{8,4},{12,8},{14,12},{10,14},{6,10},{2,6},{1,3},{5,1},... | collective-permute-start | bytes 786440 | tf_op jit(solution)/shard_map/ppermute | solution.py:23
  28.2 6.1 %collective-permute-start.11 = (bf16[64,1024]{1,0:T(8,128)(2,1)S(1)}, bf16[64,1024]{1,0:T(8,128)(2,1)S(1)}, u32[]{:S(2)}, u32[]{:S(2)}) collective-permute-start(bf16[64,1024]{1,0:T(8,128)(2,1)S(1)} %get-tuple-element.47), channel_id=1, source_target_pairs={{0,4},{4,8},{8,12},{12,14},{14,10},{10,6},{6,2},{2,0},{1,5},{5,9},... | collective-permute-start | bytes 393224 | tf_op jit(solution)/shard_map/ppermute | solution.py:23
  28.7 5.7 %collective-permute-start.13 = (bf16[64,1024]{1,0:T(8,128)(2,1)S(1)}, bf16[64,1024]{1,0:T(8,128)(2,1)S(1)}, u32[]{:S(2)}, u32[]{:S(2)}) collective-permute-start(bf16[64,1024]{1,0:T(8,128)(2,1)S(1)} %get-tuple-element.48), channel_id=1, source_target_pairs={{0,2},{4,0},{8,4},{12,8},{14,12},{10,14},{6,10},{2,6},{1,3},{5,1},... | collective-permute-start | bytes 393224 | tf_op jit(solution)/shard_map/ppermute | solution.py:23
  33.2 12.4 %copy-start.1 = (bf16[1024,512]{1,0:T(8,128)(2,1)S(1)}, bf16[1024,512]{1,0:T(8,128)(2,1)}, u32[]{:S(2)}) copy-start(bf16[1024,512]{1,0:T(8,128)(2,1)} %refs_8_.1) | copy-start | bytes 3145732
  33.2 12.3 %copy-start.2 = (bf16[16,6,1024]{2,0,1:T(8,128)(2,1)S(1)}, bf16[16,6,1024]{2,0,1:T(8,128)(2,1)}, u32[]{:S(2)}) copy-start(bf16[16,6,1024]{2,0,1:T(8,128)(2,1)} %param.22) | copy-start | bytes 589828
  33.2 12.3 %copy-start.3 = (f32[7,1024]{1,0:T(8,128)S(1)}, f32[7,1024]{1,0:T(8,128)}, u32[]{:S(2)}) copy-start(f32[7,1024]{1,0:T(8,128)} %refs_6_.1) | copy-start | bytes 86020
  33.2 12.3 %copy-start.4 = (f32[1024]{0:T(1024)S(1)}, f32[1024]{0:T(1024)}, u32[]{:S(2)}) copy-start(f32[1024]{0:T(1024)} %param.24) | copy-start | bytes 12292
  34.6 7.8 %collective-permute-start.14 = (bf16[32,3072]{1,0:T(8,128)(2,1)S(1)}, bf16[32,3072]{1,0:T(8,128)(2,1)S(1)}, u32[]{:S(2)}, u32[]{:S(2)}) collective-permute-start(bf16[32,3072]{1,0:T(8,128)(2,1)S(1)} %get-tuple-element.51), channel_id=1, source_target_pairs={{0,4},{4,8},{8,12},{12,14},{14,10},{10,6},{6,2},{2,0},{1,5},{5,9},... | collective-permute-start | bytes 589832 | tf_op jit(solution)/shard_map/ppermute | solution.py:23
  35.9 7.3 %collective-permute-start.15 = (bf16[32,3072]{1,0:T(8,128)(2,1)S(1)}, bf16[32,3072]{1,0:T(8,128)(2,1)S(1)}, u32[]{:S(2)}, u32[]{:S(2)}) collective-permute-start(bf16[32,3072]{1,0:T(8,128)(2,1)S(1)} %get-tuple-element.52), channel_id=1, source_target_pairs={{0,2},{4,0},{8,4},{12,8},{14,12},{10,14},{6,10},{2,6},{1,3},{5,1},... | collective-permute-start | bytes 589832 | tf_op jit(solution)/shard_map/ppermute | solution.py:23
  36.6 8.9 %collective-permute-start.16 = (bf16[32,3072]{1,0:T(8,128)(2,1)S(1)}, bf16[32,3072]{1,0:T(8,128)(2,1)S(1)}, u32[]{:S(2)}, u32[]{:S(2)}) collective-permute-start(bf16[32,3072]{1,0:T(8,128)(2,1)S(1)} %get-tuple-element.53), channel_id=1, source_target_pairs={{0,14},{4,10},{8,6},{12,2},{14,0},{10,4},{6,8},{2,12},{1,15},{5,11... | collective-permute-start | bytes 589832 | tf_op jit(solution)/shard_map/ppermute | solution.py:23

commit v9 on v8

--- a/solution.py
+++ b/solution.py
@@ -266,7 +266,8 @@
     count = len(sources)
     metas, (spread_ref, table_ref, *outs, hot_ref) = refs[:count], refs[count:]
     rows = metas[0].shape[0]
-    meta = jnp.concatenate([m[...] for m in metas], axis=0)
+    last = metas[0].shape[1] - spread_ref.shape[0]
+    meta = jnp.concatenate([m[:, last:] for m in metas], axis=0)
     column = lax.broadcasted_iota(jnp.int32, (8, meta.shape[1]), 1)
     digit = lax.broadcasted_iota(jnp.int32, (8, meta.shape[1]), 0)
     picks = jnp.where((column == slot_at + digit) & (digit < 2), 1.0, 0.0).astype(BF16)
@@ -296,17 +297,14 @@
 
 def frame_sums(blocks, order, split, place, code_table, spread, slot_at, sessions, steps):
     books, shard, channels = code_table.shape
-    meta_width = spread.shape[0]
     sources = list(range(len(blocks)))
-    rows, width = blocks[0].shape
+    rows = blocks[0].shape[0]
     total = rows * len(order)
-    block = pl.BlockSpec((rows, meta_width), lambda i: (0, width // meta_width - 1))
     vmem = pl.BlockSpec(memory_space=pltpu.VMEM)
     return pl.pallas_call(
         functools.partial(frames_kernel, slot_at, shard, sessions, steps, sources, order),
-        grid=(1,),
         out_shape=[jax.ShapeDtypeStruct((total // split, channels), BF16)] * split,
-        in_specs=[pl.BlockSpec(memory_space=pltpu.SMEM)] + [block] * len(sources) + [vmem] * 2,
+        in_specs=[pl.BlockSpec(memory_space=pltpu.SMEM)] + [vmem] * (len(sources) + 2),
         out_specs=[vmem] * split,
         scratch_shapes=[pltpu.VMEM((total, books * shard), BF16)],
         compiler_params=pltpu.CompilerParams(
@@ -451,7 +449,7 @@
     left = towards(near_rows, arrived, rows)
     right = towards(near_frames, frames_arrived, rows)
     one, minus, across = join(list(zip(left, right)), rows, width, code_table.shape[2])
-    last = [shift(one, 1), shift(minus, -1), shift(across, half)]
+    last = [shift(one, 1), shift(across, half), shift(minus, -1)]
     return finish(
         [(near_rows, 0)],
         [(near_frames, 0)],

time: 47.5 us -> 47.4 us (level)
  no operation moved by 1% of the time
where the time goes in v9:
time: 47.4 us; the launch traced here: 46.8 us
  starting transfers between devices  19.9 us (42%)
  Pallas kernels  14.4 us (30%)
  waiting for transfers between devices  11.7 us (25%)
  between operations  0.78 us (2%)
    ppermute x14, starting transfers between devices, shift(): return lax.ppermute(value, 'expert', pairs)  18.8 us
    ppermute x14, waiting for transfers between devices, shift(): return lax.ppermute(value, 'expert', pairs)  11.7 us
    pallas_call x2, Pallas kernels, experts(): pl.pallas_call(functools.partial(experts_kernel, width, lax.axis_size('ex...  5.75 us
    pallas_call x1, Pallas kernels, load(): pl.pallas_call(functools.partial(load_kernel, code_at, books, shard), out...  3.78 us
    pallas_call x2, Pallas kernels, frame_sums(): pl.pallas_call(functools.partial(frames_kernel, slot_at, shard, sessions,...  2.18 us
    pallas_call x1, Pallas kernels, pack(): pl.pallas_call(functools.partial(pack_kernel, columns, n_wave), out_shape...  1.46 us
    pallas_call x1, Pallas kernels, finish(): pl.pallas_call(functools.partial(finish_kernel, *numbered[0][0], width),...  1.1 us
    ppermute x3, starting transfers between devices, swap_wave(): return lax.ppermute(value, 'wave', [(0, 1), (1, 0)])  1.03 us
  transfers between devices with their start and end apart: 17, of which 6 were waited for; matrix products, arithmetic and copies ran while one was open for 0% of the time, Pallas kernels for 25%

profile of v9, /device:TPU:0, one launch (start us, length us, event | category | flops | bytes accessed | tf_op | source)
XLA Modules:
  0.0 46.8 jit_solution(4201537085434143721)
XLA Ops:
  0.6 1.5 %pack.1.refs_0_ = bf16[32,2176]{1,0:T(8,128)(2,1)S(1)} custom-call(s32[1]{0:T(128)} %bitcast._.place_ref, bf16[16,2,2048]{2,1,0:T(2,128)(2,1)} %refs_0_.1, s32[2,8,16]{2,1,0:T(8,128)} %bitcast.15, f32[2,8,16]{2,1,0:T(8,128)} %bitcast.16, s32[16,2,16]{2,1,0:T(2,128)} %refs_3_.1, s32[1,16]{1,0:T(1,128)} %bitcast.17), custom_call_target="tpu_custom_call" | custom-call | tf_op jit(solution)/shard_map/pack/pallas_call | solution.py:161
  2.1 0.5 %collective-permute-start.2 = (bf16[2,2048,384]{2,1,0:T(8,128)(2,1)}, bf16[2,2048,384]{2,1,0:T(8,128)(2,1)S(1)}, u32[]{:S(2)}, u32[]{:S(2)}) collective-permute-start(bf16[2,2048,384]{2,1,0:T(8,128)(2,1)} %refs_1_.1), channel_id=1, source_target_pairs={{0,1},{1,0},{2,3},{3,2},{4,5},{5,4},{6,7},{7,6},{8,9},{9,8},{10,11... | collective-permute-start | bytes 9437192 | tf_op jit(solution)/shard_map/ppermute | solution.py:27
  2.6 0.1 collective-permute-start.6
  2.7 0.4 collective-permute-start.8
  3.1 2.6 %collective-permute-start = (bf16[32,2176]{1,0:T(8,128)(2,1)S(1)}, bf16[32,2176]{1,0:T(8,128)(2,1)S(1)}, u32[]{:S(2)}, u32[]{:S(2)}) collective-permute-start(bf16[32,2176]{1,0:T(8,128)(2,1)S(1)} %pack.1.refs_0_), channel_id=1, source_target_pairs={{0,2},{4,0},{8,4},{12,8},{14,12},{10,14},{6,10},{2,6},{1,3},{5,1},... | collective-permute-start | bytes 417800 | tf_op jit(solution)/shard_map/ppermute | solution.py:23
  5.7 0.1 collective-permute-start.3
  5.8 3.8 %load.1 = (bf16[2,2048,384]{2,1,0:T(8,128)(2,1)S(1)}, bf16[2,2048,384]{2,1,0:T(8,128)(2,1)S(1)}, bf16[768,2048]{1,0:T(8,128)(2,1)S(1)}, bf16[128,2048]{1,0:T(8,128)(2,1)S(1)}) custom-call(bf16[32,2176]{1,0:T(8,128)(2,1)S(1)} %pack.1.refs_0_, bf16[2,2048,384]{2,1,0:T(8,128)(2,1)} %refs_1_.1, bf16[2,2048,384]{2,1,0:T(8,128)(2,1)} %refs_2_.1, ...), custom_call_target="tpu_custom_call" | custom-call | bytes 9437184 | tf_op jit(solution)/shard_map/load/pallas_call | solution.py:193
  9.6 0.5 %collective-permute-done.refs_1_ = bf16[32,2176]{1,0:T(8,128)(2,1)S(1)} collective-permute-done((bf16[32,2176]{1,0:T(8,128)(2,1)S(1)}, bf16[32,2176]{1,0:T(8,128)(2,1)S(1)}, u32[]{:S(2)}, u32[]{:S(2)}) %collective-permute-start) | collective-permute-done | bytes 139296 | tf_op jit(solution)/shard_map/ppermute | solution.py:23
  10.1 1.7 %collective-permute-start.1 = (bf16[32,2176]{1,0:T(8,128)(2,1)S(1)}, bf16[32,2176]{1,0:T(8,128)(2,1)S(1)}, u32[]{:S(2)}, u32[]{:S(2)}) collective-permute-start(bf16[32,2176]{1,0:T(8,128)(2,1)S(1)} %collective-permute-done.refs_1_), channel_id=1, source_target_pairs={{0,2},{4,0},{8,4},{12,8},{14,12},{10,14},{6,10},{2,6},{1,3},{5,1},... | collective-permute-start | bytes 417800 | tf_op jit(solution)/shard_map/ppermute | solution.py:23
  11.8 0.0 collective-permute-done.3.refs_7_.refs_2_
  11.8 0.3 collective-permute-start.4
  12.1 3.4 %collective-permute-done.1.refs_0_.refs_2_ = bf16[32,2176]{1,0:T(8,128)(2,1)S(1)} collective-permute-done((bf16[32,2176]{1,0:T(8,128)(2,1)S(1)}, bf16[32,2176]{1,0:T(8,128)(2,1)S(1)}, u32[]{:S(2)}, u32[]{:S(2)}) %collective-permute-start.1) | collective-permute-done | bytes 139296 | tf_op jit(solution)/shard_map/ppermute | solution.py:23
  15.5 0.0 collective-permute-done.2.refs_7_
  15.5 1.6 %collective-permute-start.7 = (bf16[32,2176]{1,0:T(8,128)(2,1)S(1)}, bf16[32,2176]{1,0:T(8,128)(2,1)S(1)}, u32[]{:S(2)}, u32[]{:S(2)}) collective-permute-start(bf16[32,2176]{1,0:T(8,128)(2,1)S(1)} %collective-permute-done.1.refs_0_.refs_2_), channel_id=1, source_target_pairs={{0,2},{4,0},{8,4},{12,8},{14,12},{10,14},{6,10},{2,6},{1,3},{5,1},... | collective-permute-start | bytes 417800 | tf_op jit(solution)/shard_map/ppermute | solution.py:23
  17.1 0.0 collective-permute-done.4.refs_2_.refs_6_
  17.1 0.4 collective-permute-start.5
  17.5 0.0 collective-permute-done.6.refs_8_
  17.5 3.0 %collective-permute-done.7.refs_3_ = bf16[32,2176]{1,0:T(8,128)(2,1)S(1)} collective-permute-done((bf16[32,2176]{1,0:T(8,128)(2,1)S(1)}, bf16[32,2176]{1,0:T(8,128)(2,1)S(1)}, u32[]{:S(2)}, u32[]{:S(2)}) %collective-permute-start.7) | collective-permute-done | bytes 139296 | tf_op jit(solution)/shard_map/ppermute | solution.py:23
  20.5 1.6 %collective-permute-start.9 = (bf16[32,2176]{1,0:T(8,128)(2,1)S(1)}, bf16[32,2176]{1,0:T(8,128)(2,1)S(1)}, u32[]{:S(2)}, u32[]{:S(2)}) collective-permute-start(bf16[32,2176]{1,0:T(8,128)(2,1)S(1)} %collective-permute-done.7.refs_3_), channel_id=1, source_target_pairs={{0,2},{4,0},{8,4},{12,8},{14,12},{10,14},{6,10},{2,6},{1,3},{5,1},... | collective-permute-start | bytes 417800 | tf_op jit(solution)/shard_map/ppermute | solution.py:23
  22.1 0.0 collective-permute-done.5.refs_1_.refs_5_
  22.1 0.0 collective-permute-done.8.refs_9_
  22.1 2.9 %experts.2 = (bf16[64,2048]{1,0:T(8,128)(2,1)S(1)}, bf16[64,2048]{1,0:T(8,128)(2,1)S(1)}) custom-call(s32[1]{0:T(128)} %bitcast._.place_ref, bf16[32,2176]{1,0:T(8,128)(2,1)S(1)} %collective-permute-done.1.refs_0_.refs_2_, bf16[32,2176]{1,0:T(8,128)(2,1)S(1)} %collective-permute-done.5.refs_1_.refs_5_, ...), custom_call_target="tpu_custom_call" | custom-call | flops 2415919104 | bytes 18874368 | tf_op jit(solution)/shard_map/experts/pallas_call | solution.py:244
  25.1 0.5 collective-permute-start.10
  25.5 1.6 %collective-permute-start.12 = (bf16[64,2048]{1,0:T(8,128)(2,1)S(1)}, bf16[64,2048]{1,0:T(8,128)(2,1)S(1)}, u32[]{:S(2)}, u32[]{:S(2)}) collective-permute-start(bf16[64,2048]{1,0:T(8,128)(2,1)S(1)} %get-tuple-element.43), channel_id=1, source_target_pairs={{0,2},{4,0},{8,4},{12,8},{14,12},{10,14},{6,10},{2,6},{1,3},{5,1},... | collective-permute-start | bytes 786440 | tf_op jit(solution)/shard_map/ppermute | solution.py:23
  27.1 0.0 collective-permute-done.9.refs_4_.refs_3_
  27.1 0.0 copy-done
  27.1 1.1 %frame_sums.2 = (bf16[64,1024]{1,0:T(8,128)(2,1)S(1)}, bf16[64,1024]{1,0:T(8,128)(2,1)S(1)}) custom-call(s32[1]{0:T(128)} %bitcast._.place_ref, bf16[32,2176]{1,0:T(8,128)(2,1)S(1)} %pack.1.refs_0_, bf16[32,2176]{1,0:T(8,128)(2,1)S(1)} %collective-permute-done.refs_1_, bf16[32,2176]{1,0:T(8,128)(2,1)S(1)} %collective-permute-done.1.refs_0_.refs_2_, ...), custom_call_target="tpu_custom_call" | custom-call | flops 536870912 | bytes 4194304 | tf_op jit(solution)/shard_map/frame_sums/pallas_call | solution.py:304
  28.2 0.5 collective-permute-start.11
  28.7 1.6 %collective-permute-start.13 = (bf16[64,1024]{1,0:T(8,128)(2,1)S(1)}, bf16[64,1024]{1,0:T(8,128)(2,1)S(1)}, u32[]{:S(2)}, u32[]{:S(2)}) collective-permute-start(bf16[64,1024]{1,0:T(8,128)(2,1)S(1)} %get-tuple-element.48), channel_id=1, source_target_pairs={{0,2},{4,0},{8,4},{12,8},{14,12},{10,14},{6,10},{2,6},{1,3},{5,1},... | collective-permute-start | bytes 393224 | tf_op jit(solution)/shard_map/ppermute | solution.py:23
  30.3 2.9 %experts.3.refs_0_ = bf16[128,2048]{1,0:T(8,128)(2,1)S(1)} custom-call(s32[1]{0:T(128)} %bitcast._.place_ref, bf16[32,2176]{1,0:T(8,128)(2,1)S(1)} %pack.1.refs_0_, bf16[32,2176]{1,0:T(8,128)(2,1)S(1)} %collective-permute-done.refs_1_, bf16[32,2176]{1,0:T(8,128)(2,1)S(1)} %collective-permute-done.3.refs_7_.refs_2_, ...), custom_call_target="tpu_custom_call" | custom-call | flops 2415919104 | bytes 18874368 | tf_op jit(solution)/shard_map/experts/pallas_call | solution.py:244
  33.2 0.0 copy-start.1
  33.2 0.0 copy-start.2
  33.2 0.0 copy-start.3
  33.2 0.0 copy-start.4
  33.2 1.1 %frame_sums.3.refs_2_.refs_1_ = bf16[128,1024]{1,0:T(8,128)(2,1)S(1)} custom-call(s32[1]{0:T(128)} %bitcast._.place_ref, bf16[32,2176]{1,0:T(8,128)(2,1)S(1)} %pack.1.refs_0_, bf16[32,2176]{1,0:T(8,128)(2,1)S(1)} %collective-permute-done.refs_1_, bf16[32,2176]{1,0:T(8,128)(2,1)S(1)} %collective-permute-done.1.refs_0_.refs_2_, ...), custom_call_target="tpu_custom_call" | custom-call | flops 536870912 | bytes 4194304 | tf_op jit(solution)/shard_map/frame_sums/pallas_call | solution.py:304
  34.3 0.0 collective-permute-done.10.refs_1_
  34.3 0.0 collective-permute-done.12.refs_4_
  34.3 0.0 collective-permute-done.11.refs_3_
  34.4 0.0 collective-permute-done.13.refs_5_
  34.4 0.2 join.1
  34.5 1.4 %collective-permute-start.14 = (bf16[32,3072]{1,0:T(8,128)(2,1)S(1)}, bf16[32,3072]{1,0:T(8,128)(2,1)S(1)}, u32[]{:S(2)}, u32[]{:S(2)}) collective-permute-start(bf16[32,3072]{1,0:T(8,128)(2,1)S(1)} %get-tuple-element.51), channel_id=1, source_target_pairs={{0,4},{4,8},{8,12},{12,14},{14,10},{10,6},{6,2},{2,0},{1,5},{5,9},... | collective-permute-start | bytes 589832 | tf_op jit(solution)/shard_map/ppermute | solution.py:23
  35.9 3.7 %collective-permute-start.15 = (bf16[32,3072]{1,0:T(8,128)(2,1)S(1)}, bf16[32,3072]{1,0:T(8,128)(2,1)S(1)}, u32[]{:S(2)}, u32[]{:S(2)}) collective-permute-start(bf16[32,3072]{1,0:T(8,128)(2,1)S(1)} %get-tuple-element.52), channel_id=1, source_target_pairs={{0,14},{4,10},{8,6},{12,2},{14,0},{10,4},{6,8},{2,12},{1,15},{5,11... | collective-permute-start | bytes 589832 | tf_op jit(solution)/shard_map/ppermute | solution.py:23
  39.6 1.3 %collective-permute-start.16 = (bf16[32,3072]{1,0:T(8,128)(2,1)S(1)}, bf16[32,3072]{1,0:T(8,128)(2,1)S(1)}, u32[]{:S(2)}, u32[]{:S(2)}) collective-permute-start(bf16[32,3072]{1,0:T(8,128)(2,1)S(1)} %get-tuple-element.53), channel_id=1, source_target_pairs={{0,2},{4,0},{8,4},{12,8},{14,12},{10,14},{6,10},{2,6},{1,3},{5,1},... | collective-permute-start | bytes 589832 | tf_op jit(solution)/shard_map/ppermute | solution.py:23
  40.9 1.5 %collective-permute-done.14.refs_2_ = bf16[32,3072]{1,0:T(8,128)(2,1)S(1)} collective-permute-done((bf16[32,3072]{1,0:T(8,128)(2,1)S(1)}, bf16[32,3072]{1,0:T(8,128)(2,1)S(1)}, u32[]{:S(2)}, u32[]{:S(2)}) %collective-permute-start.14) | collective-permute-done | bytes 196640 | tf_op jit(solution)/shard_map/ppermute | solution.py:23
  42.4 3.1 %collective-permute-done.15.refs_3_ = bf16[32,3072]{1,0:T(8,128)(2,1)S(1)} collective-permute-done((bf16[32,3072]{1,0:T(8,128)(2,1)S(1)}, bf16[32,3072]{1,0:T(8,128)(2,1)S(1)}, u32[]{:S(2)}, u32[]{:S(2)}) %collective-permute-start.15) | collective-permute-done | bytes 196640 | tf_op jit(solution)/shard_map/ppermute | solution.py:23
  45.5 0.2 collective-permute-done.16.refs_4_
  45.7 0.0 copy-done.4
  45.7 1.1 %finish.1 = (bf16[16,2,2048]{2,1,0:T(2,128)(2,1)}, bf16[16,2,512]{2,1,0:T(2,128)(2,1)}, bf16[6,16,1024]{2,1,0:T(8,128)(2,1)}) custom-call(bf16[128,2048]{1,0:T(8,128)(2,1)S(1)} %experts.3.refs_0_, bf16[128,1024]{1,0:T(8,128)(2,1)S(1)} %frame_sums.3.refs_2_.refs_1_, bf16[32,3072]{1,0:T(8,128)(2,1)S(1)} %collective-permute-done.14.refs_2_, ...), custom_call_target="tpu_custom_call" | custom-call | bytes 2097152 | tf_op jit(solution)/shard_map/finish/pallas_call | solution.py:354
  (4 shorter events, 0.0 us)
Async XLA Ops:
  2.1 13.4 %collective-permute-start.2 = (bf16[2,2048,384]{2,1,0:T(8,128)(2,1)}, bf16[2,2048,384]{2,1,0:T(8,128)(2,1)S(1)}, u32[]{:S(2)}, u32[]{:S(2)}) collective-permute-start(bf16[2,2048,384]{2,1,0:T(8,128)(2,1)} %refs_1_.1), channel_id=1, source_target_pairs={{0,1},{1,0},{2,3},{3,2},{4,5},{5,4},{6,7},{7,6},{8,9},{9,8},{10,11... | collective-permute-start | bytes 9437192 | tf_op jit(solution)/shard_map/ppermute | solution.py:27
  2.6 14.9 %collective-permute-start.6 = (bf16[2,2048,384]{2,1,0:T(8,128)(2,1)}, bf16[2,2048,384]{2,1,0:T(8,128)(2,1)S(1)}, u32[]{:S(2)}, u32[]{:S(2)}) collective-permute-start(bf16[2,2048,384]{2,1,0:T(8,128)(2,1)} %refs_2_.1), channel_id=1, source_target_pairs={{0,1},{1,0},{2,3},{3,2},{4,5},{5,4},{6,7},{7,6},{8,9},{9,8},{10,11... | collective-permute-start | bytes 9437192 | tf_op jit(solution)/shard_map/ppermute | solution.py:27
  2.7 19.4 %collective-permute-start.8 = (bf16[768,2048]{1,0:T(8,128)(2,1)}, bf16[768,2048]{1,0:T(8,128)(2,1)S(1)}, u32[]{:S(2)}, u32[]{:S(2)}) collective-permute-start(bf16[768,2048]{1,0:T(8,128)(2,1)} %bitcast.13), channel_id=1, source_target_pairs={{0,1},{1,0},{2,3},{3,2},{4,5},{5,4},{6,7},{7,6},{8,9},{9,8},{10,11... | collective-permute-start | bytes 9437192 | tf_op jit(solution)/shard_map/ppermute | solution.py:27
  3.1 6.9 %collective-permute-start = (bf16[32,2176]{1,0:T(8,128)(2,1)S(1)}, bf16[32,2176]{1,0:T(8,128)(2,1)S(1)}, u32[]{:S(2)}, u32[]{:S(2)}) collective-permute-start(bf16[32,2176]{1,0:T(8,128)(2,1)S(1)} %pack.1.refs_0_), channel_id=1, source_target_pairs={{0,2},{4,0},{8,4},{12,8},{14,12},{10,14},{6,10},{2,6},{1,3},{5,1},... | collective-permute-start | bytes 417800 | tf_op jit(solution)/shard_map/ppermute | solution.py:23
  5.7 6.0 %collective-permute-start.3 = (bf16[32,2176]{1,0:T(8,128)(2,1)S(1)}, bf16[32,2176]{1,0:T(8,128)(2,1)S(1)}, u32[]{:S(2)}, u32[]{:S(2)}) collective-permute-start(bf16[32,2176]{1,0:T(8,128)(2,1)S(1)} %pack.1.refs_0_), channel_id=1, source_target_pairs={{0,4},{4,8},{8,12},{12,14},{14,10},{10,6},{6,2},{2,0},{1,5},{5,9},... | collective-permute-start | bytes 417800 | tf_op jit(solution)/shard_map/ppermute | solution.py:23
  10.0 17.1 %copy-start = (bf16[16,128,1024]{2,1,0:T(8,128)(2,1)S(1)}, bf16[16,128,1024]{2,1,0:T(8,128)(2,1)}, u32[]{:S(2)}) copy-start(bf16[16,128,1024]{2,1,0:T(8,128)(2,1)} %param.21) | copy-start | bytes 12582916
  10.1 5.4 %collective-permute-start.1 = (bf16[32,2176]{1,0:T(8,128)(2,1)S(1)}, bf16[32,2176]{1,0:T(8,128)(2,1)S(1)}, u32[]{:S(2)}, u32[]{:S(2)}) collective-permute-start(bf16[32,2176]{1,0:T(8,128)(2,1)S(1)} %collective-permute-done.refs_1_), channel_id=1, source_target_pairs={{0,2},{4,0},{8,4},{12,8},{14,12},{10,14},{6,10},{2,6},{1,3},{5,1},... | collective-permute-start | bytes 417800 | tf_op jit(solution)/shard_map/ppermute | solution.py:23
  11.8 5.3 %collective-permute-start.4 = (bf16[32,2176]{1,0:T(8,128)(2,1)S(1)}, bf16[32,2176]{1,0:T(8,128)(2,1)S(1)}, u32[]{:S(2)}, u32[]{:S(2)}) collective-permute-start(bf16[32,2176]{1,0:T(8,128)(2,1)S(1)} %collective-permute-done.3.refs_7_.refs_2_), channel_id=1, source_target_pairs={{0,4},{4,8},{8,12},{12,14},{14,10},{10,6},{6,2},{2,0},{1,5},{5,9},... | collective-permute-start | bytes 417800 | tf_op jit(solution)/shard_map/ppermute | solution.py:23
  15.5 5.1 %collective-permute-start.7 = (bf16[32,2176]{1,0:T(8,128)(2,1)S(1)}, bf16[32,2176]{1,0:T(8,128)(2,1)S(1)}, u32[]{:S(2)}, u32[]{:S(2)}) collective-permute-start(bf16[32,2176]{1,0:T(8,128)(2,1)S(1)} %collective-permute-done.1.refs_0_.refs_2_), channel_id=1, source_target_pairs={{0,2},{4,0},{8,4},{12,8},{14,12},{10,14},{6,10},{2,6},{1,3},{5,1},... | collective-permute-start | bytes 417800 | tf_op jit(solution)/shard_map/ppermute | solution.py:23
  17.1 5.1 %collective-permute-start.5 = (bf16[32,2176]{1,0:T(8,128)(2,1)S(1)}, bf16[32,2176]{1,0:T(8,128)(2,1)S(1)}, u32[]{:S(2)}, u32[]{:S(2)}) collective-permute-start(bf16[32,2176]{1,0:T(8,128)(2,1)S(1)} %collective-permute-done.4.refs_2_.refs_6_), channel_id=1, source_target_pairs={{0,4},{4,8},{8,12},{12,14},{14,10},{10,6},{6,2},{2,0},{1,5},{5,9},... | collective-permute-start | bytes 417800 | tf_op jit(solution)/shard_map/ppermute | solution.py:23
  20.5 6.6 %collective-permute-start.9 = (bf16[32,2176]{1,0:T(8,128)(2,1)S(1)}, bf16[32,2176]{1,0:T(8,128)(2,1)S(1)}, u32[]{:S(2)}, u32[]{:S(2)}) collective-permute-start(bf16[32,2176]{1,0:T(8,128)(2,1)S(1)} %collective-permute-done.7.refs_3_), channel_id=1, source_target_pairs={{0,2},{4,0},{8,4},{12,8},{14,12},{10,14},{6,10},{2,6},{1,3},{5,1},... | collective-permute-start | bytes 417800 | tf_op jit(solution)/shard_map/ppermute | solution.py:23
  25.1 9.3 %collective-permute-start.10 = (bf16[64,2048]{1,0:T(8,128)(2,1)S(1)}, bf16[64,2048]{1,0:T(8,128)(2,1)S(1)}, u32[]{:S(2)}, u32[]{:S(2)}) collective-permute-start(bf16[64,2048]{1,0:T(8,128)(2,1)S(1)} %get-tuple-element.42), channel_id=1, source_target_pairs={{0,4},{4,8},{8,12},{12,14},{14,10},{10,6},{6,2},{2,0},{1,5},{5,9},... | collective-permute-start | bytes 786440 | tf_op jit(solution)/shard_map/ppermute | solution.py:23
  25.5 8.8 %collective-permute-start.12 = (bf16[64,2048]{1,0:T(8,128)(2,1)S(1)}, bf16[64,2048]{1,0:T(8,128)(2,1)S(1)}, u32[]{:S(2)}, u32[]{:S(2)}) collective-permute-start(bf16[64,2048]{1,0:T(8,128)(2,1)S(1)} %get-tuple-element.43), channel_id=1, source_target_pairs={{0,2},{4,0},{8,4},{12,8},{14,12},{10,14},{6,10},{2,6},{1,3},{5,1},... | collective-permute-start | bytes 786440 | tf_op jit(solution)/shard_map/ppermute | solution.py:23
  28.2 6.1 %collective-permute-start.11 = (bf16[64,1024]{1,0:T(8,128)(2,1)S(1)}, bf16[64,1024]{1,0:T(8,128)(2,1)S(1)}, u32[]{:S(2)}, u32[]{:S(2)}) collective-permute-start(bf16[64,1024]{1,0:T(8,128)(2,1)S(1)} %get-tuple-element.47), channel_id=1, source_target_pairs={{0,4},{4,8},{8,12},{12,14},{14,10},{10,6},{6,2},{2,0},{1,5},{5,9},... | collective-permute-start | bytes 393224 | tf_op jit(solution)/shard_map/ppermute | solution.py:23
  28.7 5.7 %collective-permute-start.13 = (bf16[64,1024]{1,0:T(8,128)(2,1)S(1)}, bf16[64,1024]{1,0:T(8,128)(2,1)S(1)}, u32[]{:S(2)}, u32[]{:S(2)}) collective-permute-start(bf16[64,1024]{1,0:T(8,128)(2,1)S(1)} %get-tuple-element.48), channel_id=1, source_target_pairs={{0,2},{4,0},{8,4},{12,8},{14,12},{10,14},{6,10},{2,6},{1,3},{5,1},... | collective-permute-start | bytes 393224 | tf_op jit(solution)/shard_map/ppermute | solution.py:23
  33.2 12.6 %copy-start.1 = (bf16[1024,512]{1,0:T(8,128)(2,1)S(1)}, bf16[1024,512]{1,0:T(8,128)(2,1)}, u32[]{:S(2)}) copy-start(bf16[1024,512]{1,0:T(8,128)(2,1)} %refs_8_.1) | copy-start | bytes 3145732
  33.2 12.5 %copy-start.2 = (bf16[16,6,1024]{2,0,1:T(8,128)(2,1)S(1)}, bf16[16,6,1024]{2,0,1:T(8,128)(2,1)}, u32[]{:S(2)}) copy-start(bf16[16,6,1024]{2,0,1:T(8,128)(2,1)} %param.22) | copy-start | bytes 589828
  33.2 12.5 %copy-start.3 = (f32[7,1024]{1,0:T(8,128)S(1)}, f32[7,1024]{1,0:T(8,128)}, u32[]{:S(2)}) copy-start(f32[7,1024]{1,0:T(8,128)} %refs_6_.1) | copy-start | bytes 86020
  33.2 12.5 %copy-start.4 = (f32[1024]{0:T(1024)S(1)}, f32[1024]{0:T(1024)}, u32[]{:S(2)}) copy-start(f32[1024]{0:T(1024)} %param.24) | copy-start | bytes 12292
  34.5 7.8 %collective-permute-start.14 = (bf16[32,3072]{1,0:T(8,128)(2,1)S(1)}, bf16[32,3072]{1,0:T(8,128)(2,1)S(1)}, u32[]{:S(2)}, u32[]{:S(2)}) collective-permute-start(bf16[32,3072]{1,0:T(8,128)(2,1)S(1)} %get-tuple-element.51), channel_id=1, source_target_pairs={{0,4},{4,8},{8,12},{12,14},{14,10},{10,6},{6,2},{2,0},{1,5},{5,9},... | collective-permute-start | bytes 589832 | tf_op jit(solution)/shard_map/ppermute | solution.py:23
  35.9 9.6 %collective-permute-start.15 = (bf16[32,3072]{1,0:T(8,128)(2,1)S(1)}, bf16[32,3072]{1,0:T(8,128)(2,1)S(1)}, u32[]{:S(2)}, u32[]{:S(2)}) collective-permute-start(bf16[32,3072]{1,0:T(8,128)(2,1)S(1)} %get-tuple-element.52), channel_id=1, source_target_pairs={{0,14},{4,10},{8,6},{12,2},{14,0},{10,4},{6,8},{2,12},{1,15},{5,11... | collective-permute-start | bytes 589832 | tf_op jit(solution)/shard_map/ppermute | solution.py:23
  39.6 6.1 %collective-permute-start.16 = (bf16[32,3072]{1,0:T(8,128)(2,1)S(1)}, bf16[32,3072]{1,0:T(8,128)(2,1)S(1)}, u32[]{:S(2)}, u32[]{:S(2)}) collective-permute-start(bf16[32,3072]{1,0:T(8,128)(2,1)S(1)} %get-tuple-element.53), channel_id=1, source_target_pairs={{0,2},{4,0},{8,4},{12,8},{14,12},{10,14},{6,10},{2,6},{1,3},{5,1},... | collective-permute-start | bytes 589832 | tf_op jit(solution)/shard_map/ppermute | solution.py:23

commit v10 on v8

--- a/solution.py
+++ b/solution.py
@@ -321,6 +321,49 @@
     )(place, *[blocks[k] for k in sources], spread, code_table.reshape(books * shard, channels))
 
 
+def near_kernel(for_experts, for_frames, near, width, place_ref, *refs):
+    count = len(for_frames[-2])
+    sources, weights = refs[:count], refs[count:-7]
+    spread_ref, table_ref, rows_out, frames_out, rows_ref, act_ref, hot_ref = refs[-7:]
+    blocks = [sources[k] for k in near]
+    metas = [m.at[:, width : m.shape[1]] for m in sources]
+    experts_kernel(*for_experts, place_ref, *blocks, *weights, rows_out, rows_ref, act_ref)
+    frames_kernel(*for_frames, place_ref, *metas, spread_ref, table_ref, frames_out, hot_ref)
+
+
+def near_sums(blocks, near, place, held, code_table, spread, slot_at, sessions, steps):
+    local, width, units = held[0][0].shape
+    books, shard, channels = code_table.shape
+    rows = blocks[0].shape[0]
+    total = rows * len(near)
+    vmem = pl.BlockSpec(memory_space=pltpu.VMEM)
+    weights = [v for part in held for v in part]
+    sources = [blocks[k] for k in range(len(blocks))]
+    for_experts = (width, lax.axis_size("expert") * local, len(near), 1)
+    for_frames = (slot_at, shard, sessions, steps, list(range(len(sources))), near)
+    return pl.pallas_call(
+        functools.partial(near_kernel, for_experts, for_frames, near, width),
+        out_shape=[jax.ShapeDtypeStruct((total, size), BF16) for size in (width, channels)],
+        in_specs=[pl.BlockSpec(memory_space=pltpu.SMEM)]
+        + [vmem] * (len(sources) + len(weights) + 2),
+        out_specs=[vmem] * 2,
+        scratch_shapes=[
+            pltpu.VMEM((total, width), BF16),
+            pltpu.VMEM((total, local * units), BF16),
+            pltpu.VMEM((total, books * shard), BF16),
+        ],
+        compiler_params=pltpu.CompilerParams(
+            vmem_limit_bytes=2 * VMEM_LIMIT + 12 * total * rows * len(sources)
+        ),
+        cost_estimate=pl.CostEstimate(
+            flops=6 * total * width * units * local * len(held),
+            bytes_accessed=2 * sum(v.size for v in weights),
+            transcendentals=total * units * local * len(held),
+        ),
+        name="near_sums",
+    )(place, *sources, *weights, spread, code_table.reshape(books * shard, channels))
+
+
 def finish_kernel(left, right, whole, width, *refs):
     state_ref, taps_ref, bias_ref, up_ref, mixed_ref, wave_ref, new_ref = refs[-7:]
     past, sessions, _ = state_ref.shape
@@ -445,13 +488,13 @@
     far_frames = frames([k for group in far for k in group], 2 * len(far), turn)
     frames_arrived = carry(list(zip(far_frames[::2], far_frames[1::2])))
     (turn,) = after((place,), far_frames)
-    (near_rows,) = experts([blocks[k] for k in near], 1, turn, held)
-    (turn,) = after((place,), near_rows)
-    (near_frames,) = frames(near, 1, turn)
+    near_rows, near_frames = near_sums(
+        blocks, near, turn, held, code_table, spread, columns[1], sessions, steps
+    )
     left = towards(near_rows, arrived, rows)
     right = towards(near_frames, frames_arrived, rows)
     one, minus, across = join(list(zip(left, right)), rows, width, code_table.shape[2])
-    last = [shift(one, 1), shift(minus, -1), shift(across, half)]
+    last = [shift(one, 1), shift(across, half), shift(minus, -1)]
     return finish(
         [(near_rows, 0)],
         [(near_frames, 0)],

time: 47.5 us -> 47.3 us (level)
    pallas_call x0 -> x1, Pallas kernels: none -> 3.76 us  [near_sums(): pl.pallas_call(functools.partial(near_kernel, for_experts, for_frames, ne...]
    pallas_call x2 -> x1, Pallas kernels: 5.75 us -> 2.8 us  [experts(): pl.pallas_call(functools.partial(experts_kernel, width, lax.axis_size('ex...]
    pallas_call x2 -> x1, Pallas kernels: 2.19 us -> 1.1 us  [frame_sums(): pl.pallas_call(functools.partial(frames_kernel, slot_at, shard, sessions,...]
where the time goes in v10:
time: 47.3 us; the launch traced here: 46.6 us
  starting transfers between devices  20.2 us (43%)
  Pallas kernels  14.1 us (30%)
  waiting for transfers between devices  11.5 us (24%)
  between operations  0.74 us (2%)
    ppermute x14, starting transfers between devices, shift(): return lax.ppermute(value, 'expert', pairs)  19.2 us
    ppermute x14, waiting for transfers between devices, shift(): return lax.ppermute(value, 'expert', pairs)  11.5 us
    pallas_call x1, Pallas kernels, load(): pl.pallas_call(functools.partial(load_kernel, code_at, books, shard), out...  3.78 us
    pallas_call x1, Pallas kernels, near_sums(): pl.pallas_call(functools.partial(near_kernel, for_experts, for_frames, ne...  3.76 us
    pallas_call x1, Pallas kernels, experts(): pl.pallas_call(functools.partial(experts_kernel, width, lax.axis_size('ex...  2.8 us
    pallas_call x1, Pallas kernels, pack(): pl.pallas_call(functools.partial(pack_kernel, columns, n_wave), out_shape...  1.46 us
    pallas_call x1, Pallas kernels, frame_sums(): pl.pallas_call(functools.partial(frames_kernel, slot_at, shard, sessions,...  1.1 us
    pallas_call x1, Pallas kernels, finish(): pl.pallas_call(functools.partial(finish_kernel, *numbered[0][0], width),...  1.09 us
  transfers between devices with their start and end apart: 17, of which 6 were waited for; matrix products, arithmetic and copies ran while one was open for 0% of the time, Pallas kernels for 25%

profile of v10, /device:TPU:0, one launch (start us, length us, event | category | flops | bytes accessed | tf_op | source)
XLA Modules:
  0.0 46.6 jit_solution(12858635754985507317)
XLA Ops:
  0.6 1.5 %pack.1.refs_0_ = bf16[32,2176]{1,0:T(8,128)(2,1)S(1)} custom-call(s32[1]{0:T(128)} %bitcast._.place_ref, bf16[16,2,2048]{2,1,0:T(2,128)(2,1)} %refs_0_.1, s32[2,8,16]{2,1,0:T(8,128)} %bitcast.15, f32[2,8,16]{2,1,0:T(8,128)} %bitcast.16, s32[16,2,16]{2,1,0:T(2,128)} %refs_3_.1, s32[1,16]{1,0:T(1,128)} %bitcast.17), custom_call_target="tpu_custom_call" | custom-call | tf_op jit(solution)/shard_map/pack/pallas_call | solution.py:161
  2.1 0.5 %collective-permute-start.2 = (bf16[2,2048,384]{2,1,0:T(8,128)(2,1)}, bf16[2,2048,384]{2,1,0:T(8,128)(2,1)S(1)}, u32[]{:S(2)}, u32[]{:S(2)}) collective-permute-start(bf16[2,2048,384]{2,1,0:T(8,128)(2,1)} %refs_1_.1), channel_id=1, source_target_pairs={{0,1},{1,0},{2,3},{3,2},{4,5},{5,4},{6,7},{7,6},{8,9},{9,8},{10,11... | collective-permute-start | bytes 9437192 | tf_op jit(solution)/shard_map/ppermute | solution.py:27
  2.6 0.1 collective-permute-start.6
  2.7 0.4 collective-permute-start.8
  3.1 2.6 %collective-permute-start = (bf16[32,2176]{1,0:T(8,128)(2,1)S(1)}, bf16[32,2176]{1,0:T(8,128)(2,1)S(1)}, u32[]{:S(2)}, u32[]{:S(2)}) collective-permute-start(bf16[32,2176]{1,0:T(8,128)(2,1)S(1)} %pack.1.refs_0_), channel_id=1, source_target_pairs={{0,2},{4,0},{8,4},{12,8},{14,12},{10,14},{6,10},{2,6},{1,3},{5,1},... | collective-permute-start | bytes 417800 | tf_op jit(solution)/shard_map/ppermute | solution.py:23
  5.7 0.1 collective-permute-start.3
  5.8 3.8 %load.1 = (bf16[2,2048,384]{2,1,0:T(8,128)(2,1)S(1)}, bf16[2,2048,384]{2,1,0:T(8,128)(2,1)S(1)}, bf16[768,2048]{1,0:T(8,128)(2,1)S(1)}, bf16[128,2048]{1,0:T(8,128)(2,1)S(1)}) custom-call(bf16[32,2176]{1,0:T(8,128)(2,1)S(1)} %pack.1.refs_0_, bf16[2,2048,384]{2,1,0:T(8,128)(2,1)} %refs_1_.1, bf16[2,2048,384]{2,1,0:T(8,128)(2,1)} %refs_2_.1, ...), custom_call_target="tpu_custom_call" | custom-call | bytes 9437184 | tf_op jit(solution)/shard_map/load/pallas_call | solution.py:193
  9.6 0.5 %collective-permute-done.refs_1_ = bf16[32,2176]{1,0:T(8,128)(2,1)S(1)} collective-permute-done((bf16[32,2176]{1,0:T(8,128)(2,1)S(1)}, bf16[32,2176]{1,0:T(8,128)(2,1)S(1)}, u32[]{:S(2)}, u32[]{:S(2)}) %collective-permute-start) | collective-permute-done | bytes 139296 | tf_op jit(solution)/shard_map/ppermute | solution.py:23
  10.0 0.0 copy-start
  10.1 1.7 %collective-permute-start.1 = (bf16[32,2176]{1,0:T(8,128)(2,1)S(1)}, bf16[32,2176]{1,0:T(8,128)(2,1)S(1)}, u32[]{:S(2)}, u32[]{:S(2)}) collective-permute-start(bf16[32,2176]{1,0:T(8,128)(2,1)S(1)} %collective-permute-done.refs_1_), channel_id=1, source_target_pairs={{0,2},{4,0},{8,4},{12,8},{14,12},{10,14},{6,10},{2,6},{1,3},{5,1},... | collective-permute-start | bytes 417800 | tf_op jit(solution)/shard_map/ppermute | solution.py:23
  11.8 0.0 collective-permute-done.3.refs_7_
  11.8 0.3 collective-permute-start.4
  12.1 3.4 %collective-permute-done.1.refs_0_.refs_2_ = bf16[32,2176]{1,0:T(8,128)(2,1)S(1)} collective-permute-done((bf16[32,2176]{1,0:T(8,128)(2,1)S(1)}, bf16[32,2176]{1,0:T(8,128)(2,1)S(1)}, u32[]{:S(2)}, u32[]{:S(2)}) %collective-permute-start.1) | collective-permute-done | bytes 139296 | tf_op jit(solution)/shard_map/ppermute | solution.py:23
  15.5 0.0 collective-permute-done.2.refs_7_.refs_11_
  15.5 1.6 %collective-permute-start.7 = (bf16[32,2176]{1,0:T(8,128)(2,1)S(1)}, bf16[32,2176]{1,0:T(8,128)(2,1)S(1)}, u32[]{:S(2)}, u32[]{:S(2)}) collective-permute-start(bf16[32,2176]{1,0:T(8,128)(2,1)S(1)} %collective-permute-done.1.refs_0_.refs_2_), channel_id=1, source_target_pairs={{0,2},{4,0},{8,4},{12,8},{14,12},{10,14},{6,10},{2,6},{1,3},{5,1},... | collective-permute-start | bytes 417800 | tf_op jit(solution)/shard_map/ppermute | solution.py:23
  17.1 0.0 collective-permute-done.4.refs_2_.refs_6_
  17.1 0.4 collective-permute-start.5
  17.5 0.0 collective-permute-done.6.refs_8_.refs_12_
  17.5 3.0 %collective-permute-done.7.refs_3_ = bf16[32,2176]{1,0:T(8,128)(2,1)S(1)} collective-permute-done((bf16[32,2176]{1,0:T(8,128)(2,1)S(1)}, bf16[32,2176]{1,0:T(8,128)(2,1)S(1)}, u32[]{:S(2)}, u32[]{:S(2)}) %collective-permute-start.7) | collective-permute-done | bytes 139296 | tf_op jit(solution)/shard_map/ppermute | solution.py:23
  20.5 1.6 %collective-permute-start.9 = (bf16[32,2176]{1,0:T(8,128)(2,1)S(1)}, bf16[32,2176]{1,0:T(8,128)(2,1)S(1)}, u32[]{:S(2)}, u32[]{:S(2)}) collective-permute-start(bf16[32,2176]{1,0:T(8,128)(2,1)S(1)} %collective-permute-done.7.refs_3_), channel_id=1, source_target_pairs={{0,2},{4,0},{8,4},{12,8},{14,12},{10,14},{6,10},{2,6},{1,3},{5,1},... | collective-permute-start | bytes 417800 | tf_op jit(solution)/shard_map/ppermute | solution.py:23
  22.1 0.0 collective-permute-done.5.refs_1_.refs_5_
  22.1 0.0 collective-permute-done.8.refs_9_.refs_13_
  22.1 2.8 %experts.1 = (bf16[64,2048]{1,0:T(8,128)(2,1)S(1)}, bf16[64,2048]{1,0:T(8,128)(2,1)S(1)}) custom-call(s32[1]{0:T(128)} %bitcast._.place_ref, bf16[32,2176]{1,0:T(8,128)(2,1)S(1)} %collective-permute-done.1.refs_0_.refs_2_, bf16[32,2176]{1,0:T(8,128)(2,1)S(1)} %collective-permute-done.5.refs_1_.refs_5_, ...), custom_call_target="tpu_custom_call" | custom-call | flops 2415919104 | bytes 18874368 | tf_op jit(solution)/shard_map/experts/pallas_call | solution.py:244
  25.0 0.5 %collective-permute-start.10 = (bf16[64,2048]{1,0:T(8,128)(2,1)S(1)}, bf16[64,2048]{1,0:T(8,128)(2,1)S(1)}, u32[]{:S(2)}, u32[]{:S(2)}) collective-permute-start(bf16[64,2048]{1,0:T(8,128)(2,1)S(1)} %get-tuple-element.43), channel_id=1, source_target_pairs={{0,4},{4,8},{8,12},{12,14},{14,10},{10,6},{6,2},{2,0},{1,5},{5,9},... | collective-permute-start | bytes 786440 | tf_op jit(solution)/shard_map/ppermute | solution.py:23
  25.4 1.6 %collective-permute-start.12 = (bf16[64,2048]{1,0:T(8,128)(2,1)S(1)}, bf16[64,2048]{1,0:T(8,128)(2,1)S(1)}, u32[]{:S(2)}, u32[]{:S(2)}) collective-permute-start(bf16[64,2048]{1,0:T(8,128)(2,1)S(1)} %get-tuple-element.44), channel_id=1, source_target_pairs={{0,2},{4,0},{8,4},{12,8},{14,12},{10,14},{6,10},{2,6},{1,3},{5,1},... | collective-permute-start | bytes 786440 | tf_op jit(solution)/shard_map/ppermute | solution.py:23
  27.0 0.0 collective-permute-done.9.refs_4_
  27.0 0.0 copy-done
  27.1 1.1 %frame_sums.1 = (bf16[64,1024]{1,0:T(8,128)(2,1)S(1)}, bf16[64,1024]{1,0:T(8,128)(2,1)S(1)}) custom-call(s32[1]{0:T(128)} %bitcast._.place_ref, bf16[32,2176]{1,0:T(8,128)(2,1)S(1)} %pack.1.refs_0_, bf16[32,2176]{1,0:T(8,128)(2,1)S(1)} %collective-permute-done.refs_1_, bf16[32,2176]{1,0:T(8,128)(2,1)S(1)} %collective-permute-done.1.refs_0_.refs_2_, ...), custom_call_target="tpu_custom_call" | custom-call | flops 536870912 | bytes 4194304 | tf_op jit(solution)/shard_map/frame_sums/pallas_call | solution.py:305
  28.2 0.5 %collective-permute-start.11 = (bf16[64,1024]{1,0:T(8,128)(2,1)S(1)}, bf16[64,1024]{1,0:T(8,128)(2,1)S(1)}, u32[]{:S(2)}, u32[]{:S(2)}) collective-permute-start(bf16[64,1024]{1,0:T(8,128)(2,1)S(1)} %get-tuple-element.48), channel_id=1, source_target_pairs={{0,4},{4,8},{8,12},{12,14},{14,10},{10,6},{6,2},{2,0},{1,5},{5,9},... | collective-permute-start | bytes 393224 | tf_op jit(solution)/shard_map/ppermute | solution.py:23
  28.7 0.0 copy-start.1
  28.7 1.6 %collective-permute-start.13 = (bf16[64,1024]{1,0:T(8,128)(2,1)S(1)}, bf16[64,1024]{1,0:T(8,128)(2,1)S(1)}, u32[]{:S(2)}, u32[]{:S(2)}) collective-permute-start(bf16[64,1024]{1,0:T(8,128)(2,1)S(1)} %get-tuple-element.49), channel_id=1, source_target_pairs={{0,2},{4,0},{8,4},{12,8},{14,12},{10,14},{6,10},{2,6},{1,3},{5,1},... | collective-permute-start | bytes 393224 | tf_op jit(solution)/shard_map/ppermute | solution.py:23
  30.3 3.8 %near_sums.1 = (bf16[128,2048]{1,0:T(8,128)(2,1)S(1)}, bf16[128,1024]{1,0:T(8,128)(2,1)S(1)}) custom-call(s32[1]{0:T(128)} %bitcast._.place_ref, bf16[32,2176]{1,0:T(8,128)(2,1)S(1)} %pack.1.refs_0_, bf16[32,2176]{1,0:T(8,128)(2,1)S(1)} %collective-permute-done.refs_1_, bf16[32,2176]{1,0:T(8,128)(2,1)S(1)} %collective-permute-done.1.refs_0_.refs_2_, ...), custom_call_target="tpu_custom_call" | custom-call | flops 2415919104 | bytes 18874368 | tf_op jit(solution)/shard_map/near_sums/pallas_call | solution.py:344
  34.1 0.0 collective-permute-done.10.refs_1_
  34.1 0.0 collective-permute-done.12.refs_4_
  34.1 0.0 collective-permute-done.11.refs_3_
  34.1 0.0 collective-permute-done.13.refs_5_
  34.1 0.2 join.1
  34.3 1.6 %collective-permute-start.14 = (bf16[32,3072]{1,0:T(8,128)(2,1)S(1)}, bf16[32,3072]{1,0:T(8,128)(2,1)S(1)}, u32[]{:S(2)}, u32[]{:S(2)}) collective-permute-start(bf16[32,3072]{1,0:T(8,128)(2,1)S(1)} %get-tuple-element.53), channel_id=1, source_target_pairs={{0,4},{4,8},{8,12},{12,14},{14,10},{10,6},{6,2},{2,0},{1,5},{5,9},... | collective-permute-start | bytes 589832 | tf_op jit(solution)/shard_map/ppermute | solution.py:23
  35.9 3.5 %collective-permute-start.15 = (bf16[32,3072]{1,0:T(8,128)(2,1)S(1)}, bf16[32,3072]{1,0:T(8,128)(2,1)S(1)}, u32[]{:S(2)}, u32[]{:S(2)}) collective-permute-start(bf16[32,3072]{1,0:T(8,128)(2,1)S(1)} %get-tuple-element.54), channel_id=1, source_target_pairs={{0,14},{4,10},{8,6},{12,2},{14,0},{10,4},{6,8},{2,12},{1,15},{5,11... | collective-permute-start | bytes 589832 | tf_op jit(solution)/shard_map/ppermute | solution.py:23
  39.4 1.5 %collective-permute-start.16 = (bf16[32,3072]{1,0:T(8,128)(2,1)S(1)}, bf16[32,3072]{1,0:T(8,128)(2,1)S(1)}, u32[]{:S(2)}, u32[]{:S(2)}) collective-permute-start(bf16[32,3072]{1,0:T(8,128)(2,1)S(1)} %get-tuple-element.55), channel_id=1, source_target_pairs={{0,2},{4,0},{8,4},{12,8},{14,12},{10,14},{6,10},{2,6},{1,3},{5,1},... | collective-permute-start | bytes 589832 | tf_op jit(solution)/shard_map/ppermute | solution.py:23
  40.9 1.2 %collective-permute-done.14.refs_2_ = bf16[32,3072]{1,0:T(8,128)(2,1)S(1)} collective-permute-done((bf16[32,3072]{1,0:T(8,128)(2,1)S(1)}, bf16[32,3072]{1,0:T(8,128)(2,1)S(1)}, u32[]{:S(2)}, u32[]{:S(2)}) %collective-permute-start.14) | collective-permute-done | bytes 196640 | tf_op jit(solution)/shard_map/ppermute | solution.py:23
  42.1 3.3 %collective-permute-done.15.refs_3_ = bf16[32,3072]{1,0:T(8,128)(2,1)S(1)} collective-permute-done((bf16[32,3072]{1,0:T(8,128)(2,1)S(1)}, bf16[32,3072]{1,0:T(8,128)(2,1)S(1)}, u32[]{:S(2)}, u32[]{:S(2)}) %collective-permute-start.15) | collective-permute-done | bytes 196640 | tf_op jit(solution)/shard_map/ppermute | solution.py:23
  45.4 0.1 collective-permute-done.16.refs_4_
  45.5 0.0 copy-done.1
  45.5 0.0 copy-done.2
  45.5 0.0 copy-done.3
  45.5 0.0 copy-done.4
  45.5 1.1 %finish.1 = (bf16[16,2,2048]{2,1,0:T(2,128)(2,1)}, bf16[16,2,512]{2,1,0:T(2,128)(2,1)}, bf16[6,16,1024]{2,1,0:T(8,128)(2,1)}) custom-call(bf16[128,2048]{1,0:T(8,128)(2,1)S(1)} %get-tuple-element.51.refs_0_, bf16[128,1024]{1,0:T(8,128)(2,1)S(1)} %get-tuple-element.52.refs_2_.refs_1_, bf16[32,3072]{1,0:T(8,128)(2,1)S(1)} %collective-permute-done.14.refs_2_, ...), custom_call_target="tpu_custom_call" | custom-call | bytes 2097152 | tf_op jit(solution)/shard_map/finish/pallas_call | solution.py:399
  (3 shorter events, 0.0 us)
Async XLA Ops:
  2.1 13.4 %collective-permute-start.2 = (bf16[2,2048,384]{2,1,0:T(8,128)(2,1)}, bf16[2,2048,384]{2,1,0:T(8,128)(2,1)S(1)}, u32[]{:S(2)}, u32[]{:S(2)}) collective-permute-start(bf16[2,2048,384]{2,1,0:T(8,128)(2,1)} %refs_1_.1), channel_id=1, source_target_pairs={{0,1},{1,0},{2,3},{3,2},{4,5},{5,4},{6,7},{7,6},{8,9},{9,8},{10,11... | collective-permute-start | bytes 9437192 | tf_op jit(solution)/shard_map/ppermute | solution.py:27
  2.6 14.9 %collective-permute-start.6 = (bf16[2,2048,384]{2,1,0:T(8,128)(2,1)}, bf16[2,2048,384]{2,1,0:T(8,128)(2,1)S(1)}, u32[]{:S(2)}, u32[]{:S(2)}) collective-permute-start(bf16[2,2048,384]{2,1,0:T(8,128)(2,1)} %refs_2_.1), channel_id=1, source_target_pairs={{0,1},{1,0},{2,3},{3,2},{4,5},{5,4},{6,7},{7,6},{8,9},{9,8},{10,11... | collective-permute-start | bytes 9437192 | tf_op jit(solution)/shard_map/ppermute | solution.py:27
  2.7 19.4 %collective-permute-start.8 = (bf16[768,2048]{1,0:T(8,128)(2,1)}, bf16[768,2048]{1,0:T(8,128)(2,1)S(1)}, u32[]{:S(2)}, u32[]{:S(2)}) collective-permute-start(bf16[768,2048]{1,0:T(8,128)(2,1)} %bitcast.13), channel_id=1, source_target_pairs={{0,1},{1,0},{2,3},{3,2},{4,5},{5,4},{6,7},{7,6},{8,9},{9,8},{10,11... | collective-permute-start | bytes 9437192 | tf_op jit(solution)/shard_map/ppermute | solution.py:27
  3.1 6.9 %collective-permute-start = (bf16[32,2176]{1,0:T(8,128)(2,1)S(1)}, bf16[32,2176]{1,0:T(8,128)(2,1)S(1)}, u32[]{:S(2)}, u32[]{:S(2)}) collective-permute-start(bf16[32,2176]{1,0:T(8,128)(2,1)S(1)} %pack.1.refs_0_), channel_id=1, source_target_pairs={{0,2},{4,0},{8,4},{12,8},{14,12},{10,14},{6,10},{2,6},{1,3},{5,1},... | collective-permute-start | bytes 417800 | tf_op jit(solution)/shard_map/ppermute | solution.py:23
  5.7 6.0 %collective-permute-start.3 = (bf16[32,2176]{1,0:T(8,128)(2,1)S(1)}, bf16[32,2176]{1,0:T(8,128)(2,1)S(1)}, u32[]{:S(2)}, u32[]{:S(2)}) collective-permute-start(bf16[32,2176]{1,0:T(8,128)(2,1)S(1)} %pack.1.refs_0_), channel_id=1, source_target_pairs={{0,4},{4,8},{8,12},{12,14},{14,10},{10,6},{6,2},{2,0},{1,5},{5,9},... | collective-permute-start | bytes 417800 | tf_op jit(solution)/shard_map/ppermute | solution.py:23
  10.0 17.0 %copy-start = (bf16[16,128,1024]{2,1,0:T(8,128)(2,1)S(1)}, bf16[16,128,1024]{2,1,0:T(8,128)(2,1)}, u32[]{:S(2)}) copy-start(bf16[16,128,1024]{2,1,0:T(8,128)(2,1)} %param.21) | copy-start | bytes 12582916
  10.1 5.4 %collective-permute-start.1 = (bf16[32,2176]{1,0:T(8,128)(2,1)S(1)}, bf16[32,2176]{1,0:T(8,128)(2,1)S(1)}, u32[]{:S(2)}, u32[]{:S(2)}) collective-permute-start(bf16[32,2176]{1,0:T(8,128)(2,1)S(1)} %collective-permute-done.refs_1_), channel_id=1, source_target_pairs={{0,2},{4,0},{8,4},{12,8},{14,12},{10,14},{6,10},{2,6},{1,3},{5,1},... | collective-permute-start | bytes 417800 | tf_op jit(solution)/shard_map/ppermute | solution.py:23
  11.8 5.3 %collective-permute-start.4 = (bf16[32,2176]{1,0:T(8,128)(2,1)S(1)}, bf16[32,2176]{1,0:T(8,128)(2,1)S(1)}, u32[]{:S(2)}, u32[]{:S(2)}) collective-permute-start(bf16[32,2176]{1,0:T(8,128)(2,1)S(1)} %collective-permute-done.3.refs_7_), channel_id=1, source_target_pairs={{0,4},{4,8},{8,12},{12,14},{14,10},{10,6},{6,2},{2,0},{1,5},{5,9},... | collective-permute-start | bytes 417800 | tf_op jit(solution)/shard_map/ppermute | solution.py:23
  15.5 5.1 %collective-permute-start.7 = (bf16[32,2176]{1,0:T(8,128)(2,1)S(1)}, bf16[32,2176]{1,0:T(8,128)(2,1)S(1)}, u32[]{:S(2)}, u32[]{:S(2)}) collective-permute-start(bf16[32,2176]{1,0:T(8,128)(2,1)S(1)} %collective-permute-done.1.refs_0_.refs_2_), channel_id=1, source_target_pairs={{0,2},{4,0},{8,4},{12,8},{14,12},{10,14},{6,10},{2,6},{1,3},{5,1},... | collective-permute-start | bytes 417800 | tf_op jit(solution)/shard_map/ppermute | solution.py:23
  17.1 5.1 %collective-permute-start.5 = (bf16[32,2176]{1,0:T(8,128)(2,1)S(1)}, bf16[32,2176]{1,0:T(8,128)(2,1)S(1)}, u32[]{:S(2)}, u32[]{:S(2)}) collective-permute-start(bf16[32,2176]{1,0:T(8,128)(2,1)S(1)} %collective-permute-done.4.refs_2_.refs_6_), channel_id=1, source_target_pairs={{0,4},{4,8},{8,12},{12,14},{14,10},{10,6},{6,2},{2,0},{1,5},{5,9},... | collective-permute-start | bytes 417800 | tf_op jit(solution)/shard_map/ppermute | solution.py:23
  20.5 6.5 %collective-permute-start.9 = (bf16[32,2176]{1,0:T(8,128)(2,1)S(1)}, bf16[32,2176]{1,0:T(8,128)(2,1)S(1)}, u32[]{:S(2)}, u32[]{:S(2)}) collective-permute-start(bf16[32,2176]{1,0:T(8,128)(2,1)S(1)} %collective-permute-done.7.refs_3_), channel_id=1, source_target_pairs={{0,2},{4,0},{8,4},{12,8},{14,12},{10,14},{6,10},{2,6},{1,3},{5,1},... | collective-permute-start | bytes 417800 | tf_op jit(solution)/shard_map/ppermute | solution.py:23
  25.0 9.1 %collective-permute-start.10 = (bf16[64,2048]{1,0:T(8,128)(2,1)S(1)}, bf16[64,2048]{1,0:T(8,128)(2,1)S(1)}, u32[]{:S(2)}, u32[]{:S(2)}) collective-permute-start(bf16[64,2048]{1,0:T(8,128)(2,1)S(1)} %get-tuple-element.43), channel_id=1, source_target_pairs={{0,4},{4,8},{8,12},{12,14},{14,10},{10,6},{6,2},{2,0},{1,5},{5,9},... | collective-permute-start | bytes 786440 | tf_op jit(solution)/shard_map/ppermute | solution.py:23
  25.4 8.6 %collective-permute-start.12 = (bf16[64,2048]{1,0:T(8,128)(2,1)S(1)}, bf16[64,2048]{1,0:T(8,128)(2,1)S(1)}, u32[]{:S(2)}, u32[]{:S(2)}) collective-permute-start(bf16[64,2048]{1,0:T(8,128)(2,1)S(1)} %get-tuple-element.44), channel_id=1, source_target_pairs={{0,2},{4,0},{8,4},{12,8},{14,12},{10,14},{6,10},{2,6},{1,3},{5,1},... | collective-permute-start | bytes 786440 | tf_op jit(solution)/shard_map/ppermute | solution.py:23
  28.2 5.9 %collective-permute-start.11 = (bf16[64,1024]{1,0:T(8,128)(2,1)S(1)}, bf16[64,1024]{1,0:T(8,128)(2,1)S(1)}, u32[]{:S(2)}, u32[]{:S(2)}) collective-permute-start(bf16[64,1024]{1,0:T(8,128)(2,1)S(1)} %get-tuple-element.48), channel_id=1, source_target_pairs={{0,4},{4,8},{8,12},{12,14},{14,10},{10,6},{6,2},{2,0},{1,5},{5,9},... | collective-permute-start | bytes 393224 | tf_op jit(solution)/shard_map/ppermute | solution.py:23
  28.7 16.8 %copy-start.1 = (bf16[1024,512]{1,0:T(8,128)(2,1)S(1)}, bf16[1024,512]{1,0:T(8,128)(2,1)}, u32[]{:S(2)}) copy-start(bf16[1024,512]{1,0:T(8,128)(2,1)} %refs_8_.1) | copy-start | bytes 3145732
  28.7 16.8 %copy-start.2 = (bf16[16,6,1024]{2,0,1:T(8,128)(2,1)S(1)}, bf16[16,6,1024]{2,0,1:T(8,128)(2,1)}, u32[]{:S(2)}) copy-start(bf16[16,6,1024]{2,0,1:T(8,128)(2,1)} %param.22) | copy-start | bytes 589828
  28.7 16.8 %copy-start.3 = (f32[7,1024]{1,0:T(8,128)S(1)}, f32[7,1024]{1,0:T(8,128)}, u32[]{:S(2)}) copy-start(f32[7,1024]{1,0:T(8,128)} %refs_6_.1) | copy-start | bytes 86020
  28.7 16.8 %copy-start.4 = (f32[1024]{0:T(1024)S(1)}, f32[1024]{0:T(1024)}, u32[]{:S(2)}) copy-start(f32[1024]{0:T(1024)} %param.24) | copy-start | bytes 12292
  28.7 5.4 %collective-permute-start.13 = (bf16[64,1024]{1,0:T(8,128)(2,1)S(1)}, bf16[64,1024]{1,0:T(8,128)(2,1)S(1)}, u32[]{:S(2)}, u32[]{:S(2)}) collective-permute-start(bf16[64,1024]{1,0:T(8,128)(2,1)S(1)} %get-tuple-element.49), channel_id=1, source_target_pairs={{0,2},{4,0},{8,4},{12,8},{14,12},{10,14},{6,10},{2,6},{1,3},{5,1},... | collective-permute-start | bytes 393224 | tf_op jit(solution)/shard_map/ppermute | solution.py:23
  34.3 7.8 %collective-permute-start.14 = (bf16[32,3072]{1,0:T(8,128)(2,1)S(1)}, bf16[32,3072]{1,0:T(8,128)(2,1)S(1)}, u32[]{:S(2)}, u32[]{:S(2)}) collective-permute-start(bf16[32,3072]{1,0:T(8,128)(2,1)S(1)} %get-tuple-element.53), channel_id=1, source_target_pairs={{0,4},{4,8},{8,12},{12,14},{14,10},{10,6},{6,2},{2,0},{1,5},{5,9},... | collective-permute-start | bytes 589832 | tf_op jit(solution)/shard_map/ppermute | solution.py:23
  35.9 9.5 %collective-permute-start.15 = (bf16[32,3072]{1,0:T(8,128)(2,1)S(1)}, bf16[32,3072]{1,0:T(8,128)(2,1)S(1)}, u32[]{:S(2)}, u32[]{:S(2)}) collective-permute-start(bf16[32,3072]{1,0:T(8,128)(2,1)S(1)} %get-tuple-element.54), channel_id=1, source_target_pairs={{0,14},{4,10},{8,6},{12,2},{14,0},{10,4},{6,8},{2,12},{1,15},{5,11... | collective-permute-start | bytes 589832 | tf_op jit(solution)/shard_map/ppermute | solution.py:23
  39.4 6.1 %collective-permute-start.16 = (bf16[32,3072]{1,0:T(8,128)(2,1)S(1)}, bf16[32,3072]{1,0:T(8,128)(2,1)S(1)}, u32[]{:S(2)}, u32[]{:S(2)}) collective-permute-start(bf16[32,3072]{1,0:T(8,128)(2,1)S(1)} %get-tuple-element.55), channel_id=1, source_target_pairs={{0,2},{4,0},{8,4},{12,8},{14,12},{10,14},{6,10},{2,6},{1,3},{5,1},... | collective-permute-start | bytes 589832 | tf_op jit(solution)/shard_map/ppermute | solution.py:23

commit v11 on v10

--- a/solution.py
+++ b/solution.py
@@ -266,7 +266,8 @@
     count = len(sources)
     metas, (spread_ref, table_ref, *outs, hot_ref) = refs[:count], refs[count:]
     rows = metas[0].shape[0]
-    meta = jnp.concatenate([m[...] for m in metas], axis=0)
+    last = metas[0].shape[1] - spread_ref.shape[0]
+    meta = jnp.concatenate([m[:, last:] for m in metas], axis=0)
     column = lax.broadcasted_iota(jnp.int32, (8, meta.shape[1]), 1)
     digit = lax.broadcasted_iota(jnp.int32, (8, meta.shape[1]), 0)
     picks = jnp.where((column == slot_at + digit) & (digit < 2), 1.0, 0.0).astype(BF16)
@@ -296,17 +297,14 @@
 
 def frame_sums(blocks, order, split, place, code_table, spread, slot_at, sessions, steps):
     books, shard, channels = code_table.shape
-    meta_width = spread.shape[0]
     sources = list(range(len(blocks)))
-    rows, width = blocks[0].shape
+    rows = blocks[0].shape[0]
     total = rows * len(order)
-    block = pl.BlockSpec((rows, meta_width), lambda i: (0, width // meta_width - 1))
     vmem = pl.BlockSpec(memory_space=pltpu.VMEM)
     return pl.pallas_call(
         functools.partial(frames_kernel, slot_at, shard, sessions, steps, sources, order),
-        grid=(1,),
         out_shape=[jax.ShapeDtypeStruct((total // split, channels), BF16)] * split,
-        in_specs=[pl.BlockSpec(memory_space=pltpu.SMEM)] + [block] * len(sources) + [vmem] * 2,
+        in_specs=[pl.BlockSpec(memory_space=pltpu.SMEM)] + [vmem] * (len(sources) + 2),
         out_specs=[vmem] * split,
         scratch_shapes=[pltpu.VMEM((total, books * shard), BF16)],
         compiler_params=pltpu.CompilerParams(
@@ -321,14 +319,13 @@
     )(place, *[blocks[k] for k in sources], spread, code_table.reshape(books * shard, channels))
 
 
-def near_kernel(for_experts, for_frames, near, width, place_ref, *refs):
+def near_kernel(for_experts, for_frames, near, place_ref, *refs):
     count = len(for_frames[-2])
     sources, weights = refs[:count], refs[count:-7]
     spread_ref, table_ref, rows_out, frames_out, rows_ref, act_ref, hot_ref = refs[-7:]
     blocks = [sources[k] for k in near]
-    metas = [m.at[:, width : m.shape[1]] for m in sources]
     experts_kernel(*for_experts, place_ref, *blocks, *weights, rows_out, rows_ref, act_ref)
-    frames_kernel(*for_frames, place_ref, *metas, spread_ref, table_ref, frames_out, hot_ref)
+    frames_kernel(*for_frames, place_ref, *sources, spread_ref, table_ref, frames_out, hot_ref)
 
 
 def near_sums(blocks, near, place, held, code_table, spread, slot_at, sessions, steps):
@@ -342,7 +339,7 @@
     for_experts = (width, lax.axis_size("expert") * local, len(near), 1)
     for_frames = (slot_at, shard, sessions, steps, list(range(len(sources))), near)
     return pl.pallas_call(
-        functools.partial(near_kernel, for_experts, for_frames, near, width),
+        functools.partial(near_kernel, for_experts, for_frames, near),
         out_shape=[jax.ShapeDtypeStruct((total, size), BF16) for size in (width, channels)],
         in_specs=[pl.BlockSpec(memory_space=pltpu.SMEM)]
         + [vmem] * (len(sources) + len(weights) + 2),

time: 47.3 us -> 47.3 us (level)
  no operation moved by 1% of the time
where the time goes in v11:
time: 47.3 us; the launch traced here: 46.5 us
  starting transfers between devices  20.2 us (43%)
  Pallas kernels  14.1 us (30%)
  waiting for transfers between devices  11.4 us (24%)
  between operations  0.74 us (2%)
    ppermute x14, starting transfers between devices, shift(): return lax.ppermute(value, 'expert', pairs)  19.2 us
    ppermute x14, waiting for transfers between devices, shift(): return lax.ppermute(value, 'expert', pairs)  11.4 us
    pallas_call x1, Pallas kernels, load(): pl.pallas_call(functools.partial(load_kernel, code_at, books, shard), out...  3.78 us
    pallas_call x1, Pallas kernels, near_sums(): pl.pallas_call(functools.partial(near_kernel, for_experts, for_frames, ne...  3.75 us
    pallas_call x1, Pallas kernels, experts(): pl.pallas_call(functools.partial(experts_kernel, width, lax.axis_size('ex...  2.8 us
    pallas_call x1, Pallas kernels, pack(): pl.pallas_call(functools.partial(pack_kernel, columns, n_wave), out_shape...  1.46 us
    pallas_call x1, Pallas kernels, finish(): pl.pallas_call(functools.partial(finish_kernel, *numbered[0][0], width),...  1.09 us
    pallas_call x1, Pallas kernels, frame_sums(): pl.pallas_call(functools.partial(frames_kernel, slot_at, shard, sessions,...  1.09 us
  transfers between devices with their start and end apart: 17, of which 6 were waited for; matrix products, arithmetic and copies ran while one was open for 0% of the time, Pallas kernels for 25%

profile of v11, /device:TPU:0, one launch (start us, length us, event | category | flops | bytes accessed | tf_op | source)
XLA Modules:
  0.0 46.5 jit_solution(17518087427862024171)
XLA Ops:
  0.6 1.5 %pack.1.refs_0_ = bf16[32,2176]{1,0:T(8,128)(2,1)S(1)} custom-call(s32[1]{0:T(128)} %bitcast._.place_ref, bf16[16,2,2048]{2,1,0:T(2,128)(2,1)} %refs_0_.1, s32[2,8,16]{2,1,0:T(8,128)} %bitcast.15, f32[2,8,16]{2,1,0:T(8,128)} %bitcast.16, s32[16,2,16]{2,1,0:T(2,128)} %refs_3_.1, s32[1,16]{1,0:T(1,128)} %bitcast.17), custom_call_target="tpu_custom_call" | custom-call | tf_op jit(solution)/shard_map/pack/pallas_call | solution.py:161
  2.1 0.5 %collective-permute-start.2 = (bf16[2,2048,384]{2,1,0:T(8,128)(2,1)}, bf16[2,2048,384]{2,1,0:T(8,128)(2,1)S(1)}, u32[]{:S(2)}, u32[]{:S(2)}) collective-permute-start(bf16[2,2048,384]{2,1,0:T(8,128)(2,1)} %refs_1_.1), channel_id=1, source_target_pairs={{0,1},{1,0},{2,3},{3,2},{4,5},{5,4},{6,7},{7,6},{8,9},{9,8},{10,11... | collective-permute-start | bytes 9437192 | tf_op jit(solution)/shard_map/ppermute | solution.py:27
  2.6 0.1 collective-permute-start.6
  2.7 0.4 collective-permute-start.8
  3.1 2.6 %collective-permute-start = (bf16[32,2176]{1,0:T(8,128)(2,1)S(1)}, bf16[32,2176]{1,0:T(8,128)(2,1)S(1)}, u32[]{:S(2)}, u32[]{:S(2)}) collective-permute-start(bf16[32,2176]{1,0:T(8,128)(2,1)S(1)} %pack.1.refs_0_), channel_id=1, source_target_pairs={{0,2},{4,0},{8,4},{12,8},{14,12},{10,14},{6,10},{2,6},{1,3},{5,1},... | collective-permute-start | bytes 417800 | tf_op jit(solution)/shard_map/ppermute | solution.py:23
  5.7 0.1 collective-permute-start.3
  5.8 3.8 %load.1 = (bf16[2,2048,384]{2,1,0:T(8,128)(2,1)S(1)}, bf16[2,2048,384]{2,1,0:T(8,128)(2,1)S(1)}, bf16[768,2048]{1,0:T(8,128)(2,1)S(1)}, bf16[128,2048]{1,0:T(8,128)(2,1)S(1)}) custom-call(bf16[32,2176]{1,0:T(8,128)(2,1)S(1)} %pack.1.refs_0_, bf16[2,2048,384]{2,1,0:T(8,128)(2,1)} %refs_1_.1, bf16[2,2048,384]{2,1,0:T(8,128)(2,1)} %refs_2_.1, ...), custom_call_target="tpu_custom_call" | custom-call | bytes 9437184 | tf_op jit(solution)/shard_map/load/pallas_call | solution.py:193
  9.6 0.5 %collective-permute-done.refs_1_ = bf16[32,2176]{1,0:T(8,128)(2,1)S(1)} collective-permute-done((bf16[32,2176]{1,0:T(8,128)(2,1)S(1)}, bf16[32,2176]{1,0:T(8,128)(2,1)S(1)}, u32[]{:S(2)}, u32[]{:S(2)}) %collective-permute-start) | collective-permute-done | bytes 139296 | tf_op jit(solution)/shard_map/ppermute | solution.py:23
  10.1 1.7 %collective-permute-start.1 = (bf16[32,2176]{1,0:T(8,128)(2,1)S(1)}, bf16[32,2176]{1,0:T(8,128)(2,1)S(1)}, u32[]{:S(2)}, u32[]{:S(2)}) collective-permute-start(bf16[32,2176]{1,0:T(8,128)(2,1)S(1)} %collective-permute-done.refs_1_), channel_id=1, source_target_pairs={{0,2},{4,0},{8,4},{12,8},{14,12},{10,14},{6,10},{2,6},{1,3},{5,1},... | collective-permute-start | bytes 417800 | tf_op jit(solution)/shard_map/ppermute | solution.py:23
  11.8 0.0 collective-permute-done.3.refs_7_
  11.8 0.3 collective-permute-start.4
  12.1 3.4 %collective-permute-done.1.refs_0_.refs_2_ = bf16[32,2176]{1,0:T(8,128)(2,1)S(1)} collective-permute-done((bf16[32,2176]{1,0:T(8,128)(2,1)S(1)}, bf16[32,2176]{1,0:T(8,128)(2,1)S(1)}, u32[]{:S(2)}, u32[]{:S(2)}) %collective-permute-start.1) | collective-permute-done | bytes 139296 | tf_op jit(solution)/shard_map/ppermute | solution.py:23
  15.5 0.0 collective-permute-done.2.refs_7_.refs_11_
  15.5 1.6 %collective-permute-start.7 = (bf16[32,2176]{1,0:T(8,128)(2,1)S(1)}, bf16[32,2176]{1,0:T(8,128)(2,1)S(1)}, u32[]{:S(2)}, u32[]{:S(2)}) collective-permute-start(bf16[32,2176]{1,0:T(8,128)(2,1)S(1)} %collective-permute-done.1.refs_0_.refs_2_), channel_id=1, source_target_pairs={{0,2},{4,0},{8,4},{12,8},{14,12},{10,14},{6,10},{2,6},{1,3},{5,1},... | collective-permute-start | bytes 417800 | tf_op jit(solution)/shard_map/ppermute | solution.py:23
  17.1 0.0 collective-permute-done.4.refs_2_.refs_6_
  17.1 0.4 collective-permute-start.5
  17.5 0.0 collective-permute-done.6.refs_8_.refs_12_
  17.5 3.0 %collective-permute-done.7.refs_3_ = bf16[32,2176]{1,0:T(8,128)(2,1)S(1)} collective-permute-done((bf16[32,2176]{1,0:T(8,128)(2,1)S(1)}, bf16[32,2176]{1,0:T(8,128)(2,1)S(1)}, u32[]{:S(2)}, u32[]{:S(2)}) %collective-permute-start.7) | collective-permute-done | bytes 139296 | tf_op jit(solution)/shard_map/ppermute | solution.py:23
  20.5 1.6 %collective-permute-start.9 = (bf16[32,2176]{1,0:T(8,128)(2,1)S(1)}, bf16[32,2176]{1,0:T(8,128)(2,1)S(1)}, u32[]{:S(2)}, u32[]{:S(2)}) collective-permute-start(bf16[32,2176]{1,0:T(8,128)(2,1)S(1)} %collective-permute-done.7.refs_3_), channel_id=1, source_target_pairs={{0,2},{4,0},{8,4},{12,8},{14,12},{10,14},{6,10},{2,6},{1,3},{5,1},... | collective-permute-start | bytes 417800 | tf_op jit(solution)/shard_map/ppermute | solution.py:23
  22.1 0.0 collective-permute-done.5.refs_1_.refs_5_
  22.1 0.0 collective-permute-done.8.refs_9_.refs_13_
  22.1 2.8 %experts.1 = (bf16[64,2048]{1,0:T(8,128)(2,1)S(1)}, bf16[64,2048]{1,0:T(8,128)(2,1)S(1)}) custom-call(s32[1]{0:T(128)} %bitcast._.place_ref, bf16[32,2176]{1,0:T(8,128)(2,1)S(1)} %collective-permute-done.1.refs_0_.refs_2_, bf16[32,2176]{1,0:T(8,128)(2,1)S(1)} %collective-permute-done.5.refs_1_.refs_5_, ...), custom_call_target="tpu_custom_call" | custom-call | flops 2415919104 | bytes 18874368 | tf_op jit(solution)/shard_map/experts/pallas_call | solution.py:244
  25.0 0.5 %collective-permute-start.10 = (bf16[64,2048]{1,0:T(8,128)(2,1)S(1)}, bf16[64,2048]{1,0:T(8,128)(2,1)S(1)}, u32[]{:S(2)}, u32[]{:S(2)}) collective-permute-start(bf16[64,2048]{1,0:T(8,128)(2,1)S(1)} %get-tuple-element.43), channel_id=1, source_target_pairs={{0,4},{4,8},{8,12},{12,14},{14,10},{10,6},{6,2},{2,0},{1,5},{5,9},... | collective-permute-start | bytes 786440 | tf_op jit(solution)/shard_map/ppermute | solution.py:23
  25.4 1.6 %collective-permute-start.12 = (bf16[64,2048]{1,0:T(8,128)(2,1)S(1)}, bf16[64,2048]{1,0:T(8,128)(2,1)S(1)}, u32[]{:S(2)}, u32[]{:S(2)}) collective-permute-start(bf16[64,2048]{1,0:T(8,128)(2,1)S(1)} %get-tuple-element.44), channel_id=1, source_target_pairs={{0,2},{4,0},{8,4},{12,8},{14,12},{10,14},{6,10},{2,6},{1,3},{5,1},... | collective-permute-start | bytes 786440 | tf_op jit(solution)/shard_map/ppermute | solution.py:23
  27.0 0.0 collective-permute-done.9.refs_4_
  27.0 0.0 copy-done
  27.0 1.1 %frame_sums.1 = (bf16[64,1024]{1,0:T(8,128)(2,1)S(1)}, bf16[64,1024]{1,0:T(8,128)(2,1)S(1)}) custom-call(s32[1]{0:T(128)} %bitcast._.place_ref, bf16[32,2176]{1,0:T(8,128)(2,1)S(1)} %pack.1.refs_0_, bf16[32,2176]{1,0:T(8,128)(2,1)S(1)} %collective-permute-done.refs_1_, bf16[32,2176]{1,0:T(8,128)(2,1)S(1)} %collective-permute-done.1.refs_0_.refs_2_, ...), custom_call_target="tpu_custom_call" | custom-call | flops 536870912 | bytes 4194304 | tf_op jit(solution)/shard_map/frame_sums/pallas_call | solution.py:304
  28.1 0.6 %collective-permute-start.11 = (bf16[64,1024]{1,0:T(8,128)(2,1)S(1)}, bf16[64,1024]{1,0:T(8,128)(2,1)S(1)}, u32[]{:S(2)}, u32[]{:S(2)}) collective-permute-start(bf16[64,1024]{1,0:T(8,128)(2,1)S(1)} %get-tuple-element.48), channel_id=1, source_target_pairs={{0,4},{4,8},{8,12},{12,14},{14,10},{10,6},{6,2},{2,0},{1,5},{5,9},... | collective-permute-start | bytes 393224 | tf_op jit(solution)/shard_map/ppermute | solution.py:23
  28.7 0.0 copy-start.1
  28.7 0.0 copy-start.2
  28.7 1.6 %collective-permute-start.13 = (bf16[64,1024]{1,0:T(8,128)(2,1)S(1)}, bf16[64,1024]{1,0:T(8,128)(2,1)S(1)}, u32[]{:S(2)}, u32[]{:S(2)}) collective-permute-start(bf16[64,1024]{1,0:T(8,128)(2,1)S(1)} %get-tuple-element.49), channel_id=1, source_target_pairs={{0,2},{4,0},{8,4},{12,8},{14,12},{10,14},{6,10},{2,6},{1,3},{5,1},... | collective-permute-start | bytes 393224 | tf_op jit(solution)/shard_map/ppermute | solution.py:23
  30.3 3.8 %near_sums.1 = (bf16[128,2048]{1,0:T(8,128)(2,1)S(1)}, bf16[128,1024]{1,0:T(8,128)(2,1)S(1)}) custom-call(s32[1]{0:T(128)} %bitcast._.place_ref, bf16[32,2176]{1,0:T(8,128)(2,1)S(1)} %pack.1.refs_0_, bf16[32,2176]{1,0:T(8,128)(2,1)S(1)} %collective-permute-done.refs_1_, bf16[32,2176]{1,0:T(8,128)(2,1)S(1)} %collective-permute-done.1.refs_0_.refs_2_, ...), custom_call_target="tpu_custom_call" | custom-call | flops 2415919104 | bytes 18874368 | tf_op jit(solution)/shard_map/near_sums/pallas_call | solution.py:341
  34.0 0.0 collective-permute-done.10.refs_1_
  34.0 0.0 collective-permute-done.12.refs_4_
  34.0 0.0 collective-permute-done.11.refs_3_
  34.1 0.0 collective-permute-done.13.refs_5_
  34.1 0.2 join.1
  34.2 1.7 %collective-permute-start.14 = (bf16[32,3072]{1,0:T(8,128)(2,1)S(1)}, bf16[32,3072]{1,0:T(8,128)(2,1)S(1)}, u32[]{:S(2)}, u32[]{:S(2)}) collective-permute-start(bf16[32,3072]{1,0:T(8,128)(2,1)S(1)} %get-tuple-element.53), channel_id=1, source_target_pairs={{0,4},{4,8},{8,12},{12,14},{14,10},{10,6},{6,2},{2,0},{1,5},{5,9},... | collective-permute-start | bytes 589832 | tf_op jit(solution)/shard_map/ppermute | solution.py:23
  35.9 3.5 %collective-permute-start.15 = (bf16[32,3072]{1,0:T(8,128)(2,1)S(1)}, bf16[32,3072]{1,0:T(8,128)(2,1)S(1)}, u32[]{:S(2)}, u32[]{:S(2)}) collective-permute-start(bf16[32,3072]{1,0:T(8,128)(2,1)S(1)} %get-tuple-element.54), channel_id=1, source_target_pairs={{0,14},{4,10},{8,6},{12,2},{14,0},{10,4},{6,8},{2,12},{1,15},{5,11... | collective-permute-start | bytes 589832 | tf_op jit(solution)/shard_map/ppermute | solution.py:23
  39.4 1.5 %collective-permute-start.16 = (bf16[32,3072]{1,0:T(8,128)(2,1)S(1)}, bf16[32,3072]{1,0:T(8,128)(2,1)S(1)}, u32[]{:S(2)}, u32[]{:S(2)}) collective-permute-start(bf16[32,3072]{1,0:T(8,128)(2,1)S(1)} %get-tuple-element.55), channel_id=1, source_target_pairs={{0,2},{4,0},{8,4},{12,8},{14,12},{10,14},{6,10},{2,6},{1,3},{5,1},... | collective-permute-start | bytes 589832 | tf_op jit(solution)/shard_map/ppermute | solution.py:23
  40.9 1.2 %collective-permute-done.14.refs_2_ = bf16[32,3072]{1,0:T(8,128)(2,1)S(1)} collective-permute-done((bf16[32,3072]{1,0:T(8,128)(2,1)S(1)}, bf16[32,3072]{1,0:T(8,128)(2,1)S(1)}, u32[]{:S(2)}, u32[]{:S(2)}) %collective-permute-start.14) | collective-permute-done | bytes 196640 | tf_op jit(solution)/shard_map/ppermute | solution.py:23
  42.1 3.3 %collective-permute-done.15.refs_3_ = bf16[32,3072]{1,0:T(8,128)(2,1)S(1)} collective-permute-done((bf16[32,3072]{1,0:T(8,128)(2,1)S(1)}, bf16[32,3072]{1,0:T(8,128)(2,1)S(1)}, u32[]{:S(2)}, u32[]{:S(2)}) %collective-permute-start.15) | collective-permute-done | bytes 196640 | tf_op jit(solution)/shard_map/ppermute | solution.py:23
  45.4 0.1 collective-permute-done.16.refs_4_
  45.4 0.0 copy-done.1
  45.4 0.0 copy-done.2
  45.4 0.0 copy-done.3
  45.4 0.0 copy-done.4
  45.5 1.1 %finish.1 = (bf16[16,2,2048]{2,1,0:T(2,128)(2,1)}, bf16[16,2,512]{2,1,0:T(2,128)(2,1)}, bf16[6,16,1024]{2,1,0:T(8,128)(2,1)}) custom-call(bf16[128,2048]{1,0:T(8,128)(2,1)S(1)} %get-tuple-element.51.refs_0_, bf16[128,1024]{1,0:T(8,128)(2,1)S(1)} %get-tuple-element.52.refs_2_.refs_1_, bf16[32,3072]{1,0:T(8,128)(2,1)S(1)} %collective-permute-done.14.refs_2_, ...), custom_call_target="tpu_custom_call" | custom-call | bytes 2097152 | tf_op jit(solution)/shard_map/finish/pallas_call | solution.py:396
  (3 shorter events, 0.0 us)
Async XLA Ops:
  2.1 13.4 %collective-permute-start.2 = (bf16[2,2048,384]{2,1,0:T(8,128)(2,1)}, bf16[2,2048,384]{2,1,0:T(8,128)(2,1)S(1)}, u32[]{:S(2)}, u32[]{:S(2)}) collective-permute-start(bf16[2,2048,384]{2,1,0:T(8,128)(2,1)} %refs_1_.1), channel_id=1, source_target_pairs={{0,1},{1,0},{2,3},{3,2},{4,5},{5,4},{6,7},{7,6},{8,9},{9,8},{10,11... | collective-permute-start | bytes 9437192 | tf_op jit(solution)/shard_map/ppermute | solution.py:27
  2.6 14.9 %collective-permute-start.6 = (bf16[2,2048,384]{2,1,0:T(8,128)(2,1)}, bf16[2,2048,384]{2,1,0:T(8,128)(2,1)S(1)}, u32[]{:S(2)}, u32[]{:S(2)}) collective-permute-start(bf16[2,2048,384]{2,1,0:T(8,128)(2,1)} %refs_2_.1), channel_id=1, source_target_pairs={{0,1},{1,0},{2,3},{3,2},{4,5},{5,4},{6,7},{7,6},{8,9},{9,8},{10,11... | collective-permute-start | bytes 9437192 | tf_op jit(solution)/shard_map/ppermute | solution.py:27
  2.7 19.4 %collective-permute-start.8 = (bf16[768,2048]{1,0:T(8,128)(2,1)}, bf16[768,2048]{1,0:T(8,128)(2,1)S(1)}, u32[]{:S(2)}, u32[]{:S(2)}) collective-permute-start(bf16[768,2048]{1,0:T(8,128)(2,1)} %bitcast.13), channel_id=1, source_target_pairs={{0,1},{1,0},{2,3},{3,2},{4,5},{5,4},{6,7},{7,6},{8,9},{9,8},{10,11... | collective-permute-start | bytes 9437192 | tf_op jit(solution)/shard_map/ppermute | solution.py:27
  3.1 6.9 %collective-permute-start = (bf16[32,2176]{1,0:T(8,128)(2,1)S(1)}, bf16[32,2176]{1,0:T(8,128)(2,1)S(1)}, u32[]{:S(2)}, u32[]{:S(2)}) collective-permute-start(bf16[32,2176]{1,0:T(8,128)(2,1)S(1)} %pack.1.refs_0_), channel_id=1, source_target_pairs={{0,2},{4,0},{8,4},{12,8},{14,12},{10,14},{6,10},{2,6},{1,3},{5,1},... | collective-permute-start | bytes 417800 | tf_op jit(solution)/shard_map/ppermute | solution.py:23
  5.7 6.0 %collective-permute-start.3 = (bf16[32,2176]{1,0:T(8,128)(2,1)S(1)}, bf16[32,2176]{1,0:T(8,128)(2,1)S(1)}, u32[]{:S(2)}, u32[]{:S(2)}) collective-permute-start(bf16[32,2176]{1,0:T(8,128)(2,1)S(1)} %pack.1.refs_0_), channel_id=1, source_target_pairs={{0,4},{4,8},{8,12},{12,14},{14,10},{10,6},{6,2},{2,0},{1,5},{5,9},... | collective-permute-start | bytes 417800 | tf_op jit(solution)/shard_map/ppermute | solution.py:23
  10.0 17.0 %copy-start = (bf16[16,128,1024]{2,1,0:T(8,128)(2,1)S(1)}, bf16[16,128,1024]{2,1,0:T(8,128)(2,1)}, u32[]{:S(2)}) copy-start(bf16[16,128,1024]{2,1,0:T(8,128)(2,1)} %param.21) | copy-start | bytes 12582916
  10.1 5.4 %collective-permute-start.1 = (bf16[32,2176]{1,0:T(8,128)(2,1)S(1)}, bf16[32,2176]{1,0:T(8,128)(2,1)S(1)}, u32[]{:S(2)}, u32[]{:S(2)}) collective-permute-start(bf16[32,2176]{1,0:T(8,128)(2,1)S(1)} %collective-permute-done.refs_1_), channel_id=1, source_target_pairs={{0,2},{4,0},{8,4},{12,8},{14,12},{10,14},{6,10},{2,6},{1,3},{5,1},... | collective-permute-start | bytes 417800 | tf_op jit(solution)/shard_map/ppermute | solution.py:23
  11.8 5.3 %collective-permute-start.4 = (bf16[32,2176]{1,0:T(8,128)(2,1)S(1)}, bf16[32,2176]{1,0:T(8,128)(2,1)S(1)}, u32[]{:S(2)}, u32[]{:S(2)}) collective-permute-start(bf16[32,2176]{1,0:T(8,128)(2,1)S(1)} %collective-permute-done.3.refs_7_), channel_id=1, source_target_pairs={{0,4},{4,8},{8,12},{12,14},{14,10},{10,6},{6,2},{2,0},{1,5},{5,9},... | collective-permute-start | bytes 417800 | tf_op jit(solution)/shard_map/ppermute | solution.py:23
  15.5 5.1 %collective-permute-start.7 = (bf16[32,2176]{1,0:T(8,128)(2,1)S(1)}, bf16[32,2176]{1,0:T(8,128)(2,1)S(1)}, u32[]{:S(2)}, u32[]{:S(2)}) collective-permute-start(bf16[32,2176]{1,0:T(8,128)(2,1)S(1)} %collective-permute-done.1.refs_0_.refs_2_), channel_id=1, source_target_pairs={{0,2},{4,0},{8,4},{12,8},{14,12},{10,14},{6,10},{2,6},{1,3},{5,1},... | collective-permute-start | bytes 417800 | tf_op jit(solution)/shard_map/ppermute | solution.py:23
  17.1 5.1 %collective-permute-start.5 = (bf16[32,2176]{1,0:T(8,128)(2,1)S(1)}, bf16[32,2176]{1,0:T(8,128)(2,1)S(1)}, u32[]{:S(2)}, u32[]{:S(2)}) collective-permute-start(bf16[32,2176]{1,0:T(8,128)(2,1)S(1)} %collective-permute-done.4.refs_2_.refs_6_), channel_id=1, source_target_pairs={{0,4},{4,8},{8,12},{12,14},{14,10},{10,6},{6,2},{2,0},{1,5},{5,9},... | collective-permute-start | bytes 417800 | tf_op jit(solution)/shard_map/ppermute | solution.py:23
  20.5 6.5 %collective-permute-start.9 = (bf16[32,2176]{1,0:T(8,128)(2,1)S(1)}, bf16[32,2176]{1,0:T(8,128)(2,1)S(1)}, u32[]{:S(2)}, u32[]{:S(2)}) collective-permute-start(bf16[32,2176]{1,0:T(8,128)(2,1)S(1)} %collective-permute-done.7.refs_3_), channel_id=1, source_target_pairs={{0,2},{4,0},{8,4},{12,8},{14,12},{10,14},{6,10},{2,6},{1,3},{5,1},... | collective-permute-start | bytes 417800 | tf_op jit(solution)/shard_map/ppermute | solution.py:23
  25.0 9.1 %collective-permute-start.10 = (bf16[64,2048]{1,0:T(8,128)(2,1)S(1)}, bf16[64,2048]{1,0:T(8,128)(2,1)S(1)}, u32[]{:S(2)}, u32[]{:S(2)}) collective-permute-start(bf16[64,2048]{1,0:T(8,128)(2,1)S(1)} %get-tuple-element.43), channel_id=1, source_target_pairs={{0,4},{4,8},{8,12},{12,14},{14,10},{10,6},{6,2},{2,0},{1,5},{5,9},... | collective-permute-start | bytes 786440 | tf_op jit(solution)/shard_map/ppermute | solution.py:23
  25.4 8.6 %collective-permute-start.12 = (bf16[64,2048]{1,0:T(8,128)(2,1)S(1)}, bf16[64,2048]{1,0:T(8,128)(2,1)S(1)}, u32[]{:S(2)}, u32[]{:S(2)}) collective-permute-start(bf16[64,2048]{1,0:T(8,128)(2,1)S(1)} %get-tuple-element.44), channel_id=1, source_target_pairs={{0,2},{4,0},{8,4},{12,8},{14,12},{10,14},{6,10},{2,6},{1,3},{5,1},... | collective-permute-start | bytes 786440 | tf_op jit(solution)/shard_map/ppermute | solution.py:23
  28.1 5.9 %collective-permute-start.11 = (bf16[64,1024]{1,0:T(8,128)(2,1)S(1)}, bf16[64,1024]{1,0:T(8,128)(2,1)S(1)}, u32[]{:S(2)}, u32[]{:S(2)}) collective-permute-start(bf16[64,1024]{1,0:T(8,128)(2,1)S(1)} %get-tuple-element.48), channel_id=1, source_target_pairs={{0,4},{4,8},{8,12},{12,14},{14,10},{10,6},{6,2},{2,0},{1,5},{5,9},... | collective-permute-start | bytes 393224 | tf_op jit(solution)/shard_map/ppermute | solution.py:23
  28.7 16.7 %copy-start.1 = (bf16[1024,512]{1,0:T(8,128)(2,1)S(1)}, bf16[1024,512]{1,0:T(8,128)(2,1)}, u32[]{:S(2)}) copy-start(bf16[1024,512]{1,0:T(8,128)(2,1)} %refs_8_.1) | copy-start | bytes 3145732
  28.7 16.7 %copy-start.2 = (bf16[16,6,1024]{2,0,1:T(8,128)(2,1)S(1)}, bf16[16,6,1024]{2,0,1:T(8,128)(2,1)}, u32[]{:S(2)}) copy-start(bf16[16,6,1024]{2,0,1:T(8,128)(2,1)} %param.22) | copy-start | bytes 589828
  28.7 16.8 %copy-start.3 = (f32[7,1024]{1,0:T(8,128)S(1)}, f32[7,1024]{1,0:T(8,128)}, u32[]{:S(2)}) copy-start(f32[7,1024]{1,0:T(8,128)} %refs_6_.1) | copy-start | bytes 86020
  28.7 16.8 %copy-start.4 = (f32[1024]{0:T(1024)S(1)}, f32[1024]{0:T(1024)}, u32[]{:S(2)}) copy-start(f32[1024]{0:T(1024)} %param.24) | copy-start | bytes 12292
  28.7 5.4 %collective-permute-start.13 = (bf16[64,1024]{1,0:T(8,128)(2,1)S(1)}, bf16[64,1024]{1,0:T(8,128)(2,1)S(1)}, u32[]{:S(2)}, u32[]{:S(2)}) collective-permute-start(bf16[64,1024]{1,0:T(8,128)(2,1)S(1)} %get-tuple-element.49), channel_id=1, source_target_pairs={{0,2},{4,0},{8,4},{12,8},{14,12},{10,14},{6,10},{2,6},{1,3},{5,1},... | collective-permute-start | bytes 393224 | tf_op jit(solution)/shard_map/ppermute | solution.py:23
  34.2 7.8 %collective-permute-start.14 = (bf16[32,3072]{1,0:T(8,128)(2,1)S(1)}, bf16[32,3072]{1,0:T(8,128)(2,1)S(1)}, u32[]{:S(2)}, u32[]{:S(2)}) collective-permute-start(bf16[32,3072]{1,0:T(8,128)(2,1)S(1)} %get-tuple-element.53), channel_id=1, source_target_pairs={{0,4},{4,8},{8,12},{12,14},{14,10},{10,6},{6,2},{2,0},{1,5},{5,9},... | collective-permute-start | bytes 589832 | tf_op jit(solution)/shard_map/ppermute | solution.py:23
  35.9 9.5 %collective-permute-start.15 = (bf16[32,3072]{1,0:T(8,128)(2,1)S(1)}, bf16[32,3072]{1,0:T(8,128)(2,1)S(1)}, u32[]{:S(2)}, u32[]{:S(2)}) collective-permute-start(bf16[32,3072]{1,0:T(8,128)(2,1)S(1)} %get-tuple-element.54), channel_id=1, source_target_pairs={{0,14},{4,10},{8,6},{12,2},{14,0},{10,4},{6,8},{2,12},{1,15},{5,11... | collective-permute-start | bytes 589832 | tf_op jit(solution)/shard_map/ppermute | solution.py:23
  39.4 6.1 %collective-permute-start.16 = (bf16[32,3072]{1,0:T(8,128)(2,1)S(1)}, bf16[32,3072]{1,0:T(8,128)(2,1)S(1)}, u32[]{:S(2)}, u32[]{:S(2)}) collective-permute-start(bf16[32,3072]{1,0:T(8,128)(2,1)S(1)} %get-tuple-element.55), channel_id=1, source_target_pairs={{0,2},{4,0},{8,4},{12,8},{14,12},{10,14},{6,10},{2,6},{1,3},{5,1},... | collective-permute-start | bytes 589832 | tf_op jit(solution)/shard_map/ppermute | solution.py:23
